TPU v7x, 32 devices: a whole 2x2x4 slice. The times are simulated.
32 devices in a mesh: section: 4 (over z), tensor: 8 (over y, x, core).
Axes of the slice: x: 2, y: 2, z: 4, core: 2. Of those that a mesh axis runs over, the one named last changes fastest.
Arguments:
- text: bfloat16 [4, 256, 8192], P('section', 'tensor'), may hold values from -6 to 6
- features: bfloat16 [192, 8192], P(None, 'tensor'), may hold values from -6 to 6
- in_gain: bfloat16 [4, 8192], P('section'), may hold values from 0.5 to 1.5
- w_query: bfloat16 [4, 8192, 4096], P('section', None, 'tensor'), may hold values from -0.0625 to 0.0625
- q_gain: bfloat16 [4, 128], P('section'), may hold values from 0.099609375 to 1.8984375
- w_key_value: bfloat16 [4, 8192, 2048], P('section', 'tensor'), may hold values from -0.0625 to 0.0625
- k_gain: bfloat16 [4, 128], P('section'), may hold values from 0.099609375 to 1.8984375
- tile_count: int32 [2], replicated, may hold values from 1 to 4, as said below
- image_start: int32 [2], replicated, may hold values from 1 to 127
- grad_out: bfloat16 [4, 256, 4096], P('section', None, 'tensor'), may hold values from -6 to 6
Outputs:
- attended: bfloat16 [4, 256, 4096], P('section', None, 'tensor')
- feature_grad: float32 [192, 8192], P('section', 'tensor')
Inputs may be any that keep to these rules, and one draw needn't show every extreme that they name: `tile_count`: some sample has 4 tiles.
All inputs are finite; a program needn't handle non-finite values.
Results may differ from a plain program's by a relative error of at most 0.0089.
Values may be sent and summed in bfloat16 or wider, within the bound.
No kernel may reach another device: no remote copies, remote signals or barrier semaphores. Data moves between devices by JAX's collectives and lax.ppermute only.
A program may use at most 64 MiB of HBM per device.

v0:
```python
import functools

import jax
import jax.numpy as jnp
from jax import lax
from jax.experimental import pallas as pl
from jax.experimental.pallas import tpu as pltpu
from jax.sharding import PartitionSpec as P

KV_HEADS = 8
HEAD_DIM = 128
TILES = 4
TILE_LEN = 24
TXT_TOK = 128
MB = 2
SLOTS = TILES * TILE_LEN

eps = 1e-05

F32 = jnp.float32
BF16 = jnp.bfloat16
MIB = 1 << 20


def whole(memory=pltpu.VMEM):
    return pl.BlockSpec(memory_space=memory)


def dot_nn(a, b):
    return jnp.dot(a, b, preferred_element_type=F32)


def dot_nt(a, b):
    return lax.dot_general(a, b, (((1,), (1,)), ((), ())), preferred_element_type=F32)


def dot_tn(a, b):
    return lax.dot_general(a, b, (((0,), (0,)), ((), ())), preferred_element_type=F32)


def params(mib):
    return pltpu.CompilerParams(vmem_limit_bytes=mib * MIB)


def cost(flops, size):
    return pl.CostEstimate(flops=flops, bytes_accessed=size, transcendentals=0)


def here():
    return lax.axis_index("tensor")


def head_columns(head):
    return [
        pl.ds(pl.multiple_of((half * KV_HEADS + head) * HEAD_DIM, HEAD_DIM), HEAD_DIM)
        for half in range(2)
    ]


def kv_kernel(per_kv, pairs, odd, feat_ref, weight_ref, *refs):
    features = feat_ref[...]
    for j in range(pairs):
        head = lax.div(lax.bitwise_xor(here(), 2 * j + odd), per_kv)
        weight = jnp.concatenate([weight_ref[0, :, c] for c in head_columns(head)], axis=1)
        total = dot_nn(features, weight)
        out_ref = refs[j - pairs]
        if not odd:
            total = total + refs[j][...]
        out_ref[...] = total.astype(out_ref.dtype)


def kv_partial(features, weight, count, other=None):
    rows, depth = features.shape
    pairs = count // 2
    odd = 1 if other is None else 0
    out_shape = [
        jax.ShapeDtypeStruct((rows, 2 * HEAD_DIM), F32 if odd or j == 0 else BF16)
        for j in range(pairs)
    ]
    operands = (features, weight, *(other or ()))
    return pl.pallas_call(
        functools.partial(kv_kernel, count // KV_HEADS, pairs, odd),
        in_specs=[whole()] * len(operands),
        out_specs=[whole()] * pairs,
        out_shape=out_shape,
        compiler_params=params(24),
        cost_estimate=cost(0, 0),
        name="kv_partial_other_core" if odd else "kv_partial_own_core",
    )(*operands)


def query_kernel(shape, start, *refs):
    gain_ref, weight_ref, q_gain_ref, refs = refs[0], refs[1], refs[2], refs[3:]
    groups = []
    for parts in shape:
        groups.append(refs[:parts])
        refs = refs[parts:]
    depth, heads_width = weight_ref.shape[1:]
    width = sum(part.shape[1] for part in groups[0])
    last = start + width == depth
    span = 1024

    def columns(parts, c):
        for part in parts:
            if c < part.shape[1]:
                return part[:, c : c + span].astype(F32)
            c -= part.shape[1]

    if start:
        raw, squares, refs = refs[0][...], refs[1][:, :1], refs[2:]
    else:
        raw, squares = 0.0, 0.0
    for c in range(0, width, span):
        x = jnp.concatenate([columns(parts, c) for parts in groups], axis=0)
        squares = squares + jnp.sum(x * x, axis=-1, keepdims=True)
        cols = slice(start + c, start + c + span)
        scaled = (x * gain_ref[:, cols].astype(F32)).astype(BF16)
        raw = raw + dot_nn(scaled, weight_ref[0, cols, :])
    if not last:
        refs[0][...] = raw
        refs[1][...] = jnp.broadcast_to(squares, refs[1].shape)
        return
    out_ref = refs[0]
    inverse = lax.rsqrt(squares / depth + eps)
    q_gain = q_gain_ref[...].astype(F32)
    for c in range(0, heads_width, HEAD_DIM):
        head = raw[:, c : c + HEAD_DIM] * inverse
        q_inverse = lax.rsqrt(jnp.mean(head * head, axis=-1, keepdims=True) + eps)
        out_ref[:, c : c + HEAD_DIM] = (head * q_inverse * q_gain).astype(BF16)


def queries_of(groups, gain, weight, q_gain, name, start=0, before=()):
    arrays = [part for parts in groups for part in parts]
    rows = sum(parts[0].shape[0] for parts in groups)
    depth, heads_width = weight.shape[1:]
    last = start + sum(part.shape[1] for part in groups[0]) == depth
    if last:
        out_shape = [jax.ShapeDtypeStruct((rows, heads_width), BF16)]
    else:
        out_shape = [jax.ShapeDtypeStruct((rows, w), F32) for w in (heads_width, HEAD_DIM)]
    out = pl.pallas_call(
        functools.partial(query_kernel, [len(parts) for parts in groups], start),
        in_specs=[whole()] * (3 + len(arrays) + len(before)),
        out_specs=[whole()] * len(out_shape),
        out_shape=out_shape,
        compiler_params=params(24),
        cost_estimate=cost(0, 0),
        name=name,
    )(gain, weight, q_gain, *arrays, *before)
    return out[0] if last else out


def attention_kernel(places, count, rows, last, sizes, *refs):
    if not last:
        count_ref, start_ref, refs = refs[0], refs[1], refs[2:]
    queries_refs, refs = refs[:sizes], refs[sizes:]
    grad_ref, k_gain_ref, refs = refs[0], refs[1], refs[2:]
    narrow = rows % 16 != 0
    if narrow:
        refs, grad_rows = refs[:-1], refs[-1]
        grad_rows[...] = grad_ref[0].astype(F32)
    if last:
        d_keys_in, d_values_in, keys_ref, values_ref, hat_ref, inverse_ref, token_ref, slot_ref = refs[:8]
        att_ref, block_ref, d_keys_ref, d_values_ref = refs[8:]
        d_keys_ref[...] = d_keys_in[...]
        d_values_ref[...] = d_values_in[...]
    else:
        parts = refs[:-9]
        att_ref, d_keys_ref, d_values_ref, keys_ref, values_ref = refs[-9:-4]
        hat_ref, inverse_ref, token_ref, slot_ref = refs[-4:]
        kv = sum(part[...].astype(F32) for part in parts)
        key_raw = kv[:, :HEAD_DIM]
        inverse = lax.rsqrt(jnp.mean(key_raw * key_raw, axis=-1, keepdims=True) + eps)
        hat_ref[...] = key_raw * inverse
        inverse_ref[...] = jnp.broadcast_to(inverse, key_raw.shape)
        keys_ref[...] = (key_raw * inverse * k_gain_ref[...].astype(F32)).astype(BF16)
        values_ref[...] = kv[:, HEAD_DIM:].astype(BF16)
        d_keys_ref[...] = jnp.zeros_like(d_keys_ref)
        d_values_ref[...] = jnp.zeros_like(d_values_ref)
        for b in range(MB):
            token = lax.broadcasted_iota(jnp.int32, (TXT_TOK, HEAD_DIM), 0)
            token_ref[b * TXT_TOK : (b + 1) * TXT_TOK, :] = (token >= start_ref[b]).astype(F32)
            slot = lax.broadcasted_iota(jnp.int32, slot_ref.shape[1:], 1)
            slot_ref[b] = (slot < count_ref[b] * TILE_LEN).astype(F32)

    scale = HEAD_DIM ** (-0.5)
    heads = grad_ref.shape[2] // HEAD_DIM
    per_sample = count // MB
    mine = lax.div(here(), per_sample)
    blocks = [
        (p, ref, i * rows) for group, ref in zip(places, queries_refs) for i, p in enumerate(group)
    ]
    for far in range(MB):
        chosen = [block for block in blocks if block[0] // per_sample == far]
        if not chosen:
            continue
        sample = lax.bitwise_xor(mine, far)
        img = pl.ds(pl.multiple_of(sample * SLOTS, SLOTS), SLOTS)
        keys, values = keys_ref[img, :], values_ref[img, :]
        live = slot_ref[sample][:1, :] > 0
        spots = [
            pl.ds(pl.multiple_of(lax.bitwise_xor(here(), p) * rows, rows), rows)
            for p, _, _ in chosen
        ]
        masks = [token_ref[spot, :] for spot in spots]
        queries, upstream = [], []
        for h in range(heads):
            cols = slice(h * HEAD_DIM, (h + 1) * HEAD_DIM)
            for (p, ref, at), mask, spot in zip(chosen, masks, spots):
                queries.append(ref[at : at + rows, cols])
                grad = grad_rows[spot, cols] if narrow else grad_ref[0, spot, cols].astype(F32)
                upstream.append((grad * mask).astype(BF16))
        queries = jnp.concatenate(queries, axis=0)
        upstream = jnp.concatenate(upstream, axis=0)
        scores = dot_nt(queries, keys) * scale
        exponent = jnp.where(live, jnp.exp(scores), 0.0)
        probs = exponent * (1.0 / jnp.sum(exponent, axis=-1, keepdims=True))
        weights = probs.astype(BF16)
        head_out = dot_nn(weights, values)
        step = 0
        for h in range(heads):
            cols = slice(h * HEAD_DIM, (h + 1) * HEAD_DIM)
            for block, mask in zip(chosen, masks):
                at = blocks.index(block) * rows
                att_ref[at : at + rows, cols] = head_out[step : step + rows] * mask
                step += rows
        d_weights = dot_nt(upstream, values)
        inner = jnp.sum(probs * d_weights, axis=-1, keepdims=True)
        d_scores = (probs * (d_weights - inner) * scale).astype(BF16)
        d_keys_ref[img, :] += dot_tn(d_scores, queries)
        d_values_ref[img, :] += dot_tn(weights, upstream)
    if last:
        hat = hat_ref[...]
        scaled = d_keys_ref[...] * k_gain_ref[...].astype(F32)
        d_raw = inverse_ref[...] * (
            scaled - hat * jnp.mean(hat * scaled, axis=-1, keepdims=True)
        )
        block_ref[:, :HEAD_DIM] = d_raw.astype(BF16)
        block_ref[:, HEAD_DIM:] = d_values_ref[...].astype(BF16)


def attention(scalars, queries, places, count, grad_out, k_gain, state, last):
    rows, width = grad_out.shape[1] // count, grad_out.shape[2]
    image_rows = MB * SLOTS
    vector = jax.ShapeDtypeStruct((image_rows, HEAD_DIM), F32)
    rounded = jax.ShapeDtypeStruct((image_rows, HEAD_DIM), BF16)
    attended = jax.ShapeDtypeStruct((sum(map(len, places)) * rows, width), F32)
    scratch = []
    if last:
        out_shape = [attended, jax.ShapeDtypeStruct((image_rows, 2 * HEAD_DIM), BF16)]
        scratch += [pltpu.VMEM(vector.shape, F32)] * 2
    else:
        token = jax.ShapeDtypeStruct((grad_out.shape[1], HEAD_DIM), F32)
        slot = jax.ShapeDtypeStruct((MB, 8, SLOTS), F32)
        out_shape = [attended, vector, vector, rounded, rounded, vector, vector, token, slot]
    if rows % 16 != 0:
        scratch += [pltpu.VMEM(grad_out.shape[1:], F32)]
    operands = [*queries, grad_out, k_gain, *state]
    return pl.pallas_call(
        functools.partial(attention_kernel, places, count, rows, last, len(queries)),
        in_specs=[whole(pltpu.SMEM)] * len(scalars) + [whole()] * len(operands),
        out_specs=[whole()] * len(out_shape),
        out_shape=out_shape,
        scratch_shapes=scratch,
        compiler_params=params(24),
        cost_estimate=cost(0, 0),
        name="attention_last" if last else "attention_first",
    )(*scalars, *operands)


def assemble_kernel(places, rows, *refs):
    refs, out_ref, held = refs[:-2], refs[-2], refs[-1]
    for group, ref in zip(places, refs):
        for i, p in enumerate(group):
            at = pl.multiple_of(lax.bitwise_xor(here(), p) * rows, rows)
            held[pl.ds(at, rows), :] = ref[i * rows : (i + 1) * rows, :]
    out_ref[0] = held[...].astype(BF16)


def assemble(places, arrays, like):
    rows = arrays[0].shape[0] // len(places[0])
    return pl.pallas_call(
        functools.partial(assemble_kernel, places, rows),
        in_specs=[whole()] * len(arrays),
        out_specs=whole(),
        out_shape=jax.ShapeDtypeStruct(like.shape, BF16),
        scratch_shapes=[pltpu.VMEM(like.shape[1:], F32)],
        compiler_params=params(24),
        cost_estimate=cost(0, 0),
        name="attended_rows",
    )(*arrays)


def grad_kernel(distances, per_kv, sections, first, last, *refs):
    blocks, weight_ref, refs = refs[: len(distances)], refs[len(distances)], refs[len(distances) + 1 :]
    if not first:
        before_ref, refs = refs[0], refs[1:]
    total = refs[-1]
    image_rows, width = total.shape
    heads = []
    for i in range(0, len(distances), per_kv):
        head = lax.div(lax.bitwise_xor(here(), distances[i]), per_kv)
        if per_kv == 1:
            block = blocks[i][...]
        else:
            block = sum(b[...].astype(F32) for b in blocks[i : i + per_kv]).astype(BF16)
        heads.append((head_columns(head), block))
    span = 256
    for c in range(0, width, span):
        cols = slice(c, c + span)
        part = 0.0 if first else before_ref[:, cols]
        for columns, block in heads:
            weight = jnp.concatenate([weight_ref[0, cols, k] for k in columns], axis=1)
            part = part + dot_nt(block, weight)
        total[:, cols] = part
    if last:
        rows = image_rows // sections
        for k in range(sections):
            to = lax.rem(lax.axis_index("section") + k, sections)
            piece = total[pl.ds(pl.multiple_of(to * rows, rows), rows), :]
            refs[k][...] = piece.astype(refs[k].dtype)


def feature_gradient(blocks, weight, per_kv, sections, before=None, last=True):
    distances = [p for p, _ in blocks]
    arrays = [block for _, block in blocks]
    image_rows = arrays[0].shape[0]
    width, depth = weight.shape[1:]
    rows = image_rows // sections
    if last:
        out_shape = [
            jax.ShapeDtypeStruct((rows, width), F32 if k == 0 else BF16) for k in range(sections)
        ]
        out_specs = [whole()] * sections
        scratch = [pltpu.VMEM((image_rows, width), F32)]
    else:
        out_shape = jax.ShapeDtypeStruct((image_rows, width), F32)
        out_specs = whole()
        scratch = []
    operands = [*arrays, weight] + ([] if before is None else [before])
    return pl.pallas_call(
        functools.partial(grad_kernel, distances, per_kv, sections, before is None, last),
        in_specs=[whole()] * len(operands),
        out_specs=out_specs,
        out_shape=out_shape,
        scratch_shapes=scratch,
        compiler_params=params(24),
        cost_estimate=cost(0, 0),
        name="feature_grad_last" if last else "feature_grad_first",
    )(*operands)


def shards(
    text, features, in_gain, w_query, q_gain, w_key_value, k_gain, tile_count, image_start, grad_out
):
    count = lax.axis_size("tensor")
    sections = lax.axis_size("section")
    per_kv = count // KV_HEADS

    def swap(x, distance):
        return lax.ppermute(x, "tensor", [(i, i ^ distance) for i in range(count)])

    own_text = text[0]
    bits = [1 << b for b in range(1, count.bit_length() - 1)]
    width = own_text.shape[1] // 2
    direct = {bit: swap(own_text, bit) for bit in bits}
    def queries(blocks, name, **more):
        return queries_of(list(blocks.values()), in_gain, w_query, q_gain, name, **more)

    def both_cores(blocks):
        out = {}
        for p, x in blocks.items():
            out[p] = [x]
            out[p ^ 1] = [swap(x, 1)]
        return out

    def fast_swap(arrays):
        return [swap(x, 1) for x in arrays]

    other_heads = kv_partial(features, w_key_value, count)
    own, *outgoing = kv_partial(features, w_key_value, count, fast_swap(other_heads))
    parts = [own] + [swap(x, 2 * (j + 1)) for j, x in enumerate(outgoing)]
    direct, parts = lax.optimization_barrier((direct, parts))
    near = both_cores({0: own_text})
    q_near = queries(near, "queries_own_chip")
    forwarded = []
    for half, order in enumerate((bits, bits[::-1])):
        first = half * width
        held, passed = {0: None}, {}
        for bit in order:
            for p in list(held):
                if p == 0:
                    held[bit] = direct[bit][:, first : first + width]
                else:
                    held[p ^ bit] = passed[p ^ bit] = swap(held[p], bit)
        forwarded.append(dict(sorted(passed.items())))

    next_to = both_cores(direct)
    q_next = queries(next_to, "queries_neighbours")

    early, *state = attention(
        [tile_count, image_start],
        [q_near, q_next],
        [list(near), list(next_to)],
        count,
        grad_out,
        k_gain,
        parts,
        last=False,
    )
    first_half, state = lax.optimization_barrier((forwarded[0], state))
    far = both_cores(first_half)
    second_half, far = lax.optimization_barrier((forwarded[1], far))
    sums = queries(far, "queries_forwarded_first")
    far = both_cores(second_half)
    q_far = queries(far, "queries_forwarded_last", start=width, before=sums)
    late, block = attention([], [q_far], [list(far)], count, grad_out, k_gain, state, last=True)
    attended = assemble([list(near) + list(next_to), list(far)], [early, late], grad_out)

    blocks = {0: block}
    blocks.update({p: swap(block, p) for p in range(count - 2, 0, -2)})
    blocks.update({p ^ 1: swap(x, 1) for p, x in blocks.items()})
    before = None
    if per_kv == 1:
        soon = {p: blocks.pop(p) for p in [1, *range(0, count, 2)]}
        before = feature_gradient(sorted(soon.items()), w_key_value, per_kv, sections, last=False)
    pieces = feature_gradient(sorted(blocks.items(), reverse=True), w_key_value, per_kv, sections, before)
    feature_grad, leaving = pieces[0], pieces[1:]
    arrived = []
    for k in range(1, sections):
        perm = [(i, (i + k) % sections) for i in range(sections)]
        arrived.append(lax.ppermute(leaving[k - 1], "section", perm))
    for x in arrived:
        feature_grad = feature_grad + x.astype(F32)
    return (attended, feature_grad)


def solution(mesh):
    return jax.shard_map(
        shards,
        mesh=mesh,
        in_specs=(
            P("section", "tensor", None),
            P(None, "tensor"),
            P("section", None),
            P("section", None, "tensor"),
            P("section", None),
            P("section", "tensor", None),
            P("section", None),
            P(),
            P(),
            P("section", None, "tensor"),
        ),
        out_specs=(P("section", None, "tensor"), P("section", "tensor")),
        check_vma=False,
    )
```

profile of v0, /device:TPU:0, one launch (start us, length us, event | category | flops | bytes accessed | tf_op | source)
XLA Modules:
  0.0 57.5 jit_solution(2111064617106045328)
XLA Ops:
  0.6 3.0 %collective-permute-start.1 = (bf16[32,8192]{1,0:T(8,128)(2,1)}, bf16[32,8192]{1,0:T(8,128)(2,1)S(1)}, u32[]{:S(2)}, u32[]{:S(2)}) collective-permute-start(bf16[32,8192]{1,0:T(8,128)(2,1)} %bitcast.1), channel_id=1, source_target_pairs={{0,2},{1,3},{2,0},{3,1},{4,6},{5,7},{6,4},{7,5},{8,10},{9,11},{10,... | collective-permute-start | bytes 1572872 | tf_op jit(solution)/shard_map/ppermute | solution.py:361
  3.6 1.5 %collective-permute-start.2 = (bf16[32,8192]{1,0:T(8,128)(2,1)}, bf16[32,8192]{1,0:T(8,128)(2,1)S(1)}, u32[]{:S(2)}, u32[]{:S(2)}) collective-permute-start(bf16[32,8192]{1,0:T(8,128)(2,1)} %bitcast.2), channel_id=1, source_target_pairs={{0,4},{1,5},{2,6},{3,7},{4,0},{5,1},{6,2},{7,3},{8,12},{9,13},{10,... | collective-permute-start | bytes 1572872 | tf_op jit(solution)/shard_map/ppermute | solution.py:361
  5.2 2.2 %copy-done.1 = bf16[1,1024,2048]{2,1,0:T(8,128)(2,1)S(1)} copy-done((bf16[1,1024,2048]{2,1,0:T(8,128)(2,1)S(1)}, bf16[1,1024,2048]{2,1,0:T(8,128)(2,1)}, u32[]{:S(2)}) %copy-start.1) | copy-done | bytes 4194328
  7.4 1.0 %copy-done.3 = bf16[192,1024]{1,0:T(8,128)(2,1)S(1)} copy-done((bf16[192,1024]{1,0:T(8,128)(2,1)S(1)}, bf16[192,1024]{1,0:T(8,128)(2,1)}, u32[]{:S(2)}) %copy-start.3) | copy-done | bytes 393240
  11.2 0.9 %collective-permute-done.6.refs_3_ = f32[192,256]{1,0:T(8,128)S(1)} collective-permute-done((f32[192,256]{1,0:T(8,128)S(1)}, f32[192,256]{1,0:T(8,128)S(1)}, u32[]{:S(2)}, u32[]{:S(2)}) %collective-permute-start.6) | collective-permute-done | bytes 196640 | tf_op jit(solution)/shard_map/ppermute | solution.py:361
  14.3 2.3 %collective-permute-start.9 = (bf16[192,256]{1,0:T(8,128)(2,1)S(1)}, bf16[192,256]{1,0:T(8,128)(2,1)S(1)}, u32[]{:S(2)}, u32[]{:S(2)}) collective-permute-start(bf16[192,256]{1,0:T(8,128)(2,1)S(1)} %get-tuple-element.52), channel_id=1, source_target_pairs={{0,6},{1,7},{2,4},{3,5},{4,2},{5,3},{6,0},{7,1},{8,14},{9,15},{10,... | collective-permute-start | bytes 294920 | tf_op jit(solution)/shard_map/ppermute | solution.py:361
  16.5 1.8 %collective-permute-done.7.refs_7_ = bf16[192,256]{1,0:T(8,128)(2,1)S(1)} collective-permute-done((bf16[192,256]{1,0:T(8,128)(2,1)S(1)}, bf16[192,256]{1,0:T(8,128)(2,1)S(1)}, u32[]{:S(2)}, u32[]{:S(2)}) %collective-permute-start.7) | collective-permute-done | bytes 98336 | tf_op jit(solution)/shard_map/ppermute | solution.py:361
  18.3 3.1 %collective-permute-done.8.refs_8_ = bf16[192,256]{1,0:T(8,128)(2,1)S(1)} collective-permute-done((bf16[192,256]{1,0:T(8,128)(2,1)S(1)}, bf16[192,256]{1,0:T(8,128)(2,1)S(1)}, u32[]{:S(2)}, u32[]{:S(2)}) %collective-permute-start.8) | collective-permute-done | bytes 98336 | tf_op jit(solution)/shard_map/ppermute | solution.py:361
  22.1 1.6 %collective-permute-start.13 = (bf16[32,4096]{1,0:T(8,128)(2,1)S(1)}, bf16[32,4096]{1,0:T(8,128)(2,1)S(1)}, u32[]{:S(2)}, u32[]{:S(2)}) collective-permute-start(bf16[32,4096]{1,0:T(8,128)(2,1)S(1)} %slice.7), channel_id=1, source_target_pairs={{0,4},{1,5},{2,6},{3,7},{4,0},{5,1},{6,2},{7,3},{8,12},{9,13},{10,... | collective-permute-start | bytes 786440 | tf_op jit(solution)/shard_map/ppermute | solution.py:361
  24.3 1.7 %queries_own_chip.1.refs_2_ = bf16[64,512]{1,0:T(8,128)(2,1)S(1)} custom-call(bf16[1,8192]{1,0:T(2,128)(2,1)S(1)} %copy-done.5, bf16[1,8192,512]{2,1,0:T(8,128)(2,1)S(1)} %copy-done, bf16[1,128]{1,0:T(2,128)(2,1)S(1)} %copy-done.7, bf16[32,8192]{1,0:T(8,128)(2,1)S(1)} %bitcast.4, bf16[32,8192]{1,0:T(8,128)(2,1)S(1)} %collective-permute-done.refs_4_), custom_call_target="tpu_custom_call" | custom-call | tf_op jit(solution)/shard_map/queries_own_chip/pallas_call | solution.py:141
  26.1 1.7 %queries_neighbours.1.refs_3_ = bf16[128,512]{1,0:T(8,128)(2,1)S(1)} custom-call(bf16[1,8192]{1,0:T(2,128)(2,1)S(1)} %copy-done.5, bf16[1,8192,512]{2,1,0:T(8,128)(2,1)S(1)} %copy-done, bf16[1,128]{1,0:T(2,128)(2,1)S(1)} %copy-done.7, bf16[32,8192]{1,0:T(8,128)(2,1)S(1)} %collective-permute-done.1.refs_3_, ...), custom_call_target="tpu_custom_call" | custom-call | tf_op jit(solution)/shard_map/queries_neighbours/pallas_call | solution.py:141
  27.8 1.9 %attention_first.1 = (f32[192,512]{1,0:T(8,128)S(1)}, f32[192,128]{1,0:T(8,128)S(1)}, f32[192,128]{1,0:T(8,128)S(1)}, bf16[192,128]{1,0:T(8,128)(2,1)S(1)}, bf16...) custom-call(s32[2]{0:T(128)S(1)} %copy-done.9, ...), custom_call_target="tpu_custom_call" | custom-call | tf_op jit(solution)/shard_map/attention_first/pallas_call | solution.py:259
  30.4 1.4 %collective-permute-done.12.refs_3_ = bf16[32,4096]{1,0:T(8,128)(2,1)S(1)} collective-permute-done((bf16[32,4096]{1,0:T(8,128)(2,1)S(1)}, bf16[32,4096]{1,0:T(8,128)(2,1)S(1)}, u32[]{:S(2)}, u32[]{:S(2)}) %collective-permute-start.12) | collective-permute-done | bytes 262176 | tf_op jit(solution)/shard_map/ppermute | solution.py:361
  33.5 1.0 %queries_forwarded_last.1.refs_0_ = bf16[64,512]{1,0:T(8,128)(2,1)S(1)} custom-call(bf16[1,8192]{1,0:T(2,128)(2,1)S(1)} %copy-done.5, bf16[1,8192,512]{2,1,0:T(8,128)(2,1)S(1)} %copy-done, bf16[1,128]{1,0:T(2,128)(2,1)S(1)} %copy-done.7, bf16[32,4096]{1,0:T(8,128)(2,1)S(1)} %collective-permute-done.12.refs_3_, ...), custom_call_target="tpu_custom_call" | custom-call | tf_op jit(solution)/shard_map/queries_forwarded_last/pallas_call | solution.py:141
  35.3 1.6 %collective-permute-start.16 = (bf16[192,256]{1,0:T(8,128)(2,1)S(1)}, bf16[192,256]{1,0:T(8,128)(2,1)S(1)}, u32[]{:S(2)}, u32[]{:S(2)}) collective-permute-start(bf16[192,256]{1,0:T(8,128)(2,1)S(1)} %get-tuple-element.83.refs_0_), channel_id=1, source_target_pairs={{0,6},{1,7},{2,4},{3,5},{4,2},{5,3},{6,0},{7,1},{8,14},{9,15},{10,... | collective-permute-start | bytes 294920 | tf_op jit(solution)/shard_map/ppermute | solution.py:361
  36.9 1.1 %collective-permute-start.18 = (bf16[192,256]{1,0:T(8,128)(2,1)S(1)}, bf16[192,256]{1,0:T(8,128)(2,1)S(1)}, u32[]{:S(2)}, u32[]{:S(2)}) collective-permute-start(bf16[192,256]{1,0:T(8,128)(2,1)S(1)} %get-tuple-element.83.refs_0_), channel_id=1, source_target_pairs={{0,4},{1,5},{2,6},{3,7},{4,0},{5,1},{6,2},{7,3},{8,12},{9,13},{10,... | collective-permute-start | bytes 294920 | tf_op jit(solution)/shard_map/ppermute | solution.py:361
  38.9 2.9 %collective-permute-done.16.refs_4_ = bf16[192,256]{1,0:T(8,128)(2,1)S(1)} collective-permute-done((bf16[192,256]{1,0:T(8,128)(2,1)S(1)}, bf16[192,256]{1,0:T(8,128)(2,1)S(1)}, u32[]{:S(2)}, u32[]{:S(2)}) %collective-permute-start.16) | collective-permute-done | bytes 98336 | tf_op jit(solution)/shard_map/ppermute | solution.py:361
  41.8 1.4 %collective-permute-done.18.refs_3_ = bf16[192,256]{1,0:T(8,128)(2,1)S(1)} collective-permute-done((bf16[192,256]{1,0:T(8,128)(2,1)S(1)}, bf16[192,256]{1,0:T(8,128)(2,1)S(1)}, u32[]{:S(2)}, u32[]{:S(2)}) %collective-permute-start.18) | collective-permute-done | bytes 98336 | tf_op jit(solution)/shard_map/ppermute | solution.py:361
  43.7 1.1 %feature_grad_first.1.refs_4_ = f32[192,1024]{1,0:T(8,128)S(1)} custom-call(bf16[192,256]{1,0:T(8,128)(2,1)S(1)} %get-tuple-element.83.refs_0_, bf16[192,256]{1,0:T(8,128)(2,1)S(1)} %collective-permute-done.22.refs_1_, bf16[192,256]{1,0:T(8,128)(2,1)S(1)} %collective-permute-done.20.refs_2_, bf16[192,256]{1,0:T(8,128)(2,1)S(1)} %collective-permute-done.18.refs_3_, ...), custom_call_target="tpu_custom_call" | custom-call | tf_op jit(solution)/shard_map/feature_grad_first/pallas_call | solution.py:341
  45.7 1.6 %collective-permute-start.23 = (bf16[48,1024]{1,0:T(8,128)(2,1)S(1)}, bf16[48,1024]{1,0:T(8,128)(2,1)S(1)}, u32[]{:S(2)}, u32[]{:S(2)}) collective-permute-start(bf16[48,1024]{1,0:T(8,128)(2,1)S(1)} %get-tuple-element.85), channel_id=1, source_target_pairs={{0,8},{8,16},{16,24},{24,0},{1,9},{9,17},{17,25},{25,1},{2,10},{10... | collective-permute-start | bytes 294920 | tf_op jit(solution)/shard_map/ppermute | solution.py:432
  47.3 2.6 %collective-permute-start.24 = (bf16[48,1024]{1,0:T(8,128)(2,1)S(1)}, bf16[48,1024]{1,0:T(8,128)(2,1)S(1)}, u32[]{:S(2)}, u32[]{:S(2)}) collective-permute-start(bf16[48,1024]{1,0:T(8,128)(2,1)S(1)} %get-tuple-element.86), channel_id=1, source_target_pairs={{0,16},{8,24},{16,0},{24,8},{1,17},{9,25},{17,1},{25,9},{2,18},{10... | collective-permute-start | bytes 294920 | tf_op jit(solution)/shard_map/ppermute | solution.py:432
  49.9 1.4 %collective-permute-start.25 = (bf16[48,1024]{1,0:T(8,128)(2,1)S(1)}, bf16[48,1024]{1,0:T(8,128)(2,1)S(1)}, u32[]{:S(2)}, u32[]{:S(2)}) collective-permute-start(bf16[48,1024]{1,0:T(8,128)(2,1)S(1)} %get-tuple-element.87), channel_id=1, source_target_pairs={{0,24},{8,0},{16,8},{24,16},{1,25},{9,1},{17,9},{25,17},{2,26},{10... | collective-permute-start | bytes 294920 | tf_op jit(solution)/shard_map/ppermute | solution.py:432
  52.0 1.2 %collective-permute-done.23 = bf16[48,1024]{1,0:T(8,128)(2,1)S(1)} collective-permute-done((bf16[48,1024]{1,0:T(8,128)(2,1)S(1)}, bf16[48,1024]{1,0:T(8,128)(2,1)S(1)}, u32[]{:S(2)}, u32[]{:S(2)}) %collective-permute-start.23) | collective-permute-done | bytes 98336 | tf_op jit(solution)/shard_map/ppermute | solution.py:432
  53.2 3.6 %collective-permute-done.24 = bf16[48,1024]{1,0:T(8,128)(2,1)S(1)} collective-permute-done((bf16[48,1024]{1,0:T(8,128)(2,1)S(1)}, bf16[48,1024]{1,0:T(8,128)(2,1)S(1)}, u32[]{:S(2)}, u32[]{:S(2)}) %collective-permute-start.24) | collective-permute-done | bytes 98336 | tf_op jit(solution)/shard_map/ppermute | solution.py:432
  (64 shorter events, 13.2 us)
Async XLA Ops:
  0.6 20.8 %collective-permute-start.1 = (bf16[32,8192]{1,0:T(8,128)(2,1)}, bf16[32,8192]{1,0:T(8,128)(2,1)S(1)}, u32[]{:S(2)}, u32[]{:S(2)}) collective-permute-start(bf16[32,8192]{1,0:T(8,128)(2,1)} %bitcast.1), channel_id=1, source_target_pairs={{0,2},{1,3},{2,0},{3,1},{4,6},{5,7},{6,4},{7,5},{8,10},{9,11},{10,... | collective-permute-start | bytes 1572872 | tf_op jit(solution)/shard_map/ppermute | solution.py:361
  3.6 17.8 %collective-permute-start.2 = (bf16[32,8192]{1,0:T(8,128)(2,1)}, bf16[32,8192]{1,0:T(8,128)(2,1)S(1)}, u32[]{:S(2)}, u32[]{:S(2)}) collective-permute-start(bf16[32,8192]{1,0:T(8,128)(2,1)} %bitcast.2), channel_id=1, source_target_pairs={{0,4},{1,5},{2,6},{3,7},{4,0},{5,1},{6,2},{7,3},{8,12},{9,13},{10,... | collective-permute-start | bytes 1572872 | tf_op jit(solution)/shard_map/ppermute | solution.py:361
  9.2 1.5 %collective-permute-start.3 = (f32[192,256]{1,0:T(8,128)S(1)}, f32[192,256]{1,0:T(8,128)S(1)}, u32[]{:S(2)}, u32[]{:S(2)}) collective-permute-start(f32[192,256]{1,0:T(8,128)S(1)} %get-tuple-element.45), channel_id=1, source_target_pairs={{0,1},{1,0},{2,3},{3,2},{4,5},{5,4},{6,7},{7,6},{8,9},{9,8},{10,11... | collective-permute-start | bytes 589832 | tf_op jit(solution)/shard_map/ppermute | solution.py:361
  9.3 1.7 %collective-permute-start.4 = (f32[192,256]{1,0:T(8,128)S(1)}, f32[192,256]{1,0:T(8,128)S(1)}, u32[]{:S(2)}, u32[]{:S(2)}) collective-permute-start(f32[192,256]{1,0:T(8,128)S(1)} %get-tuple-element.46), channel_id=1, source_target_pairs={{0,1},{1,0},{2,3},{3,2},{4,5},{5,4},{6,7},{7,6},{8,9},{9,8},{10,11... | collective-permute-start | bytes 589832 | tf_op jit(solution)/shard_map/ppermute | solution.py:361
  13.0 5.3 %collective-permute-start.7 = (bf16[192,256]{1,0:T(8,128)(2,1)S(1)}, bf16[192,256]{1,0:T(8,128)(2,1)S(1)}, u32[]{:S(2)}, u32[]{:S(2)}) collective-permute-start(bf16[192,256]{1,0:T(8,128)(2,1)S(1)} %get-tuple-element.50), channel_id=1, source_target_pairs={{0,2},{1,3},{2,0},{3,1},{4,6},{5,7},{6,4},{7,5},{8,10},{9,11},{10,... | collective-permute-start | bytes 294920 | tf_op jit(solution)/shard_map/ppermute | solution.py:361
  13.8 7.6 %collective-permute-start.8 = (bf16[192,256]{1,0:T(8,128)(2,1)S(1)}, bf16[192,256]{1,0:T(8,128)(2,1)S(1)}, u32[]{:S(2)}, u32[]{:S(2)}) collective-permute-start(bf16[192,256]{1,0:T(8,128)(2,1)S(1)} %get-tuple-element.51), channel_id=1, source_target_pairs={{0,4},{1,5},{2,6},{3,7},{4,0},{5,1},{6,2},{7,3},{8,12},{9,13},{10,... | collective-permute-start | bytes 294920 | tf_op jit(solution)/shard_map/ppermute | solution.py:361
  14.3 7.2 %collective-permute-start.9 = (bf16[192,256]{1,0:T(8,128)(2,1)S(1)}, bf16[192,256]{1,0:T(8,128)(2,1)S(1)}, u32[]{:S(2)}, u32[]{:S(2)}) collective-permute-start(bf16[192,256]{1,0:T(8,128)(2,1)S(1)} %get-tuple-element.52), channel_id=1, source_target_pairs={{0,6},{1,7},{2,4},{3,5},{4,2},{5,3},{6,0},{7,1},{8,14},{9,15},{10,... | collective-permute-start | bytes 294920 | tf_op jit(solution)/shard_map/ppermute | solution.py:361
  18.3 6.0 %collective-permute-start = (bf16[32,8192]{1,0:T(8,128)(2,1)S(1)}, bf16[32,8192]{1,0:T(8,128)(2,1)S(1)}, u32[]{:S(2)}, u32[]{:S(2)}) collective-permute-start(bf16[32,8192]{1,0:T(8,128)(2,1)S(1)} %bitcast.3), channel_id=1, source_target_pairs={{0,1},{1,0},{2,3},{3,2},{4,5},{5,4},{6,7},{7,6},{8,9},{9,8},{10,11... | collective-permute-start | bytes 1572872 | tf_op jit(solution)/shard_map/ppermute | solution.py:361
  21.5 4.6 %collective-permute-start.10 = (bf16[32,8192]{1,0:T(8,128)(2,1)S(1)}, bf16[32,8192]{1,0:T(8,128)(2,1)S(1)}, u32[]{:S(2)}, u32[]{:S(2)}) collective-permute-start(bf16[32,8192]{1,0:T(8,128)(2,1)S(1)} %collective-permute-done.1.refs_3_), channel_id=1, source_target_pairs={{0,1},{1,0},{2,3},{3,2},{4,5},{5,4},{6,7},{7,6},{8,9},{9,8},{10,11... | collective-permute-start | bytes 1572872 | tf_op jit(solution)/shard_map/ppermute | solution.py:361
  21.5 4.5 %collective-permute-start.11 = (bf16[32,8192]{1,0:T(8,128)(2,1)S(1)}, bf16[32,8192]{1,0:T(8,128)(2,1)S(1)}, u32[]{:S(2)}, u32[]{:S(2)}) collective-permute-start(bf16[32,8192]{1,0:T(8,128)(2,1)S(1)} %collective-permute-done.2.refs_5_), channel_id=1, source_target_pairs={{0,1},{1,0},{2,3},{3,2},{4,5},{5,4},{6,7},{7,6},{8,9},{9,8},{10,11... | collective-permute-start | bytes 1572872 | tf_op jit(solution)/shard_map/ppermute | solution.py:361
  22.1 8.4 %collective-permute-start.13 = (bf16[32,4096]{1,0:T(8,128)(2,1)S(1)}, bf16[32,4096]{1,0:T(8,128)(2,1)S(1)}, u32[]{:S(2)}, u32[]{:S(2)}) collective-permute-start(bf16[32,4096]{1,0:T(8,128)(2,1)S(1)} %slice.7), channel_id=1, source_target_pairs={{0,4},{1,5},{2,6},{3,7},{4,0},{5,1},{6,2},{7,3},{8,12},{9,13},{10,... | collective-permute-start | bytes 786440 | tf_op jit(solution)/shard_map/ppermute | solution.py:361
  23.7 8.1 %collective-permute-start.12 = (bf16[32,4096]{1,0:T(8,128)(2,1)S(1)}, bf16[32,4096]{1,0:T(8,128)(2,1)S(1)}, u32[]{:S(2)}, u32[]{:S(2)}) collective-permute-start(bf16[32,4096]{1,0:T(8,128)(2,1)S(1)} %slice.6), channel_id=1, source_target_pairs={{0,2},{1,3},{2,0},{3,1},{4,6},{5,7},{6,4},{7,5},{8,10},{9,11},{10,... | collective-permute-start | bytes 786440 | tf_op jit(solution)/shard_map/ppermute | solution.py:361
  30.4 1.5 %collective-permute-start.14 = (bf16[32,4096]{1,0:T(8,128)(2,1)S(1)}, bf16[32,4096]{1,0:T(8,128)(2,1)S(1)}, u32[]{:S(2)}, u32[]{:S(2)}) collective-permute-start(bf16[32,4096]{1,0:T(8,128)(2,1)S(1)} %collective-permute-done.13.refs_3_), channel_id=1, source_target_pairs={{0,1},{1,0},{2,3},{3,2},{4,5},{5,4},{6,7},{7,6},{8,9},{9,8},{10,11... | collective-permute-start | bytes 786440 | tf_op jit(solution)/shard_map/ppermute | solution.py:361
  32.0 1.5 %collective-permute-start.15 = (bf16[32,4096]{1,0:T(8,128)(2,1)S(1)}, bf16[32,4096]{1,0:T(8,128)(2,1)S(1)}, u32[]{:S(2)}, u32[]{:S(2)}) collective-permute-start(bf16[32,4096]{1,0:T(8,128)(2,1)S(1)} %collective-permute-done.12.refs_3_), channel_id=1, source_target_pairs={{0,1},{1,0},{2,3},{3,2},{4,5},{5,4},{6,7},{7,6},{8,9},{9,8},{10,11... | collective-permute-start | bytes 786440 | tf_op jit(solution)/shard_map/ppermute | solution.py:361
  35.3 6.5 %collective-permute-start.16 = (bf16[192,256]{1,0:T(8,128)(2,1)S(1)}, bf16[192,256]{1,0:T(8,128)(2,1)S(1)}, u32[]{:S(2)}, u32[]{:S(2)}) collective-permute-start(bf16[192,256]{1,0:T(8,128)(2,1)S(1)} %get-tuple-element.83.refs_0_), channel_id=1, source_target_pairs={{0,6},{1,7},{2,4},{3,5},{4,2},{5,3},{6,0},{7,1},{8,14},{9,15},{10,... | collective-permute-start | bytes 294920 | tf_op jit(solution)/shard_map/ppermute | solution.py:361
  36.9 6.4 %collective-permute-start.18 = (bf16[192,256]{1,0:T(8,128)(2,1)S(1)}, bf16[192,256]{1,0:T(8,128)(2,1)S(1)}, u32[]{:S(2)}, u32[]{:S(2)}) collective-permute-start(bf16[192,256]{1,0:T(8,128)(2,1)S(1)} %get-tuple-element.83.refs_0_), channel_id=1, source_target_pairs={{0,4},{1,5},{2,6},{3,7},{4,0},{5,1},{6,2},{7,3},{8,12},{9,13},{10,... | collective-permute-start | bytes 294920 | tf_op jit(solution)/shard_map/ppermute | solution.py:361
  38.0 5.3 %collective-permute-start.20 = (bf16[192,256]{1,0:T(8,128)(2,1)S(1)}, bf16[192,256]{1,0:T(8,128)(2,1)S(1)}, u32[]{:S(2)}, u32[]{:S(2)}) collective-permute-start(bf16[192,256]{1,0:T(8,128)(2,1)S(1)} %get-tuple-element.83.refs_0_), channel_id=1, source_target_pairs={{0,2},{1,3},{2,0},{3,1},{4,6},{5,7},{6,4},{7,5},{8,10},{9,11},{10,... | collective-permute-start | bytes 294920 | tf_op jit(solution)/shard_map/ppermute | solution.py:361
  38.9 4.9 %collective-permute-start.22 = (bf16[192,256]{1,0:T(8,128)(2,1)S(1)}, bf16[192,256]{1,0:T(8,128)(2,1)S(1)}, u32[]{:S(2)}, u32[]{:S(2)}) collective-permute-start(bf16[192,256]{1,0:T(8,128)(2,1)S(1)} %get-tuple-element.83.refs_0_), channel_id=1, source_target_pairs={{0,1},{1,0},{2,3},{3,2},{4,5},{5,4},{6,7},{7,6},{8,9},{9,8},{10,11... | collective-permute-start | bytes 294920 | tf_op jit(solution)/shard_map/ppermute | solution.py:361
  41.8 3.0 %collective-permute-start.17 = (bf16[192,256]{1,0:T(8,128)(2,1)S(1)}, bf16[192,256]{1,0:T(8,128)(2,1)S(1)}, u32[]{:S(2)}, u32[]{:S(2)}) collective-permute-start(bf16[192,256]{1,0:T(8,128)(2,1)S(1)} %collective-permute-done.16.refs_4_), channel_id=1, source_target_pairs={{0,1},{1,0},{2,3},{3,2},{4,5},{5,4},{6,7},{7,6},{8,9},{9,8},{10,11... | collective-permute-start | bytes 294920 | tf_op jit(solution)/shard_map/ppermute | solution.py:361
  43.2 1.6 %collective-permute-start.19 = (bf16[192,256]{1,0:T(8,128)(2,1)S(1)}, bf16[192,256]{1,0:T(8,128)(2,1)S(1)}, u32[]{:S(2)}, u32[]{:S(2)}) collective-permute-start(bf16[192,256]{1,0:T(8,128)(2,1)S(1)} %collective-permute-done.18.refs_3_), channel_id=1, source_target_pairs={{0,1},{1,0},{2,3},{3,2},{4,5},{5,4},{6,7},{7,6},{8,9},{9,8},{10,11... | collective-permute-start | bytes 294920 | tf_op jit(solution)/shard_map/ppermute | solution.py:361
  43.3 1.5 %collective-permute-start.21 = (bf16[192,256]{1,0:T(8,128)(2,1)S(1)}, bf16[192,256]{1,0:T(8,128)(2,1)S(1)}, u32[]{:S(2)}, u32[]{:S(2)}) collective-permute-start(bf16[192,256]{1,0:T(8,128)(2,1)S(1)} %collective-permute-done.20.refs_2_), channel_id=1, source_target_pairs={{0,1},{1,0},{2,3},{3,2},{4,5},{5,4},{6,7},{7,6},{8,9},{9,8},{10,11... | collective-permute-start | bytes 294920 | tf_op jit(solution)/shard_map/ppermute | solution.py:361
  45.7 7.6 %collective-permute-start.23 = (bf16[48,1024]{1,0:T(8,128)(2,1)S(1)}, bf16[48,1024]{1,0:T(8,128)(2,1)S(1)}, u32[]{:S(2)}, u32[]{:S(2)}) collective-permute-start(bf16[48,1024]{1,0:T(8,128)(2,1)S(1)} %get-tuple-element.85), channel_id=1, source_target_pairs={{0,8},{8,16},{16,24},{24,0},{1,9},{9,17},{17,25},{25,1},{2,10},{10... | collective-permute-start | bytes 294920 | tf_op jit(solution)/shard_map/ppermute | solution.py:432
  47.3 9.5 %collective-permute-start.24 = (bf16[48,1024]{1,0:T(8,128)(2,1)S(1)}, bf16[48,1024]{1,0:T(8,128)(2,1)S(1)}, u32[]{:S(2)}, u32[]{:S(2)}) collective-permute-start(bf16[48,1024]{1,0:T(8,128)(2,1)S(1)} %get-tuple-element.86), channel_id=1, source_target_pairs={{0,16},{8,24},{16,0},{24,8},{1,17},{9,25},{17,1},{25,9},{2,18},{10... | collective-permute-start | bytes 294920 | tf_op jit(solution)/shard_map/ppermute | solution.py:432
  49.9 6.9 %collective-permute-start.25 = (bf16[48,1024]{1,0:T(8,128)(2,1)S(1)}, bf16[48,1024]{1,0:T(8,128)(2,1)S(1)}, u32[]{:S(2)}, u32[]{:S(2)}) collective-permute-start(bf16[48,1024]{1,0:T(8,128)(2,1)S(1)} %get-tuple-element.87), channel_id=1, source_target_pairs={{0,24},{8,0},{16,8},{24,16},{1,25},{9,1},{17,9},{25,17},{2,26},{10... | collective-permute-start | bytes 294920 | tf_op jit(solution)/shard_map/ppermute | solution.py:432
  (13 other events, 101.5 us)
where the time goes:
time: 57.7 us; the launch traced here: 57.5 us
  starting transfers between devices  21.3 us (37%)
  waiting for transfers between devices  19.1 us (33%)
  Pallas kernels  12.3 us (21%)
  local copies, waits for them, and re-layouts  3.26 us (6%)
  between operations  0.87 us (2%)
  other arithmetic  0.72 us (1%)
    ppermute x23, starting transfers between devices, swap(): return lax.ppermute(x, 'tensor', [(i, i ^ distance) for i in range(count)])  15.7 us
    ppermute x23, waiting for transfers between devices, swap(): return lax.ppermute(x, 'tensor', [(i, i ^ distance) for i in range(count)])  14.3 us
    ppermute x3, starting transfers between devices, shards(): arrived.append(lax.ppermute(leaving[k - 1], 'section', perm))  5.57 us
    pallas_call x4, Pallas kernels, queries_of(): pl.pallas_call(functools.partial(query_kernel, [len(parts) for parts in g...  5.25 us
    ppermute x3, waiting for transfers between devices, shards(): arrived.append(lax.ppermute(leaving[k - 1], 'section', perm))  4.81 us
    unnamed x22, local copies, waits for them, and re-layouts  3.23 us
    pallas_call x2, Pallas kernels, attention(): pl.pallas_call(functools.partial(attention_kernel, places, count, rows, l...  2.69 us
    pallas_call x2, Pallas kernels, feature_gradient(): pl.pallas_call(functools.partial(grad_kernel, distances, per_kv, sections...  1.9 us
  transfers between devices with their start and end apart: 26, of which 15 were waited for; matrix products, arithmetic and copies ran while one was open for 0% of the time, Pallas kernels for 17%

commit v1 on v0

--- a/solution.py
+++ b/solution.py
@@ -50,6 +50,19 @@
     return lax.axis_index("tensor")
 
 
+def of_core(pair):
+    even, odd = pair
+    return even if even == odd else even + lax.rem(here(), 2) * (odd - even)
+
+
+def partner_at(pair):
+    return lax.bitwise_xor(here(), of_core(pair))
+
+
+def other_core(pair):
+    return (1 ^ pair[1], 1 ^ pair[0])
+
+
 def head_columns(head):
     return [
         pl.ds(pl.multiple_of((half * KV_HEADS + head) * HEAD_DIM, HEAD_DIM), HEAD_DIM)
@@ -57,39 +70,37 @@
     ]
 
 
-def kv_kernel(per_kv, pairs, odd, feat_ref, weight_ref, *refs):
+def kv_kernel(per_kv, pairs, feat_ref, weight_ref, *refs):
     features = feat_ref[...]
-    for j in range(pairs):
-        head = lax.div(lax.bitwise_xor(here(), 2 * j + odd), per_kv)
+    for j, pair in enumerate(pairs):
+        head = lax.div(partner_at(pair), per_kv)
         weight = jnp.concatenate([weight_ref[0, :, c] for c in head_columns(head)], axis=1)
         total = dot_nn(features, weight)
-        out_ref = refs[j - pairs]
-        if not odd:
+        out_ref = refs[j - len(pairs)]
+        if len(refs) > len(pairs):
             total = total + refs[j][...]
         out_ref[...] = total.astype(out_ref.dtype)
 
 
-def kv_partial(features, weight, count, other=None):
-    rows, depth = features.shape
-    pairs = count // 2
-    odd = 1 if other is None else 0
+def kv_partial(features, weight, per_kv, pairs, other=()):
+    rows = features.shape[0]
+    operands = (features, weight, *other)
     out_shape = [
-        jax.ShapeDtypeStruct((rows, 2 * HEAD_DIM), F32 if odd or j == 0 else BF16)
-        for j in range(pairs)
+        jax.ShapeDtypeStruct((rows, 2 * HEAD_DIM), BF16 if other and j > 0 else F32)
+        for j in range(len(pairs))
     ]
-    operands = (features, weight, *(other or ()))
     return pl.pallas_call(
-        functools.partial(kv_kernel, count // KV_HEADS, pairs, odd),
+        functools.partial(kv_kernel, per_kv, pairs),
         in_specs=[whole()] * len(operands),
-        out_specs=[whole()] * pairs,
+        out_specs=[whole()] * len(pairs),
         out_shape=out_shape,
         compiler_params=params(24),
         cost_estimate=cost(0, 0),
-        name="kv_partial_other_core" if odd else "kv_partial_own_core",
+        name="kv_partial_own_core" if other else "kv_partial_other_core",
     )(*operands)
 
 
-def query_kernel(shape, start, *refs):
+def query_kernel(shape, slots, start, *refs):
     gain_ref, weight_ref, q_gain_ref, refs = refs[0], refs[1], refs[2], refs[3:]
     groups = []
     for parts in shape:
@@ -120,29 +131,42 @@
         refs[0][...] = raw
         refs[1][...] = jnp.broadcast_to(squares, refs[1].shape)
         return
-    out_ref = refs[0]
+    out_ref = refs[-1]
+    rows = groups[0][0].shape[0]
     inverse = lax.rsqrt(squares / depth + eps)
     q_gain = q_gain_ref[...].astype(F32)
     for c in range(0, heads_width, HEAD_DIM):
         head = raw[:, c : c + HEAD_DIM] * inverse
         q_inverse = lax.rsqrt(jnp.mean(head * head, axis=-1, keepdims=True) + eps)
-        out_ref[:, c : c + HEAD_DIM] = (head * q_inverse * q_gain).astype(BF16)
-
-
-def queries_of(groups, gain, weight, q_gain, name, start=0, before=()):
+        head = head * q_inverse * q_gain
+        for i, pair in enumerate(slots):
+            at = of_core(pair) * rows
+            if pair[0] != pair[1]:
+                at = pl.multiple_of(at, rows)
+            part = head[i * rows : (i + 1) * rows]
+            out_ref[pl.ds(at, rows), c : c + HEAD_DIM] = part.astype(out_ref.dtype)
+    if len(refs) > 1:
+        refs[0][...] = out_ref[...].astype(BF16)
+
+
+def queries_of(groups, slots, gain, weight, q_gain, name, start=0, before=()):
     arrays = [part for parts in groups for part in parts]
     rows = sum(parts[0].shape[0] for parts in groups)
     depth, heads_width = weight.shape[1:]
     last = start + sum(part.shape[1] for part in groups[0]) == depth
+    scratch = []
     if last:
         out_shape = [jax.ShapeDtypeStruct((rows, heads_width), BF16)]
+        if arrays[0].shape[0] % 16 != 0:
+            scratch.append(pltpu.VMEM((rows, heads_width), F32))
     else:
         out_shape = [jax.ShapeDtypeStruct((rows, w), F32) for w in (heads_width, HEAD_DIM)]
     out = pl.pallas_call(
-        functools.partial(query_kernel, [len(parts) for parts in groups], start),
+        functools.partial(query_kernel, [len(parts) for parts in groups], slots, start),
         in_specs=[whole()] * (3 + len(arrays) + len(before)),
         out_specs=[whole()] * len(out_shape),
         out_shape=out_shape,
+        scratch_shapes=scratch,
         compiler_params=params(24),
         cost_estimate=cost(0, 0),
         name=name,
@@ -291,20 +315,26 @@
     )(*arrays)
 
 
-def grad_kernel(distances, per_kv, sections, first, last, *refs):
-    blocks, weight_ref, refs = refs[: len(distances)], refs[len(distances)], refs[len(distances) + 1 :]
+def grad_kernel(pairs, per_kv, sections, first, last, *refs):
+    blocks, weight_ref, refs = refs[: len(pairs)], refs[len(pairs)], refs[len(pairs) + 1 :]
     if not first:
         before_ref, refs = refs[0], refs[1:]
+    if per_kv > 1:
+        refs, sums = refs[:-1], refs[-1]
+        sums[...] = jnp.zeros_like(sums)
     total = refs[-1]
     image_rows, width = total.shape
     heads = []
-    for i in range(0, len(distances), per_kv):
-        head = lax.div(lax.bitwise_xor(here(), distances[i]), per_kv)
+    for block, pair in zip(blocks, pairs):
+        columns = head_columns(lax.div(partner_at(pair), per_kv))
         if per_kv == 1:
-            block = blocks[i][...]
+            heads.append((columns, block[...]))
         else:
-            block = sum(b[...].astype(F32) for b in blocks[i : i + per_kv]).astype(BF16)
-        heads.append((head_columns(head), block))
+            for half, k in enumerate(columns):
+                part = block[:, half * HEAD_DIM : (half + 1) * HEAD_DIM]
+                sums[:, k] += part.astype(F32)
+    if per_kv > 1:
+        heads = [((slice(None),), sums[...].astype(BF16))]
     span = 256
     for c in range(0, width, span):
         cols = slice(c, c + span)
@@ -322,8 +352,7 @@
 
 
 def feature_gradient(blocks, weight, per_kv, sections, before=None, last=True):
-    distances = [p for p, _ in blocks]
-    arrays = [block for _, block in blocks]
+    pairs, arrays = list(blocks), list(blocks.values())
     image_rows = arrays[0].shape[0]
     width, depth = weight.shape[1:]
     rows = image_rows // sections
@@ -337,9 +366,11 @@
         out_shape = jax.ShapeDtypeStruct((image_rows, width), F32)
         out_specs = whole()
         scratch = []
+    if per_kv > 1:
+        scratch.append(pltpu.VMEM((image_rows, depth), F32))
     operands = [*arrays, weight] + ([] if before is None else [before])
     return pl.pallas_call(
-        functools.partial(grad_kernel, distances, per_kv, sections, before is None, last),
+        functools.partial(grad_kernel, pairs, per_kv, sections, before is None, last),
         in_specs=[whole()] * len(operands),
         out_specs=out_specs,
         out_shape=out_shape,
@@ -357,51 +388,66 @@
     sections = lax.axis_size("section")
     per_kv = count // KV_HEADS
 
-    def swap(x, distance):
-        return lax.ppermute(x, "tensor", [(i, i ^ distance) for i in range(count)])
+    def exchange(x, pair):
+        return lax.ppermute(x, "tensor", [(i, i ^ pair[i % 2]) for i in range(count)])
+
+    def swap(x):
+        return exchange(x, (1, 1))
+
+    bits = [1 << b for b in range(1, count.bit_length() - 1)]
+    steps = len(bits)
+
+    def distance(mask):
+        taken = [s for s in range(steps) if mask >> s & 1]
+        return sum(bits[s] for s in taken), sum(bits[steps - 1 - s] for s in taken)
+
+    masks = range(1, 1 << steps)
 
     own_text = text[0]
-    bits = [1 << b for b in range(1, count.bit_length() - 1)]
     width = own_text.shape[1] // 2
-    direct = {bit: swap(own_text, bit) for bit in bits}
-    def queries(blocks, name, **more):
-        return queries_of(list(blocks.values()), in_gain, w_query, q_gain, name, **more)
+    direct = {1 << s: exchange(own_text, distance(1 << s)) for s in range(steps)}
 
     def both_cores(blocks):
         out = {}
-        for p, x in blocks.items():
-            out[p] = [x]
-            out[p ^ 1] = [swap(x, 1)]
+        for pair, x in blocks.items():
+            out[pair] = [x]
+            out[other_core(pair)] = [swap(x)]
         return out
 
-    def fast_swap(arrays):
-        return [swap(x, 1) for x in arrays]
-
-    other_heads = kv_partial(features, w_key_value, count)
-    own, *outgoing = kv_partial(features, w_key_value, count, fast_swap(other_heads))
-    parts = [own] + [swap(x, 2 * (j + 1)) for j, x in enumerate(outgoing)]
+    def places_of(blocks):
+        return sorted(even for even, _ in blocks)
+
+    def queries(blocks, name, **more):
+        order = places_of(blocks)
+        slots = [(order.index(even), order.index(odd)) for even, odd in blocks]
+        groups = list(blocks.values())
+        return queries_of(groups, slots, in_gain, w_query, q_gain, name, **more)
+
+    kv_pairs = [distance(mask) for mask in range(1 << steps)]
+    other_heads = kv_partial(features, w_key_value, per_kv, [other_core(pair) for pair in kv_pairs])
+    other_heads = [swap(x) for x in other_heads]
+    own, *outgoing = kv_partial(features, w_key_value, per_kv, kv_pairs, other_heads)
+    parts = [own] + [exchange(x, pair) for x, pair in zip(outgoing, kv_pairs[1:])]
     direct, parts = lax.optimization_barrier((direct, parts))
-    near = both_cores({0: own_text})
+    near = both_cores({(0, 0): own_text})
     q_near = queries(near, "queries_own_chip")
     forwarded = []
-    for half, order in enumerate((bits, bits[::-1])):
-        first = half * width
-        held, passed = {0: None}, {}
-        for bit in order:
-            for p in list(held):
-                if p == 0:
-                    held[bit] = direct[bit][:, first : first + width]
-                else:
-                    held[p ^ bit] = passed[p ^ bit] = swap(held[p], bit)
-        forwarded.append(dict(sorted(passed.items())))
-
-    next_to = both_cores(direct)
+    for first in (0, width):
+        held = {mask: x[:, first : first + width] for mask, x in direct.items()}
+        passed = {}
+        for s in range(1, steps):
+            for mask in range(1, 1 << s):
+                more = mask | 1 << s
+                held[more] = passed[distance(more)] = exchange(held[mask], distance(1 << s))
+        forwarded.append(passed)
+
+    next_to = both_cores({distance(mask): x for mask, x in direct.items()})
     q_next = queries(next_to, "queries_neighbours")
 
     early, *state = attention(
         [tile_count, image_start],
         [q_near, q_next],
-        [list(near), list(next_to)],
+        [places_of(near), places_of(next_to)],
         count,
         grad_out,
         k_gain,
@@ -414,17 +460,19 @@
     sums = queries(far, "queries_forwarded_first")
     far = both_cores(second_half)
     q_far = queries(far, "queries_forwarded_last", start=width, before=sums)
-    late, block = attention([], [q_far], [list(far)], count, grad_out, k_gain, state, last=True)
-    attended = assemble([list(near) + list(next_to), list(far)], [early, late], grad_out)
-
-    blocks = {0: block}
-    blocks.update({p: swap(block, p) for p in range(count - 2, 0, -2)})
-    blocks.update({p ^ 1: swap(x, 1) for p, x in blocks.items()})
+    far = places_of(far)
+    late, block = attention([], [q_far], [far], count, grad_out, k_gain, state, last=True)
+    attended = assemble([places_of(near) + places_of(next_to), far], [early, late], grad_out)
+
+    same_core = {(0, 0): block}
+    same_core.update({distance(m): exchange(block, distance(m)) for m in reversed(masks)})
+    swapped = {other_core(pair): swap(x) for pair, x in same_core.items()}
     before = None
+    blocks = {**same_core, **swapped}
     if per_kv == 1:
-        soon = {p: blocks.pop(p) for p in [1, *range(0, count, 2)]}
-        before = feature_gradient(sorted(soon.items()), w_key_value, per_kv, sections, last=False)
-    pieces = feature_gradient(sorted(blocks.items(), reverse=True), w_key_value, per_kv, sections, before)
+        soon = {pair: blocks.pop(pair) for pair in [*same_core, (1, 1)]}
+        before = feature_gradient(soon, w_key_value, per_kv, sections, last=False)
+    pieces = feature_gradient(blocks, w_key_value, per_kv, sections, before)
     feature_grad, leaving = pieces[0], pieces[1:]
     arrived = []
     for k in range(1, sections):

time: 57.7 us -> 57 us (0.988)
  waiting for transfers between devices: 19.1 us -> 18.2 us
    ppermute x23, waiting for transfers between devices: 14.3 us -> 13.5 us  [exchange(): lax.ppermute(x, 'tensor', [(i, i ^ pair[i % 2]) for i in range(count)])]
  transfers between devices with their start and end apart: 26 -> 26, of which waited for: 15 -> 12; matrix products, arithmetic and copies ran while one was open for 0% -> 0% of each run, Pallas kernels for 17% -> 17%
where the time goes in v1:
time: 57 us; the launch traced here: 56.8 us
  starting transfers between devices  21.5 us (38%)
  waiting for transfers between devices  18.2 us (32%)
  Pallas kernels  12.2 us (21%)
  local copies, waits for them, and re-layouts  3.25 us (6%)
  between operations  0.86 us (2%)
  other arithmetic  0.72 us (1%)
    ppermute x23, starting transfers between devices, exchange(): lax.ppermute(x, 'tensor', [(i, i ^ pair[i % 2]) for i in range(count)])  15.8 us
    ppermute x23, waiting for transfers between devices, exchange(): lax.ppermute(x, 'tensor', [(i, i ^ pair[i % 2]) for i in range(count)])  13.5 us
    ppermute x3, starting transfers between devices, shards(): arrived.append(lax.ppermute(leaving[k - 1], 'section', perm))  5.72 us
    pallas_call x4, Pallas kernels, queries_of(): pl.pallas_call(functools.partial(query_kernel, [len(parts) for parts in g...  5.26 us
    ppermute x3, waiting for transfers between devices, shards(): arrived.append(lax.ppermute(leaving[k - 1], 'section', perm))  4.77 us
    unnamed x22, local copies, waits for them, and re-layouts  3.22 us
    pallas_call x2, Pallas kernels, attention(): pl.pallas_call(functools.partial(attention_kernel, places, count, rows, l...  2.69 us
    pallas_call x2, Pallas kernels, feature_gradient(): pl.pallas_call(functools.partial(grad_kernel, pairs, per_kv, sections, be...  1.89 us
  transfers between devices with their start and end apart: 26, of which 12 were waited for; matrix products, arithmetic and copies ran while one was open for 0% of the time, Pallas kernels for 17%

profile of v1, /device:TPU:0, one launch (start us, length us, event | category | flops | bytes accessed | tf_op | source)
XLA Modules:
  0.0 56.8 jit_solution(6522534730893198043)
XLA Ops:
  0.6 3.0 %collective-permute-start.1 = (bf16[32,8192]{1,0:T(8,128)(2,1)}, bf16[32,8192]{1,0:T(8,128)(2,1)S(1)}, u32[]{:S(2)}, u32[]{:S(2)}) collective-permute-start(bf16[32,8192]{1,0:T(8,128)(2,1)} %bitcast.1), channel_id=1, source_target_pairs={{0,2},{1,5},{2,0},{3,7},{4,6},{5,1},{6,4},{7,3},{8,10},{9,13},{10,... | collective-permute-start | bytes 1572872 | tf_op jit(solution)/shard_map/ppermute | solution.py:392
  3.6 1.5 %collective-permute-start.2 = (bf16[32,8192]{1,0:T(8,128)(2,1)}, bf16[32,8192]{1,0:T(8,128)(2,1)S(1)}, u32[]{:S(2)}, u32[]{:S(2)}) collective-permute-start(bf16[32,8192]{1,0:T(8,128)(2,1)} %bitcast.2), channel_id=1, source_target_pairs={{0,4},{1,3},{2,6},{3,1},{4,0},{5,7},{6,2},{7,5},{8,12},{9,11},{10,... | collective-permute-start | bytes 1572872 | tf_op jit(solution)/shard_map/ppermute | solution.py:392
  5.2 2.2 %copy-done.1 = bf16[1,1024,2048]{2,1,0:T(8,128)(2,1)S(1)} copy-done((bf16[1,1024,2048]{2,1,0:T(8,128)(2,1)S(1)}, bf16[1,1024,2048]{2,1,0:T(8,128)(2,1)}, u32[]{:S(2)}) %copy-start.1) | copy-done | bytes 4194328
  7.4 1.0 %copy-done.3 = bf16[192,1024]{1,0:T(8,128)(2,1)S(1)} copy-done((bf16[192,1024]{1,0:T(8,128)(2,1)S(1)}, bf16[192,1024]{1,0:T(8,128)(2,1)}, u32[]{:S(2)}) %copy-start.3) | copy-done | bytes 393240
  11.2 0.9 %collective-permute-done.6.refs_3_ = f32[192,256]{1,0:T(8,128)S(1)} collective-permute-done((f32[192,256]{1,0:T(8,128)S(1)}, f32[192,256]{1,0:T(8,128)S(1)}, u32[]{:S(2)}, u32[]{:S(2)}) %collective-permute-start.6) | collective-permute-done | bytes 196640 | tf_op jit(solution)/shard_map/ppermute | solution.py:392
  14.2 2.3 %collective-permute-start.9 = (bf16[192,256]{1,0:T(8,128)(2,1)S(1)}, bf16[192,256]{1,0:T(8,128)(2,1)S(1)}, u32[]{:S(2)}, u32[]{:S(2)}) collective-permute-start(bf16[192,256]{1,0:T(8,128)(2,1)S(1)} %get-tuple-element.52), channel_id=1, source_target_pairs={{0,6},{1,7},{2,4},{3,5},{4,2},{5,3},{6,0},{7,1},{8,14},{9,15},{10,... | collective-permute-start | bytes 294920 | tf_op jit(solution)/shard_map/ppermute | solution.py:392
  16.5 2.2 %collective-permute-done.7.refs_7_ = bf16[192,256]{1,0:T(8,128)(2,1)S(1)} collective-permute-done((bf16[192,256]{1,0:T(8,128)(2,1)S(1)}, bf16[192,256]{1,0:T(8,128)(2,1)S(1)}, u32[]{:S(2)}, u32[]{:S(2)}) %collective-permute-start.7) | collective-permute-done | bytes 98336 | tf_op jit(solution)/shard_map/ppermute | solution.py:392
  18.8 2.5 %collective-permute-done.9.refs_9_ = bf16[192,256]{1,0:T(8,128)(2,1)S(1)} collective-permute-done((bf16[192,256]{1,0:T(8,128)(2,1)S(1)}, bf16[192,256]{1,0:T(8,128)(2,1)S(1)}, u32[]{:S(2)}, u32[]{:S(2)}) %collective-permute-start.9) | collective-permute-done | bytes 98336 | tf_op jit(solution)/shard_map/ppermute | solution.py:392
  21.8 1.1 %collective-permute-start.13 = (bf16[32,4096]{1,0:T(8,128)(2,1)S(1)}, bf16[32,4096]{1,0:T(8,128)(2,1)S(1)}, u32[]{:S(2)}, u32[]{:S(2)}) collective-permute-start(bf16[32,4096]{1,0:T(8,128)(2,1)S(1)} %get-tuple-element.88), channel_id=1, source_target_pairs={{0,4},{1,3},{2,6},{3,1},{4,0},{5,7},{6,2},{7,5},{8,12},{9,11},{10,... | collective-permute-start | bytes 786440 | tf_op jit(solution)/shard_map/ppermute | solution.py:392
  22.9 1.1 %collective-permute-start.12 = (bf16[32,4096]{1,0:T(8,128)(2,1)S(1)}, bf16[32,4096]{1,0:T(8,128)(2,1)S(1)}, u32[]{:S(2)}, u32[]{:S(2)}) collective-permute-start(bf16[32,4096]{1,0:T(8,128)(2,1)S(1)} %get-tuple-element.89), channel_id=1, source_target_pairs={{0,4},{1,3},{2,6},{3,1},{4,0},{5,7},{6,2},{7,5},{8,12},{9,11},{10,... | collective-permute-start | bytes 786440 | tf_op jit(solution)/shard_map/ppermute | solution.py:392
  24.0 1.7 %queries_own_chip.1.refs_2_ = bf16[64,512]{1,0:T(8,128)(2,1)S(1)} custom-call(bf16[1,8192]{1,0:T(2,128)(2,1)S(1)} %copy-done.5, bf16[1,8192,512]{2,1,0:T(8,128)(2,1)S(1)} %copy-done, bf16[1,128]{1,0:T(2,128)(2,1)S(1)} %copy-done.7, bf16[32,8192]{1,0:T(8,128)(2,1)S(1)} %bitcast.4, bf16[32,8192]{1,0:T(8,128)(2,1)S(1)} %collective-permute-done.refs_4_), custom_call_target="tpu_custom_call" | custom-call | tf_op jit(solution)/shard_map/queries_own_chip/pallas_call | solution.py:164
  25.8 1.7 %queries_neighbours.1.refs_3_ = bf16[128,512]{1,0:T(8,128)(2,1)S(1)} custom-call(bf16[1,8192]{1,0:T(2,128)(2,1)S(1)} %copy-done.5, bf16[1,8192,512]{2,1,0:T(8,128)(2,1)S(1)} %copy-done, bf16[1,128]{1,0:T(2,128)(2,1)S(1)} %copy-done.7, bf16[32,8192]{1,0:T(8,128)(2,1)S(1)} %collective-permute-done.1.refs_3_, ...), custom_call_target="tpu_custom_call" | custom-call | tf_op jit(solution)/shard_map/queries_neighbours/pallas_call | solution.py:164
  27.5 1.9 %attention_first.1 = (f32[192,512]{1,0:T(8,128)S(1)}, f32[192,128]{1,0:T(8,128)S(1)}, f32[192,128]{1,0:T(8,128)S(1)}, bf16[192,128]{1,0:T(8,128)(2,1)S(1)}, bf16...) custom-call(s32[2]{0:T(128)S(1)} %copy-done.9, ...), custom_call_target="tpu_custom_call" | custom-call | tf_op jit(solution)/shard_map/attention_first/pallas_call | solution.py:283
  29.5 1.6 %collective-permute-done.12.refs_3_ = bf16[32,4096]{1,0:T(8,128)(2,1)S(1)} collective-permute-done((bf16[32,4096]{1,0:T(8,128)(2,1)S(1)}, bf16[32,4096]{1,0:T(8,128)(2,1)S(1)}, u32[]{:S(2)}, u32[]{:S(2)}) %collective-permute-start.12) | collective-permute-done | bytes 262176 | tf_op jit(solution)/shard_map/ppermute | solution.py:392
  32.6 1.0 %queries_forwarded_last.1.refs_0_ = bf16[64,512]{1,0:T(8,128)(2,1)S(1)} custom-call(bf16[1,8192]{1,0:T(2,128)(2,1)S(1)} %copy-done.5, bf16[1,8192,512]{2,1,0:T(8,128)(2,1)S(1)} %copy-done, bf16[1,128]{1,0:T(2,128)(2,1)S(1)} %copy-done.7, bf16[32,4096]{1,0:T(8,128)(2,1)S(1)} %collective-permute-done.12.refs_3_, ...), custom_call_target="tpu_custom_call" | custom-call | tf_op jit(solution)/shard_map/queries_forwarded_last/pallas_call | solution.py:164
  34.4 2.4 %collective-permute-start.16 = (bf16[192,256]{1,0:T(8,128)(2,1)S(1)}, bf16[192,256]{1,0:T(8,128)(2,1)S(1)}, u32[]{:S(2)}, u32[]{:S(2)}) collective-permute-start(bf16[192,256]{1,0:T(8,128)(2,1)S(1)} %get-tuple-element.83.refs_0_), channel_id=1, source_target_pairs={{0,6},{1,7},{2,4},{3,5},{4,2},{5,3},{6,0},{7,1},{8,14},{9,15},{10,... | collective-permute-start | bytes 294920 | tf_op jit(solution)/shard_map/ppermute | solution.py:392
  38.0 3.0 %collective-permute-done.16.refs_1_ = bf16[192,256]{1,0:T(8,128)(2,1)S(1)} collective-permute-done((bf16[192,256]{1,0:T(8,128)(2,1)S(1)}, bf16[192,256]{1,0:T(8,128)(2,1)S(1)}, u32[]{:S(2)}, u32[]{:S(2)}) %collective-permute-start.16) | collective-permute-done | bytes 98336 | tf_op jit(solution)/shard_map/ppermute | solution.py:392
  41.0 1.4 %collective-permute-done.18.refs_2_ = bf16[192,256]{1,0:T(8,128)(2,1)S(1)} collective-permute-done((bf16[192,256]{1,0:T(8,128)(2,1)S(1)}, bf16[192,256]{1,0:T(8,128)(2,1)S(1)}, u32[]{:S(2)}, u32[]{:S(2)}) %collective-permute-start.18) | collective-permute-done | bytes 98336 | tf_op jit(solution)/shard_map/ppermute | solution.py:392
  42.9 1.1 %feature_grad_first.1.refs_4_ = f32[192,1024]{1,0:T(8,128)S(1)} custom-call(bf16[192,256]{1,0:T(8,128)(2,1)S(1)} %get-tuple-element.83.refs_0_, bf16[192,256]{1,0:T(8,128)(2,1)S(1)} %collective-permute-done.16.refs_1_, bf16[192,256]{1,0:T(8,128)(2,1)S(1)} %collective-permute-done.18.refs_2_, bf16[192,256]{1,0:T(8,128)(2,1)S(1)} %collective-permute-done.20.refs_3_, ...), custom_call_target="tpu_custom_call" | custom-call | tf_op jit(solution)/shard_map/feature_grad_first/pallas_call | solution.py:372
  44.8 1.8 %collective-permute-start.23 = (bf16[48,1024]{1,0:T(8,128)(2,1)S(1)}, bf16[48,1024]{1,0:T(8,128)(2,1)S(1)}, u32[]{:S(2)}, u32[]{:S(2)}) collective-permute-start(bf16[48,1024]{1,0:T(8,128)(2,1)S(1)} %get-tuple-element.85), channel_id=1, source_target_pairs={{0,8},{8,16},{16,24},{24,0},{1,9},{9,17},{17,25},{25,1},{2,10},{10... | collective-permute-start | bytes 294920 | tf_op jit(solution)/shard_map/ppermute | solution.py:480
  46.6 2.6 %collective-permute-start.24 = (bf16[48,1024]{1,0:T(8,128)(2,1)S(1)}, bf16[48,1024]{1,0:T(8,128)(2,1)S(1)}, u32[]{:S(2)}, u32[]{:S(2)}) collective-permute-start(bf16[48,1024]{1,0:T(8,128)(2,1)S(1)} %get-tuple-element.86), channel_id=1, source_target_pairs={{0,16},{8,24},{16,0},{24,8},{1,17},{9,25},{17,1},{25,9},{2,18},{10... | collective-permute-start | bytes 294920 | tf_op jit(solution)/shard_map/ppermute | solution.py:480
  49.2 1.3 %collective-permute-start.25 = (bf16[48,1024]{1,0:T(8,128)(2,1)S(1)}, bf16[48,1024]{1,0:T(8,128)(2,1)S(1)}, u32[]{:S(2)}, u32[]{:S(2)}) collective-permute-start(bf16[48,1024]{1,0:T(8,128)(2,1)S(1)} %get-tuple-element.87), channel_id=1, source_target_pairs={{0,24},{8,0},{16,8},{24,16},{1,25},{9,1},{17,9},{25,17},{2,26},{10... | collective-permute-start | bytes 294920 | tf_op jit(solution)/shard_map/ppermute | solution.py:480
  51.3 1.1 %collective-permute-done.23 = bf16[48,1024]{1,0:T(8,128)(2,1)S(1)} collective-permute-done((bf16[48,1024]{1,0:T(8,128)(2,1)S(1)}, bf16[48,1024]{1,0:T(8,128)(2,1)S(1)}, u32[]{:S(2)}, u32[]{:S(2)}) %collective-permute-start.23) | collective-permute-done | bytes 98336 | tf_op jit(solution)/shard_map/ppermute | solution.py:480
  52.3 3.7 %collective-permute-done.24 = bf16[48,1024]{1,0:T(8,128)(2,1)S(1)} collective-permute-done((bf16[48,1024]{1,0:T(8,128)(2,1)S(1)}, bf16[48,1024]{1,0:T(8,128)(2,1)S(1)}, u32[]{:S(2)}, u32[]{:S(2)}) %collective-permute-start.24) | collective-permute-done | bytes 98336 | tf_op jit(solution)/shard_map/ppermute | solution.py:480
  (63 shorter events, 11.9 us)
Async XLA Ops:
  0.6 20.6 %collective-permute-start.1 = (bf16[32,8192]{1,0:T(8,128)(2,1)}, bf16[32,8192]{1,0:T(8,128)(2,1)S(1)}, u32[]{:S(2)}, u32[]{:S(2)}) collective-permute-start(bf16[32,8192]{1,0:T(8,128)(2,1)} %bitcast.1), channel_id=1, source_target_pairs={{0,2},{1,5},{2,0},{3,7},{4,6},{5,1},{6,4},{7,3},{8,10},{9,13},{10,... | collective-permute-start | bytes 1572872 | tf_op jit(solution)/shard_map/ppermute | solution.py:392
  3.6 17.6 %collective-permute-start.2 = (bf16[32,8192]{1,0:T(8,128)(2,1)}, bf16[32,8192]{1,0:T(8,128)(2,1)S(1)}, u32[]{:S(2)}, u32[]{:S(2)}) collective-permute-start(bf16[32,8192]{1,0:T(8,128)(2,1)} %bitcast.2), channel_id=1, source_target_pairs={{0,4},{1,3},{2,6},{3,1},{4,0},{5,7},{6,2},{7,5},{8,12},{9,11},{10,... | collective-permute-start | bytes 1572872 | tf_op jit(solution)/shard_map/ppermute | solution.py:392
  9.2 1.5 %collective-permute-start.3 = (f32[192,256]{1,0:T(8,128)S(1)}, f32[192,256]{1,0:T(8,128)S(1)}, u32[]{:S(2)}, u32[]{:S(2)}) collective-permute-start(f32[192,256]{1,0:T(8,128)S(1)} %get-tuple-element.45), channel_id=1, source_target_pairs={{0,1},{1,0},{2,3},{3,2},{4,5},{5,4},{6,7},{7,6},{8,9},{9,8},{10,11... | collective-permute-start | bytes 589832 | tf_op jit(solution)/shard_map/ppermute | solution.py:392
  9.3 1.7 %collective-permute-start.4 = (f32[192,256]{1,0:T(8,128)S(1)}, f32[192,256]{1,0:T(8,128)S(1)}, u32[]{:S(2)}, u32[]{:S(2)}) collective-permute-start(f32[192,256]{1,0:T(8,128)S(1)} %get-tuple-element.46), channel_id=1, source_target_pairs={{0,1},{1,0},{2,3},{3,2},{4,5},{5,4},{6,7},{7,6},{8,9},{9,8},{10,11... | collective-permute-start | bytes 589832 | tf_op jit(solution)/shard_map/ppermute | solution.py:392
  12.9 5.8 %collective-permute-start.7 = (bf16[192,256]{1,0:T(8,128)(2,1)S(1)}, bf16[192,256]{1,0:T(8,128)(2,1)S(1)}, u32[]{:S(2)}, u32[]{:S(2)}) collective-permute-start(bf16[192,256]{1,0:T(8,128)(2,1)S(1)} %get-tuple-element.50), channel_id=1, source_target_pairs={{0,2},{1,5},{2,0},{3,7},{4,6},{5,1},{6,4},{7,3},{8,10},{9,13},{10,... | collective-permute-start | bytes 294920 | tf_op jit(solution)/shard_map/ppermute | solution.py:392
  13.8 5.0 %collective-permute-start.8 = (bf16[192,256]{1,0:T(8,128)(2,1)S(1)}, bf16[192,256]{1,0:T(8,128)(2,1)S(1)}, u32[]{:S(2)}, u32[]{:S(2)}) collective-permute-start(bf16[192,256]{1,0:T(8,128)(2,1)S(1)} %get-tuple-element.51), channel_id=1, source_target_pairs={{0,4},{1,3},{2,6},{3,1},{4,0},{5,7},{6,2},{7,5},{8,12},{9,11},{10,... | collective-permute-start | bytes 294920 | tf_op jit(solution)/shard_map/ppermute | solution.py:392
  14.2 7.1 %collective-permute-start.9 = (bf16[192,256]{1,0:T(8,128)(2,1)S(1)}, bf16[192,256]{1,0:T(8,128)(2,1)S(1)}, u32[]{:S(2)}, u32[]{:S(2)}) collective-permute-start(bf16[192,256]{1,0:T(8,128)(2,1)S(1)} %get-tuple-element.52), channel_id=1, source_target_pairs={{0,6},{1,7},{2,4},{3,5},{4,2},{5,3},{6,0},{7,1},{8,14},{9,15},{10,... | collective-permute-start | bytes 294920 | tf_op jit(solution)/shard_map/ppermute | solution.py:392
  18.7 5.3 %collective-permute-start = (bf16[32,8192]{1,0:T(8,128)(2,1)S(1)}, bf16[32,8192]{1,0:T(8,128)(2,1)S(1)}, u32[]{:S(2)}, u32[]{:S(2)}) collective-permute-start(bf16[32,8192]{1,0:T(8,128)(2,1)S(1)} %bitcast.3), channel_id=1, source_target_pairs={{0,1},{1,0},{2,3},{3,2},{4,5},{5,4},{6,7},{7,6},{8,9},{9,8},{10,11... | collective-permute-start | bytes 1572872 | tf_op jit(solution)/shard_map/ppermute | solution.py:392
  21.3 4.5 %collective-permute-start.10 = (bf16[32,8192]{1,0:T(8,128)(2,1)S(1)}, bf16[32,8192]{1,0:T(8,128)(2,1)S(1)}, u32[]{:S(2)}, u32[]{:S(2)}) collective-permute-start(bf16[32,8192]{1,0:T(8,128)(2,1)S(1)} %collective-permute-done.1.refs_3_), channel_id=1, source_target_pairs={{0,1},{1,0},{2,3},{3,2},{4,5},{5,4},{6,7},{7,6},{8,9},{9,8},{10,11... | collective-permute-start | bytes 1572872 | tf_op jit(solution)/shard_map/ppermute | solution.py:392
  21.3 4.5 %collective-permute-start.11 = (bf16[32,8192]{1,0:T(8,128)(2,1)S(1)}, bf16[32,8192]{1,0:T(8,128)(2,1)S(1)}, u32[]{:S(2)}, u32[]{:S(2)}) collective-permute-start(bf16[32,8192]{1,0:T(8,128)(2,1)S(1)} %collective-permute-done.2.refs_5_), channel_id=1, source_target_pairs={{0,1},{1,0},{2,3},{3,2},{4,5},{5,4},{6,7},{7,6},{8,9},{9,8},{10,11... | collective-permute-start | bytes 1572872 | tf_op jit(solution)/shard_map/ppermute | solution.py:392
  21.8 7.6 %collective-permute-start.13 = (bf16[32,4096]{1,0:T(8,128)(2,1)S(1)}, bf16[32,4096]{1,0:T(8,128)(2,1)S(1)}, u32[]{:S(2)}, u32[]{:S(2)}) collective-permute-start(bf16[32,4096]{1,0:T(8,128)(2,1)S(1)} %get-tuple-element.88), channel_id=1, source_target_pairs={{0,4},{1,3},{2,6},{3,1},{4,0},{5,7},{6,2},{7,5},{8,12},{9,11},{10,... | collective-permute-start | bytes 786440 | tf_op jit(solution)/shard_map/ppermute | solution.py:392
  22.9 8.1 %collective-permute-start.12 = (bf16[32,4096]{1,0:T(8,128)(2,1)S(1)}, bf16[32,4096]{1,0:T(8,128)(2,1)S(1)}, u32[]{:S(2)}, u32[]{:S(2)}) collective-permute-start(bf16[32,4096]{1,0:T(8,128)(2,1)S(1)} %get-tuple-element.89), channel_id=1, source_target_pairs={{0,4},{1,3},{2,6},{3,1},{4,0},{5,7},{6,2},{7,5},{8,12},{9,11},{10,... | collective-permute-start | bytes 786440 | tf_op jit(solution)/shard_map/ppermute | solution.py:392
  29.4 1.7 %collective-permute-start.14 = (bf16[32,4096]{1,0:T(8,128)(2,1)S(1)}, bf16[32,4096]{1,0:T(8,128)(2,1)S(1)}, u32[]{:S(2)}, u32[]{:S(2)}) collective-permute-start(bf16[32,4096]{1,0:T(8,128)(2,1)S(1)} %collective-permute-done.13.refs_3_), channel_id=1, source_target_pairs={{0,1},{1,0},{2,3},{3,2},{4,5},{5,4},{6,7},{7,6},{8,9},{9,8},{10,11... | collective-permute-start | bytes 786440 | tf_op jit(solution)/shard_map/ppermute | solution.py:392
  31.1 1.5 %collective-permute-start.15 = (bf16[32,4096]{1,0:T(8,128)(2,1)S(1)}, bf16[32,4096]{1,0:T(8,128)(2,1)S(1)}, u32[]{:S(2)}, u32[]{:S(2)}) collective-permute-start(bf16[32,4096]{1,0:T(8,128)(2,1)S(1)} %collective-permute-done.12.refs_3_), channel_id=1, source_target_pairs={{0,1},{1,0},{2,3},{3,2},{4,5},{5,4},{6,7},{7,6},{8,9},{9,8},{10,11... | collective-permute-start | bytes 786440 | tf_op jit(solution)/shard_map/ppermute | solution.py:392
  34.4 6.5 %collective-permute-start.16 = (bf16[192,256]{1,0:T(8,128)(2,1)S(1)}, bf16[192,256]{1,0:T(8,128)(2,1)S(1)}, u32[]{:S(2)}, u32[]{:S(2)}) collective-permute-start(bf16[192,256]{1,0:T(8,128)(2,1)S(1)} %get-tuple-element.83.refs_0_), channel_id=1, source_target_pairs={{0,6},{1,7},{2,4},{3,5},{4,2},{5,3},{6,0},{7,1},{8,14},{9,15},{10,... | collective-permute-start | bytes 294920 | tf_op jit(solution)/shard_map/ppermute | solution.py:392
  36.9 5.5 %collective-permute-start.18 = (bf16[192,256]{1,0:T(8,128)(2,1)S(1)}, bf16[192,256]{1,0:T(8,128)(2,1)S(1)}, u32[]{:S(2)}, u32[]{:S(2)}) collective-permute-start(bf16[192,256]{1,0:T(8,128)(2,1)S(1)} %get-tuple-element.83.refs_0_), channel_id=1, source_target_pairs={{0,4},{1,3},{2,6},{3,1},{4,0},{5,7},{6,2},{7,5},{8,12},{9,11},{10,... | collective-permute-start | bytes 294920 | tf_op jit(solution)/shard_map/ppermute | solution.py:392
  37.6 4.7 %collective-permute-start.20 = (bf16[192,256]{1,0:T(8,128)(2,1)S(1)}, bf16[192,256]{1,0:T(8,128)(2,1)S(1)}, u32[]{:S(2)}, u32[]{:S(2)}) collective-permute-start(bf16[192,256]{1,0:T(8,128)(2,1)S(1)} %get-tuple-element.83.refs_0_), channel_id=1, source_target_pairs={{0,2},{1,5},{2,0},{3,7},{4,6},{5,1},{6,4},{7,3},{8,10},{9,13},{10,... | collective-permute-start | bytes 294920 | tf_op jit(solution)/shard_map/ppermute | solution.py:392
  38.0 4.9 %collective-permute-start.22 = (bf16[192,256]{1,0:T(8,128)(2,1)S(1)}, bf16[192,256]{1,0:T(8,128)(2,1)S(1)}, u32[]{:S(2)}, u32[]{:S(2)}) collective-permute-start(bf16[192,256]{1,0:T(8,128)(2,1)S(1)} %get-tuple-element.83.refs_0_), channel_id=1, source_target_pairs={{0,1},{1,0},{2,3},{3,2},{4,5},{5,4},{6,7},{7,6},{8,9},{9,8},{10,11... | collective-permute-start | bytes 294920 | tf_op jit(solution)/shard_map/ppermute | solution.py:392
  41.0 2.9 %collective-permute-start.17 = (bf16[192,256]{1,0:T(8,128)(2,1)S(1)}, bf16[192,256]{1,0:T(8,128)(2,1)S(1)}, u32[]{:S(2)}, u32[]{:S(2)}) collective-permute-start(bf16[192,256]{1,0:T(8,128)(2,1)S(1)} %collective-permute-done.16.refs_1_), channel_id=1, source_target_pairs={{0,1},{1,0},{2,3},{3,2},{4,5},{5,4},{6,7},{7,6},{8,9},{9,8},{10,11... | collective-permute-start | bytes 294920 | tf_op jit(solution)/shard_map/ppermute | solution.py:392
  42.3 1.6 %collective-permute-start.19 = (bf16[192,256]{1,0:T(8,128)(2,1)S(1)}, bf16[192,256]{1,0:T(8,128)(2,1)S(1)}, u32[]{:S(2)}, u32[]{:S(2)}) collective-permute-start(bf16[192,256]{1,0:T(8,128)(2,1)S(1)} %collective-permute-done.18.refs_2_), channel_id=1, source_target_pairs={{0,1},{1,0},{2,3},{3,2},{4,5},{5,4},{6,7},{7,6},{8,9},{9,8},{10,11... | collective-permute-start | bytes 294920 | tf_op jit(solution)/shard_map/ppermute | solution.py:392
  42.3 1.6 %collective-permute-start.21 = (bf16[192,256]{1,0:T(8,128)(2,1)S(1)}, bf16[192,256]{1,0:T(8,128)(2,1)S(1)}, u32[]{:S(2)}, u32[]{:S(2)}) collective-permute-start(bf16[192,256]{1,0:T(8,128)(2,1)S(1)} %collective-permute-done.20.refs_3_), channel_id=1, source_target_pairs={{0,1},{1,0},{2,3},{3,2},{4,5},{5,4},{6,7},{7,6},{8,9},{9,8},{10,11... | collective-permute-start | bytes 294920 | tf_op jit(solution)/shard_map/ppermute | solution.py:392
  44.8 7.6 %collective-permute-start.23 = (bf16[48,1024]{1,0:T(8,128)(2,1)S(1)}, bf16[48,1024]{1,0:T(8,128)(2,1)S(1)}, u32[]{:S(2)}, u32[]{:S(2)}) collective-permute-start(bf16[48,1024]{1,0:T(8,128)(2,1)S(1)} %get-tuple-element.85), channel_id=1, source_target_pairs={{0,8},{8,16},{16,24},{24,0},{1,9},{9,17},{17,25},{25,1},{2,10},{10... | collective-permute-start | bytes 294920 | tf_op jit(solution)/shard_map/ppermute | solution.py:480
  46.6 9.5 %collective-permute-start.24 = (bf16[48,1024]{1,0:T(8,128)(2,1)S(1)}, bf16[48,1024]{1,0:T(8,128)(2,1)S(1)}, u32[]{:S(2)}, u32[]{:S(2)}) collective-permute-start(bf16[48,1024]{1,0:T(8,128)(2,1)S(1)} %get-tuple-element.86), channel_id=1, source_target_pairs={{0,16},{8,24},{16,0},{24,8},{1,17},{9,25},{17,1},{25,9},{2,18},{10... | collective-permute-start | bytes 294920 | tf_op jit(solution)/shard_map/ppermute | solution.py:480
  49.2 6.9 %collective-permute-start.25 = (bf16[48,1024]{1,0:T(8,128)(2,1)S(1)}, bf16[48,1024]{1,0:T(8,128)(2,1)S(1)}, u32[]{:S(2)}, u32[]{:S(2)}) collective-permute-start(bf16[48,1024]{1,0:T(8,128)(2,1)S(1)} %get-tuple-element.87), channel_id=1, source_target_pairs={{0,24},{8,0},{16,8},{24,16},{1,25},{9,1},{17,9},{25,17},{2,26},{10... | collective-permute-start | bytes 294920 | tf_op jit(solution)/shard_map/ppermute | solution.py:480
  (13 other events, 102.9 us)

commit v2 on v1

--- a/solution.py
+++ b/solution.py
@@ -86,7 +86,7 @@
     rows = features.shape[0]
     operands = (features, weight, *other)
     out_shape = [
-        jax.ShapeDtypeStruct((rows, 2 * HEAD_DIM), BF16 if other and j > 0 else F32)
+        jax.ShapeDtypeStruct((rows, 2 * HEAD_DIM), BF16 if other and j % 2 else F32)
         for j in range(len(pairs))
     ]
     return pl.pallas_call(
@@ -98,6 +98,27 @@
         cost_estimate=cost(0, 0),
         name="kv_partial_own_core" if other else "kv_partial_other_core",
     )(*operands)
+
+
+def kv_sum_kernel(*refs):
+    size = len(refs) // 3
+    for kept_ref, came_ref, out_ref in zip(refs, refs[size:], refs[2 * size :]):
+        total = kept_ref[...] + came_ref[...].astype(F32)
+        out_ref[...] = total.astype(out_ref.dtype)
+
+
+def kv_sum(kept, came):
+    return pl.pallas_call(
+        kv_sum_kernel,
+        in_specs=[whole()] * (2 * len(kept)),
+        out_specs=[whole()] * len(kept),
+        out_shape=[
+            jax.ShapeDtypeStruct(x.shape, BF16 if i % 2 else F32) for i, x in enumerate(kept)
+        ],
+        compiler_params=params(24),
+        cost_estimate=cost(0, 0),
+        name="kv_sum",
+    )(*kept, *came)
 
 
 def query_kernel(shape, slots, start, *refs):
@@ -426,9 +447,14 @@
     kv_pairs = [distance(mask) for mask in range(1 << steps)]
     other_heads = kv_partial(features, w_key_value, per_kv, [other_core(pair) for pair in kv_pairs])
     other_heads = [swap(x) for x in other_heads]
-    own, *outgoing = kv_partial(features, w_key_value, per_kv, kv_pairs, other_heads)
-    parts = [own] + [exchange(x, pair) for x, pair in zip(outgoing, kv_pairs[1:])]
-    direct, parts = lax.optimization_barrier((direct, parts))
+    sums = kv_partial(features, w_key_value, per_kv, kv_pairs, other_heads)
+    for step in range(steps):
+        kept, came = sums[::2], [exchange(x, distance(1 << step)) for x in sums[1::2]]
+        if step == 0:
+            direct, came = lax.optimization_barrier((direct, came))
+        if step < steps - 1:
+            sums = kv_sum(kept, came)
+    parts = [kept[0], came[0]]
     near = both_cores({(0, 0): own_text})
     q_near = queries(near, "queries_own_chip")
     forwarded = []
@@ -458,8 +484,10 @@
     far = both_cores(first_half)
     second_half, far = lax.optimization_barrier((forwarded[1], far))
     sums = queries(far, "queries_forwarded_first")
-    far = both_cores(second_half)
-    q_far = queries(far, "queries_forwarded_last", start=width, before=sums)
+    pieces = {pair: jnp.split(x, 2, axis=1) for pair, x in second_half.items()}
+    far, rest = [both_cores({pair: x[i] for pair, x in pieces.items()}) for i in range(2)]
+    sums = queries(far, "queries_forwarded_second", start=width, before=sums)
+    q_far = queries(rest, "queries_forwarded_last", start=3 * width // 2, before=sums)
     far = places_of(far)
     late, block = attention([], [q_far], [far], count, grad_out, k_gain, state, last=True)
     attended = assemble([places_of(near) + places_of(next_to), far], [early, late], grad_out)

time: 57 us -> 56.6 us (level)
  waiting for transfers between devices: 18.2 us -> 17.5 us
    ppermute x23 -> x24, waiting for transfers between devices: 13.5 us -> 12.8 us  [exchange(): lax.ppermute(x, 'tensor', [(i, i ^ pair[i % 2]) for i in range(count)])]
    ppermute x23 -> x24, starting transfers between devices: 15.8 us -> 15.6 us  [exchange(): lax.ppermute(x, 'tensor', [(i, i ^ pair[i % 2]) for i in range(count)])]
    pallas_call x4 -> x5, Pallas kernels: 5.26 us -> 5.36 us  [queries_of(): pl.pallas_call(functools.partial(query_kernel, [len(parts) for parts in g...]
  transfers between devices with their start and end apart: 26 -> 27, of which waited for: 12 -> 14; matrix products, arithmetic and copies ran while one was open for 0% -> 0% of each run, Pallas kernels for 17% -> 18%
where the time goes in v2:
time: 56.6 us; the launch traced here: 56.4 us
  starting transfers between devices  21.7 us (38%)
  waiting for transfers between devices  17.5 us (31%)
  Pallas kernels  12.4 us (22%)
  local copies, waits for them, and re-layouts  3.27 us (6%)
  between operations  0.87 us (2%)
  other arithmetic  0.72 us (1%)
    ppermute x24, starting transfers between devices, exchange(): lax.ppermute(x, 'tensor', [(i, i ^ pair[i % 2]) for i in range(count)])  15.6 us
    ppermute x24, waiting for transfers between devices, exchange(): lax.ppermute(x, 'tensor', [(i, i ^ pair[i % 2]) for i in range(count)])  12.8 us
    ppermute x3, starting transfers between devices, shards(): arrived.append(lax.ppermute(leaving[k - 1], 'section', perm))  6.09 us
    pallas_call x5, Pallas kernels, queries_of(): pl.pallas_call(functools.partial(query_kernel, [len(parts) for parts in g...  5.36 us
    ppermute x3, waiting for transfers between devices, shards(): arrived.append(lax.ppermute(leaving[k - 1], 'section', perm))  4.77 us
    unnamed x22, local copies, waits for them, and re-layouts  3.22 us
    pallas_call x2, Pallas kernels, attention(): pl.pallas_call(functools.partial(attention_kernel, places, count, rows, l...  2.66 us
    pallas_call x2, Pallas kernels, feature_gradient(): pl.pallas_call(functools.partial(grad_kernel, pairs, per_kv, sections, be...  1.9 us
  transfers between devices with their start and end apart: 27, of which 14 were waited for; matrix products, arithmetic and copies ran while one was open for 0% of the time, Pallas kernels for 18%

profile of v2, /device:TPU:0, one launch (start us, length us, event | category | flops | bytes accessed | tf_op | source)
XLA Modules:
  0.0 56.4 jit_solution(1621347824746100795)
XLA Ops:
  0.6 3.0 %collective-permute-start.1 = (bf16[32,8192]{1,0:T(8,128)(2,1)}, bf16[32,8192]{1,0:T(8,128)(2,1)S(1)}, u32[]{:S(2)}, u32[]{:S(2)}) collective-permute-start(bf16[32,8192]{1,0:T(8,128)(2,1)} %bitcast.1), channel_id=1, source_target_pairs={{0,2},{1,5},{2,0},{3,7},{4,6},{5,1},{6,4},{7,3},{8,10},{9,13},{10,... | collective-permute-start | bytes 1572872 | tf_op jit(solution)/shard_map/ppermute | solution.py:413
  3.6 1.5 %collective-permute-start.2 = (bf16[32,8192]{1,0:T(8,128)(2,1)}, bf16[32,8192]{1,0:T(8,128)(2,1)S(1)}, u32[]{:S(2)}, u32[]{:S(2)}) collective-permute-start(bf16[32,8192]{1,0:T(8,128)(2,1)} %bitcast.2), channel_id=1, source_target_pairs={{0,4},{1,3},{2,6},{3,1},{4,0},{5,7},{6,2},{7,5},{8,12},{9,11},{10,... | collective-permute-start | bytes 1572872 | tf_op jit(solution)/shard_map/ppermute | solution.py:413
  5.2 2.2 %copy-done.1 = bf16[1,1024,2048]{2,1,0:T(8,128)(2,1)S(1)} copy-done((bf16[1,1024,2048]{2,1,0:T(8,128)(2,1)S(1)}, bf16[1,1024,2048]{2,1,0:T(8,128)(2,1)}, u32[]{:S(2)}) %copy-start.1) | copy-done | bytes 4194328
  7.4 1.0 %copy-done.3 = bf16[192,1024]{1,0:T(8,128)(2,1)S(1)} copy-done((bf16[192,1024]{1,0:T(8,128)(2,1)S(1)}, bf16[192,1024]{1,0:T(8,128)(2,1)}, u32[]{:S(2)}) %copy-start.3) | copy-done | bytes 393240
  11.2 0.9 %collective-permute-done.6.refs_3_ = f32[192,256]{1,0:T(8,128)S(1)} collective-permute-done((f32[192,256]{1,0:T(8,128)S(1)}, f32[192,256]{1,0:T(8,128)S(1)}, u32[]{:S(2)}, u32[]{:S(2)}) %collective-permute-start.6) | collective-permute-done | bytes 196640 | tf_op jit(solution)/shard_map/ppermute | solution.py:413
  13.8 1.3 %collective-permute-start.8 = (bf16[192,256]{1,0:T(8,128)(2,1)S(1)}, bf16[192,256]{1,0:T(8,128)(2,1)S(1)}, u32[]{:S(2)}, u32[]{:S(2)}) collective-permute-start(bf16[192,256]{1,0:T(8,128)(2,1)S(1)} %get-tuple-element.52), channel_id=1, source_target_pairs={{0,2},{1,5},{2,0},{3,7},{4,6},{5,1},{6,4},{7,3},{8,10},{9,13},{10,... | collective-permute-start | bytes 294920 | tf_op jit(solution)/shard_map/ppermute | solution.py:413
  15.0 2.6 %collective-permute-done.7.refs_2_ = bf16[192,256]{1,0:T(8,128)(2,1)S(1)} collective-permute-done((bf16[192,256]{1,0:T(8,128)(2,1)S(1)}, bf16[192,256]{1,0:T(8,128)(2,1)S(1)}, u32[]{:S(2)}, u32[]{:S(2)}) %collective-permute-start.7) | collective-permute-done | bytes 98336 | tf_op jit(solution)/shard_map/ppermute | solution.py:413
  17.7 1.1 %collective-permute-done.8.refs_3_ = bf16[192,256]{1,0:T(8,128)(2,1)S(1)} collective-permute-done((bf16[192,256]{1,0:T(8,128)(2,1)S(1)}, bf16[192,256]{1,0:T(8,128)(2,1)S(1)}, u32[]{:S(2)}, u32[]{:S(2)}) %collective-permute-start.8) | collective-permute-done | bytes 98336 | tf_op jit(solution)/shard_map/ppermute | solution.py:413
  19.3 1.1 %collective-permute-start.13 = (bf16[32,4096]{1,0:T(8,128)(2,1)S(1)}, bf16[32,4096]{1,0:T(8,128)(2,1)S(1)}, u32[]{:S(2)}, u32[]{:S(2)}) collective-permute-start(bf16[32,4096]{1,0:T(8,128)(2,1)S(1)} %get-tuple-element.92), channel_id=1, source_target_pairs={{0,4},{1,3},{2,6},{3,1},{4,0},{5,7},{6,2},{7,5},{8,12},{9,11},{10,... | collective-permute-start | bytes 786440 | tf_op jit(solution)/shard_map/ppermute | solution.py:413
  20.4 1.1 %collective-permute-start.11 = (bf16[192,256]{1,0:T(8,128)(2,1)S(1)}, bf16[192,256]{1,0:T(8,128)(2,1)S(1)}, u32[]{:S(2)}, u32[]{:S(2)}) collective-permute-start(bf16[192,256]{1,0:T(8,128)(2,1)S(1)} %get-tuple-element.60), channel_id=1, source_target_pairs={{0,4},{1,3},{2,6},{3,1},{4,0},{5,7},{6,2},{7,5},{8,12},{9,11},{10,... | collective-permute-start | bytes 294920 | tf_op jit(solution)/shard_map/ppermute | solution.py:413
  21.5 1.1 %collective-permute-start.12 = (bf16[32,4096]{1,0:T(8,128)(2,1)S(1)}, bf16[32,4096]{1,0:T(8,128)(2,1)S(1)}, u32[]{:S(2)}, u32[]{:S(2)}) collective-permute-start(bf16[32,4096]{1,0:T(8,128)(2,1)S(1)} %get-tuple-element.93), channel_id=1, source_target_pairs={{0,4},{1,3},{2,6},{3,1},{4,0},{5,7},{6,2},{7,5},{8,12},{9,11},{10,... | collective-permute-start | bytes 786440 | tf_op jit(solution)/shard_map/ppermute | solution.py:413
  22.6 1.7 %queries_own_chip.1.refs_2_ = bf16[64,512]{1,0:T(8,128)(2,1)S(1)} custom-call(bf16[1,8192]{1,0:T(2,128)(2,1)S(1)} %copy-done.5, bf16[1,8192,512]{2,1,0:T(8,128)(2,1)S(1)} %copy-done, bf16[1,128]{1,0:T(2,128)(2,1)S(1)} %copy-done.7, bf16[32,8192]{1,0:T(8,128)(2,1)S(1)} %bitcast.4, bf16[32,8192]{1,0:T(8,128)(2,1)S(1)} %collective-permute-done.refs_4_), custom_call_target="tpu_custom_call" | custom-call | tf_op jit(solution)/shard_map/queries_own_chip/pallas_call | solution.py:185
  24.3 1.7 %queries_neighbours.1.refs_3_ = bf16[128,512]{1,0:T(8,128)(2,1)S(1)} custom-call(bf16[1,8192]{1,0:T(2,128)(2,1)S(1)} %copy-done.5, bf16[1,8192,512]{2,1,0:T(8,128)(2,1)S(1)} %copy-done, bf16[1,128]{1,0:T(2,128)(2,1)S(1)} %copy-done.7, bf16[32,8192]{1,0:T(8,128)(2,1)S(1)} %collective-permute-done.1.refs_3_, ...), custom_call_target="tpu_custom_call" | custom-call | tf_op jit(solution)/shard_map/queries_neighbours/pallas_call | solution.py:185
  26.8 1.9 %attention_first.1 = (f32[192,512]{1,0:T(8,128)S(1)}, f32[192,128]{1,0:T(8,128)S(1)}, f32[192,128]{1,0:T(8,128)S(1)}, bf16[192,128]{1,0:T(8,128)(2,1)S(1)}, bf16...) custom-call(s32[2]{0:T(128)S(1)} %copy-done.9, ...), custom_call_target="tpu_custom_call" | custom-call | tf_op jit(solution)/shard_map/attention_first/pallas_call | solution.py:304
  33.7 2.1 %collective-permute-start.17 = (bf16[192,256]{1,0:T(8,128)(2,1)S(1)}, bf16[192,256]{1,0:T(8,128)(2,1)S(1)}, u32[]{:S(2)}, u32[]{:S(2)}) collective-permute-start(bf16[192,256]{1,0:T(8,128)(2,1)S(1)} %get-tuple-element.87.refs_0_), channel_id=1, source_target_pairs={{0,6},{1,7},{2,4},{3,5},{4,2},{5,3},{6,0},{7,1},{8,14},{9,15},{10,... | collective-permute-start | bytes 294920 | tf_op jit(solution)/shard_map/ppermute | solution.py:413
  35.8 1.4 %collective-permute-start.19 = (bf16[192,256]{1,0:T(8,128)(2,1)S(1)}, bf16[192,256]{1,0:T(8,128)(2,1)S(1)}, u32[]{:S(2)}, u32[]{:S(2)}) collective-permute-start(bf16[192,256]{1,0:T(8,128)(2,1)S(1)} %get-tuple-element.87.refs_0_), channel_id=1, source_target_pairs={{0,4},{1,3},{2,6},{3,1},{4,0},{5,7},{6,2},{7,5},{8,12},{9,11},{10,... | collective-permute-start | bytes 294920 | tf_op jit(solution)/shard_map/ppermute | solution.py:413
  37.3 2.6 %collective-permute-done.17.refs_1_ = bf16[192,256]{1,0:T(8,128)(2,1)S(1)} collective-permute-done((bf16[192,256]{1,0:T(8,128)(2,1)S(1)}, bf16[192,256]{1,0:T(8,128)(2,1)S(1)}, u32[]{:S(2)}, u32[]{:S(2)}) %collective-permute-start.17) | collective-permute-done | bytes 98336 | tf_op jit(solution)/shard_map/ppermute | solution.py:413
  39.9 1.7 %collective-permute-done.19.refs_2_ = bf16[192,256]{1,0:T(8,128)(2,1)S(1)} collective-permute-done((bf16[192,256]{1,0:T(8,128)(2,1)S(1)}, bf16[192,256]{1,0:T(8,128)(2,1)S(1)}, u32[]{:S(2)}, u32[]{:S(2)}) %collective-permute-start.19) | collective-permute-done | bytes 98336 | tf_op jit(solution)/shard_map/ppermute | solution.py:413
  42.1 1.1 %feature_grad_first.1.refs_4_ = f32[192,1024]{1,0:T(8,128)S(1)} custom-call(bf16[192,256]{1,0:T(8,128)(2,1)S(1)} %get-tuple-element.87.refs_0_, bf16[192,256]{1,0:T(8,128)(2,1)S(1)} %collective-permute-done.17.refs_1_, bf16[192,256]{1,0:T(8,128)(2,1)S(1)} %collective-permute-done.19.refs_2_, bf16[192,256]{1,0:T(8,128)(2,1)S(1)} %collective-permute-done.21.refs_3_, ...), custom_call_target="tpu_custom_call" | custom-call | tf_op jit(solution)/shard_map/feature_grad_first/pallas_call | solution.py:393
  44.1 2.1 %collective-permute-start.24 = (bf16[48,1024]{1,0:T(8,128)(2,1)S(1)}, bf16[48,1024]{1,0:T(8,128)(2,1)S(1)}, u32[]{:S(2)}, u32[]{:S(2)}) collective-permute-start(bf16[48,1024]{1,0:T(8,128)(2,1)S(1)} %get-tuple-element.89), channel_id=1, source_target_pairs={{0,8},{8,16},{16,24},{24,0},{1,9},{9,17},{17,25},{25,1},{2,10},{10... | collective-permute-start | bytes 294920 | tf_op jit(solution)/shard_map/ppermute | solution.py:508
  46.2 2.6 %collective-permute-start.25 = (bf16[48,1024]{1,0:T(8,128)(2,1)S(1)}, bf16[48,1024]{1,0:T(8,128)(2,1)S(1)}, u32[]{:S(2)}, u32[]{:S(2)}) collective-permute-start(bf16[48,1024]{1,0:T(8,128)(2,1)S(1)} %get-tuple-element.90), channel_id=1, source_target_pairs={{0,16},{8,24},{16,0},{24,8},{1,17},{9,25},{17,1},{25,9},{2,18},{10... | collective-permute-start | bytes 294920 | tf_op jit(solution)/shard_map/ppermute | solution.py:508
  48.8 1.3 %collective-permute-start.26 = (bf16[48,1024]{1,0:T(8,128)(2,1)S(1)}, bf16[48,1024]{1,0:T(8,128)(2,1)S(1)}, u32[]{:S(2)}, u32[]{:S(2)}) collective-permute-start(bf16[48,1024]{1,0:T(8,128)(2,1)S(1)} %get-tuple-element.91), channel_id=1, source_target_pairs={{0,24},{8,0},{16,8},{24,16},{1,25},{9,1},{17,9},{25,17},{2,26},{10... | collective-permute-start | bytes 294920 | tf_op jit(solution)/shard_map/ppermute | solution.py:508
  50.9 1.0 %collective-permute-done.24 = bf16[48,1024]{1,0:T(8,128)(2,1)S(1)} collective-permute-done((bf16[48,1024]{1,0:T(8,128)(2,1)S(1)}, bf16[48,1024]{1,0:T(8,128)(2,1)S(1)}, u32[]{:S(2)}, u32[]{:S(2)}) %collective-permute-start.24) | collective-permute-done | bytes 98336 | tf_op jit(solution)/shard_map/ppermute | solution.py:508
  51.9 3.8 %collective-permute-done.25 = bf16[48,1024]{1,0:T(8,128)(2,1)S(1)} collective-permute-done((bf16[48,1024]{1,0:T(8,128)(2,1)S(1)}, bf16[48,1024]{1,0:T(8,128)(2,1)S(1)}, u32[]{:S(2)}, u32[]{:S(2)}) %collective-permute-start.25) | collective-permute-done | bytes 98336 | tf_op jit(solution)/shard_map/ppermute | solution.py:508
  (68 shorter events, 13.7 us)
Async XLA Ops:
  0.6 18.1 %collective-permute-start.1 = (bf16[32,8192]{1,0:T(8,128)(2,1)}, bf16[32,8192]{1,0:T(8,128)(2,1)S(1)}, u32[]{:S(2)}, u32[]{:S(2)}) collective-permute-start(bf16[32,8192]{1,0:T(8,128)(2,1)} %bitcast.1), channel_id=1, source_target_pairs={{0,2},{1,5},{2,0},{3,7},{4,6},{5,1},{6,4},{7,3},{8,10},{9,13},{10,... | collective-permute-start | bytes 1572872 | tf_op jit(solution)/shard_map/ppermute | solution.py:413
  3.6 15.1 %collective-permute-start.2 = (bf16[32,8192]{1,0:T(8,128)(2,1)}, bf16[32,8192]{1,0:T(8,128)(2,1)S(1)}, u32[]{:S(2)}, u32[]{:S(2)}) collective-permute-start(bf16[32,8192]{1,0:T(8,128)(2,1)} %bitcast.2), channel_id=1, source_target_pairs={{0,4},{1,3},{2,6},{3,1},{4,0},{5,7},{6,2},{7,5},{8,12},{9,11},{10,... | collective-permute-start | bytes 1572872 | tf_op jit(solution)/shard_map/ppermute | solution.py:413
  9.2 1.5 %collective-permute-start.3 = (f32[192,256]{1,0:T(8,128)S(1)}, f32[192,256]{1,0:T(8,128)S(1)}, u32[]{:S(2)}, u32[]{:S(2)}) collective-permute-start(f32[192,256]{1,0:T(8,128)S(1)} %get-tuple-element.47), channel_id=1, source_target_pairs={{0,1},{1,0},{2,3},{3,2},{4,5},{5,4},{6,7},{7,6},{8,9},{9,8},{10,11... | collective-permute-start | bytes 589832 | tf_op jit(solution)/shard_map/ppermute | solution.py:413
  9.3 1.7 %collective-permute-start.4 = (f32[192,256]{1,0:T(8,128)S(1)}, f32[192,256]{1,0:T(8,128)S(1)}, u32[]{:S(2)}, u32[]{:S(2)}) collective-permute-start(f32[192,256]{1,0:T(8,128)S(1)} %get-tuple-element.48), channel_id=1, source_target_pairs={{0,1},{1,0},{2,3},{3,2},{4,5},{5,4},{6,7},{7,6},{8,9},{9,8},{10,11... | collective-permute-start | bytes 589832 | tf_op jit(solution)/shard_map/ppermute | solution.py:413
  9.8 1.5 %collective-permute-start.5 = (f32[192,256]{1,0:T(8,128)S(1)}, f32[192,256]{1,0:T(8,128)S(1)}, u32[]{:S(2)}, u32[]{:S(2)}) collective-permute-start(f32[192,256]{1,0:T(8,128)S(1)} %get-tuple-element.49), channel_id=1, source_target_pairs={{0,1},{1,0},{2,3},{3,2},{4,5},{5,4},{6,7},{7,6},{8,9},{9,8},{10,11... | collective-permute-start | bytes 589832 | tf_op jit(solution)/shard_map/ppermute | solution.py:413
  12.9 4.7 %collective-permute-start.7 = (bf16[192,256]{1,0:T(8,128)(2,1)S(1)}, bf16[192,256]{1,0:T(8,128)(2,1)S(1)}, u32[]{:S(2)}, u32[]{:S(2)}) collective-permute-start(bf16[192,256]{1,0:T(8,128)(2,1)S(1)} %get-tuple-element.51), channel_id=1, source_target_pairs={{0,2},{1,5},{2,0},{3,7},{4,6},{5,1},{6,4},{7,3},{8,10},{9,13},{10,... | collective-permute-start | bytes 294920 | tf_op jit(solution)/shard_map/ppermute | solution.py:413
  13.8 5.0 %collective-permute-start.8 = (bf16[192,256]{1,0:T(8,128)(2,1)S(1)}, bf16[192,256]{1,0:T(8,128)(2,1)S(1)}, u32[]{:S(2)}, u32[]{:S(2)}) collective-permute-start(bf16[192,256]{1,0:T(8,128)(2,1)S(1)} %get-tuple-element.52), channel_id=1, source_target_pairs={{0,2},{1,5},{2,0},{3,7},{4,6},{5,1},{6,4},{7,3},{8,10},{9,13},{10,... | collective-permute-start | bytes 294920 | tf_op jit(solution)/shard_map/ppermute | solution.py:413
  15.0 6.5 %collective-permute-start = (bf16[32,8192]{1,0:T(8,128)(2,1)S(1)}, bf16[32,8192]{1,0:T(8,128)(2,1)S(1)}, u32[]{:S(2)}, u32[]{:S(2)}) collective-permute-start(bf16[32,8192]{1,0:T(8,128)(2,1)S(1)} %bitcast.3), channel_id=1, source_target_pairs={{0,1},{1,0},{2,3},{3,2},{4,5},{5,4},{6,7},{7,6},{8,9},{9,8},{10,11... | collective-permute-start | bytes 1572872 | tf_op jit(solution)/shard_map/ppermute | solution.py:413
  18.7 5.6 %collective-permute-start.9 = (bf16[32,8192]{1,0:T(8,128)(2,1)S(1)}, bf16[32,8192]{1,0:T(8,128)(2,1)S(1)}, u32[]{:S(2)}, u32[]{:S(2)}) collective-permute-start(bf16[32,8192]{1,0:T(8,128)(2,1)S(1)} %collective-permute-done.1.refs_3_), channel_id=1, source_target_pairs={{0,1},{1,0},{2,3},{3,2},{4,5},{5,4},{6,7},{7,6},{8,9},{9,8},{10,11... | collective-permute-start | bytes 1572872 | tf_op jit(solution)/shard_map/ppermute | solution.py:413
  18.8 5.6 %collective-permute-start.10 = (bf16[32,8192]{1,0:T(8,128)(2,1)S(1)}, bf16[32,8192]{1,0:T(8,128)(2,1)S(1)}, u32[]{:S(2)}, u32[]{:S(2)}) collective-permute-start(bf16[32,8192]{1,0:T(8,128)(2,1)S(1)} %collective-permute-done.2.refs_5_), channel_id=1, source_target_pairs={{0,1},{1,0},{2,3},{3,2},{4,5},{5,4},{6,7},{7,6},{8,9},{9,8},{10,11... | collective-permute-start | bytes 1572872 | tf_op jit(solution)/shard_map/ppermute | solution.py:413
  19.3 9.4 %collective-permute-start.13 = (bf16[32,4096]{1,0:T(8,128)(2,1)S(1)}, bf16[32,4096]{1,0:T(8,128)(2,1)S(1)}, u32[]{:S(2)}, u32[]{:S(2)}) collective-permute-start(bf16[32,4096]{1,0:T(8,128)(2,1)S(1)} %get-tuple-element.92), channel_id=1, source_target_pairs={{0,4},{1,3},{2,6},{3,1},{4,0},{5,7},{6,2},{7,5},{8,12},{9,11},{10,... | collective-permute-start | bytes 786440 | tf_op jit(solution)/shard_map/ppermute | solution.py:413
  20.4 6.4 %collective-permute-start.11 = (bf16[192,256]{1,0:T(8,128)(2,1)S(1)}, bf16[192,256]{1,0:T(8,128)(2,1)S(1)}, u32[]{:S(2)}, u32[]{:S(2)}) collective-permute-start(bf16[192,256]{1,0:T(8,128)(2,1)S(1)} %get-tuple-element.60), channel_id=1, source_target_pairs={{0,4},{1,3},{2,6},{3,1},{4,0},{5,7},{6,2},{7,5},{8,12},{9,11},{10,... | collective-permute-start | bytes 294920 | tf_op jit(solution)/shard_map/ppermute | solution.py:413
  21.5 8.1 %collective-permute-start.12 = (bf16[32,4096]{1,0:T(8,128)(2,1)S(1)}, bf16[32,4096]{1,0:T(8,128)(2,1)S(1)}, u32[]{:S(2)}, u32[]{:S(2)}) collective-permute-start(bf16[32,4096]{1,0:T(8,128)(2,1)S(1)} %get-tuple-element.93), channel_id=1, source_target_pairs={{0,4},{1,3},{2,6},{3,1},{4,0},{5,7},{6,2},{7,5},{8,12},{9,11},{10,... | collective-permute-start | bytes 786440 | tf_op jit(solution)/shard_map/ppermute | solution.py:413
  28.7 1.6 %collective-permute-start.14 = (bf16[32,4096]{1,0:T(8,128)(2,1)S(1)}, bf16[32,4096]{1,0:T(8,128)(2,1)S(1)}, u32[]{:S(2)}, u32[]{:S(2)}) collective-permute-start(bf16[32,4096]{1,0:T(8,128)(2,1)S(1)} %collective-permute-done.13.refs_3_), channel_id=1, source_target_pairs={{0,1},{1,0},{2,3},{3,2},{4,5},{5,4},{6,7},{7,6},{8,9},{9,8},{10,11... | collective-permute-start | bytes 786440 | tf_op jit(solution)/shard_map/ppermute | solution.py:413
  30.5 1.8 %collective-permute-start.15 = (bf16[32,2048]{1,0:T(8,128)(2,1)S(1)}, bf16[32,2048]{1,0:T(8,128)(2,1)S(1)}, u32[]{:S(2)}, u32[]{:S(2)}) collective-permute-start(bf16[32,2048]{1,0:T(8,128)(2,1)S(1)} %get-tuple-element.95.refs_3_), channel_id=1, source_target_pairs={{0,1},{1,0},{2,3},{3,2},{4,5},{5,4},{6,7},{7,6},{8,9},{9,8},{10,11... | collective-permute-start | bytes 393224 | tf_op jit(solution)/shard_map/ppermute | solution.py:413
  33.7 6.2 %collective-permute-start.17 = (bf16[192,256]{1,0:T(8,128)(2,1)S(1)}, bf16[192,256]{1,0:T(8,128)(2,1)S(1)}, u32[]{:S(2)}, u32[]{:S(2)}) collective-permute-start(bf16[192,256]{1,0:T(8,128)(2,1)S(1)} %get-tuple-element.87.refs_0_), channel_id=1, source_target_pairs={{0,6},{1,7},{2,4},{3,5},{4,2},{5,3},{6,0},{7,1},{8,14},{9,15},{10,... | collective-permute-start | bytes 294920 | tf_op jit(solution)/shard_map/ppermute | solution.py:413
  35.8 5.8 %collective-permute-start.19 = (bf16[192,256]{1,0:T(8,128)(2,1)S(1)}, bf16[192,256]{1,0:T(8,128)(2,1)S(1)}, u32[]{:S(2)}, u32[]{:S(2)}) collective-permute-start(bf16[192,256]{1,0:T(8,128)(2,1)S(1)} %get-tuple-element.87.refs_0_), channel_id=1, source_target_pairs={{0,4},{1,3},{2,6},{3,1},{4,0},{5,7},{6,2},{7,5},{8,12},{9,11},{10,... | collective-permute-start | bytes 294920 | tf_op jit(solution)/shard_map/ppermute | solution.py:413
  37.2 4.6 %collective-permute-start.21 = (bf16[192,256]{1,0:T(8,128)(2,1)S(1)}, bf16[192,256]{1,0:T(8,128)(2,1)S(1)}, u32[]{:S(2)}, u32[]{:S(2)}) collective-permute-start(bf16[192,256]{1,0:T(8,128)(2,1)S(1)} %get-tuple-element.87.refs_0_), channel_id=1, source_target_pairs={{0,2},{1,5},{2,0},{3,7},{4,6},{5,1},{6,4},{7,3},{8,10},{9,13},{10,... | collective-permute-start | bytes 294920 | tf_op jit(solution)/shard_map/ppermute | solution.py:413
  37.3 4.9 %collective-permute-start.23 = (bf16[192,256]{1,0:T(8,128)(2,1)S(1)}, bf16[192,256]{1,0:T(8,128)(2,1)S(1)}, u32[]{:S(2)}, u32[]{:S(2)}) collective-permute-start(bf16[192,256]{1,0:T(8,128)(2,1)S(1)} %get-tuple-element.87.refs_0_), channel_id=1, source_target_pairs={{0,1},{1,0},{2,3},{3,2},{4,5},{5,4},{6,7},{7,6},{8,9},{9,8},{10,11... | collective-permute-start | bytes 294920 | tf_op jit(solution)/shard_map/ppermute | solution.py:413
  39.9 3.3 %collective-permute-start.18 = (bf16[192,256]{1,0:T(8,128)(2,1)S(1)}, bf16[192,256]{1,0:T(8,128)(2,1)S(1)}, u32[]{:S(2)}, u32[]{:S(2)}) collective-permute-start(bf16[192,256]{1,0:T(8,128)(2,1)S(1)} %collective-permute-done.17.refs_1_), channel_id=1, source_target_pairs={{0,1},{1,0},{2,3},{3,2},{4,5},{5,4},{6,7},{7,6},{8,9},{9,8},{10,11... | collective-permute-start | bytes 294920 | tf_op jit(solution)/shard_map/ppermute | solution.py:413
  41.6 1.6 %collective-permute-start.20 = (bf16[192,256]{1,0:T(8,128)(2,1)S(1)}, bf16[192,256]{1,0:T(8,128)(2,1)S(1)}, u32[]{:S(2)}, u32[]{:S(2)}) collective-permute-start(bf16[192,256]{1,0:T(8,128)(2,1)S(1)} %collective-permute-done.19.refs_2_), channel_id=1, source_target_pairs={{0,1},{1,0},{2,3},{3,2},{4,5},{5,4},{6,7},{7,6},{8,9},{9,8},{10,11... | collective-permute-start | bytes 294920 | tf_op jit(solution)/shard_map/ppermute | solution.py:413
  44.1 7.9 %collective-permute-start.24 = (bf16[48,1024]{1,0:T(8,128)(2,1)S(1)}, bf16[48,1024]{1,0:T(8,128)(2,1)S(1)}, u32[]{:S(2)}, u32[]{:S(2)}) collective-permute-start(bf16[48,1024]{1,0:T(8,128)(2,1)S(1)} %get-tuple-element.89), channel_id=1, source_target_pairs={{0,8},{8,16},{16,24},{24,0},{1,9},{9,17},{17,25},{25,1},{2,10},{10... | collective-permute-start | bytes 294920 | tf_op jit(solution)/shard_map/ppermute | solution.py:508
  46.2 9.5 %collective-permute-start.25 = (bf16[48,1024]{1,0:T(8,128)(2,1)S(1)}, bf16[48,1024]{1,0:T(8,128)(2,1)S(1)}, u32[]{:S(2)}, u32[]{:S(2)}) collective-permute-start(bf16[48,1024]{1,0:T(8,128)(2,1)S(1)} %get-tuple-element.90), channel_id=1, source_target_pairs={{0,16},{8,24},{16,0},{24,8},{1,17},{9,25},{17,1},{25,9},{2,18},{10... | collective-permute-start | bytes 294920 | tf_op jit(solution)/shard_map/ppermute | solution.py:508
  48.8 6.9 %collective-permute-start.26 = (bf16[48,1024]{1,0:T(8,128)(2,1)S(1)}, bf16[48,1024]{1,0:T(8,128)(2,1)S(1)}, u32[]{:S(2)}, u32[]{:S(2)}) collective-permute-start(bf16[48,1024]{1,0:T(8,128)(2,1)S(1)} %get-tuple-element.91), channel_id=1, source_target_pairs={{0,24},{8,0},{16,8},{24,16},{1,25},{9,1},{17,9},{25,17},{2,26},{10... | collective-permute-start | bytes 294920 | tf_op jit(solution)/shard_map/ppermute | solution.py:508
  (14 other events, 96.1 us)

commit v3 on v2

--- a/solution.py
+++ b/solution.py
@@ -83,17 +83,16 @@
 
 
 def kv_partial(features, weight, per_kv, pairs, other=()):
-    rows = features.shape[0]
     operands = (features, weight, *other)
-    out_shape = [
-        jax.ShapeDtypeStruct((rows, 2 * HEAD_DIM), BF16 if other and j % 2 else F32)
-        for j in range(len(pairs))
-    ]
+    shape = (features.shape[0], 2 * HEAD_DIM)
     return pl.pallas_call(
         functools.partial(kv_kernel, per_kv, pairs),
         in_specs=[whole()] * len(operands),
         out_specs=[whole()] * len(pairs),
-        out_shape=out_shape,
+        out_shape=[
+            jax.ShapeDtypeStruct(shape, BF16 if other and j % 2 else F32)
+            for j in range(len(pairs))
+        ],
         compiler_params=params(24),
         cost_estimate=cost(0, 0),
         name="kv_partial_own_core" if other else "kv_partial_other_core",
@@ -121,7 +120,19 @@
     )(*kept, *came)
 
 
-def query_kernel(shape, slots, start, *refs):
+def live_masks(count_ref, start_ref, token_ref, slot_ref):
+    for b in range(MB):
+        token = lax.broadcasted_iota(jnp.int32, (TXT_TOK, HEAD_DIM), 0)
+        token_ref[b * TXT_TOK : (b + 1) * TXT_TOK, :] = (token >= start_ref[b]).astype(F32)
+        slot = lax.broadcasted_iota(jnp.int32, slot_ref.shape[1:], 1)
+        slot_ref[b] = (slot < count_ref[b] * TILE_LEN).astype(F32)
+
+
+def query_kernel(shape, slots, start, scalars, scratch, *refs):
+    if scalars:
+        end = len(refs) - scratch
+        live_masks(refs[0], refs[1], refs[end - 2], refs[end - 1])
+        refs = refs[2 : end - 2] + refs[end:]
     gain_ref, weight_ref, q_gain_ref, refs = refs[0], refs[1], refs[2], refs[3:]
     groups = []
     for parts in shape:
@@ -170,7 +181,7 @@
         refs[0][...] = out_ref[...].astype(BF16)
 
 
-def queries_of(groups, slots, gain, weight, q_gain, name, start=0, before=()):
+def queries_of(groups, slots, gain, weight, q_gain, name, start=0, before=(), scalars=()):
     arrays = [part for parts in groups for part in parts]
     rows = sum(parts[0].shape[0] for parts in groups)
     depth, heads_width = weight.shape[1:]
@@ -180,24 +191,34 @@
         out_shape = [jax.ShapeDtypeStruct((rows, heads_width), BF16)]
         if arrays[0].shape[0] % 16 != 0:
             scratch.append(pltpu.VMEM((rows, heads_width), F32))
+        if scalars:
+            out_shape.append(jax.ShapeDtypeStruct((MB * TXT_TOK, HEAD_DIM), F32))
+            out_shape.append(jax.ShapeDtypeStruct((MB, 8, SLOTS), F32))
     else:
         out_shape = [jax.ShapeDtypeStruct((rows, w), F32) for w in (heads_width, HEAD_DIM)]
     out = pl.pallas_call(
-        functools.partial(query_kernel, [len(parts) for parts in groups], slots, start),
-        in_specs=[whole()] * (3 + len(arrays) + len(before)),
+        functools.partial(
+            query_kernel,
+            [len(parts) for parts in groups],
+            slots,
+            start,
+            len(scalars),
+            len(scratch),
+        ),
+        in_specs=[whole(pltpu.SMEM)] * len(scalars)
+        + [whole()] * (3 + len(arrays) + len(before)),
         out_specs=[whole()] * len(out_shape),
         out_shape=out_shape,
         scratch_shapes=scratch,
         compiler_params=params(24),
         cost_estimate=cost(0, 0),
         name=name,
-    )(gain, weight, q_gain, *arrays, *before)
-    return out[0] if last else out
+    )(*scalars, gain, weight, q_gain, *arrays, *before)
+    return out[0] if last and not scalars else out
 
 
 def attention_kernel(places, count, rows, last, sizes, *refs):
-    if not last:
-        count_ref, start_ref, refs = refs[0], refs[1], refs[2:]
+    token_ref, slot_ref, refs = refs[0], refs[1], refs[2:]
     queries_refs, refs = refs[:sizes], refs[sizes:]
     grad_ref, k_gain_ref, refs = refs[0], refs[1], refs[2:]
     narrow = rows % 16 != 0
@@ -205,14 +226,13 @@
         refs, grad_rows = refs[:-1], refs[-1]
         grad_rows[...] = grad_ref[0].astype(F32)
     if last:
-        d_keys_in, d_values_in, keys_ref, values_ref, hat_ref, inverse_ref, token_ref, slot_ref = refs[:8]
-        att_ref, block_ref, d_keys_ref, d_values_ref = refs[8:]
+        d_keys_in, d_values_in, keys_ref, values_ref, hat_ref, inverse_ref = refs[:6]
+        att_ref, block_ref, d_keys_ref, d_values_ref = refs[6:]
         d_keys_ref[...] = d_keys_in[...]
         d_values_ref[...] = d_values_in[...]
     else:
-        parts = refs[:-9]
-        att_ref, d_keys_ref, d_values_ref, keys_ref, values_ref = refs[-9:-4]
-        hat_ref, inverse_ref, token_ref, slot_ref = refs[-4:]
+        parts = refs[:-7]
+        att_ref, d_keys_ref, d_values_ref, keys_ref, values_ref, hat_ref, inverse_ref = refs[-7:]
         kv = sum(part[...].astype(F32) for part in parts)
         key_raw = kv[:, :HEAD_DIM]
         inverse = lax.rsqrt(jnp.mean(key_raw * key_raw, axis=-1, keepdims=True) + eps)
@@ -222,11 +242,6 @@
         values_ref[...] = kv[:, HEAD_DIM:].astype(BF16)
         d_keys_ref[...] = jnp.zeros_like(d_keys_ref)
         d_values_ref[...] = jnp.zeros_like(d_values_ref)
-        for b in range(MB):
-            token = lax.broadcasted_iota(jnp.int32, (TXT_TOK, HEAD_DIM), 0)
-            token_ref[b * TXT_TOK : (b + 1) * TXT_TOK, :] = (token >= start_ref[b]).astype(F32)
-            slot = lax.broadcasted_iota(jnp.int32, slot_ref.shape[1:], 1)
-            slot_ref[b] = (slot < count_ref[b] * TILE_LEN).astype(F32)
 
     scale = HEAD_DIM ** (-0.5)
     heads = grad_ref.shape[2] // HEAD_DIM
@@ -284,7 +299,7 @@
         block_ref[:, HEAD_DIM:] = d_values_ref[...].astype(BF16)
 
 
-def attention(scalars, queries, places, count, grad_out, k_gain, state, last):
+def attention(live, queries, places, count, grad_out, k_gain, state, last):
     rows, width = grad_out.shape[1] // count, grad_out.shape[2]
     image_rows = MB * SLOTS
     vector = jax.ShapeDtypeStruct((image_rows, HEAD_DIM), F32)
@@ -295,22 +310,20 @@
         out_shape = [attended, jax.ShapeDtypeStruct((image_rows, 2 * HEAD_DIM), BF16)]
         scratch += [pltpu.VMEM(vector.shape, F32)] * 2
     else:
-        token = jax.ShapeDtypeStruct((grad_out.shape[1], HEAD_DIM), F32)
-        slot = jax.ShapeDtypeStruct((MB, 8, SLOTS), F32)
-        out_shape = [attended, vector, vector, rounded, rounded, vector, vector, token, slot]
+        out_shape = [attended, vector, vector, rounded, rounded, vector, vector]
     if rows % 16 != 0:
         scratch += [pltpu.VMEM(grad_out.shape[1:], F32)]
     operands = [*queries, grad_out, k_gain, *state]
     return pl.pallas_call(
         functools.partial(attention_kernel, places, count, rows, last, len(queries)),
-        in_specs=[whole(pltpu.SMEM)] * len(scalars) + [whole()] * len(operands),
+        in_specs=[whole()] * (2 + len(operands)),
         out_specs=[whole()] * len(out_shape),
         out_shape=out_shape,
         scratch_shapes=scratch,
         compiler_params=params(24),
         cost_estimate=cost(0, 0),
         name="attention_last" if last else "attention_first",
-    )(*scalars, *operands)
+    )(*live, *operands)
 
 
 def assemble_kernel(places, rows, *refs):
@@ -456,7 +469,8 @@
             sums = kv_sum(kept, came)
     parts = [kept[0], came[0]]
     near = both_cores({(0, 0): own_text})
-    q_near = queries(near, "queries_own_chip")
+    scalars = (tile_count, image_start)
+    q_near, *live = queries(near, "queries_own_chip", scalars=scalars)
     forwarded = []
     for first in (0, width):
         held = {mask: x[:, first : first + width] for mask, x in direct.items()}
@@ -471,7 +485,7 @@
     q_next = queries(next_to, "queries_neighbours")
 
     early, *state = attention(
-        [tile_count, image_start],
+        live,
         [q_near, q_next],
         [places_of(near), places_of(next_to)],
         count,
@@ -489,7 +503,7 @@
     sums = queries(far, "queries_forwarded_second", start=width, before=sums)
     q_far = queries(rest, "queries_forwarded_last", start=3 * width // 2, before=sums)
     far = places_of(far)
-    late, block = attention([], [q_far], [far], count, grad_out, k_gain, state, last=True)
+    late, block = attention(live, [q_far], [far], count, grad_out, k_gain, state, last=True)
     attended = assemble([places_of(near) + places_of(next_to), far], [early, late], grad_out)
 
     same_core = {(0, 0): block}

time: 56.6 us -> 56 us (0.989)
  no operation moved by 1% of the time
where the time goes in v3:
time: 56 us; the launch traced here: 55.9 us
  starting transfers between devices  21.6 us (39%)
  waiting for transfers between devices  17 us (30%)
  Pallas kernels  12.3 us (22%)
  local copies, waits for them, and re-layouts  3.27 us (6%)
  between operations  0.86 us (2%)
  other arithmetic  0.72 us (1%)
    ppermute x24, starting transfers between devices, exchange(): lax.ppermute(x, 'tensor', [(i, i ^ pair[i % 2]) for i in range(count)])  15.5 us
    ppermute x24, waiting for transfers between devices, exchange(): lax.ppermute(x, 'tensor', [(i, i ^ pair[i % 2]) for i in range(count)])  12.2 us
    ppermute x3, starting transfers between devices, shards(): arrived.append(lax.ppermute(leaving[k - 1], 'section', perm))  6.09 us
    pallas_call x5, Pallas kernels, queries_of(): pl.pallas_call(functools.partial(query_kernel, [len(parts) for parts in g...  5.91 us
    ppermute x3, waiting for transfers between devices, shards(): arrived.append(lax.ppermute(leaving[k - 1], 'section', perm))  4.78 us
    unnamed x22, local copies, waits for them, and re-layouts  3.22 us
    pallas_call x2, Pallas kernels, attention(): pl.pallas_call(functools.partial(attention_kernel, places, count, rows, l...  2.11 us
    pallas_call x2, Pallas kernels, feature_gradient(): pl.pallas_call(functools.partial(grad_kernel, pairs, per_kv, sections, be...  1.89 us
  transfers between devices with their start and end apart: 27, of which 14 were waited for; matrix products, arithmetic and copies ran while one was open for 0% of the time, Pallas kernels for 18%

profile of v3, /device:TPU:0, one launch (start us, length us, event | category | flops | bytes accessed | tf_op | source)
XLA Modules:
  0.0 55.9 jit_solution(13597544875751880881)
XLA Ops:
  0.6 3.0 %collective-permute-start.1 = (bf16[32,8192]{1,0:T(8,128)(2,1)}, bf16[32,8192]{1,0:T(8,128)(2,1)S(1)}, u32[]{:S(2)}, u32[]{:S(2)}) collective-permute-start(bf16[32,8192]{1,0:T(8,128)(2,1)} %bitcast.1), channel_id=1, source_target_pairs={{0,2},{1,5},{2,0},{3,7},{4,6},{5,1},{6,4},{7,3},{8,10},{9,13},{10,... | collective-permute-start | bytes 1572872 | tf_op jit(solution)/shard_map/ppermute | solution.py:426
  3.6 1.5 %collective-permute-start.2 = (bf16[32,8192]{1,0:T(8,128)(2,1)}, bf16[32,8192]{1,0:T(8,128)(2,1)S(1)}, u32[]{:S(2)}, u32[]{:S(2)}) collective-permute-start(bf16[32,8192]{1,0:T(8,128)(2,1)} %bitcast.2), channel_id=1, source_target_pairs={{0,4},{1,3},{2,6},{3,1},{4,0},{5,7},{6,2},{7,5},{8,12},{9,11},{10,... | collective-permute-start | bytes 1572872 | tf_op jit(solution)/shard_map/ppermute | solution.py:426
  5.2 2.2 %copy-done.1 = bf16[1,1024,2048]{2,1,0:T(8,128)(2,1)S(1)} copy-done((bf16[1,1024,2048]{2,1,0:T(8,128)(2,1)S(1)}, bf16[1,1024,2048]{2,1,0:T(8,128)(2,1)}, u32[]{:S(2)}) %copy-start.1) | copy-done | bytes 4194328
  7.4 1.0 %copy-done.3 = bf16[192,1024]{1,0:T(8,128)(2,1)S(1)} copy-done((bf16[192,1024]{1,0:T(8,128)(2,1)S(1)}, bf16[192,1024]{1,0:T(8,128)(2,1)}, u32[]{:S(2)}) %copy-start.3) | copy-done | bytes 393240
  13.8 1.3 %collective-permute-start.8 = (bf16[192,256]{1,0:T(8,128)(2,1)S(1)}, bf16[192,256]{1,0:T(8,128)(2,1)S(1)}, u32[]{:S(2)}, u32[]{:S(2)}) collective-permute-start(bf16[192,256]{1,0:T(8,128)(2,1)S(1)} %get-tuple-element.54), channel_id=1, source_target_pairs={{0,2},{1,5},{2,0},{3,7},{4,6},{5,1},{6,4},{7,3},{8,10},{9,13},{10,... | collective-permute-start | bytes 294920 | tf_op jit(solution)/shard_map/ppermute | solution.py:426
  15.1 2.6 %collective-permute-done.7.refs_2_ = bf16[192,256]{1,0:T(8,128)(2,1)S(1)} collective-permute-done((bf16[192,256]{1,0:T(8,128)(2,1)S(1)}, bf16[192,256]{1,0:T(8,128)(2,1)S(1)}, u32[]{:S(2)}, u32[]{:S(2)}) %collective-permute-start.7) | collective-permute-done | bytes 98336 | tf_op jit(solution)/shard_map/ppermute | solution.py:426
  17.7 1.1 %collective-permute-done.8.refs_3_ = bf16[192,256]{1,0:T(8,128)(2,1)S(1)} collective-permute-done((bf16[192,256]{1,0:T(8,128)(2,1)S(1)}, bf16[192,256]{1,0:T(8,128)(2,1)S(1)}, u32[]{:S(2)}, u32[]{:S(2)}) %collective-permute-start.8) | collective-permute-done | bytes 98336 | tf_op jit(solution)/shard_map/ppermute | solution.py:426
  19.3 1.1 %collective-permute-start.13 = (bf16[32,4096]{1,0:T(8,128)(2,1)S(1)}, bf16[32,4096]{1,0:T(8,128)(2,1)S(1)}, u32[]{:S(2)}, u32[]{:S(2)}) collective-permute-start(bf16[32,4096]{1,0:T(8,128)(2,1)S(1)} %get-tuple-element.90), channel_id=1, source_target_pairs={{0,4},{1,3},{2,6},{3,1},{4,0},{5,7},{6,2},{7,5},{8,12},{9,11},{10,... | collective-permute-start | bytes 786440 | tf_op jit(solution)/shard_map/ppermute | solution.py:426
  20.4 1.1 %collective-permute-start.11 = (bf16[192,256]{1,0:T(8,128)(2,1)S(1)}, bf16[192,256]{1,0:T(8,128)(2,1)S(1)}, u32[]{:S(2)}, u32[]{:S(2)}) collective-permute-start(bf16[192,256]{1,0:T(8,128)(2,1)S(1)} %get-tuple-element.62), channel_id=1, source_target_pairs={{0,4},{1,3},{2,6},{3,1},{4,0},{5,7},{6,2},{7,5},{8,12},{9,11},{10,... | collective-permute-start | bytes 294920 | tf_op jit(solution)/shard_map/ppermute | solution.py:426
  21.5 1.0 %collective-permute-start.12 = (bf16[32,4096]{1,0:T(8,128)(2,1)S(1)}, bf16[32,4096]{1,0:T(8,128)(2,1)S(1)}, u32[]{:S(2)}, u32[]{:S(2)}) collective-permute-start(bf16[32,4096]{1,0:T(8,128)(2,1)S(1)} %get-tuple-element.91), channel_id=1, source_target_pairs={{0,4},{1,3},{2,6},{3,1},{4,0},{5,7},{6,2},{7,5},{8,12},{9,11},{10,... | collective-permute-start | bytes 786440 | tf_op jit(solution)/shard_map/ppermute | solution.py:426
  22.5 2.3 %queries_own_chip.1 = (bf16[64,512]{1,0:T(8,128)(2,1)S(1)}, f32[256,128]{1,0:T(8,128)S(1)}, f32[2,8,96]{2,1,0:T(8,128)S(1)}) custom-call(s32[2]{0:T(128)S(1)} %copy-done.9, s32[2]{0:T(128)S(1)} %copy-done.10, bf16[1,8192]{1,0:T(2,128)(2,1)S(1)} %copy-done.5, bf16[1,8192,512]{2,1,0:T(8,128)(2,1)S(1)} %copy-done, bf16[1,128]{1,0:T(2,128)(2,1)S(1)} %copy-done.7, ...), custom_call_target="tpu_custom_call" | custom-call | tf_op jit(solution)/shard_map/queries_own_chip/pallas_call | solution.py:199
  24.8 1.7 %queries_neighbours.1.refs_3_ = bf16[128,512]{1,0:T(8,128)(2,1)S(1)} custom-call(bf16[1,8192]{1,0:T(2,128)(2,1)S(1)} %copy-done.5, bf16[1,8192,512]{2,1,0:T(8,128)(2,1)S(1)} %copy-done, bf16[1,128]{1,0:T(2,128)(2,1)S(1)} %copy-done.7, bf16[32,8192]{1,0:T(8,128)(2,1)S(1)} %collective-permute-done.1.refs_3_, ...), custom_call_target="tpu_custom_call" | custom-call | tf_op jit(solution)/shard_map/queries_neighbours/pallas_call | solution.py:199
  26.8 1.3 %attention_first.1 = (f32[192,512]{1,0:T(8,128)S(1)}, f32[192,128]{1,0:T(8,128)S(1)}, f32[192,128]{1,0:T(8,128)S(1)}, bf16[192,128]{1,0:T(8,128)(2,1)S(1)}, bf16...) custom-call(f32[256,128]{1,0:T(8,128)S(1)} %get-tuple-element.46.refs_0_, ...), custom_call_target="tpu_custom_call" | custom-call | tf_op jit(solution)/shard_map/attention_first/pallas_call | solution.py:317
  28.2 1.4 %collective-permute-done.12 = bf16[32,4096]{1,0:T(8,128)(2,1)S(1)} collective-permute-done((bf16[32,4096]{1,0:T(8,128)(2,1)S(1)}, bf16[32,4096]{1,0:T(8,128)(2,1)S(1)}, u32[]{:S(2)}, u32[]{:S(2)}) %collective-permute-start.12) | collective-permute-done | bytes 262176 | tf_op jit(solution)/shard_map/ppermute | solution.py:426
  33.1 2.3 %collective-permute-start.17 = (bf16[192,256]{1,0:T(8,128)(2,1)S(1)}, bf16[192,256]{1,0:T(8,128)(2,1)S(1)}, u32[]{:S(2)}, u32[]{:S(2)}) collective-permute-start(bf16[192,256]{1,0:T(8,128)(2,1)S(1)} %get-tuple-element.85.refs_0_), channel_id=1, source_target_pairs={{0,6},{1,7},{2,4},{3,5},{4,2},{5,3},{6,0},{7,1},{8,14},{9,15},{10,... | collective-permute-start | bytes 294920 | tf_op jit(solution)/shard_map/ppermute | solution.py:426
  35.4 1.2 %collective-permute-start.19 = (bf16[192,256]{1,0:T(8,128)(2,1)S(1)}, bf16[192,256]{1,0:T(8,128)(2,1)S(1)}, u32[]{:S(2)}, u32[]{:S(2)}) collective-permute-start(bf16[192,256]{1,0:T(8,128)(2,1)S(1)} %get-tuple-element.85.refs_0_), channel_id=1, source_target_pairs={{0,4},{1,3},{2,6},{3,1},{4,0},{5,7},{6,2},{7,5},{8,12},{9,11},{10,... | collective-permute-start | bytes 294920 | tf_op jit(solution)/shard_map/ppermute | solution.py:426
  36.7 2.6 %collective-permute-done.17.refs_1_ = bf16[192,256]{1,0:T(8,128)(2,1)S(1)} collective-permute-done((bf16[192,256]{1,0:T(8,128)(2,1)S(1)}, bf16[192,256]{1,0:T(8,128)(2,1)S(1)}, u32[]{:S(2)}, u32[]{:S(2)}) %collective-permute-start.17) | collective-permute-done | bytes 98336 | tf_op jit(solution)/shard_map/ppermute | solution.py:426
  39.3 1.7 %collective-permute-done.19.refs_2_ = bf16[192,256]{1,0:T(8,128)(2,1)S(1)} collective-permute-done((bf16[192,256]{1,0:T(8,128)(2,1)S(1)}, bf16[192,256]{1,0:T(8,128)(2,1)S(1)}, u32[]{:S(2)}, u32[]{:S(2)}) %collective-permute-start.19) | collective-permute-done | bytes 98336 | tf_op jit(solution)/shard_map/ppermute | solution.py:426
  41.6 1.1 %feature_grad_first.1.refs_4_ = f32[192,1024]{1,0:T(8,128)S(1)} custom-call(bf16[192,256]{1,0:T(8,128)(2,1)S(1)} %get-tuple-element.85.refs_0_, bf16[192,256]{1,0:T(8,128)(2,1)S(1)} %collective-permute-done.17.refs_1_, bf16[192,256]{1,0:T(8,128)(2,1)S(1)} %collective-permute-done.19.refs_2_, bf16[192,256]{1,0:T(8,128)(2,1)S(1)} %collective-permute-done.21.refs_3_, ...), custom_call_target="tpu_custom_call" | custom-call | tf_op jit(solution)/shard_map/feature_grad_first/pallas_call | solution.py:406
  43.5 2.2 %collective-permute-start.24 = (bf16[48,1024]{1,0:T(8,128)(2,1)S(1)}, bf16[48,1024]{1,0:T(8,128)(2,1)S(1)}, u32[]{:S(2)}, u32[]{:S(2)}) collective-permute-start(bf16[48,1024]{1,0:T(8,128)(2,1)S(1)} %get-tuple-element.87), channel_id=1, source_target_pairs={{0,8},{8,16},{16,24},{24,0},{1,9},{9,17},{17,25},{25,1},{2,10},{10... | collective-permute-start | bytes 294920 | tf_op jit(solution)/shard_map/ppermute | solution.py:522
  45.6 2.6 %collective-permute-start.25 = (bf16[48,1024]{1,0:T(8,128)(2,1)S(1)}, bf16[48,1024]{1,0:T(8,128)(2,1)S(1)}, u32[]{:S(2)}, u32[]{:S(2)}) collective-permute-start(bf16[48,1024]{1,0:T(8,128)(2,1)S(1)} %get-tuple-element.88), channel_id=1, source_target_pairs={{0,16},{8,24},{16,0},{24,8},{1,17},{9,25},{17,1},{25,9},{2,18},{10... | collective-permute-start | bytes 294920 | tf_op jit(solution)/shard_map/ppermute | solution.py:522
  48.2 1.3 %collective-permute-start.26 = (bf16[48,1024]{1,0:T(8,128)(2,1)S(1)}, bf16[48,1024]{1,0:T(8,128)(2,1)S(1)}, u32[]{:S(2)}, u32[]{:S(2)}) collective-permute-start(bf16[48,1024]{1,0:T(8,128)(2,1)S(1)} %get-tuple-element.89), channel_id=1, source_target_pairs={{0,24},{8,0},{16,8},{24,16},{1,25},{9,1},{17,9},{25,17},{2,26},{10... | collective-permute-start | bytes 294920 | tf_op jit(solution)/shard_map/ppermute | solution.py:522
  50.3 1.0 %collective-permute-done.24 = bf16[48,1024]{1,0:T(8,128)(2,1)S(1)} collective-permute-done((bf16[48,1024]{1,0:T(8,128)(2,1)S(1)}, bf16[48,1024]{1,0:T(8,128)(2,1)S(1)}, u32[]{:S(2)}, u32[]{:S(2)}) %collective-permute-start.24) | collective-permute-done | bytes 98336 | tf_op jit(solution)/shard_map/ppermute | solution.py:522
  51.3 3.8 %collective-permute-done.25 = bf16[48,1024]{1,0:T(8,128)(2,1)S(1)} collective-permute-done((bf16[48,1024]{1,0:T(8,128)(2,1)S(1)}, bf16[48,1024]{1,0:T(8,128)(2,1)S(1)}, u32[]{:S(2)}, u32[]{:S(2)}) %collective-permute-start.25) | collective-permute-done | bytes 98336 | tf_op jit(solution)/shard_map/ppermute | solution.py:522
  (68 shorter events, 12.7 us)
Async XLA Ops:
  0.6 18.1 %collective-permute-start.1 = (bf16[32,8192]{1,0:T(8,128)(2,1)}, bf16[32,8192]{1,0:T(8,128)(2,1)S(1)}, u32[]{:S(2)}, u32[]{:S(2)}) collective-permute-start(bf16[32,8192]{1,0:T(8,128)(2,1)} %bitcast.1), channel_id=1, source_target_pairs={{0,2},{1,5},{2,0},{3,7},{4,6},{5,1},{6,4},{7,3},{8,10},{9,13},{10,... | collective-permute-start | bytes 1572872 | tf_op jit(solution)/shard_map/ppermute | solution.py:426
  3.6 15.1 %collective-permute-start.2 = (bf16[32,8192]{1,0:T(8,128)(2,1)}, bf16[32,8192]{1,0:T(8,128)(2,1)S(1)}, u32[]{:S(2)}, u32[]{:S(2)}) collective-permute-start(bf16[32,8192]{1,0:T(8,128)(2,1)} %bitcast.2), channel_id=1, source_target_pairs={{0,4},{1,3},{2,6},{3,1},{4,0},{5,7},{6,2},{7,5},{8,12},{9,11},{10,... | collective-permute-start | bytes 1572872 | tf_op jit(solution)/shard_map/ppermute | solution.py:426
  9.2 1.5 %collective-permute-start.3 = (f32[192,256]{1,0:T(8,128)S(1)}, f32[192,256]{1,0:T(8,128)S(1)}, u32[]{:S(2)}, u32[]{:S(2)}) collective-permute-start(f32[192,256]{1,0:T(8,128)S(1)} %get-tuple-element.49), channel_id=1, source_target_pairs={{0,1},{1,0},{2,3},{3,2},{4,5},{5,4},{6,7},{7,6},{8,9},{9,8},{10,11... | collective-permute-start | bytes 589832 | tf_op jit(solution)/shard_map/ppermute | solution.py:426
  9.3 1.7 %collective-permute-start.4 = (f32[192,256]{1,0:T(8,128)S(1)}, f32[192,256]{1,0:T(8,128)S(1)}, u32[]{:S(2)}, u32[]{:S(2)}) collective-permute-start(f32[192,256]{1,0:T(8,128)S(1)} %get-tuple-element.50), channel_id=1, source_target_pairs={{0,1},{1,0},{2,3},{3,2},{4,5},{5,4},{6,7},{7,6},{8,9},{9,8},{10,11... | collective-permute-start | bytes 589832 | tf_op jit(solution)/shard_map/ppermute | solution.py:426
  9.8 1.5 %collective-permute-start.5 = (f32[192,256]{1,0:T(8,128)S(1)}, f32[192,256]{1,0:T(8,128)S(1)}, u32[]{:S(2)}, u32[]{:S(2)}) collective-permute-start(f32[192,256]{1,0:T(8,128)S(1)} %get-tuple-element.51), channel_id=1, source_target_pairs={{0,1},{1,0},{2,3},{3,2},{4,5},{5,4},{6,7},{7,6},{8,9},{9,8},{10,11... | collective-permute-start | bytes 589832 | tf_op jit(solution)/shard_map/ppermute | solution.py:426
  13.0 4.7 %collective-permute-start.7 = (bf16[192,256]{1,0:T(8,128)(2,1)S(1)}, bf16[192,256]{1,0:T(8,128)(2,1)S(1)}, u32[]{:S(2)}, u32[]{:S(2)}) collective-permute-start(bf16[192,256]{1,0:T(8,128)(2,1)S(1)} %get-tuple-element.53), channel_id=1, source_target_pairs={{0,2},{1,5},{2,0},{3,7},{4,6},{5,1},{6,4},{7,3},{8,10},{9,13},{10,... | collective-permute-start | bytes 294920 | tf_op jit(solution)/shard_map/ppermute | solution.py:426
  13.8 4.9 %collective-permute-start.8 = (bf16[192,256]{1,0:T(8,128)(2,1)S(1)}, bf16[192,256]{1,0:T(8,128)(2,1)S(1)}, u32[]{:S(2)}, u32[]{:S(2)}) collective-permute-start(bf16[192,256]{1,0:T(8,128)(2,1)S(1)} %get-tuple-element.54), channel_id=1, source_target_pairs={{0,2},{1,5},{2,0},{3,7},{4,6},{5,1},{6,4},{7,3},{8,10},{9,13},{10,... | collective-permute-start | bytes 294920 | tf_op jit(solution)/shard_map/ppermute | solution.py:426
  15.1 6.4 %collective-permute-start = (bf16[32,8192]{1,0:T(8,128)(2,1)S(1)}, bf16[32,8192]{1,0:T(8,128)(2,1)S(1)}, u32[]{:S(2)}, u32[]{:S(2)}) collective-permute-start(bf16[32,8192]{1,0:T(8,128)(2,1)S(1)} %bitcast.3), channel_id=1, source_target_pairs={{0,1},{1,0},{2,3},{3,2},{4,5},{5,4},{6,7},{7,6},{8,9},{9,8},{10,11... | collective-permute-start | bytes 1572872 | tf_op jit(solution)/shard_map/ppermute | solution.py:426
  18.7 6.1 %collective-permute-start.9 = (bf16[32,8192]{1,0:T(8,128)(2,1)S(1)}, bf16[32,8192]{1,0:T(8,128)(2,1)S(1)}, u32[]{:S(2)}, u32[]{:S(2)}) collective-permute-start(bf16[32,8192]{1,0:T(8,128)(2,1)S(1)} %collective-permute-done.1.refs_3_), channel_id=1, source_target_pairs={{0,1},{1,0},{2,3},{3,2},{4,5},{5,4},{6,7},{7,6},{8,9},{9,8},{10,11... | collective-permute-start | bytes 1572872 | tf_op jit(solution)/shard_map/ppermute | solution.py:426
  18.8 6.1 %collective-permute-start.10 = (bf16[32,8192]{1,0:T(8,128)(2,1)S(1)}, bf16[32,8192]{1,0:T(8,128)(2,1)S(1)}, u32[]{:S(2)}, u32[]{:S(2)}) collective-permute-start(bf16[32,8192]{1,0:T(8,128)(2,1)S(1)} %collective-permute-done.2.refs_5_), channel_id=1, source_target_pairs={{0,1},{1,0},{2,3},{3,2},{4,5},{5,4},{6,7},{7,6},{8,9},{9,8},{10,11... | collective-permute-start | bytes 1572872 | tf_op jit(solution)/shard_map/ppermute | solution.py:426
  19.3 8.8 %collective-permute-start.13 = (bf16[32,4096]{1,0:T(8,128)(2,1)S(1)}, bf16[32,4096]{1,0:T(8,128)(2,1)S(1)}, u32[]{:S(2)}, u32[]{:S(2)}) collective-permute-start(bf16[32,4096]{1,0:T(8,128)(2,1)S(1)} %get-tuple-element.90), channel_id=1, source_target_pairs={{0,4},{1,3},{2,6},{3,1},{4,0},{5,7},{6,2},{7,5},{8,12},{9,11},{10,... | collective-permute-start | bytes 786440 | tf_op jit(solution)/shard_map/ppermute | solution.py:426
  20.4 6.4 %collective-permute-start.11 = (bf16[192,256]{1,0:T(8,128)(2,1)S(1)}, bf16[192,256]{1,0:T(8,128)(2,1)S(1)}, u32[]{:S(2)}, u32[]{:S(2)}) collective-permute-start(bf16[192,256]{1,0:T(8,128)(2,1)S(1)} %get-tuple-element.62), channel_id=1, source_target_pairs={{0,4},{1,3},{2,6},{3,1},{4,0},{5,7},{6,2},{7,5},{8,12},{9,11},{10,... | collective-permute-start | bytes 294920 | tf_op jit(solution)/shard_map/ppermute | solution.py:426
  21.5 8.1 %collective-permute-start.12 = (bf16[32,4096]{1,0:T(8,128)(2,1)S(1)}, bf16[32,4096]{1,0:T(8,128)(2,1)S(1)}, u32[]{:S(2)}, u32[]{:S(2)}) collective-permute-start(bf16[32,4096]{1,0:T(8,128)(2,1)S(1)} %get-tuple-element.91), channel_id=1, source_target_pairs={{0,4},{1,3},{2,6},{3,1},{4,0},{5,7},{6,2},{7,5},{8,12},{9,11},{10,... | collective-permute-start | bytes 786440 | tf_op jit(solution)/shard_map/ppermute | solution.py:426
  28.1 1.6 %collective-permute-start.14 = (bf16[32,4096]{1,0:T(8,128)(2,1)S(1)}, bf16[32,4096]{1,0:T(8,128)(2,1)S(1)}, u32[]{:S(2)}, u32[]{:S(2)}) collective-permute-start(bf16[32,4096]{1,0:T(8,128)(2,1)S(1)} %collective-permute-done.13.refs_3_), channel_id=1, source_target_pairs={{0,1},{1,0},{2,3},{3,2},{4,5},{5,4},{6,7},{7,6},{8,9},{9,8},{10,11... | collective-permute-start | bytes 786440 | tf_op jit(solution)/shard_map/ppermute | solution.py:426
  29.9 1.8 %collective-permute-start.15 = (bf16[32,2048]{1,0:T(8,128)(2,1)S(1)}, bf16[32,2048]{1,0:T(8,128)(2,1)S(1)}, u32[]{:S(2)}, u32[]{:S(2)}) collective-permute-start(bf16[32,2048]{1,0:T(8,128)(2,1)S(1)} %get-tuple-element.93.refs_3_), channel_id=1, source_target_pairs={{0,1},{1,0},{2,3},{3,2},{4,5},{5,4},{6,7},{7,6},{8,9},{9,8},{10,11... | collective-permute-start | bytes 393224 | tf_op jit(solution)/shard_map/ppermute | solution.py:426
  33.1 6.2 %collective-permute-start.17 = (bf16[192,256]{1,0:T(8,128)(2,1)S(1)}, bf16[192,256]{1,0:T(8,128)(2,1)S(1)}, u32[]{:S(2)}, u32[]{:S(2)}) collective-permute-start(bf16[192,256]{1,0:T(8,128)(2,1)S(1)} %get-tuple-element.85.refs_0_), channel_id=1, source_target_pairs={{0,6},{1,7},{2,4},{3,5},{4,2},{5,3},{6,0},{7,1},{8,14},{9,15},{10,... | collective-permute-start | bytes 294920 | tf_op jit(solution)/shard_map/ppermute | solution.py:426
  35.4 5.6 %collective-permute-start.19 = (bf16[192,256]{1,0:T(8,128)(2,1)S(1)}, bf16[192,256]{1,0:T(8,128)(2,1)S(1)}, u32[]{:S(2)}, u32[]{:S(2)}) collective-permute-start(bf16[192,256]{1,0:T(8,128)(2,1)S(1)} %get-tuple-element.85.refs_0_), channel_id=1, source_target_pairs={{0,4},{1,3},{2,6},{3,1},{4,0},{5,7},{6,2},{7,5},{8,12},{9,11},{10,... | collective-permute-start | bytes 294920 | tf_op jit(solution)/shard_map/ppermute | solution.py:426
  36.7 4.6 %collective-permute-start.21 = (bf16[192,256]{1,0:T(8,128)(2,1)S(1)}, bf16[192,256]{1,0:T(8,128)(2,1)S(1)}, u32[]{:S(2)}, u32[]{:S(2)}) collective-permute-start(bf16[192,256]{1,0:T(8,128)(2,1)S(1)} %get-tuple-element.85.refs_0_), channel_id=1, source_target_pairs={{0,2},{1,5},{2,0},{3,7},{4,6},{5,1},{6,4},{7,3},{8,10},{9,13},{10,... | collective-permute-start | bytes 294920 | tf_op jit(solution)/shard_map/ppermute | solution.py:426
  36.7 4.9 %collective-permute-start.23 = (bf16[192,256]{1,0:T(8,128)(2,1)S(1)}, bf16[192,256]{1,0:T(8,128)(2,1)S(1)}, u32[]{:S(2)}, u32[]{:S(2)}) collective-permute-start(bf16[192,256]{1,0:T(8,128)(2,1)S(1)} %get-tuple-element.85.refs_0_), channel_id=1, source_target_pairs={{0,1},{1,0},{2,3},{3,2},{4,5},{5,4},{6,7},{7,6},{8,9},{9,8},{10,11... | collective-permute-start | bytes 294920 | tf_op jit(solution)/shard_map/ppermute | solution.py:426
  39.3 3.3 %collective-permute-start.18 = (bf16[192,256]{1,0:T(8,128)(2,1)S(1)}, bf16[192,256]{1,0:T(8,128)(2,1)S(1)}, u32[]{:S(2)}, u32[]{:S(2)}) collective-permute-start(bf16[192,256]{1,0:T(8,128)(2,1)S(1)} %collective-permute-done.17.refs_1_), channel_id=1, source_target_pairs={{0,1},{1,0},{2,3},{3,2},{4,5},{5,4},{6,7},{7,6},{8,9},{9,8},{10,11... | collective-permute-start | bytes 294920 | tf_op jit(solution)/shard_map/ppermute | solution.py:426
  41.0 1.6 %collective-permute-start.20 = (bf16[192,256]{1,0:T(8,128)(2,1)S(1)}, bf16[192,256]{1,0:T(8,128)(2,1)S(1)}, u32[]{:S(2)}, u32[]{:S(2)}) collective-permute-start(bf16[192,256]{1,0:T(8,128)(2,1)S(1)} %collective-permute-done.19.refs_2_), channel_id=1, source_target_pairs={{0,1},{1,0},{2,3},{3,2},{4,5},{5,4},{6,7},{7,6},{8,9},{9,8},{10,11... | collective-permute-start | bytes 294920 | tf_op jit(solution)/shard_map/ppermute | solution.py:426
  43.5 7.9 %collective-permute-start.24 = (bf16[48,1024]{1,0:T(8,128)(2,1)S(1)}, bf16[48,1024]{1,0:T(8,128)(2,1)S(1)}, u32[]{:S(2)}, u32[]{:S(2)}) collective-permute-start(bf16[48,1024]{1,0:T(8,128)(2,1)S(1)} %get-tuple-element.87), channel_id=1, source_target_pairs={{0,8},{8,16},{16,24},{24,0},{1,9},{9,17},{17,25},{25,1},{2,10},{10... | collective-permute-start | bytes 294920 | tf_op jit(solution)/shard_map/ppermute | solution.py:522
  45.6 9.5 %collective-permute-start.25 = (bf16[48,1024]{1,0:T(8,128)(2,1)S(1)}, bf16[48,1024]{1,0:T(8,128)(2,1)S(1)}, u32[]{:S(2)}, u32[]{:S(2)}) collective-permute-start(bf16[48,1024]{1,0:T(8,128)(2,1)S(1)} %get-tuple-element.88), channel_id=1, source_target_pairs={{0,16},{8,24},{16,0},{24,8},{1,17},{9,25},{17,1},{25,9},{2,18},{10... | collective-permute-start | bytes 294920 | tf_op jit(solution)/shard_map/ppermute | solution.py:522
  48.2 6.9 %collective-permute-start.26 = (bf16[48,1024]{1,0:T(8,128)(2,1)S(1)}, bf16[48,1024]{1,0:T(8,128)(2,1)S(1)}, u32[]{:S(2)}, u32[]{:S(2)}) collective-permute-start(bf16[48,1024]{1,0:T(8,128)(2,1)S(1)} %get-tuple-element.89), channel_id=1, source_target_pairs={{0,24},{8,0},{16,8},{24,16},{1,25},{9,1},{17,9},{25,17},{2,26},{10... | collective-permute-start | bytes 294920 | tf_op jit(solution)/shard_map/ppermute | solution.py:522
  (14 other events, 113.5 us)

commit v4 on v3

--- a/solution.py
+++ b/solution.py
@@ -507,12 +507,13 @@
     attended = assemble([places_of(near) + places_of(next_to), far], [early, late], grad_out)
 
     same_core = {(0, 0): block}
-    same_core.update({distance(m): exchange(block, distance(m)) for m in reversed(masks)})
+    same_core.update({distance(m): exchange(block, distance(m)) for m in masks})
     swapped = {other_core(pair): swap(x) for pair, x in same_core.items()}
     before = None
     blocks = {**same_core, **swapped}
     if per_kv == 1:
-        soon = {pair: blocks.pop(pair) for pair in [*same_core, (1, 1)]}
+        first = [*same_core, *list(swapped)[:2]]
+        soon = {pair: blocks.pop(pair) for pair in first}
         before = feature_gradient(soon, w_key_value, per_kv, sections, last=False)
     pieces = feature_gradient(blocks, w_key_value, per_kv, sections, before)
     feature_grad, leaving = pieces[0], pieces[1:]

time: 56 us -> 56.3 us (level)
    ppermute x24, waiting for transfers between devices: 12.2 us -> 12.8 us  [exchange(): lax.ppermute(x, 'tensor', [(i, i ^ pair[i % 2]) for i in range(count)])]
  transfers between devices with their start and end apart: 27 -> 27, of which waited for: 14 -> 13; matrix products, arithmetic and copies ran while one was open for 0% -> 0% of each run, Pallas kernels for 18% -> 18%
where the time goes in v4:
time: 56.3 us; the launch traced here: 56.1 us
  starting transfers between devices  21.4 us (38%)
  waiting for transfers between devices  17.5 us (31%)
  Pallas kernels  12.3 us (22%)
  local copies, waits for them, and re-layouts  3.27 us (6%)
  between operations  0.86 us (2%)
  other arithmetic  0.72 us (1%)
    ppermute x24, starting transfers between devices, exchange(): lax.ppermute(x, 'tensor', [(i, i ^ pair[i % 2]) for i in range(count)])  15.9 us
    ppermute x24, waiting for transfers between devices, exchange(): lax.ppermute(x, 'tensor', [(i, i ^ pair[i % 2]) for i in range(count)])  12.8 us
    pallas_call x5, Pallas kernels, queries_of(): pl.pallas_call(functools.partial(query_kernel, [len(parts) for parts in g...  5.91 us
    ppermute x3, starting transfers between devices, shards(): arrived.append(lax.ppermute(leaving[k - 1], 'section', perm))  5.58 us
    ppermute x3, waiting for transfers between devices, shards(): arrived.append(lax.ppermute(leaving[k - 1], 'section', perm))  4.65 us
    unnamed x22, local copies, waits for them, and re-layouts  3.22 us
    pallas_call x2, Pallas kernels, attention(): pl.pallas_call(functools.partial(attention_kernel, places, count, rows, l...  2.12 us
    pallas_call x2, Pallas kernels, feature_gradient(): pl.pallas_call(functools.partial(grad_kernel, pairs, per_kv, sections, be...  1.86 us
  transfers between devices with their start and end apart: 27, of which 13 were waited for; matrix products, arithmetic and copies ran while one was open for 0% of the time, Pallas kernels for 18%

profile of v4, /device:TPU:0, one launch (start us, length us, event | category | flops | bytes accessed | tf_op | source)
XLA Modules:
  0.0 56.1 jit_solution(15753005208911610460)
XLA Ops:
  0.6 3.0 %collective-permute-start.1 = (bf16[32,8192]{1,0:T(8,128)(2,1)}, bf16[32,8192]{1,0:T(8,128)(2,1)S(1)}, u32[]{:S(2)}, u32[]{:S(2)}) collective-permute-start(bf16[32,8192]{1,0:T(8,128)(2,1)} %bitcast.1), channel_id=1, source_target_pairs={{0,2},{1,5},{2,0},{3,7},{4,6},{5,1},{6,4},{7,3},{8,10},{9,13},{10,... | collective-permute-start | bytes 1572872 | tf_op jit(solution)/shard_map/ppermute | solution.py:426
  3.6 1.5 %collective-permute-start.2 = (bf16[32,8192]{1,0:T(8,128)(2,1)}, bf16[32,8192]{1,0:T(8,128)(2,1)S(1)}, u32[]{:S(2)}, u32[]{:S(2)}) collective-permute-start(bf16[32,8192]{1,0:T(8,128)(2,1)} %bitcast.2), channel_id=1, source_target_pairs={{0,4},{1,3},{2,6},{3,1},{4,0},{5,7},{6,2},{7,5},{8,12},{9,11},{10,... | collective-permute-start | bytes 1572872 | tf_op jit(solution)/shard_map/ppermute | solution.py:426
  5.2 2.2 %copy-done.1 = bf16[1,1024,2048]{2,1,0:T(8,128)(2,1)S(1)} copy-done((bf16[1,1024,2048]{2,1,0:T(8,128)(2,1)S(1)}, bf16[1,1024,2048]{2,1,0:T(8,128)(2,1)}, u32[]{:S(2)}) %copy-start.1) | copy-done | bytes 4194328
  7.4 1.0 %copy-done.3 = bf16[192,1024]{1,0:T(8,128)(2,1)S(1)} copy-done((bf16[192,1024]{1,0:T(8,128)(2,1)S(1)}, bf16[192,1024]{1,0:T(8,128)(2,1)}, u32[]{:S(2)}) %copy-start.3) | copy-done | bytes 393240
  11.3 0.9 %collective-permute-done.6.refs_3_ = f32[192,256]{1,0:T(8,128)S(1)} collective-permute-done((f32[192,256]{1,0:T(8,128)S(1)}, f32[192,256]{1,0:T(8,128)S(1)}, u32[]{:S(2)}, u32[]{:S(2)}) %collective-permute-start.6) | collective-permute-done | bytes 196640 | tf_op jit(solution)/shard_map/ppermute | solution.py:426
  13.8 1.3 %collective-permute-start.8 = (bf16[192,256]{1,0:T(8,128)(2,1)S(1)}, bf16[192,256]{1,0:T(8,128)(2,1)S(1)}, u32[]{:S(2)}, u32[]{:S(2)}) collective-permute-start(bf16[192,256]{1,0:T(8,128)(2,1)S(1)} %get-tuple-element.54), channel_id=1, source_target_pairs={{0,2},{1,5},{2,0},{3,7},{4,6},{5,1},{6,4},{7,3},{8,10},{9,13},{10,... | collective-permute-start | bytes 294920 | tf_op jit(solution)/shard_map/ppermute | solution.py:426
  15.1 2.6 %collective-permute-done.7.refs_2_ = bf16[192,256]{1,0:T(8,128)(2,1)S(1)} collective-permute-done((bf16[192,256]{1,0:T(8,128)(2,1)S(1)}, bf16[192,256]{1,0:T(8,128)(2,1)S(1)}, u32[]{:S(2)}, u32[]{:S(2)}) %collective-permute-start.7) | collective-permute-done | bytes 98336 | tf_op jit(solution)/shard_map/ppermute | solution.py:426
  17.7 1.1 %collective-permute-done.8.refs_3_ = bf16[192,256]{1,0:T(8,128)(2,1)S(1)} collective-permute-done((bf16[192,256]{1,0:T(8,128)(2,1)S(1)}, bf16[192,256]{1,0:T(8,128)(2,1)S(1)}, u32[]{:S(2)}, u32[]{:S(2)}) %collective-permute-start.8) | collective-permute-done | bytes 98336 | tf_op jit(solution)/shard_map/ppermute | solution.py:426
  19.3 1.1 %collective-permute-start.13 = (bf16[32,4096]{1,0:T(8,128)(2,1)S(1)}, bf16[32,4096]{1,0:T(8,128)(2,1)S(1)}, u32[]{:S(2)}, u32[]{:S(2)}) collective-permute-start(bf16[32,4096]{1,0:T(8,128)(2,1)S(1)} %get-tuple-element.90), channel_id=1, source_target_pairs={{0,4},{1,3},{2,6},{3,1},{4,0},{5,7},{6,2},{7,5},{8,12},{9,11},{10,... | collective-permute-start | bytes 786440 | tf_op jit(solution)/shard_map/ppermute | solution.py:426
  20.4 1.1 %collective-permute-start.11 = (bf16[192,256]{1,0:T(8,128)(2,1)S(1)}, bf16[192,256]{1,0:T(8,128)(2,1)S(1)}, u32[]{:S(2)}, u32[]{:S(2)}) collective-permute-start(bf16[192,256]{1,0:T(8,128)(2,1)S(1)} %get-tuple-element.62), channel_id=1, source_target_pairs={{0,4},{1,3},{2,6},{3,1},{4,0},{5,7},{6,2},{7,5},{8,12},{9,11},{10,... | collective-permute-start | bytes 294920 | tf_op jit(solution)/shard_map/ppermute | solution.py:426
  21.5 1.0 %collective-permute-start.12 = (bf16[32,4096]{1,0:T(8,128)(2,1)S(1)}, bf16[32,4096]{1,0:T(8,128)(2,1)S(1)}, u32[]{:S(2)}, u32[]{:S(2)}) collective-permute-start(bf16[32,4096]{1,0:T(8,128)(2,1)S(1)} %get-tuple-element.91), channel_id=1, source_target_pairs={{0,4},{1,3},{2,6},{3,1},{4,0},{5,7},{6,2},{7,5},{8,12},{9,11},{10,... | collective-permute-start | bytes 786440 | tf_op jit(solution)/shard_map/ppermute | solution.py:426
  22.5 2.3 %queries_own_chip.1 = (bf16[64,512]{1,0:T(8,128)(2,1)S(1)}, f32[256,128]{1,0:T(8,128)S(1)}, f32[2,8,96]{2,1,0:T(8,128)S(1)}) custom-call(s32[2]{0:T(128)S(1)} %copy-done.9, s32[2]{0:T(128)S(1)} %copy-done.10, bf16[1,8192]{1,0:T(2,128)(2,1)S(1)} %copy-done.5, bf16[1,8192,512]{2,1,0:T(8,128)(2,1)S(1)} %copy-done, bf16[1,128]{1,0:T(2,128)(2,1)S(1)} %copy-done.7, ...), custom_call_target="tpu_custom_call" | custom-call | tf_op jit(solution)/shard_map/queries_own_chip/pallas_call | solution.py:199
  24.8 1.7 %queries_neighbours.1.refs_3_ = bf16[128,512]{1,0:T(8,128)(2,1)S(1)} custom-call(bf16[1,8192]{1,0:T(2,128)(2,1)S(1)} %copy-done.5, bf16[1,8192,512]{2,1,0:T(8,128)(2,1)S(1)} %copy-done, bf16[1,128]{1,0:T(2,128)(2,1)S(1)} %copy-done.7, bf16[32,8192]{1,0:T(8,128)(2,1)S(1)} %collective-permute-done.1.refs_3_, ...), custom_call_target="tpu_custom_call" | custom-call | tf_op jit(solution)/shard_map/queries_neighbours/pallas_call | solution.py:199
  26.8 1.3 %attention_first.1 = (f32[192,512]{1,0:T(8,128)S(1)}, f32[192,128]{1,0:T(8,128)S(1)}, f32[192,128]{1,0:T(8,128)S(1)}, bf16[192,128]{1,0:T(8,128)(2,1)S(1)}, bf16...) custom-call(f32[256,128]{1,0:T(8,128)S(1)} %get-tuple-element.46.refs_0_, ...), custom_call_target="tpu_custom_call" | custom-call | tf_op jit(solution)/shard_map/attention_first/pallas_call | solution.py:317
  28.2 1.4 %collective-permute-done.12 = bf16[32,4096]{1,0:T(8,128)(2,1)S(1)} collective-permute-done((bf16[32,4096]{1,0:T(8,128)(2,1)S(1)}, bf16[32,4096]{1,0:T(8,128)(2,1)S(1)}, u32[]{:S(2)}, u32[]{:S(2)}) %collective-permute-start.12) | collective-permute-done | bytes 262176 | tf_op jit(solution)/shard_map/ppermute | solution.py:426
  33.1 2.1 %collective-permute-start.21 = (bf16[192,256]{1,0:T(8,128)(2,1)S(1)}, bf16[192,256]{1,0:T(8,128)(2,1)S(1)}, u32[]{:S(2)}, u32[]{:S(2)}) collective-permute-start(bf16[192,256]{1,0:T(8,128)(2,1)S(1)} %get-tuple-element.85.refs_0_), channel_id=1, source_target_pairs={{0,2},{1,5},{2,0},{3,7},{4,6},{5,1},{6,4},{7,3},{8,10},{9,13},{10,... | collective-permute-start | bytes 294920 | tf_op jit(solution)/shard_map/ppermute | solution.py:426
  36.8 2.1 %collective-permute-done.21.refs_1_ = bf16[192,256]{1,0:T(8,128)(2,1)S(1)} collective-permute-done((bf16[192,256]{1,0:T(8,128)(2,1)S(1)}, bf16[192,256]{1,0:T(8,128)(2,1)S(1)}, u32[]{:S(2)}, u32[]{:S(2)}) %collective-permute-start.21) | collective-permute-done | bytes 98336 | tf_op jit(solution)/shard_map/ppermute | solution.py:426
  38.8 3.1 %collective-permute-done.17.refs_2_ = bf16[192,256]{1,0:T(8,128)(2,1)S(1)} collective-permute-done((bf16[192,256]{1,0:T(8,128)(2,1)S(1)}, bf16[192,256]{1,0:T(8,128)(2,1)S(1)}, u32[]{:S(2)}, u32[]{:S(2)}) %collective-permute-start.17) | collective-permute-done | bytes 98336 | tf_op jit(solution)/shard_map/ppermute | solution.py:426
  42.5 1.3 %feature_grad_first.1.refs_3_ = f32[192,1024]{1,0:T(8,128)S(1)} custom-call(bf16[192,256]{1,0:T(8,128)(2,1)S(1)} %get-tuple-element.85.refs_0_, bf16[192,256]{1,0:T(8,128)(2,1)S(1)} %collective-permute-done.21.refs_1_, bf16[192,256]{1,0:T(8,128)(2,1)S(1)} %collective-permute-done.17.refs_2_, bf16[192,256]{1,0:T(8,128)(2,1)S(1)} %collective-permute-done.19.refs_3_, ...), custom_call_target="tpu_custom_call" | custom-call | tf_op jit(solution)/shard_map/feature_grad_first/pallas_call | solution.py:406
  44.4 1.6 %collective-permute-start.24 = (bf16[48,1024]{1,0:T(8,128)(2,1)S(1)}, bf16[48,1024]{1,0:T(8,128)(2,1)S(1)}, u32[]{:S(2)}, u32[]{:S(2)}) collective-permute-start(bf16[48,1024]{1,0:T(8,128)(2,1)S(1)} %get-tuple-element.87), channel_id=1, source_target_pairs={{0,8},{8,16},{16,24},{24,0},{1,9},{9,17},{17,25},{25,1},{2,10},{10... | collective-permute-start | bytes 294920 | tf_op jit(solution)/shard_map/ppermute | solution.py:523
  46.0 2.6 %collective-permute-start.25 = (bf16[48,1024]{1,0:T(8,128)(2,1)S(1)}, bf16[48,1024]{1,0:T(8,128)(2,1)S(1)}, u32[]{:S(2)}, u32[]{:S(2)}) collective-permute-start(bf16[48,1024]{1,0:T(8,128)(2,1)S(1)} %get-tuple-element.88), channel_id=1, source_target_pairs={{0,16},{8,24},{16,0},{24,8},{1,17},{9,25},{17,1},{25,9},{2,18},{10... | collective-permute-start | bytes 294920 | tf_op jit(solution)/shard_map/ppermute | solution.py:523
  48.6 1.4 %collective-permute-start.26 = (bf16[48,1024]{1,0:T(8,128)(2,1)S(1)}, bf16[48,1024]{1,0:T(8,128)(2,1)S(1)}, u32[]{:S(2)}, u32[]{:S(2)}) collective-permute-start(bf16[48,1024]{1,0:T(8,128)(2,1)S(1)} %get-tuple-element.89), channel_id=1, source_target_pairs={{0,24},{8,0},{16,8},{24,16},{1,25},{9,1},{17,9},{25,17},{2,26},{10... | collective-permute-start | bytes 294920 | tf_op jit(solution)/shard_map/ppermute | solution.py:523
  50.7 1.1 %collective-permute-done.24 = bf16[48,1024]{1,0:T(8,128)(2,1)S(1)} collective-permute-done((bf16[48,1024]{1,0:T(8,128)(2,1)S(1)}, bf16[48,1024]{1,0:T(8,128)(2,1)S(1)}, u32[]{:S(2)}, u32[]{:S(2)}) %collective-permute-start.24) | collective-permute-done | bytes 98336 | tf_op jit(solution)/shard_map/ppermute | solution.py:523
  51.9 3.5 %collective-permute-done.25 = bf16[48,1024]{1,0:T(8,128)(2,1)S(1)} collective-permute-done((bf16[48,1024]{1,0:T(8,128)(2,1)S(1)}, bf16[48,1024]{1,0:T(8,128)(2,1)S(1)}, u32[]{:S(2)}, u32[]{:S(2)}) %collective-permute-start.25) | collective-permute-done | bytes 98336 | tf_op jit(solution)/shard_map/ppermute | solution.py:523
  (68 shorter events, 13.2 us)
Async XLA Ops:
  0.6 18.1 %collective-permute-start.1 = (bf16[32,8192]{1,0:T(8,128)(2,1)}, bf16[32,8192]{1,0:T(8,128)(2,1)S(1)}, u32[]{:S(2)}, u32[]{:S(2)}) collective-permute-start(bf16[32,8192]{1,0:T(8,128)(2,1)} %bitcast.1), channel_id=1, source_target_pairs={{0,2},{1,5},{2,0},{3,7},{4,6},{5,1},{6,4},{7,3},{8,10},{9,13},{10,... | collective-permute-start | bytes 1572872 | tf_op jit(solution)/shard_map/ppermute | solution.py:426
  3.6 15.1 %collective-permute-start.2 = (bf16[32,8192]{1,0:T(8,128)(2,1)}, bf16[32,8192]{1,0:T(8,128)(2,1)S(1)}, u32[]{:S(2)}, u32[]{:S(2)}) collective-permute-start(bf16[32,8192]{1,0:T(8,128)(2,1)} %bitcast.2), channel_id=1, source_target_pairs={{0,4},{1,3},{2,6},{3,1},{4,0},{5,7},{6,2},{7,5},{8,12},{9,11},{10,... | collective-permute-start | bytes 1572872 | tf_op jit(solution)/shard_map/ppermute | solution.py:426
  9.2 1.5 %collective-permute-start.3 = (f32[192,256]{1,0:T(8,128)S(1)}, f32[192,256]{1,0:T(8,128)S(1)}, u32[]{:S(2)}, u32[]{:S(2)}) collective-permute-start(f32[192,256]{1,0:T(8,128)S(1)} %get-tuple-element.49), channel_id=1, source_target_pairs={{0,1},{1,0},{2,3},{3,2},{4,5},{5,4},{6,7},{7,6},{8,9},{9,8},{10,11... | collective-permute-start | bytes 589832 | tf_op jit(solution)/shard_map/ppermute | solution.py:426
  9.3 1.7 %collective-permute-start.4 = (f32[192,256]{1,0:T(8,128)S(1)}, f32[192,256]{1,0:T(8,128)S(1)}, u32[]{:S(2)}, u32[]{:S(2)}) collective-permute-start(f32[192,256]{1,0:T(8,128)S(1)} %get-tuple-element.50), channel_id=1, source_target_pairs={{0,1},{1,0},{2,3},{3,2},{4,5},{5,4},{6,7},{7,6},{8,9},{9,8},{10,11... | collective-permute-start | bytes 589832 | tf_op jit(solution)/shard_map/ppermute | solution.py:426
  13.0 4.7 %collective-permute-start.7 = (bf16[192,256]{1,0:T(8,128)(2,1)S(1)}, bf16[192,256]{1,0:T(8,128)(2,1)S(1)}, u32[]{:S(2)}, u32[]{:S(2)}) collective-permute-start(bf16[192,256]{1,0:T(8,128)(2,1)S(1)} %get-tuple-element.53), channel_id=1, source_target_pairs={{0,2},{1,5},{2,0},{3,7},{4,6},{5,1},{6,4},{7,3},{8,10},{9,13},{10,... | collective-permute-start | bytes 294920 | tf_op jit(solution)/shard_map/ppermute | solution.py:426
  13.8 4.9 %collective-permute-start.8 = (bf16[192,256]{1,0:T(8,128)(2,1)S(1)}, bf16[192,256]{1,0:T(8,128)(2,1)S(1)}, u32[]{:S(2)}, u32[]{:S(2)}) collective-permute-start(bf16[192,256]{1,0:T(8,128)(2,1)S(1)} %get-tuple-element.54), channel_id=1, source_target_pairs={{0,2},{1,5},{2,0},{3,7},{4,6},{5,1},{6,4},{7,3},{8,10},{9,13},{10,... | collective-permute-start | bytes 294920 | tf_op jit(solution)/shard_map/ppermute | solution.py:426
  15.1 6.4 %collective-permute-start = (bf16[32,8192]{1,0:T(8,128)(2,1)S(1)}, bf16[32,8192]{1,0:T(8,128)(2,1)S(1)}, u32[]{:S(2)}, u32[]{:S(2)}) collective-permute-start(bf16[32,8192]{1,0:T(8,128)(2,1)S(1)} %bitcast.3), channel_id=1, source_target_pairs={{0,1},{1,0},{2,3},{3,2},{4,5},{5,4},{6,7},{7,6},{8,9},{9,8},{10,11... | collective-permute-start | bytes 1572872 | tf_op jit(solution)/shard_map/ppermute | solution.py:426
  18.7 6.1 %collective-permute-start.9 = (bf16[32,8192]{1,0:T(8,128)(2,1)S(1)}, bf16[32,8192]{1,0:T(8,128)(2,1)S(1)}, u32[]{:S(2)}, u32[]{:S(2)}) collective-permute-start(bf16[32,8192]{1,0:T(8,128)(2,1)S(1)} %collective-permute-done.1.refs_3_), channel_id=1, source_target_pairs={{0,1},{1,0},{2,3},{3,2},{4,5},{5,4},{6,7},{7,6},{8,9},{9,8},{10,11... | collective-permute-start | bytes 1572872 | tf_op jit(solution)/shard_map/ppermute | solution.py:426
  18.8 6.1 %collective-permute-start.10 = (bf16[32,8192]{1,0:T(8,128)(2,1)S(1)}, bf16[32,8192]{1,0:T(8,128)(2,1)S(1)}, u32[]{:S(2)}, u32[]{:S(2)}) collective-permute-start(bf16[32,8192]{1,0:T(8,128)(2,1)S(1)} %collective-permute-done.2.refs_5_), channel_id=1, source_target_pairs={{0,1},{1,0},{2,3},{3,2},{4,5},{5,4},{6,7},{7,6},{8,9},{9,8},{10,11... | collective-permute-start | bytes 1572872 | tf_op jit(solution)/shard_map/ppermute | solution.py:426
  19.3 8.8 %collective-permute-start.13 = (bf16[32,4096]{1,0:T(8,128)(2,1)S(1)}, bf16[32,4096]{1,0:T(8,128)(2,1)S(1)}, u32[]{:S(2)}, u32[]{:S(2)}) collective-permute-start(bf16[32,4096]{1,0:T(8,128)(2,1)S(1)} %get-tuple-element.90), channel_id=1, source_target_pairs={{0,4},{1,3},{2,6},{3,1},{4,0},{5,7},{6,2},{7,5},{8,12},{9,11},{10,... | collective-permute-start | bytes 786440 | tf_op jit(solution)/shard_map/ppermute | solution.py:426
  20.4 6.4 %collective-permute-start.11 = (bf16[192,256]{1,0:T(8,128)(2,1)S(1)}, bf16[192,256]{1,0:T(8,128)(2,1)S(1)}, u32[]{:S(2)}, u32[]{:S(2)}) collective-permute-start(bf16[192,256]{1,0:T(8,128)(2,1)S(1)} %get-tuple-element.62), channel_id=1, source_target_pairs={{0,4},{1,3},{2,6},{3,1},{4,0},{5,7},{6,2},{7,5},{8,12},{9,11},{10,... | collective-permute-start | bytes 294920 | tf_op jit(solution)/shard_map/ppermute | solution.py:426
  21.5 8.1 %collective-permute-start.12 = (bf16[32,4096]{1,0:T(8,128)(2,1)S(1)}, bf16[32,4096]{1,0:T(8,128)(2,1)S(1)}, u32[]{:S(2)}, u32[]{:S(2)}) collective-permute-start(bf16[32,4096]{1,0:T(8,128)(2,1)S(1)} %get-tuple-element.91), channel_id=1, source_target_pairs={{0,4},{1,3},{2,6},{3,1},{4,0},{5,7},{6,2},{7,5},{8,12},{9,11},{10,... | collective-permute-start | bytes 786440 | tf_op jit(solution)/shard_map/ppermute | solution.py:426
  28.1 1.6 %collective-permute-start.14 = (bf16[32,4096]{1,0:T(8,128)(2,1)S(1)}, bf16[32,4096]{1,0:T(8,128)(2,1)S(1)}, u32[]{:S(2)}, u32[]{:S(2)}) collective-permute-start(bf16[32,4096]{1,0:T(8,128)(2,1)S(1)} %collective-permute-done.13.refs_3_), channel_id=1, source_target_pairs={{0,1},{1,0},{2,3},{3,2},{4,5},{5,4},{6,7},{7,6},{8,9},{9,8},{10,11... | collective-permute-start | bytes 786440 | tf_op jit(solution)/shard_map/ppermute | solution.py:426
  29.9 1.8 %collective-permute-start.15 = (bf16[32,2048]{1,0:T(8,128)(2,1)S(1)}, bf16[32,2048]{1,0:T(8,128)(2,1)S(1)}, u32[]{:S(2)}, u32[]{:S(2)}) collective-permute-start(bf16[32,2048]{1,0:T(8,128)(2,1)S(1)} %get-tuple-element.93.refs_3_), channel_id=1, source_target_pairs={{0,1},{1,0},{2,3},{3,2},{4,5},{5,4},{6,7},{7,6},{8,9},{9,8},{10,11... | collective-permute-start | bytes 393224 | tf_op jit(solution)/shard_map/ppermute | solution.py:426
  33.1 5.7 %collective-permute-start.21 = (bf16[192,256]{1,0:T(8,128)(2,1)S(1)}, bf16[192,256]{1,0:T(8,128)(2,1)S(1)}, u32[]{:S(2)}, u32[]{:S(2)}) collective-permute-start(bf16[192,256]{1,0:T(8,128)(2,1)S(1)} %get-tuple-element.85.refs_0_), channel_id=1, source_target_pairs={{0,2},{1,5},{2,0},{3,7},{4,6},{5,1},{6,4},{7,3},{8,10},{9,13},{10,... | collective-permute-start | bytes 294920 | tf_op jit(solution)/shard_map/ppermute | solution.py:426
  35.2 6.7 %collective-permute-start.17 = (bf16[192,256]{1,0:T(8,128)(2,1)S(1)}, bf16[192,256]{1,0:T(8,128)(2,1)S(1)}, u32[]{:S(2)}, u32[]{:S(2)}) collective-permute-start(bf16[192,256]{1,0:T(8,128)(2,1)S(1)} %get-tuple-element.85.refs_0_), channel_id=1, source_target_pairs={{0,4},{1,3},{2,6},{3,1},{4,0},{5,7},{6,2},{7,5},{8,12},{9,11},{10,... | collective-permute-start | bytes 294920 | tf_op jit(solution)/shard_map/ppermute | solution.py:426
  36.0 5.9 %collective-permute-start.19 = (bf16[192,256]{1,0:T(8,128)(2,1)S(1)}, bf16[192,256]{1,0:T(8,128)(2,1)S(1)}, u32[]{:S(2)}, u32[]{:S(2)}) collective-permute-start(bf16[192,256]{1,0:T(8,128)(2,1)S(1)} %get-tuple-element.85.refs_0_), channel_id=1, source_target_pairs={{0,6},{1,7},{2,4},{3,5},{4,2},{5,3},{6,0},{7,1},{8,14},{9,15},{10,... | collective-permute-start | bytes 294920 | tf_op jit(solution)/shard_map/ppermute | solution.py:426
  36.8 5.7 %collective-permute-start.22 = (bf16[192,256]{1,0:T(8,128)(2,1)S(1)}, bf16[192,256]{1,0:T(8,128)(2,1)S(1)}, u32[]{:S(2)}, u32[]{:S(2)}) collective-permute-start(bf16[192,256]{1,0:T(8,128)(2,1)S(1)} %get-tuple-element.85.refs_0_), channel_id=1, source_target_pairs={{0,1},{1,0},{2,3},{3,2},{4,5},{5,4},{6,7},{7,6},{8,9},{9,8},{10,11... | collective-permute-start | bytes 294920 | tf_op jit(solution)/shard_map/ppermute | solution.py:426
  38.8 3.6 %collective-permute-start.23 = (bf16[192,256]{1,0:T(8,128)(2,1)S(1)}, bf16[192,256]{1,0:T(8,128)(2,1)S(1)}, u32[]{:S(2)}, u32[]{:S(2)}) collective-permute-start(bf16[192,256]{1,0:T(8,128)(2,1)S(1)} %collective-permute-done.21.refs_1_), channel_id=1, source_target_pairs={{0,1},{1,0},{2,3},{3,2},{4,5},{5,4},{6,7},{7,6},{8,9},{9,8},{10,11... | collective-permute-start | bytes 294920 | tf_op jit(solution)/shard_map/ppermute | solution.py:426
  41.9 1.8 %collective-permute-start.18 = (bf16[192,256]{1,0:T(8,128)(2,1)S(1)}, bf16[192,256]{1,0:T(8,128)(2,1)S(1)}, u32[]{:S(2)}, u32[]{:S(2)}) collective-permute-start(bf16[192,256]{1,0:T(8,128)(2,1)S(1)} %collective-permute-done.17.refs_2_), channel_id=1, source_target_pairs={{0,1},{1,0},{2,3},{3,2},{4,5},{5,4},{6,7},{7,6},{8,9},{9,8},{10,11... | collective-permute-start | bytes 294920 | tf_op jit(solution)/shard_map/ppermute | solution.py:426
  41.9 1.8 %collective-permute-start.20 = (bf16[192,256]{1,0:T(8,128)(2,1)S(1)}, bf16[192,256]{1,0:T(8,128)(2,1)S(1)}, u32[]{:S(2)}, u32[]{:S(2)}) collective-permute-start(bf16[192,256]{1,0:T(8,128)(2,1)S(1)} %collective-permute-done.19.refs_3_), channel_id=1, source_target_pairs={{0,1},{1,0},{2,3},{3,2},{4,5},{5,4},{6,7},{7,6},{8,9},{9,8},{10,11... | collective-permute-start | bytes 294920 | tf_op jit(solution)/shard_map/ppermute | solution.py:426
  44.4 7.5 %collective-permute-start.24 = (bf16[48,1024]{1,0:T(8,128)(2,1)S(1)}, bf16[48,1024]{1,0:T(8,128)(2,1)S(1)}, u32[]{:S(2)}, u32[]{:S(2)}) collective-permute-start(bf16[48,1024]{1,0:T(8,128)(2,1)S(1)} %get-tuple-element.87), channel_id=1, source_target_pairs={{0,8},{8,16},{16,24},{24,0},{1,9},{9,17},{17,25},{25,1},{2,10},{10... | collective-permute-start | bytes 294920 | tf_op jit(solution)/shard_map/ppermute | solution.py:523
  46.0 9.4 %collective-permute-start.25 = (bf16[48,1024]{1,0:T(8,128)(2,1)S(1)}, bf16[48,1024]{1,0:T(8,128)(2,1)S(1)}, u32[]{:S(2)}, u32[]{:S(2)}) collective-permute-start(bf16[48,1024]{1,0:T(8,128)(2,1)S(1)} %get-tuple-element.88), channel_id=1, source_target_pairs={{0,16},{8,24},{16,0},{24,8},{1,17},{9,25},{17,1},{25,9},{2,18},{10... | collective-permute-start | bytes 294920 | tf_op jit(solution)/shard_map/ppermute | solution.py:523
  48.6 6.8 %collective-permute-start.26 = (bf16[48,1024]{1,0:T(8,128)(2,1)S(1)}, bf16[48,1024]{1,0:T(8,128)(2,1)S(1)}, u32[]{:S(2)}, u32[]{:S(2)}) collective-permute-start(bf16[48,1024]{1,0:T(8,128)(2,1)S(1)} %get-tuple-element.89), channel_id=1, source_target_pairs={{0,24},{8,0},{16,8},{24,16},{1,25},{9,1},{17,9},{25,17},{2,26},{10... | collective-permute-start | bytes 294920 | tf_op jit(solution)/shard_map/ppermute | solution.py:523
  (14 other events, 114.6 us)

commit v5 on v3

--- a/solution.py
+++ b/solution.py
@@ -349,6 +349,12 @@
     )(*arrays)
 
 
+def section_at(i, k, sections):
+    if sections & (sections - 1) == 0:
+        return i ^ k
+    return (i + k) % sections if isinstance(i, int) else lax.rem(i + k, sections)
+
+
 def grad_kernel(pairs, per_kv, sections, first, last, *refs):
     blocks, weight_ref, refs = refs[: len(pairs)], refs[len(pairs)], refs[len(pairs) + 1 :]
     if not first:
@@ -380,7 +386,7 @@
     if last:
         rows = image_rows // sections
         for k in range(sections):
-            to = lax.rem(lax.axis_index("section") + k, sections)
+            to = section_at(lax.axis_index("section"), k, sections)
             piece = total[pl.ds(pl.multiple_of(to * rows, rows), rows), :]
             refs[k][...] = piece.astype(refs[k].dtype)
 
@@ -517,8 +523,8 @@
     pieces = feature_gradient(blocks, w_key_value, per_kv, sections, before)
     feature_grad, leaving = pieces[0], pieces[1:]
     arrived = []
-    for k in range(1, sections):
-        perm = [(i, (i + k) % sections) for i in range(sections)]
+    for k in range(sections - 1, 0, -1):
+        perm = [(i, section_at(i, k, sections)) for i in range(sections)]
         arrived.append(lax.ppermute(leaving[k - 1], "section", perm))
     for x in arrived:
         feature_grad = feature_grad + x.astype(F32)

time: 56 us -> 57.2 us (1.021)
  waiting for transfers between devices: 17 us -> 19.4 us
  starting transfers between devices: 21.6 us -> 20.4 us
    ppermute x3, waiting for transfers between devices: 4.78 us -> 7.2 us  [shards(): arrived.append(lax.ppermute(leaving[k - 1], 'section', perm))]
    ppermute x3, starting transfers between devices: 6.09 us -> 4.84 us  [shards(): arrived.append(lax.ppermute(leaving[k - 1], 'section', perm))]
where the time goes in v5:
time: 57.2 us; the launch traced here: 57 us
  starting transfers between devices  20.4 us (36%)
  waiting for transfers between devices  19.4 us (34%)
  Pallas kernels  12.3 us (22%)
  local copies, waits for them, and re-layouts  3.27 us (6%)
  between operations  0.86 us (2%)
  other arithmetic  0.72 us (1%)
    ppermute x24, starting transfers between devices, exchange(): lax.ppermute(x, 'tensor', [(i, i ^ pair[i % 2]) for i in range(count)])  15.5 us
    ppermute x24, waiting for transfers between devices, exchange(): lax.ppermute(x, 'tensor', [(i, i ^ pair[i % 2]) for i in range(count)])  12.2 us
    ppermute x3, waiting for transfers between devices, shards(): arrived.append(lax.ppermute(leaving[k - 1], 'section', perm))  7.2 us
    pallas_call x5, Pallas kernels, queries_of(): pl.pallas_call(functools.partial(query_kernel, [len(parts) for parts in g...  5.91 us
    ppermute x3, starting transfers between devices, shards(): arrived.append(lax.ppermute(leaving[k - 1], 'section', perm))  4.84 us
    unnamed x22, local copies, waits for them, and re-layouts  3.22 us
    pallas_call x2, Pallas kernels, attention(): pl.pallas_call(functools.partial(attention_kernel, places, count, rows, l...  2.11 us
    pallas_call x2, Pallas kernels, feature_gradient(): pl.pallas_call(functools.partial(grad_kernel, pairs, per_kv, sections, be...  1.88 us
  transfers between devices with their start and end apart: 27, of which 14 were waited for; matrix products, arithmetic and copies ran while one was open for 0% of the time, Pallas kernels for 18%

profile of v5, /device:TPU:0, one launch (start us, length us, event | category | flops | bytes accessed | tf_op | source)
XLA Modules:
  0.0 57.0 jit_solution(13806970457355145995)
XLA Ops:
  0.6 3.0 %collective-permute-start.1 = (bf16[32,8192]{1,0:T(8,128)(2,1)}, bf16[32,8192]{1,0:T(8,128)(2,1)S(1)}, u32[]{:S(2)}, u32[]{:S(2)}) collective-permute-start(bf16[32,8192]{1,0:T(8,128)(2,1)} %bitcast.1), channel_id=1, source_target_pairs={{0,2},{1,5},{2,0},{3,7},{4,6},{5,1},{6,4},{7,3},{8,10},{9,13},{10,... | collective-permute-start | bytes 1572872 | tf_op jit(solution)/shard_map/ppermute | solution.py:432
  3.6 1.5 %collective-permute-start.2 = (bf16[32,8192]{1,0:T(8,128)(2,1)}, bf16[32,8192]{1,0:T(8,128)(2,1)S(1)}, u32[]{:S(2)}, u32[]{:S(2)}) collective-permute-start(bf16[32,8192]{1,0:T(8,128)(2,1)} %bitcast.2), channel_id=1, source_target_pairs={{0,4},{1,3},{2,6},{3,1},{4,0},{5,7},{6,2},{7,5},{8,12},{9,11},{10,... | collective-permute-start | bytes 1572872 | tf_op jit(solution)/shard_map/ppermute | solution.py:432
  5.2 2.2 %copy-done.1 = bf16[1,1024,2048]{2,1,0:T(8,128)(2,1)S(1)} copy-done((bf16[1,1024,2048]{2,1,0:T(8,128)(2,1)S(1)}, bf16[1,1024,2048]{2,1,0:T(8,128)(2,1)}, u32[]{:S(2)}) %copy-start.1) | copy-done | bytes 4194328
  7.4 1.0 %copy-done.3 = bf16[192,1024]{1,0:T(8,128)(2,1)S(1)} copy-done((bf16[192,1024]{1,0:T(8,128)(2,1)S(1)}, bf16[192,1024]{1,0:T(8,128)(2,1)}, u32[]{:S(2)}) %copy-start.3) | copy-done | bytes 393240
  11.3 0.9 %collective-permute-done.6.refs_3_ = f32[192,256]{1,0:T(8,128)S(1)} collective-permute-done((f32[192,256]{1,0:T(8,128)S(1)}, f32[192,256]{1,0:T(8,128)S(1)}, u32[]{:S(2)}, u32[]{:S(2)}) %collective-permute-start.6) | collective-permute-done | bytes 196640 | tf_op jit(solution)/shard_map/ppermute | solution.py:432
  13.8 1.3 %collective-permute-start.8 = (bf16[192,256]{1,0:T(8,128)(2,1)S(1)}, bf16[192,256]{1,0:T(8,128)(2,1)S(1)}, u32[]{:S(2)}, u32[]{:S(2)}) collective-permute-start(bf16[192,256]{1,0:T(8,128)(2,1)S(1)} %get-tuple-element.54), channel_id=1, source_target_pairs={{0,2},{1,5},{2,0},{3,7},{4,6},{5,1},{6,4},{7,3},{8,10},{9,13},{10,... | collective-permute-start | bytes 294920 | tf_op jit(solution)/shard_map/ppermute | solution.py:432
  15.1 2.6 %collective-permute-done.7.refs_2_ = bf16[192,256]{1,0:T(8,128)(2,1)S(1)} collective-permute-done((bf16[192,256]{1,0:T(8,128)(2,1)S(1)}, bf16[192,256]{1,0:T(8,128)(2,1)S(1)}, u32[]{:S(2)}, u32[]{:S(2)}) %collective-permute-start.7) | collective-permute-done | bytes 98336 | tf_op jit(solution)/shard_map/ppermute | solution.py:432
  17.7 1.1 %collective-permute-done.8.refs_3_ = bf16[192,256]{1,0:T(8,128)(2,1)S(1)} collective-permute-done((bf16[192,256]{1,0:T(8,128)(2,1)S(1)}, bf16[192,256]{1,0:T(8,128)(2,1)S(1)}, u32[]{:S(2)}, u32[]{:S(2)}) %collective-permute-start.8) | collective-permute-done | bytes 98336 | tf_op jit(solution)/shard_map/ppermute | solution.py:432
  19.3 1.1 %collective-permute-start.13 = (bf16[32,4096]{1,0:T(8,128)(2,1)S(1)}, bf16[32,4096]{1,0:T(8,128)(2,1)S(1)}, u32[]{:S(2)}, u32[]{:S(2)}) collective-permute-start(bf16[32,4096]{1,0:T(8,128)(2,1)S(1)} %get-tuple-element.90), channel_id=1, source_target_pairs={{0,4},{1,3},{2,6},{3,1},{4,0},{5,7},{6,2},{7,5},{8,12},{9,11},{10,... | collective-permute-start | bytes 786440 | tf_op jit(solution)/shard_map/ppermute | solution.py:432
  20.4 1.1 %collective-permute-start.11 = (bf16[192,256]{1,0:T(8,128)(2,1)S(1)}, bf16[192,256]{1,0:T(8,128)(2,1)S(1)}, u32[]{:S(2)}, u32[]{:S(2)}) collective-permute-start(bf16[192,256]{1,0:T(8,128)(2,1)S(1)} %get-tuple-element.62), channel_id=1, source_target_pairs={{0,4},{1,3},{2,6},{3,1},{4,0},{5,7},{6,2},{7,5},{8,12},{9,11},{10,... | collective-permute-start | bytes 294920 | tf_op jit(solution)/shard_map/ppermute | solution.py:432
  21.5 1.0 %collective-permute-start.12 = (bf16[32,4096]{1,0:T(8,128)(2,1)S(1)}, bf16[32,4096]{1,0:T(8,128)(2,1)S(1)}, u32[]{:S(2)}, u32[]{:S(2)}) collective-permute-start(bf16[32,4096]{1,0:T(8,128)(2,1)S(1)} %get-tuple-element.91), channel_id=1, source_target_pairs={{0,4},{1,3},{2,6},{3,1},{4,0},{5,7},{6,2},{7,5},{8,12},{9,11},{10,... | collective-permute-start | bytes 786440 | tf_op jit(solution)/shard_map/ppermute | solution.py:432
  22.5 2.3 %queries_own_chip.1 = (bf16[64,512]{1,0:T(8,128)(2,1)S(1)}, f32[256,128]{1,0:T(8,128)S(1)}, f32[2,8,96]{2,1,0:T(8,128)S(1)}) custom-call(s32[2]{0:T(128)S(1)} %copy-done.9, s32[2]{0:T(128)S(1)} %copy-done.10, bf16[1,8192]{1,0:T(2,128)(2,1)S(1)} %copy-done.5, bf16[1,8192,512]{2,1,0:T(8,128)(2,1)S(1)} %copy-done, bf16[1,128]{1,0:T(2,128)(2,1)S(1)} %copy-done.7, ...), custom_call_target="tpu_custom_call" | custom-call | tf_op jit(solution)/shard_map/queries_own_chip/pallas_call | solution.py:199
  24.8 1.7 %queries_neighbours.1.refs_3_ = bf16[128,512]{1,0:T(8,128)(2,1)S(1)} custom-call(bf16[1,8192]{1,0:T(2,128)(2,1)S(1)} %copy-done.5, bf16[1,8192,512]{2,1,0:T(8,128)(2,1)S(1)} %copy-done, bf16[1,128]{1,0:T(2,128)(2,1)S(1)} %copy-done.7, bf16[32,8192]{1,0:T(8,128)(2,1)S(1)} %collective-permute-done.1.refs_3_, ...), custom_call_target="tpu_custom_call" | custom-call | tf_op jit(solution)/shard_map/queries_neighbours/pallas_call | solution.py:199
  26.8 1.3 %attention_first.1 = (f32[192,512]{1,0:T(8,128)S(1)}, f32[192,128]{1,0:T(8,128)S(1)}, f32[192,128]{1,0:T(8,128)S(1)}, bf16[192,128]{1,0:T(8,128)(2,1)S(1)}, bf16...) custom-call(f32[256,128]{1,0:T(8,128)S(1)} %get-tuple-element.46.refs_0_, ...), custom_call_target="tpu_custom_call" | custom-call | tf_op jit(solution)/shard_map/attention_first/pallas_call | solution.py:317
  28.2 1.4 %collective-permute-done.12 = bf16[32,4096]{1,0:T(8,128)(2,1)S(1)} collective-permute-done((bf16[32,4096]{1,0:T(8,128)(2,1)S(1)}, bf16[32,4096]{1,0:T(8,128)(2,1)S(1)}, u32[]{:S(2)}, u32[]{:S(2)}) %collective-permute-start.12) | collective-permute-done | bytes 262176 | tf_op jit(solution)/shard_map/ppermute | solution.py:432
  30.3 0.9 %queries_forwarded_first.1 = (f32[64,512]{1,0:T(8,128)S(1)}, f32[64,128]{1,0:T(8,128)S(1)}) custom-call(bf16[1,8192]{1,0:T(2,128)(2,1)S(1)} %copy-done.5, bf16[1,8192,512]{2,1,0:T(8,128)(2,1)S(1)} %copy-done, bf16[1,128]{1,0:T(2,128)(2,1)S(1)} %copy-done.7, bf16[32,4096]{1,0:T(8,128)(2,1)S(1)} %collective-permute-done.13.refs_3_, ...), custom_call_target="tpu_custom_call" | custom-call | tf_op jit(solution)/shard_map/queries_forwarded_first/pallas_call | solution.py:199
  33.1 2.3 %collective-permute-start.17 = (bf16[192,256]{1,0:T(8,128)(2,1)S(1)}, bf16[192,256]{1,0:T(8,128)(2,1)S(1)}, u32[]{:S(2)}, u32[]{:S(2)}) collective-permute-start(bf16[192,256]{1,0:T(8,128)(2,1)S(1)} %get-tuple-element.85.refs_0_), channel_id=1, source_target_pairs={{0,6},{1,7},{2,4},{3,5},{4,2},{5,3},{6,0},{7,1},{8,14},{9,15},{10,... | collective-permute-start | bytes 294920 | tf_op jit(solution)/shard_map/ppermute | solution.py:432
  35.4 1.2 %collective-permute-start.19 = (bf16[192,256]{1,0:T(8,128)(2,1)S(1)}, bf16[192,256]{1,0:T(8,128)(2,1)S(1)}, u32[]{:S(2)}, u32[]{:S(2)}) collective-permute-start(bf16[192,256]{1,0:T(8,128)(2,1)S(1)} %get-tuple-element.85.refs_0_), channel_id=1, source_target_pairs={{0,4},{1,3},{2,6},{3,1},{4,0},{5,7},{6,2},{7,5},{8,12},{9,11},{10,... | collective-permute-start | bytes 294920 | tf_op jit(solution)/shard_map/ppermute | solution.py:432
  36.7 2.6 %collective-permute-done.17.refs_1_ = bf16[192,256]{1,0:T(8,128)(2,1)S(1)} collective-permute-done((bf16[192,256]{1,0:T(8,128)(2,1)S(1)}, bf16[192,256]{1,0:T(8,128)(2,1)S(1)}, u32[]{:S(2)}, u32[]{:S(2)}) %collective-permute-start.17) | collective-permute-done | bytes 98336 | tf_op jit(solution)/shard_map/ppermute | solution.py:432
  39.3 1.7 %collective-permute-done.19.refs_2_ = bf16[192,256]{1,0:T(8,128)(2,1)S(1)} collective-permute-done((bf16[192,256]{1,0:T(8,128)(2,1)S(1)}, bf16[192,256]{1,0:T(8,128)(2,1)S(1)}, u32[]{:S(2)}, u32[]{:S(2)}) %collective-permute-start.19) | collective-permute-done | bytes 98336 | tf_op jit(solution)/shard_map/ppermute | solution.py:432
  41.6 1.1 %feature_grad_first.1.refs_4_ = f32[192,1024]{1,0:T(8,128)S(1)} custom-call(bf16[192,256]{1,0:T(8,128)(2,1)S(1)} %get-tuple-element.85.refs_0_, bf16[192,256]{1,0:T(8,128)(2,1)S(1)} %collective-permute-done.17.refs_1_, bf16[192,256]{1,0:T(8,128)(2,1)S(1)} %collective-permute-done.19.refs_2_, bf16[192,256]{1,0:T(8,128)(2,1)S(1)} %collective-permute-done.21.refs_3_, ...), custom_call_target="tpu_custom_call" | custom-call | tf_op jit(solution)/shard_map/feature_grad_first/pallas_call | solution.py:412
  43.5 4.2 %collective-permute-start.24 = (bf16[48,1024]{1,0:T(8,128)(2,1)S(1)}, bf16[48,1024]{1,0:T(8,128)(2,1)S(1)}, u32[]{:S(2)}, u32[]{:S(2)}) collective-permute-start(bf16[48,1024]{1,0:T(8,128)(2,1)S(1)} %get-tuple-element.87), channel_id=1, source_target_pairs={{0,24},{8,16},{16,8},{24,0},{1,25},{9,17},{17,9},{25,1},{2,26},{10... | collective-permute-start | bytes 294920 | tf_op jit(solution)/shard_map/ppermute | solution.py:528
  49.1 2.3 %collective-permute-done.24 = bf16[48,1024]{1,0:T(8,128)(2,1)S(1)} collective-permute-done((bf16[48,1024]{1,0:T(8,128)(2,1)S(1)}, bf16[48,1024]{1,0:T(8,128)(2,1)S(1)}, u32[]{:S(2)}, u32[]{:S(2)}) %collective-permute-start.24) | collective-permute-done | bytes 98336 | tf_op jit(solution)/shard_map/ppermute | solution.py:528
  51.4 4.9 %collective-permute-done.25 = bf16[48,1024]{1,0:T(8,128)(2,1)S(1)} collective-permute-done((bf16[48,1024]{1,0:T(8,128)(2,1)S(1)}, bf16[48,1024]{1,0:T(8,128)(2,1)S(1)}, u32[]{:S(2)}, u32[]{:S(2)}) %collective-permute-start.25) | collective-permute-done | bytes 98336 | tf_op jit(solution)/shard_map/ppermute | solution.py:528
  (68 shorter events, 11.6 us)
Async XLA Ops:
  0.6 18.1 %collective-permute-start.1 = (bf16[32,8192]{1,0:T(8,128)(2,1)}, bf16[32,8192]{1,0:T(8,128)(2,1)S(1)}, u32[]{:S(2)}, u32[]{:S(2)}) collective-permute-start(bf16[32,8192]{1,0:T(8,128)(2,1)} %bitcast.1), channel_id=1, source_target_pairs={{0,2},{1,5},{2,0},{3,7},{4,6},{5,1},{6,4},{7,3},{8,10},{9,13},{10,... | collective-permute-start | bytes 1572872 | tf_op jit(solution)/shard_map/ppermute | solution.py:432
  3.6 15.1 %collective-permute-start.2 = (bf16[32,8192]{1,0:T(8,128)(2,1)}, bf16[32,8192]{1,0:T(8,128)(2,1)S(1)}, u32[]{:S(2)}, u32[]{:S(2)}) collective-permute-start(bf16[32,8192]{1,0:T(8,128)(2,1)} %bitcast.2), channel_id=1, source_target_pairs={{0,4},{1,3},{2,6},{3,1},{4,0},{5,7},{6,2},{7,5},{8,12},{9,11},{10,... | collective-permute-start | bytes 1572872 | tf_op jit(solution)/shard_map/ppermute | solution.py:432
  9.2 1.5 %collective-permute-start.3 = (f32[192,256]{1,0:T(8,128)S(1)}, f32[192,256]{1,0:T(8,128)S(1)}, u32[]{:S(2)}, u32[]{:S(2)}) collective-permute-start(f32[192,256]{1,0:T(8,128)S(1)} %get-tuple-element.49), channel_id=1, source_target_pairs={{0,1},{1,0},{2,3},{3,2},{4,5},{5,4},{6,7},{7,6},{8,9},{9,8},{10,11... | collective-permute-start | bytes 589832 | tf_op jit(solution)/shard_map/ppermute | solution.py:432
  9.3 1.7 %collective-permute-start.4 = (f32[192,256]{1,0:T(8,128)S(1)}, f32[192,256]{1,0:T(8,128)S(1)}, u32[]{:S(2)}, u32[]{:S(2)}) collective-permute-start(f32[192,256]{1,0:T(8,128)S(1)} %get-tuple-element.50), channel_id=1, source_target_pairs={{0,1},{1,0},{2,3},{3,2},{4,5},{5,4},{6,7},{7,6},{8,9},{9,8},{10,11... | collective-permute-start | bytes 589832 | tf_op jit(solution)/shard_map/ppermute | solution.py:432
  9.8 1.5 %collective-permute-start.5 = (f32[192,256]{1,0:T(8,128)S(1)}, f32[192,256]{1,0:T(8,128)S(1)}, u32[]{:S(2)}, u32[]{:S(2)}) collective-permute-start(f32[192,256]{1,0:T(8,128)S(1)} %get-tuple-element.51), channel_id=1, source_target_pairs={{0,1},{1,0},{2,3},{3,2},{4,5},{5,4},{6,7},{7,6},{8,9},{9,8},{10,11... | collective-permute-start | bytes 589832 | tf_op jit(solution)/shard_map/ppermute | solution.py:432
  13.0 4.7 %collective-permute-start.7 = (bf16[192,256]{1,0:T(8,128)(2,1)S(1)}, bf16[192,256]{1,0:T(8,128)(2,1)S(1)}, u32[]{:S(2)}, u32[]{:S(2)}) collective-permute-start(bf16[192,256]{1,0:T(8,128)(2,1)S(1)} %get-tuple-element.53), channel_id=1, source_target_pairs={{0,2},{1,5},{2,0},{3,7},{4,6},{5,1},{6,4},{7,3},{8,10},{9,13},{10,... | collective-permute-start | bytes 294920 | tf_op jit(solution)/shard_map/ppermute | solution.py:432
  13.8 4.9 %collective-permute-start.8 = (bf16[192,256]{1,0:T(8,128)(2,1)S(1)}, bf16[192,256]{1,0:T(8,128)(2,1)S(1)}, u32[]{:S(2)}, u32[]{:S(2)}) collective-permute-start(bf16[192,256]{1,0:T(8,128)(2,1)S(1)} %get-tuple-element.54), channel_id=1, source_target_pairs={{0,2},{1,5},{2,0},{3,7},{4,6},{5,1},{6,4},{7,3},{8,10},{9,13},{10,... | collective-permute-start | bytes 294920 | tf_op jit(solution)/shard_map/ppermute | solution.py:432
  15.1 6.4 %collective-permute-start = (bf16[32,8192]{1,0:T(8,128)(2,1)S(1)}, bf16[32,8192]{1,0:T(8,128)(2,1)S(1)}, u32[]{:S(2)}, u32[]{:S(2)}) collective-permute-start(bf16[32,8192]{1,0:T(8,128)(2,1)S(1)} %bitcast.3), channel_id=1, source_target_pairs={{0,1},{1,0},{2,3},{3,2},{4,5},{5,4},{6,7},{7,6},{8,9},{9,8},{10,11... | collective-permute-start | bytes 1572872 | tf_op jit(solution)/shard_map/ppermute | solution.py:432
  18.7 6.1 %collective-permute-start.9 = (bf16[32,8192]{1,0:T(8,128)(2,1)S(1)}, bf16[32,8192]{1,0:T(8,128)(2,1)S(1)}, u32[]{:S(2)}, u32[]{:S(2)}) collective-permute-start(bf16[32,8192]{1,0:T(8,128)(2,1)S(1)} %collective-permute-done.1.refs_3_), channel_id=1, source_target_pairs={{0,1},{1,0},{2,3},{3,2},{4,5},{5,4},{6,7},{7,6},{8,9},{9,8},{10,11... | collective-permute-start | bytes 1572872 | tf_op jit(solution)/shard_map/ppermute | solution.py:432
  18.8 6.1 %collective-permute-start.10 = (bf16[32,8192]{1,0:T(8,128)(2,1)S(1)}, bf16[32,8192]{1,0:T(8,128)(2,1)S(1)}, u32[]{:S(2)}, u32[]{:S(2)}) collective-permute-start(bf16[32,8192]{1,0:T(8,128)(2,1)S(1)} %collective-permute-done.2.refs_5_), channel_id=1, source_target_pairs={{0,1},{1,0},{2,3},{3,2},{4,5},{5,4},{6,7},{7,6},{8,9},{9,8},{10,11... | collective-permute-start | bytes 1572872 | tf_op jit(solution)/shard_map/ppermute | solution.py:432
  19.3 8.8 %collective-permute-start.13 = (bf16[32,4096]{1,0:T(8,128)(2,1)S(1)}, bf16[32,4096]{1,0:T(8,128)(2,1)S(1)}, u32[]{:S(2)}, u32[]{:S(2)}) collective-permute-start(bf16[32,4096]{1,0:T(8,128)(2,1)S(1)} %get-tuple-element.90), channel_id=1, source_target_pairs={{0,4},{1,3},{2,6},{3,1},{4,0},{5,7},{6,2},{7,5},{8,12},{9,11},{10,... | collective-permute-start | bytes 786440 | tf_op jit(solution)/shard_map/ppermute | solution.py:432
  20.4 6.4 %collective-permute-start.11 = (bf16[192,256]{1,0:T(8,128)(2,1)S(1)}, bf16[192,256]{1,0:T(8,128)(2,1)S(1)}, u32[]{:S(2)}, u32[]{:S(2)}) collective-permute-start(bf16[192,256]{1,0:T(8,128)(2,1)S(1)} %get-tuple-element.62), channel_id=1, source_target_pairs={{0,4},{1,3},{2,6},{3,1},{4,0},{5,7},{6,2},{7,5},{8,12},{9,11},{10,... | collective-permute-start | bytes 294920 | tf_op jit(solution)/shard_map/ppermute | solution.py:432
  21.5 8.1 %collective-permute-start.12 = (bf16[32,4096]{1,0:T(8,128)(2,1)S(1)}, bf16[32,4096]{1,0:T(8,128)(2,1)S(1)}, u32[]{:S(2)}, u32[]{:S(2)}) collective-permute-start(bf16[32,4096]{1,0:T(8,128)(2,1)S(1)} %get-tuple-element.91), channel_id=1, source_target_pairs={{0,4},{1,3},{2,6},{3,1},{4,0},{5,7},{6,2},{7,5},{8,12},{9,11},{10,... | collective-permute-start | bytes 786440 | tf_op jit(solution)/shard_map/ppermute | solution.py:432
  28.1 1.6 %collective-permute-start.14 = (bf16[32,4096]{1,0:T(8,128)(2,1)S(1)}, bf16[32,4096]{1,0:T(8,128)(2,1)S(1)}, u32[]{:S(2)}, u32[]{:S(2)}) collective-permute-start(bf16[32,4096]{1,0:T(8,128)(2,1)S(1)} %collective-permute-done.13.refs_3_), channel_id=1, source_target_pairs={{0,1},{1,0},{2,3},{3,2},{4,5},{5,4},{6,7},{7,6},{8,9},{9,8},{10,11... | collective-permute-start | bytes 786440 | tf_op jit(solution)/shard_map/ppermute | solution.py:432
  29.9 1.8 %collective-permute-start.15 = (bf16[32,2048]{1,0:T(8,128)(2,1)S(1)}, bf16[32,2048]{1,0:T(8,128)(2,1)S(1)}, u32[]{:S(2)}, u32[]{:S(2)}) collective-permute-start(bf16[32,2048]{1,0:T(8,128)(2,1)S(1)} %get-tuple-element.93.refs_3_), channel_id=1, source_target_pairs={{0,1},{1,0},{2,3},{3,2},{4,5},{5,4},{6,7},{7,6},{8,9},{9,8},{10,11... | collective-permute-start | bytes 393224 | tf_op jit(solution)/shard_map/ppermute | solution.py:432
  33.1 6.2 %collective-permute-start.17 = (bf16[192,256]{1,0:T(8,128)(2,1)S(1)}, bf16[192,256]{1,0:T(8,128)(2,1)S(1)}, u32[]{:S(2)}, u32[]{:S(2)}) collective-permute-start(bf16[192,256]{1,0:T(8,128)(2,1)S(1)} %get-tuple-element.85.refs_0_), channel_id=1, source_target_pairs={{0,6},{1,7},{2,4},{3,5},{4,2},{5,3},{6,0},{7,1},{8,14},{9,15},{10,... | collective-permute-start | bytes 294920 | tf_op jit(solution)/shard_map/ppermute | solution.py:432
  35.4 5.6 %collective-permute-start.19 = (bf16[192,256]{1,0:T(8,128)(2,1)S(1)}, bf16[192,256]{1,0:T(8,128)(2,1)S(1)}, u32[]{:S(2)}, u32[]{:S(2)}) collective-permute-start(bf16[192,256]{1,0:T(8,128)(2,1)S(1)} %get-tuple-element.85.refs_0_), channel_id=1, source_target_pairs={{0,4},{1,3},{2,6},{3,1},{4,0},{5,7},{6,2},{7,5},{8,12},{9,11},{10,... | collective-permute-start | bytes 294920 | tf_op jit(solution)/shard_map/ppermute | solution.py:432
  36.7 4.6 %collective-permute-start.21 = (bf16[192,256]{1,0:T(8,128)(2,1)S(1)}, bf16[192,256]{1,0:T(8,128)(2,1)S(1)}, u32[]{:S(2)}, u32[]{:S(2)}) collective-permute-start(bf16[192,256]{1,0:T(8,128)(2,1)S(1)} %get-tuple-element.85.refs_0_), channel_id=1, source_target_pairs={{0,2},{1,5},{2,0},{3,7},{4,6},{5,1},{6,4},{7,3},{8,10},{9,13},{10,... | collective-permute-start | bytes 294920 | tf_op jit(solution)/shard_map/ppermute | solution.py:432
  36.7 4.9 %collective-permute-start.23 = (bf16[192,256]{1,0:T(8,128)(2,1)S(1)}, bf16[192,256]{1,0:T(8,128)(2,1)S(1)}, u32[]{:S(2)}, u32[]{:S(2)}) collective-permute-start(bf16[192,256]{1,0:T(8,128)(2,1)S(1)} %get-tuple-element.85.refs_0_), channel_id=1, source_target_pairs={{0,1},{1,0},{2,3},{3,2},{4,5},{5,4},{6,7},{7,6},{8,9},{9,8},{10,11... | collective-permute-start | bytes 294920 | tf_op jit(solution)/shard_map/ppermute | solution.py:432
  39.3 3.3 %collective-permute-start.18 = (bf16[192,256]{1,0:T(8,128)(2,1)S(1)}, bf16[192,256]{1,0:T(8,128)(2,1)S(1)}, u32[]{:S(2)}, u32[]{:S(2)}) collective-permute-start(bf16[192,256]{1,0:T(8,128)(2,1)S(1)} %collective-permute-done.17.refs_1_), channel_id=1, source_target_pairs={{0,1},{1,0},{2,3},{3,2},{4,5},{5,4},{6,7},{7,6},{8,9},{9,8},{10,11... | collective-permute-start | bytes 294920 | tf_op jit(solution)/shard_map/ppermute | solution.py:432
  41.0 1.6 %collective-permute-start.20 = (bf16[192,256]{1,0:T(8,128)(2,1)S(1)}, bf16[192,256]{1,0:T(8,128)(2,1)S(1)}, u32[]{:S(2)}, u32[]{:S(2)}) collective-permute-start(bf16[192,256]{1,0:T(8,128)(2,1)S(1)} %collective-permute-done.19.refs_2_), channel_id=1, source_target_pairs={{0,1},{1,0},{2,3},{3,2},{4,5},{5,4},{6,7},{7,6},{8,9},{9,8},{10,11... | collective-permute-start | bytes 294920 | tf_op jit(solution)/shard_map/ppermute | solution.py:432
  43.5 7.9 %collective-permute-start.24 = (bf16[48,1024]{1,0:T(8,128)(2,1)S(1)}, bf16[48,1024]{1,0:T(8,128)(2,1)S(1)}, u32[]{:S(2)}, u32[]{:S(2)}) collective-permute-start(bf16[48,1024]{1,0:T(8,128)(2,1)S(1)} %get-tuple-element.87), channel_id=1, source_target_pairs={{0,24},{8,16},{16,8},{24,0},{1,25},{9,17},{17,9},{25,1},{2,26},{10... | collective-permute-start | bytes 294920 | tf_op jit(solution)/shard_map/ppermute | solution.py:528
  47.7 8.6 %collective-permute-start.25 = (bf16[48,1024]{1,0:T(8,128)(2,1)S(1)}, bf16[48,1024]{1,0:T(8,128)(2,1)S(1)}, u32[]{:S(2)}, u32[]{:S(2)}) collective-permute-start(bf16[48,1024]{1,0:T(8,128)(2,1)S(1)} %get-tuple-element.88), channel_id=1, source_target_pairs={{0,16},{8,24},{16,0},{24,8},{1,17},{9,25},{17,1},{25,9},{2,18},{10... | collective-permute-start | bytes 294920 | tf_op jit(solution)/shard_map/ppermute | solution.py:528
  47.7 8.6 %collective-permute-start.26 = (bf16[48,1024]{1,0:T(8,128)(2,1)S(1)}, bf16[48,1024]{1,0:T(8,128)(2,1)S(1)}, u32[]{:S(2)}, u32[]{:S(2)}) collective-permute-start(bf16[48,1024]{1,0:T(8,128)(2,1)S(1)} %get-tuple-element.89), channel_id=1, source_target_pairs={{0,8},{8,0},{16,24},{24,16},{1,9},{9,1},{17,25},{25,17},{2,10},{10... | collective-permute-start | bytes 294920 | tf_op jit(solution)/shard_map/ppermute | solution.py:528
  (14 other events, 113.5 us)

commit v6 on v3

--- a/solution.py
+++ b/solution.py
@@ -141,7 +141,7 @@
     depth, heads_width = weight_ref.shape[1:]
     width = sum(part.shape[1] for part in groups[0])
     last = start + width == depth
-    span = 1024
+    span = 1024 if width % 1024 == 0 else 512
 
     def columns(parts, c):
         for part in parts:
@@ -438,7 +438,8 @@
     masks = range(1, 1 << steps)
 
     own_text = text[0]
-    width = own_text.shape[1] // 2
+    depth = own_text.shape[1]
+    cuts = (0, depth * 7 // 16, depth * 3 // 4, depth)
     direct = {1 << s: exchange(own_text, distance(1 << s)) for s in range(steps)}
 
     def both_cores(blocks):
@@ -472,8 +473,8 @@
     scalars = (tile_count, image_start)
     q_near, *live = queries(near, "queries_own_chip", scalars=scalars)
     forwarded = []
-    for first in (0, width):
-        held = {mask: x[:, first : first + width] for mask, x in direct.items()}
+    for first, last in ((0, cuts[1]), (cuts[1], depth)):
+        held = {mask: x[:, first:last] for mask, x in direct.items()}
         passed = {}
         for s in range(1, steps):
             for mask in range(1, 1 << s):
@@ -484,6 +485,11 @@
     next_to = both_cores({distance(mask): x for mask, x in direct.items()})
     q_next = queries(next_to, "queries_neighbours")
 
+    first_half, parts, q_near, q_next = lax.optimization_barrier(
+        (forwarded[0], parts, q_near, q_next)
+    )
+    far = both_cores(first_half)
+    sums = queries(far, "queries_forwarded_first")
     early, *state = attention(
         live,
         [q_near, q_next],
@@ -494,14 +500,12 @@
         parts,
         last=False,
     )
-    first_half, state = lax.optimization_barrier((forwarded[0], state))
-    far = both_cores(first_half)
-    second_half, far = lax.optimization_barrier((forwarded[1], far))
-    sums = queries(far, "queries_forwarded_first")
-    pieces = {pair: jnp.split(x, 2, axis=1) for pair, x in second_half.items()}
+    second_half, sums, state = lax.optimization_barrier((forwarded[1], sums, state))
+    split = cuts[2] - cuts[1]
+    pieces = {pair: (x[:, :split], x[:, split:]) for pair, x in second_half.items()}
     far, rest = [both_cores({pair: x[i] for pair, x in pieces.items()}) for i in range(2)]
-    sums = queries(far, "queries_forwarded_second", start=width, before=sums)
-    q_far = queries(rest, "queries_forwarded_last", start=3 * width // 2, before=sums)
+    sums = queries(far, "queries_forwarded_second", start=cuts[1], before=sums)
+    q_far = queries(rest, "queries_forwarded_last", start=cuts[2], before=sums)
     far = places_of(far)
     late, block = attention(live, [q_far], [far], count, grad_out, k_gain, state, last=True)
     attended = assemble([places_of(near) + places_of(next_to), far], [early, late], grad_out)

time: 56 us -> 56 us (level)
  transfers between devices with their start and end apart: 27 -> 27, of which waited for: 14 -> 13; matrix products, arithmetic and copies ran while one was open for 0% -> 0% of each run, Pallas kernels for 18% -> 18%
where the time goes in v6:
time: 56 us; the launch traced here: 55.8 us
  starting transfers between devices  22 us (39%)
  waiting for transfers between devices  16.5 us (29%)
  Pallas kernels  12.3 us (22%)
  local copies, waits for them, and re-layouts  3.28 us (6%)
  between operations  0.91 us (2%)
  other arithmetic  0.72 us (1%)
    ppermute x24, starting transfers between devices, exchange(): lax.ppermute(x, 'tensor', [(i, i ^ pair[i % 2]) for i in range(count)])  15.9 us
    ppermute x24, waiting for transfers between devices, exchange(): lax.ppermute(x, 'tensor', [(i, i ^ pair[i % 2]) for i in range(count)])  11.8 us
    ppermute x3, starting transfers between devices, shards(): arrived.append(lax.ppermute(leaving[k - 1], 'section', perm))  6.1 us
    pallas_call x5, Pallas kernels, queries_of(): pl.pallas_call(functools.partial(query_kernel, [len(parts) for parts in g...  5.91 us
    ppermute x3, waiting for transfers between devices, shards(): arrived.append(lax.ppermute(leaving[k - 1], 'section', perm))  4.77 us
    unnamed x22, local copies, waits for them, and re-layouts  3.22 us
    pallas_call x2, Pallas kernels, attention(): pl.pallas_call(functools.partial(attention_kernel, places, count, rows, l...  2.11 us
    pallas_call x2, Pallas kernels, feature_gradient(): pl.pallas_call(functools.partial(grad_kernel, pairs, per_kv, sections, be...  1.89 us
  transfers between devices with their start and end apart: 27, of which 13 were waited for; matrix products, arithmetic and copies ran while one was open for 0% of the time, Pallas kernels for 18%

profile of v6, /device:TPU:0, one launch (start us, length us, event | category | flops | bytes accessed | tf_op | source)
XLA Modules:
  0.0 55.8 jit_solution(17800023779593621152)
XLA Ops:
  0.6 3.0 %collective-permute-start.1 = (bf16[32,8192]{1,0:T(8,128)(2,1)}, bf16[32,8192]{1,0:T(8,128)(2,1)S(1)}, u32[]{:S(2)}, u32[]{:S(2)}) collective-permute-start(bf16[32,8192]{1,0:T(8,128)(2,1)} %bitcast.1), channel_id=1, source_target_pairs={{0,2},{1,5},{2,0},{3,7},{4,6},{5,1},{6,4},{7,3},{8,10},{9,13},{10,... | collective-permute-start | bytes 1572872 | tf_op jit(solution)/shard_map/ppermute | solution.py:426
  3.6 1.5 %collective-permute-start.2 = (bf16[32,8192]{1,0:T(8,128)(2,1)}, bf16[32,8192]{1,0:T(8,128)(2,1)S(1)}, u32[]{:S(2)}, u32[]{:S(2)}) collective-permute-start(bf16[32,8192]{1,0:T(8,128)(2,1)} %bitcast.2), channel_id=1, source_target_pairs={{0,4},{1,3},{2,6},{3,1},{4,0},{5,7},{6,2},{7,5},{8,12},{9,11},{10,... | collective-permute-start | bytes 1572872 | tf_op jit(solution)/shard_map/ppermute | solution.py:426
  5.2 2.2 %copy-done.1 = bf16[1,1024,2048]{2,1,0:T(8,128)(2,1)S(1)} copy-done((bf16[1,1024,2048]{2,1,0:T(8,128)(2,1)S(1)}, bf16[1,1024,2048]{2,1,0:T(8,128)(2,1)}, u32[]{:S(2)}) %copy-start.1) | copy-done | bytes 4194328
  7.4 1.0 %copy-done.3 = bf16[192,1024]{1,0:T(8,128)(2,1)S(1)} copy-done((bf16[192,1024]{1,0:T(8,128)(2,1)S(1)}, bf16[192,1024]{1,0:T(8,128)(2,1)}, u32[]{:S(2)}) %copy-start.3) | copy-done | bytes 393240
  11.3 0.9 %collective-permute-done.6.refs_3_ = f32[192,256]{1,0:T(8,128)S(1)} collective-permute-done((f32[192,256]{1,0:T(8,128)S(1)}, f32[192,256]{1,0:T(8,128)S(1)}, u32[]{:S(2)}, u32[]{:S(2)}) %collective-permute-start.6) | collective-permute-done | bytes 196640 | tf_op jit(solution)/shard_map/ppermute | solution.py:426
  13.8 1.3 %collective-permute-start.8 = (bf16[192,256]{1,0:T(8,128)(2,1)S(1)}, bf16[192,256]{1,0:T(8,128)(2,1)S(1)}, u32[]{:S(2)}, u32[]{:S(2)}) collective-permute-start(bf16[192,256]{1,0:T(8,128)(2,1)S(1)} %get-tuple-element.57), channel_id=1, source_target_pairs={{0,2},{1,5},{2,0},{3,7},{4,6},{5,1},{6,4},{7,3},{8,10},{9,13},{10,... | collective-permute-start | bytes 294920 | tf_op jit(solution)/shard_map/ppermute | solution.py:426
  15.1 2.6 %collective-permute-done.7.refs_2_ = bf16[192,256]{1,0:T(8,128)(2,1)S(1)} collective-permute-done((bf16[192,256]{1,0:T(8,128)(2,1)S(1)}, bf16[192,256]{1,0:T(8,128)(2,1)S(1)}, u32[]{:S(2)}, u32[]{:S(2)}) %collective-permute-start.7) | collective-permute-done | bytes 98336 | tf_op jit(solution)/shard_map/ppermute | solution.py:426
  17.7 1.1 %collective-permute-done.8.refs_3_ = bf16[192,256]{1,0:T(8,128)(2,1)S(1)} collective-permute-done((bf16[192,256]{1,0:T(8,128)(2,1)S(1)}, bf16[192,256]{1,0:T(8,128)(2,1)S(1)}, u32[]{:S(2)}, u32[]{:S(2)}) %collective-permute-start.8) | collective-permute-done | bytes 98336 | tf_op jit(solution)/shard_map/ppermute | solution.py:426
  19.3 1.1 %collective-permute-start.9 = (bf16[32,3584]{1,0:T(8,128)(2,1)S(1)}, bf16[32,3584]{1,0:T(8,128)(2,1)S(1)}, u32[]{:S(2)}, u32[]{:S(2)}) collective-permute-start(bf16[32,3584]{1,0:T(8,128)(2,1)S(1)} %slice.12), channel_id=1, source_target_pairs={{0,4},{1,3},{2,6},{3,1},{4,0},{5,7},{6,2},{7,5},{8,12},{9,11},{10,... | collective-permute-start | bytes 688136 | tf_op jit(solution)/shard_map/ppermute | solution.py:426
  20.4 1.1 %collective-permute-start.10 = (bf16[192,256]{1,0:T(8,128)(2,1)S(1)}, bf16[192,256]{1,0:T(8,128)(2,1)S(1)}, u32[]{:S(2)}, u32[]{:S(2)}) collective-permute-start(bf16[192,256]{1,0:T(8,128)(2,1)S(1)} %get-tuple-element.64), channel_id=1, source_target_pairs={{0,4},{1,3},{2,6},{3,1},{4,0},{5,7},{6,2},{7,5},{8,12},{9,11},{10,... | collective-permute-start | bytes 294920 | tf_op jit(solution)/shard_map/ppermute | solution.py:426
  21.5 1.1 %collective-permute-start.13 = (bf16[32,4608]{1,0:T(8,128)(2,1)S(1)}, bf16[32,4608]{1,0:T(8,128)(2,1)S(1)}, u32[]{:S(2)}, u32[]{:S(2)}) collective-permute-start(bf16[32,4608]{1,0:T(8,128)(2,1)S(1)} %slice.13), channel_id=1, source_target_pairs={{0,4},{1,3},{2,6},{3,1},{4,0},{5,7},{6,2},{7,5},{8,12},{9,11},{10,... | collective-permute-start | bytes 884744 | tf_op jit(solution)/shard_map/ppermute | solution.py:426
  22.6 2.3 %queries_own_chip.1 = (bf16[64,512]{1,0:T(8,128)(2,1)S(1)}, f32[256,128]{1,0:T(8,128)S(1)}, f32[2,8,96]{2,1,0:T(8,128)S(1)}) custom-call(s32[2]{0:T(128)S(1)} %copy-done.9, s32[2]{0:T(128)S(1)} %copy-done.10, bf16[1,8192]{1,0:T(2,128)(2,1)S(1)} %copy-done.5, bf16[1,8192,512]{2,1,0:T(8,128)(2,1)S(1)} %copy-done, bf16[1,128]{1,0:T(2,128)(2,1)S(1)} %copy-done.7, ...), custom_call_target="tpu_custom_call" | custom-call | tf_op jit(solution)/shard_map/queries_own_chip/pallas_call | solution.py:199
  24.9 1.7 %queries_neighbours.1.refs_3_ = bf16[128,512]{1,0:T(8,128)(2,1)S(1)} custom-call(bf16[1,8192]{1,0:T(2,128)(2,1)S(1)} %copy-done.5, bf16[1,8192,512]{2,1,0:T(8,128)(2,1)S(1)} %copy-done, bf16[1,128]{1,0:T(2,128)(2,1)S(1)} %copy-done.7, bf16[32,8192]{1,0:T(8,128)(2,1)S(1)} %collective-permute-done.1.refs_3_, ...), custom_call_target="tpu_custom_call" | custom-call | tf_op jit(solution)/shard_map/queries_neighbours/pallas_call | solution.py:199
  27.0 1.3 %attention_first.1 = (f32[192,512]{1,0:T(8,128)S(1)}, f32[192,128]{1,0:T(8,128)S(1)}, f32[192,128]{1,0:T(8,128)S(1)}, bf16[192,128]{1,0:T(8,128)(2,1)S(1)}, bf16...) custom-call(f32[256,128]{1,0:T(8,128)S(1)} %get-tuple-element.50.refs_0_, ...), custom_call_target="tpu_custom_call" | custom-call | tf_op jit(solution)/shard_map/attention_first/pallas_call | solution.py:317
  33.1 2.1 %collective-permute-start.17 = (bf16[192,256]{1,0:T(8,128)(2,1)S(1)}, bf16[192,256]{1,0:T(8,128)(2,1)S(1)}, u32[]{:S(2)}, u32[]{:S(2)}) collective-permute-start(bf16[192,256]{1,0:T(8,128)(2,1)S(1)} %get-tuple-element.93.refs_0_), channel_id=1, source_target_pairs={{0,6},{1,7},{2,4},{3,5},{4,2},{5,3},{6,0},{7,1},{8,14},{9,15},{10,... | collective-permute-start | bytes 294920 | tf_op jit(solution)/shard_map/ppermute | solution.py:426
  35.2 1.4 %collective-permute-start.19 = (bf16[192,256]{1,0:T(8,128)(2,1)S(1)}, bf16[192,256]{1,0:T(8,128)(2,1)S(1)}, u32[]{:S(2)}, u32[]{:S(2)}) collective-permute-start(bf16[192,256]{1,0:T(8,128)(2,1)S(1)} %get-tuple-element.93.refs_0_), channel_id=1, source_target_pairs={{0,4},{1,3},{2,6},{3,1},{4,0},{5,7},{6,2},{7,5},{8,12},{9,11},{10,... | collective-permute-start | bytes 294920 | tf_op jit(solution)/shard_map/ppermute | solution.py:426
  36.6 2.6 %collective-permute-done.17.refs_1_ = bf16[192,256]{1,0:T(8,128)(2,1)S(1)} collective-permute-done((bf16[192,256]{1,0:T(8,128)(2,1)S(1)}, bf16[192,256]{1,0:T(8,128)(2,1)S(1)}, u32[]{:S(2)}, u32[]{:S(2)}) %collective-permute-start.17) | collective-permute-done | bytes 98336 | tf_op jit(solution)/shard_map/ppermute | solution.py:426
  39.3 1.7 %collective-permute-done.19.refs_2_ = bf16[192,256]{1,0:T(8,128)(2,1)S(1)} collective-permute-done((bf16[192,256]{1,0:T(8,128)(2,1)S(1)}, bf16[192,256]{1,0:T(8,128)(2,1)S(1)}, u32[]{:S(2)}, u32[]{:S(2)}) %collective-permute-start.19) | collective-permute-done | bytes 98336 | tf_op jit(solution)/shard_map/ppermute | solution.py:426
  41.5 1.1 %feature_grad_first.1.refs_4_ = f32[192,1024]{1,0:T(8,128)S(1)} custom-call(bf16[192,256]{1,0:T(8,128)(2,1)S(1)} %get-tuple-element.93.refs_0_, bf16[192,256]{1,0:T(8,128)(2,1)S(1)} %collective-permute-done.17.refs_1_, bf16[192,256]{1,0:T(8,128)(2,1)S(1)} %collective-permute-done.19.refs_2_, bf16[192,256]{1,0:T(8,128)(2,1)S(1)} %collective-permute-done.21.refs_3_, ...), custom_call_target="tpu_custom_call" | custom-call | tf_op jit(solution)/shard_map/feature_grad_first/pallas_call | solution.py:406
  43.4 2.2 %collective-permute-start.24 = (bf16[48,1024]{1,0:T(8,128)(2,1)S(1)}, bf16[48,1024]{1,0:T(8,128)(2,1)S(1)}, u32[]{:S(2)}, u32[]{:S(2)}) collective-permute-start(bf16[48,1024]{1,0:T(8,128)(2,1)S(1)} %get-tuple-element.95), channel_id=1, source_target_pairs={{0,8},{8,16},{16,24},{24,0},{1,9},{9,17},{17,25},{25,1},{2,10},{10... | collective-permute-start | bytes 294920 | tf_op jit(solution)/shard_map/ppermute | solution.py:526
  45.6 2.6 %collective-permute-start.25 = (bf16[48,1024]{1,0:T(8,128)(2,1)S(1)}, bf16[48,1024]{1,0:T(8,128)(2,1)S(1)}, u32[]{:S(2)}, u32[]{:S(2)}) collective-permute-start(bf16[48,1024]{1,0:T(8,128)(2,1)S(1)} %get-tuple-element.96), channel_id=1, source_target_pairs={{0,16},{8,24},{16,0},{24,8},{1,17},{9,25},{17,1},{25,9},{2,18},{10... | collective-permute-start | bytes 294920 | tf_op jit(solution)/shard_map/ppermute | solution.py:526
  48.2 1.4 %collective-permute-start.26 = (bf16[48,1024]{1,0:T(8,128)(2,1)S(1)}, bf16[48,1024]{1,0:T(8,128)(2,1)S(1)}, u32[]{:S(2)}, u32[]{:S(2)}) collective-permute-start(bf16[48,1024]{1,0:T(8,128)(2,1)S(1)} %get-tuple-element.97), channel_id=1, source_target_pairs={{0,24},{8,0},{16,8},{24,16},{1,25},{9,1},{17,9},{25,17},{2,26},{10... | collective-permute-start | bytes 294920 | tf_op jit(solution)/shard_map/ppermute | solution.py:526
  50.3 1.0 %collective-permute-done.24 = bf16[48,1024]{1,0:T(8,128)(2,1)S(1)} collective-permute-done((bf16[48,1024]{1,0:T(8,128)(2,1)S(1)}, bf16[48,1024]{1,0:T(8,128)(2,1)S(1)}, u32[]{:S(2)}, u32[]{:S(2)}) %collective-permute-start.24) | collective-permute-done | bytes 98336 | tf_op jit(solution)/shard_map/ppermute | solution.py:526
  51.3 3.8 %collective-permute-done.25 = bf16[48,1024]{1,0:T(8,128)(2,1)S(1)} collective-permute-done((bf16[48,1024]{1,0:T(8,128)(2,1)S(1)}, bf16[48,1024]{1,0:T(8,128)(2,1)S(1)}, u32[]{:S(2)}, u32[]{:S(2)}) %collective-permute-start.25) | collective-permute-done | bytes 98336 | tf_op jit(solution)/shard_map/ppermute | solution.py:526
  (70 shorter events, 13.1 us)
Async XLA Ops:
  0.6 18.1 %collective-permute-start.1 = (bf16[32,8192]{1,0:T(8,128)(2,1)}, bf16[32,8192]{1,0:T(8,128)(2,1)S(1)}, u32[]{:S(2)}, u32[]{:S(2)}) collective-permute-start(bf16[32,8192]{1,0:T(8,128)(2,1)} %bitcast.1), channel_id=1, source_target_pairs={{0,2},{1,5},{2,0},{3,7},{4,6},{5,1},{6,4},{7,3},{8,10},{9,13},{10,... | collective-permute-start | bytes 1572872 | tf_op jit(solution)/shard_map/ppermute | solution.py:426
  3.6 15.1 %collective-permute-start.2 = (bf16[32,8192]{1,0:T(8,128)(2,1)}, bf16[32,8192]{1,0:T(8,128)(2,1)S(1)}, u32[]{:S(2)}, u32[]{:S(2)}) collective-permute-start(bf16[32,8192]{1,0:T(8,128)(2,1)} %bitcast.2), channel_id=1, source_target_pairs={{0,4},{1,3},{2,6},{3,1},{4,0},{5,7},{6,2},{7,5},{8,12},{9,11},{10,... | collective-permute-start | bytes 1572872 | tf_op jit(solution)/shard_map/ppermute | solution.py:426
  9.2 1.5 %collective-permute-start.3 = (f32[192,256]{1,0:T(8,128)S(1)}, f32[192,256]{1,0:T(8,128)S(1)}, u32[]{:S(2)}, u32[]{:S(2)}) collective-permute-start(f32[192,256]{1,0:T(8,128)S(1)} %get-tuple-element.52), channel_id=1, source_target_pairs={{0,1},{1,0},{2,3},{3,2},{4,5},{5,4},{6,7},{7,6},{8,9},{9,8},{10,11... | collective-permute-start | bytes 589832 | tf_op jit(solution)/shard_map/ppermute | solution.py:426
  9.3 1.7 %collective-permute-start.4 = (f32[192,256]{1,0:T(8,128)S(1)}, f32[192,256]{1,0:T(8,128)S(1)}, u32[]{:S(2)}, u32[]{:S(2)}) collective-permute-start(f32[192,256]{1,0:T(8,128)S(1)} %get-tuple-element.53), channel_id=1, source_target_pairs={{0,1},{1,0},{2,3},{3,2},{4,5},{5,4},{6,7},{7,6},{8,9},{9,8},{10,11... | collective-permute-start | bytes 589832 | tf_op jit(solution)/shard_map/ppermute | solution.py:426
  9.8 1.5 %collective-permute-start.5 = (f32[192,256]{1,0:T(8,128)S(1)}, f32[192,256]{1,0:T(8,128)S(1)}, u32[]{:S(2)}, u32[]{:S(2)}) collective-permute-start(f32[192,256]{1,0:T(8,128)S(1)} %get-tuple-element.54), channel_id=1, source_target_pairs={{0,1},{1,0},{2,3},{3,2},{4,5},{5,4},{6,7},{7,6},{8,9},{9,8},{10,11... | collective-permute-start | bytes 589832 | tf_op jit(solution)/shard_map/ppermute | solution.py:426
  13.0 4.7 %collective-permute-start.7 = (bf16[192,256]{1,0:T(8,128)(2,1)S(1)}, bf16[192,256]{1,0:T(8,128)(2,1)S(1)}, u32[]{:S(2)}, u32[]{:S(2)}) collective-permute-start(bf16[192,256]{1,0:T(8,128)(2,1)S(1)} %get-tuple-element.56), channel_id=1, source_target_pairs={{0,2},{1,5},{2,0},{3,7},{4,6},{5,1},{6,4},{7,3},{8,10},{9,13},{10,... | collective-permute-start | bytes 294920 | tf_op jit(solution)/shard_map/ppermute | solution.py:426
  13.8 4.9 %collective-permute-start.8 = (bf16[192,256]{1,0:T(8,128)(2,1)S(1)}, bf16[192,256]{1,0:T(8,128)(2,1)S(1)}, u32[]{:S(2)}, u32[]{:S(2)}) collective-permute-start(bf16[192,256]{1,0:T(8,128)(2,1)S(1)} %get-tuple-element.57), channel_id=1, source_target_pairs={{0,2},{1,5},{2,0},{3,7},{4,6},{5,1},{6,4},{7,3},{8,10},{9,13},{10,... | collective-permute-start | bytes 294920 | tf_op jit(solution)/shard_map/ppermute | solution.py:426
  15.1 6.5 %collective-permute-start = (bf16[32,8192]{1,0:T(8,128)(2,1)S(1)}, bf16[32,8192]{1,0:T(8,128)(2,1)S(1)}, u32[]{:S(2)}, u32[]{:S(2)}) collective-permute-start(bf16[32,8192]{1,0:T(8,128)(2,1)S(1)} %bitcast.3), channel_id=1, source_target_pairs={{0,1},{1,0},{2,3},{3,2},{4,5},{5,4},{6,7},{7,6},{8,9},{9,8},{10,11... | collective-permute-start | bytes 1572872 | tf_op jit(solution)/shard_map/ppermute | solution.py:426
  18.7 6.2 %collective-permute-start.11 = (bf16[32,8192]{1,0:T(8,128)(2,1)S(1)}, bf16[32,8192]{1,0:T(8,128)(2,1)S(1)}, u32[]{:S(2)}, u32[]{:S(2)}) collective-permute-start(bf16[32,8192]{1,0:T(8,128)(2,1)S(1)} %collective-permute-done.1.refs_3_), channel_id=1, source_target_pairs={{0,1},{1,0},{2,3},{3,2},{4,5},{5,4},{6,7},{7,6},{8,9},{9,8},{10,11... | collective-permute-start | bytes 1572872 | tf_op jit(solution)/shard_map/ppermute | solution.py:426
  18.8 6.2 %collective-permute-start.12 = (bf16[32,8192]{1,0:T(8,128)(2,1)S(1)}, bf16[32,8192]{1,0:T(8,128)(2,1)S(1)}, u32[]{:S(2)}, u32[]{:S(2)}) collective-permute-start(bf16[32,8192]{1,0:T(8,128)(2,1)S(1)} %collective-permute-done.2.refs_5_), channel_id=1, source_target_pairs={{0,1},{1,0},{2,3},{3,2},{4,5},{5,4},{6,7},{7,6},{8,9},{9,8},{10,11... | collective-permute-start | bytes 1572872 | tf_op jit(solution)/shard_map/ppermute | solution.py:426
  19.3 7.4 %collective-permute-start.9 = (bf16[32,3584]{1,0:T(8,128)(2,1)S(1)}, bf16[32,3584]{1,0:T(8,128)(2,1)S(1)}, u32[]{:S(2)}, u32[]{:S(2)}) collective-permute-start(bf16[32,3584]{1,0:T(8,128)(2,1)S(1)} %slice.12), channel_id=1, source_target_pairs={{0,4},{1,3},{2,6},{3,1},{4,0},{5,7},{6,2},{7,5},{8,12},{9,11},{10,... | collective-permute-start | bytes 688136 | tf_op jit(solution)/shard_map/ppermute | solution.py:426
  20.4 6.2 %collective-permute-start.10 = (bf16[192,256]{1,0:T(8,128)(2,1)S(1)}, bf16[192,256]{1,0:T(8,128)(2,1)S(1)}, u32[]{:S(2)}, u32[]{:S(2)}) collective-permute-start(bf16[192,256]{1,0:T(8,128)(2,1)S(1)} %get-tuple-element.64), channel_id=1, source_target_pairs={{0,4},{1,3},{2,6},{3,1},{4,0},{5,7},{6,2},{7,5},{8,12},{9,11},{10,... | collective-permute-start | bytes 294920 | tf_op jit(solution)/shard_map/ppermute | solution.py:426
  21.5 8.0 %collective-permute-start.13 = (bf16[32,4608]{1,0:T(8,128)(2,1)S(1)}, bf16[32,4608]{1,0:T(8,128)(2,1)S(1)}, u32[]{:S(2)}, u32[]{:S(2)}) collective-permute-start(bf16[32,4608]{1,0:T(8,128)(2,1)S(1)} %slice.13), channel_id=1, source_target_pairs={{0,4},{1,3},{2,6},{3,1},{4,0},{5,7},{6,2},{7,5},{8,12},{9,11},{10,... | collective-permute-start | bytes 884744 | tf_op jit(solution)/shard_map/ppermute | solution.py:426
  26.6 1.6 %collective-permute-start.14 = (bf16[32,3584]{1,0:T(8,128)(2,1)S(1)}, bf16[32,3584]{1,0:T(8,128)(2,1)S(1)}, u32[]{:S(2)}, u32[]{:S(2)}) collective-permute-start(bf16[32,3584]{1,0:T(8,128)(2,1)S(1)} %collective-permute-done.9.refs_3_), channel_id=1, source_target_pairs={{0,1},{1,0},{2,3},{3,2},{4,5},{5,4},{6,7},{7,6},{8,9},{9,8},{10,11... | collective-permute-start | bytes 688136 | tf_op jit(solution)/shard_map/ppermute | solution.py:426
  29.7 1.9 %collective-permute-start.15 = (bf16[32,2048]{1,0:T(8,128)(2,1)S(1)}, bf16[32,2048]{1,0:T(8,128)(2,1)S(1)}, u32[]{:S(2)}, u32[]{:S(2)}) collective-permute-start(bf16[32,2048]{1,0:T(8,128)(2,1)S(1)} %slice.14.refs_3_), channel_id=1, source_target_pairs={{0,1},{1,0},{2,3},{3,2},{4,5},{5,4},{6,7},{7,6},{8,9},{9,8},{10,11... | collective-permute-start | bytes 393224 | tf_op jit(solution)/shard_map/ppermute | solution.py:426
  33.1 6.2 %collective-permute-start.17 = (bf16[192,256]{1,0:T(8,128)(2,1)S(1)}, bf16[192,256]{1,0:T(8,128)(2,1)S(1)}, u32[]{:S(2)}, u32[]{:S(2)}) collective-permute-start(bf16[192,256]{1,0:T(8,128)(2,1)S(1)} %get-tuple-element.93.refs_0_), channel_id=1, source_target_pairs={{0,6},{1,7},{2,4},{3,5},{4,2},{5,3},{6,0},{7,1},{8,14},{9,15},{10,... | collective-permute-start | bytes 294920 | tf_op jit(solution)/shard_map/ppermute | solution.py:426
  35.2 5.8 %collective-permute-start.19 = (bf16[192,256]{1,0:T(8,128)(2,1)S(1)}, bf16[192,256]{1,0:T(8,128)(2,1)S(1)}, u32[]{:S(2)}, u32[]{:S(2)}) collective-permute-start(bf16[192,256]{1,0:T(8,128)(2,1)S(1)} %get-tuple-element.93.refs_0_), channel_id=1, source_target_pairs={{0,4},{1,3},{2,6},{3,1},{4,0},{5,7},{6,2},{7,5},{8,12},{9,11},{10,... | collective-permute-start | bytes 294920 | tf_op jit(solution)/shard_map/ppermute | solution.py:426
  36.6 4.6 %collective-permute-start.21 = (bf16[192,256]{1,0:T(8,128)(2,1)S(1)}, bf16[192,256]{1,0:T(8,128)(2,1)S(1)}, u32[]{:S(2)}, u32[]{:S(2)}) collective-permute-start(bf16[192,256]{1,0:T(8,128)(2,1)S(1)} %get-tuple-element.93.refs_0_), channel_id=1, source_target_pairs={{0,2},{1,5},{2,0},{3,7},{4,6},{5,1},{6,4},{7,3},{8,10},{9,13},{10,... | collective-permute-start | bytes 294920 | tf_op jit(solution)/shard_map/ppermute | solution.py:426
  36.6 4.9 %collective-permute-start.23 = (bf16[192,256]{1,0:T(8,128)(2,1)S(1)}, bf16[192,256]{1,0:T(8,128)(2,1)S(1)}, u32[]{:S(2)}, u32[]{:S(2)}) collective-permute-start(bf16[192,256]{1,0:T(8,128)(2,1)S(1)} %get-tuple-element.93.refs_0_), channel_id=1, source_target_pairs={{0,1},{1,0},{2,3},{3,2},{4,5},{5,4},{6,7},{7,6},{8,9},{9,8},{10,11... | collective-permute-start | bytes 294920 | tf_op jit(solution)/shard_map/ppermute | solution.py:426
  39.3 3.3 %collective-permute-start.18 = (bf16[192,256]{1,0:T(8,128)(2,1)S(1)}, bf16[192,256]{1,0:T(8,128)(2,1)S(1)}, u32[]{:S(2)}, u32[]{:S(2)}) collective-permute-start(bf16[192,256]{1,0:T(8,128)(2,1)S(1)} %collective-permute-done.17.refs_1_), channel_id=1, source_target_pairs={{0,1},{1,0},{2,3},{3,2},{4,5},{5,4},{6,7},{7,6},{8,9},{9,8},{10,11... | collective-permute-start | bytes 294920 | tf_op jit(solution)/shard_map/ppermute | solution.py:426
  41.0 1.6 %collective-permute-start.20 = (bf16[192,256]{1,0:T(8,128)(2,1)S(1)}, bf16[192,256]{1,0:T(8,128)(2,1)S(1)}, u32[]{:S(2)}, u32[]{:S(2)}) collective-permute-start(bf16[192,256]{1,0:T(8,128)(2,1)S(1)} %collective-permute-done.19.refs_2_), channel_id=1, source_target_pairs={{0,1},{1,0},{2,3},{3,2},{4,5},{5,4},{6,7},{7,6},{8,9},{9,8},{10,11... | collective-permute-start | bytes 294920 | tf_op jit(solution)/shard_map/ppermute | solution.py:426
  43.4 7.9 %collective-permute-start.24 = (bf16[48,1024]{1,0:T(8,128)(2,1)S(1)}, bf16[48,1024]{1,0:T(8,128)(2,1)S(1)}, u32[]{:S(2)}, u32[]{:S(2)}) collective-permute-start(bf16[48,1024]{1,0:T(8,128)(2,1)S(1)} %get-tuple-element.95), channel_id=1, source_target_pairs={{0,8},{8,16},{16,24},{24,0},{1,9},{9,17},{17,25},{25,1},{2,10},{10... | collective-permute-start | bytes 294920 | tf_op jit(solution)/shard_map/ppermute | solution.py:526
  45.6 9.5 %collective-permute-start.25 = (bf16[48,1024]{1,0:T(8,128)(2,1)S(1)}, bf16[48,1024]{1,0:T(8,128)(2,1)S(1)}, u32[]{:S(2)}, u32[]{:S(2)}) collective-permute-start(bf16[48,1024]{1,0:T(8,128)(2,1)S(1)} %get-tuple-element.96), channel_id=1, source_target_pairs={{0,16},{8,24},{16,0},{24,8},{1,17},{9,25},{17,1},{25,9},{2,18},{10... | collective-permute-start | bytes 294920 | tf_op jit(solution)/shard_map/ppermute | solution.py:526
  48.2 6.9 %collective-permute-start.26 = (bf16[48,1024]{1,0:T(8,128)(2,1)S(1)}, bf16[48,1024]{1,0:T(8,128)(2,1)S(1)}, u32[]{:S(2)}, u32[]{:S(2)}) collective-permute-start(bf16[48,1024]{1,0:T(8,128)(2,1)S(1)} %get-tuple-element.97), channel_id=1, source_target_pairs={{0,24},{8,0},{16,8},{24,16},{1,25},{9,1},{17,9},{25,17},{2,26},{10... | collective-permute-start | bytes 294920 | tf_op jit(solution)/shard_map/ppermute | solution.py:526
  (14 other events, 115.8 us)

commit v7 on v6

--- a/solution.py
+++ b/solution.py
@@ -473,14 +473,18 @@
     scalars = (tile_count, image_start)
     q_near, *live = queries(near, "queries_own_chip", scalars=scalars)
     forwarded = []
-    for first, last in ((0, cuts[1]), (cuts[1], depth)):
-        held = {mask: x[:, first:last] for mask, x in direct.items()}
-        passed = {}
-        for s in range(1, steps):
-            for mask in range(1, 1 << s):
-                more = mask | 1 << s
-                held[more] = passed[distance(more)] = exchange(held[mask], distance(1 << s))
-        forwarded.append(passed)
+    for order, columns in (
+        (range(steps), slice(0, cuts[1])),
+        (range(steps)[::-1], slice(cuts[1], depth)),
+    ):
+        held = {mask: x[:, columns] for mask, x in direct.items()}
+        known, passed = [], {}
+        for step in order:
+            for mask in known:
+                more = mask | 1 << step
+                held[more] = passed[distance(more)] = exchange(held[mask], distance(1 << step))
+            known += [mask | 1 << step for mask in known] + [1 << step]
+        forwarded.append(dict(sorted(passed.items())))
 
     next_to = both_cores({distance(mask): x for mask, x in direct.items()})
     q_next = queries(next_to, "queries_neighbours")

time: 56 us -> 58.1 us (1.038)
  starting transfers between devices: 22 us -> 23.2 us
  waiting for transfers between devices: 16.5 us -> 17.4 us
    ppermute x24, starting transfers between devices: 15.9 us -> 16.8 us  [exchange(): lax.ppermute(x, 'tensor', [(i, i ^ pair[i % 2]) for i in range(count)])]
    ppermute x24, waiting for transfers between devices: 11.8 us -> 12.7 us  [exchange(): lax.ppermute(x, 'tensor', [(i, i ^ pair[i % 2]) for i in range(count)])]
  transfers between devices with their start and end apart: 27 -> 27, of which waited for: 13 -> 15; matrix products, arithmetic and copies ran while one was open for 0% -> 0% of each run, Pallas kernels for 18% -> 17%
where the time goes in v7:
time: 58.1 us; the launch traced here: 57.9 us
  starting transfers between devices  23.2 us (40%)
  waiting for transfers between devices  17.4 us (30%)
  Pallas kernels  12.3 us (21%)
  local copies, waits for them, and re-layouts  3.28 us (6%)
  between operations  0.88 us (2%)
  other arithmetic  0.72 us (1%)
    ppermute x24, starting transfers between devices, exchange(): lax.ppermute(x, 'tensor', [(i, i ^ pair[i % 2]) for i in range(count)])  16.8 us
    ppermute x24, waiting for transfers between devices, exchange(): lax.ppermute(x, 'tensor', [(i, i ^ pair[i % 2]) for i in range(count)])  12.7 us
    ppermute x3, starting transfers between devices, shards(): arrived.append(lax.ppermute(leaving[k - 1], 'section', perm))  6.37 us
    pallas_call x5, Pallas kernels, queries_of(): pl.pallas_call(functools.partial(query_kernel, [len(parts) for parts in g...  5.9 us
    ppermute x3, waiting for transfers between devices, shards(): arrived.append(lax.ppermute(leaving[k - 1], 'section', perm))  4.77 us
    unnamed x22, local copies, waits for them, and re-layouts  3.22 us
    pallas_call x2, Pallas kernels, attention(): pl.pallas_call(functools.partial(attention_kernel, places, count, rows, l...  2.12 us
    pallas_call x2, Pallas kernels, feature_gradient(): pl.pallas_call(functools.partial(grad_kernel, pairs, per_kv, sections, be...  1.88 us
  transfers between devices with their start and end apart: 27, of which 15 were waited for; matrix products, arithmetic and copies ran while one was open for 0% of the time, Pallas kernels for 17%

profile of v7, /device:TPU:0, one launch (start us, length us, event | category | flops | bytes accessed | tf_op | source)
XLA Modules:
  0.0 57.9 jit_solution(13348144188182253814)
XLA Ops:
  0.6 3.0 %collective-permute-start.1 = (bf16[32,8192]{1,0:T(8,128)(2,1)}, bf16[32,8192]{1,0:T(8,128)(2,1)S(1)}, u32[]{:S(2)}, u32[]{:S(2)}) collective-permute-start(bf16[32,8192]{1,0:T(8,128)(2,1)} %bitcast.1), channel_id=1, source_target_pairs={{0,2},{1,5},{2,0},{3,7},{4,6},{5,1},{6,4},{7,3},{8,10},{9,13},{10,... | collective-permute-start | bytes 1572872 | tf_op jit(solution)/shard_map/ppermute | solution.py:426
  3.6 1.5 %collective-permute-start.2 = (bf16[32,8192]{1,0:T(8,128)(2,1)}, bf16[32,8192]{1,0:T(8,128)(2,1)S(1)}, u32[]{:S(2)}, u32[]{:S(2)}) collective-permute-start(bf16[32,8192]{1,0:T(8,128)(2,1)} %bitcast.2), channel_id=1, source_target_pairs={{0,4},{1,3},{2,6},{3,1},{4,0},{5,7},{6,2},{7,5},{8,12},{9,11},{10,... | collective-permute-start | bytes 1572872 | tf_op jit(solution)/shard_map/ppermute | solution.py:426
  5.2 2.2 %copy-done.1 = bf16[1,1024,2048]{2,1,0:T(8,128)(2,1)S(1)} copy-done((bf16[1,1024,2048]{2,1,0:T(8,128)(2,1)S(1)}, bf16[1,1024,2048]{2,1,0:T(8,128)(2,1)}, u32[]{:S(2)}) %copy-start.1) | copy-done | bytes 4194328
  7.4 1.0 %copy-done.3 = bf16[192,1024]{1,0:T(8,128)(2,1)S(1)} copy-done((bf16[192,1024]{1,0:T(8,128)(2,1)S(1)}, bf16[192,1024]{1,0:T(8,128)(2,1)}, u32[]{:S(2)}) %copy-start.3) | copy-done | bytes 393240
  13.8 1.3 %collective-permute-start.8 = (bf16[192,256]{1,0:T(8,128)(2,1)S(1)}, bf16[192,256]{1,0:T(8,128)(2,1)S(1)}, u32[]{:S(2)}, u32[]{:S(2)}) collective-permute-start(bf16[192,256]{1,0:T(8,128)(2,1)S(1)} %get-tuple-element.57), channel_id=1, source_target_pairs={{0,2},{1,5},{2,0},{3,7},{4,6},{5,1},{6,4},{7,3},{8,10},{9,13},{10,... | collective-permute-start | bytes 294920 | tf_op jit(solution)/shard_map/ppermute | solution.py:426
  15.1 2.6 %collective-permute-done.7.refs_2_ = bf16[192,256]{1,0:T(8,128)(2,1)S(1)} collective-permute-done((bf16[192,256]{1,0:T(8,128)(2,1)S(1)}, bf16[192,256]{1,0:T(8,128)(2,1)S(1)}, u32[]{:S(2)}, u32[]{:S(2)}) %collective-permute-start.7) | collective-permute-done | bytes 98336 | tf_op jit(solution)/shard_map/ppermute | solution.py:426
  17.7 1.1 %collective-permute-done.8.refs_3_ = bf16[192,256]{1,0:T(8,128)(2,1)S(1)} collective-permute-done((bf16[192,256]{1,0:T(8,128)(2,1)S(1)}, bf16[192,256]{1,0:T(8,128)(2,1)S(1)}, u32[]{:S(2)}, u32[]{:S(2)}) %collective-permute-start.8) | collective-permute-done | bytes 98336 | tf_op jit(solution)/shard_map/ppermute | solution.py:426
  19.3 1.1 %collective-permute-start.9 = (bf16[32,3584]{1,0:T(8,128)(2,1)S(1)}, bf16[32,3584]{1,0:T(8,128)(2,1)S(1)}, u32[]{:S(2)}, u32[]{:S(2)}) collective-permute-start(bf16[32,3584]{1,0:T(8,128)(2,1)S(1)} %slice.12), channel_id=1, source_target_pairs={{0,4},{1,3},{2,6},{3,1},{4,0},{5,7},{6,2},{7,5},{8,12},{9,11},{10,... | collective-permute-start | bytes 688136 | tf_op jit(solution)/shard_map/ppermute | solution.py:426
  20.4 1.1 %collective-permute-start.10 = (bf16[192,256]{1,0:T(8,128)(2,1)S(1)}, bf16[192,256]{1,0:T(8,128)(2,1)S(1)}, u32[]{:S(2)}, u32[]{:S(2)}) collective-permute-start(bf16[192,256]{1,0:T(8,128)(2,1)S(1)} %get-tuple-element.64), channel_id=1, source_target_pairs={{0,4},{1,3},{2,6},{3,1},{4,0},{5,7},{6,2},{7,5},{8,12},{9,11},{10,... | collective-permute-start | bytes 294920 | tf_op jit(solution)/shard_map/ppermute | solution.py:426
  21.5 2.1 %collective-permute-start.13 = (bf16[32,4608]{1,0:T(8,128)(2,1)S(1)}, bf16[32,4608]{1,0:T(8,128)(2,1)S(1)}, u32[]{:S(2)}, u32[]{:S(2)}) collective-permute-start(bf16[32,4608]{1,0:T(8,128)(2,1)S(1)} %slice.13), channel_id=1, source_target_pairs={{0,2},{1,5},{2,0},{3,7},{4,6},{5,1},{6,4},{7,3},{8,10},{9,13},{10,... | collective-permute-start | bytes 884744 | tf_op jit(solution)/shard_map/ppermute | solution.py:426
  23.6 2.3 %queries_own_chip.1 = (bf16[64,512]{1,0:T(8,128)(2,1)S(1)}, f32[256,128]{1,0:T(8,128)S(1)}, f32[2,8,96]{2,1,0:T(8,128)S(1)}) custom-call(s32[2]{0:T(128)S(1)} %copy-done.9, s32[2]{0:T(128)S(1)} %copy-done.10, bf16[1,8192]{1,0:T(2,128)(2,1)S(1)} %copy-done.5, bf16[1,8192,512]{2,1,0:T(8,128)(2,1)S(1)} %copy-done, bf16[1,128]{1,0:T(2,128)(2,1)S(1)} %copy-done.7, ...), custom_call_target="tpu_custom_call" | custom-call | tf_op jit(solution)/shard_map/queries_own_chip/pallas_call | solution.py:199
  26.0 1.7 %queries_neighbours.1.refs_3_ = bf16[128,512]{1,0:T(8,128)(2,1)S(1)} custom-call(bf16[1,8192]{1,0:T(2,128)(2,1)S(1)} %copy-done.5, bf16[1,8192,512]{2,1,0:T(8,128)(2,1)S(1)} %copy-done, bf16[1,128]{1,0:T(2,128)(2,1)S(1)} %copy-done.7, bf16[32,8192]{1,0:T(8,128)(2,1)S(1)} %collective-permute-done.1.refs_3_, ...), custom_call_target="tpu_custom_call" | custom-call | tf_op jit(solution)/shard_map/queries_neighbours/pallas_call | solution.py:199
  27.6 1.2 %collective-permute-done.10.refs_7_ = bf16[192,256]{1,0:T(8,128)(2,1)S(1)} collective-permute-done((bf16[192,256]{1,0:T(8,128)(2,1)S(1)}, bf16[192,256]{1,0:T(8,128)(2,1)S(1)}, u32[]{:S(2)}, u32[]{:S(2)}) %collective-permute-start.10) | collective-permute-done | bytes 98336 | tf_op jit(solution)/shard_map/ppermute | solution.py:426
  28.9 1.3 %attention_first.1 = (f32[192,512]{1,0:T(8,128)S(1)}, f32[192,128]{1,0:T(8,128)S(1)}, f32[192,128]{1,0:T(8,128)S(1)}, bf16[192,128]{1,0:T(8,128)(2,1)S(1)}, bf16...) custom-call(f32[256,128]{1,0:T(8,128)S(1)} %get-tuple-element.50.refs_0_, ...), custom_call_target="tpu_custom_call" | custom-call | tf_op jit(solution)/shard_map/attention_first/pallas_call | solution.py:317
  34.6 2.5 %collective-permute-start.17 = (bf16[192,256]{1,0:T(8,128)(2,1)S(1)}, bf16[192,256]{1,0:T(8,128)(2,1)S(1)}, u32[]{:S(2)}, u32[]{:S(2)}) collective-permute-start(bf16[192,256]{1,0:T(8,128)(2,1)S(1)} %get-tuple-element.93.refs_0_), channel_id=1, source_target_pairs={{0,6},{1,7},{2,4},{3,5},{4,2},{5,3},{6,0},{7,1},{8,14},{9,15},{10,... | collective-permute-start | bytes 294920 | tf_op jit(solution)/shard_map/ppermute | solution.py:426
  37.1 1.4 %collective-permute-start.19 = (bf16[192,256]{1,0:T(8,128)(2,1)S(1)}, bf16[192,256]{1,0:T(8,128)(2,1)S(1)}, u32[]{:S(2)}, u32[]{:S(2)}) collective-permute-start(bf16[192,256]{1,0:T(8,128)(2,1)S(1)} %get-tuple-element.93.refs_0_), channel_id=1, source_target_pairs={{0,4},{1,3},{2,6},{3,1},{4,0},{5,7},{6,2},{7,5},{8,12},{9,11},{10,... | collective-permute-start | bytes 294920 | tf_op jit(solution)/shard_map/ppermute | solution.py:426
  38.5 2.2 %collective-permute-done.17.refs_1_ = bf16[192,256]{1,0:T(8,128)(2,1)S(1)} collective-permute-done((bf16[192,256]{1,0:T(8,128)(2,1)S(1)}, bf16[192,256]{1,0:T(8,128)(2,1)S(1)}, u32[]{:S(2)}, u32[]{:S(2)}) %collective-permute-start.17) | collective-permute-done | bytes 98336 | tf_op jit(solution)/shard_map/ppermute | solution.py:426
  40.7 2.0 %collective-permute-done.19.refs_2_ = bf16[192,256]{1,0:T(8,128)(2,1)S(1)} collective-permute-done((bf16[192,256]{1,0:T(8,128)(2,1)S(1)}, bf16[192,256]{1,0:T(8,128)(2,1)S(1)}, u32[]{:S(2)}, u32[]{:S(2)}) %collective-permute-start.19) | collective-permute-done | bytes 98336 | tf_op jit(solution)/shard_map/ppermute | solution.py:426
  43.2 1.1 %feature_grad_first.1.refs_4_ = f32[192,1024]{1,0:T(8,128)S(1)} custom-call(bf16[192,256]{1,0:T(8,128)(2,1)S(1)} %get-tuple-element.93.refs_0_, bf16[192,256]{1,0:T(8,128)(2,1)S(1)} %collective-permute-done.17.refs_1_, bf16[192,256]{1,0:T(8,128)(2,1)S(1)} %collective-permute-done.19.refs_2_, bf16[192,256]{1,0:T(8,128)(2,1)S(1)} %collective-permute-done.21.refs_3_, ...), custom_call_target="tpu_custom_call" | custom-call | tf_op jit(solution)/shard_map/feature_grad_first/pallas_call | solution.py:406
  45.2 2.4 %collective-permute-start.24 = (bf16[48,1024]{1,0:T(8,128)(2,1)S(1)}, bf16[48,1024]{1,0:T(8,128)(2,1)S(1)}, u32[]{:S(2)}, u32[]{:S(2)}) collective-permute-start(bf16[48,1024]{1,0:T(8,128)(2,1)S(1)} %get-tuple-element.95), channel_id=1, source_target_pairs={{0,8},{8,16},{16,24},{24,0},{1,9},{9,17},{17,25},{25,1},{2,10},{10... | collective-permute-start | bytes 294920 | tf_op jit(solution)/shard_map/ppermute | solution.py:530
  47.7 2.6 %collective-permute-start.25 = (bf16[48,1024]{1,0:T(8,128)(2,1)S(1)}, bf16[48,1024]{1,0:T(8,128)(2,1)S(1)}, u32[]{:S(2)}, u32[]{:S(2)}) collective-permute-start(bf16[48,1024]{1,0:T(8,128)(2,1)S(1)} %get-tuple-element.96), channel_id=1, source_target_pairs={{0,16},{8,24},{16,0},{24,8},{1,17},{9,25},{17,1},{25,9},{2,18},{10... | collective-permute-start | bytes 294920 | tf_op jit(solution)/shard_map/ppermute | solution.py:530
  50.3 1.3 %collective-permute-start.26 = (bf16[48,1024]{1,0:T(8,128)(2,1)S(1)}, bf16[48,1024]{1,0:T(8,128)(2,1)S(1)}, u32[]{:S(2)}, u32[]{:S(2)}) collective-permute-start(bf16[48,1024]{1,0:T(8,128)(2,1)S(1)} %get-tuple-element.97), channel_id=1, source_target_pairs={{0,24},{8,0},{16,8},{24,16},{1,25},{9,1},{17,9},{25,17},{2,26},{10... | collective-permute-start | bytes 294920 | tf_op jit(solution)/shard_map/ppermute | solution.py:530
  52.4 1.0 %collective-permute-done.24 = bf16[48,1024]{1,0:T(8,128)(2,1)S(1)} collective-permute-done((bf16[48,1024]{1,0:T(8,128)(2,1)S(1)}, bf16[48,1024]{1,0:T(8,128)(2,1)S(1)}, u32[]{:S(2)}, u32[]{:S(2)}) %collective-permute-start.24) | collective-permute-done | bytes 98336 | tf_op jit(solution)/shard_map/ppermute | solution.py:530
  53.4 3.8 %collective-permute-done.25 = bf16[48,1024]{1,0:T(8,128)(2,1)S(1)} collective-permute-done((bf16[48,1024]{1,0:T(8,128)(2,1)S(1)}, bf16[48,1024]{1,0:T(8,128)(2,1)S(1)}, u32[]{:S(2)}, u32[]{:S(2)}) %collective-permute-start.25) | collective-permute-done | bytes 98336 | tf_op jit(solution)/shard_map/ppermute | solution.py:530
  (70 shorter events, 13.3 us)
Async XLA Ops:
  0.6 18.1 %collective-permute-start.1 = (bf16[32,8192]{1,0:T(8,128)(2,1)}, bf16[32,8192]{1,0:T(8,128)(2,1)S(1)}, u32[]{:S(2)}, u32[]{:S(2)}) collective-permute-start(bf16[32,8192]{1,0:T(8,128)(2,1)} %bitcast.1), channel_id=1, source_target_pairs={{0,2},{1,5},{2,0},{3,7},{4,6},{5,1},{6,4},{7,3},{8,10},{9,13},{10,... | collective-permute-start | bytes 1572872 | tf_op jit(solution)/shard_map/ppermute | solution.py:426
  3.6 15.1 %collective-permute-start.2 = (bf16[32,8192]{1,0:T(8,128)(2,1)}, bf16[32,8192]{1,0:T(8,128)(2,1)S(1)}, u32[]{:S(2)}, u32[]{:S(2)}) collective-permute-start(bf16[32,8192]{1,0:T(8,128)(2,1)} %bitcast.2), channel_id=1, source_target_pairs={{0,4},{1,3},{2,6},{3,1},{4,0},{5,7},{6,2},{7,5},{8,12},{9,11},{10,... | collective-permute-start | bytes 1572872 | tf_op jit(solution)/shard_map/ppermute | solution.py:426
  9.2 1.5 %collective-permute-start.3 = (f32[192,256]{1,0:T(8,128)S(1)}, f32[192,256]{1,0:T(8,128)S(1)}, u32[]{:S(2)}, u32[]{:S(2)}) collective-permute-start(f32[192,256]{1,0:T(8,128)S(1)} %get-tuple-element.52), channel_id=1, source_target_pairs={{0,1},{1,0},{2,3},{3,2},{4,5},{5,4},{6,7},{7,6},{8,9},{9,8},{10,11... | collective-permute-start | bytes 589832 | tf_op jit(solution)/shard_map/ppermute | solution.py:426
  9.3 1.7 %collective-permute-start.4 = (f32[192,256]{1,0:T(8,128)S(1)}, f32[192,256]{1,0:T(8,128)S(1)}, u32[]{:S(2)}, u32[]{:S(2)}) collective-permute-start(f32[192,256]{1,0:T(8,128)S(1)} %get-tuple-element.53), channel_id=1, source_target_pairs={{0,1},{1,0},{2,3},{3,2},{4,5},{5,4},{6,7},{7,6},{8,9},{9,8},{10,11... | collective-permute-start | bytes 589832 | tf_op jit(solution)/shard_map/ppermute | solution.py:426
  9.8 1.5 %collective-permute-start.5 = (f32[192,256]{1,0:T(8,128)S(1)}, f32[192,256]{1,0:T(8,128)S(1)}, u32[]{:S(2)}, u32[]{:S(2)}) collective-permute-start(f32[192,256]{1,0:T(8,128)S(1)} %get-tuple-element.54), channel_id=1, source_target_pairs={{0,1},{1,0},{2,3},{3,2},{4,5},{5,4},{6,7},{7,6},{8,9},{9,8},{10,11... | collective-permute-start | bytes 589832 | tf_op jit(solution)/shard_map/ppermute | solution.py:426
  13.0 4.7 %collective-permute-start.7 = (bf16[192,256]{1,0:T(8,128)(2,1)S(1)}, bf16[192,256]{1,0:T(8,128)(2,1)S(1)}, u32[]{:S(2)}, u32[]{:S(2)}) collective-permute-start(bf16[192,256]{1,0:T(8,128)(2,1)S(1)} %get-tuple-element.56), channel_id=1, source_target_pairs={{0,2},{1,5},{2,0},{3,7},{4,6},{5,1},{6,4},{7,3},{8,10},{9,13},{10,... | collective-permute-start | bytes 294920 | tf_op jit(solution)/shard_map/ppermute | solution.py:426
  13.8 4.9 %collective-permute-start.8 = (bf16[192,256]{1,0:T(8,128)(2,1)S(1)}, bf16[192,256]{1,0:T(8,128)(2,1)S(1)}, u32[]{:S(2)}, u32[]{:S(2)}) collective-permute-start(bf16[192,256]{1,0:T(8,128)(2,1)S(1)} %get-tuple-element.57), channel_id=1, source_target_pairs={{0,2},{1,5},{2,0},{3,7},{4,6},{5,1},{6,4},{7,3},{8,10},{9,13},{10,... | collective-permute-start | bytes 294920 | tf_op jit(solution)/shard_map/ppermute | solution.py:426
  15.1 6.5 %collective-permute-start = (bf16[32,8192]{1,0:T(8,128)(2,1)S(1)}, bf16[32,8192]{1,0:T(8,128)(2,1)S(1)}, u32[]{:S(2)}, u32[]{:S(2)}) collective-permute-start(bf16[32,8192]{1,0:T(8,128)(2,1)S(1)} %bitcast.3), channel_id=1, source_target_pairs={{0,1},{1,0},{2,3},{3,2},{4,5},{5,4},{6,7},{7,6},{8,9},{9,8},{10,11... | collective-permute-start | bytes 1572872 | tf_op jit(solution)/shard_map/ppermute | solution.py:426
  18.7 7.2 %collective-permute-start.11 = (bf16[32,8192]{1,0:T(8,128)(2,1)S(1)}, bf16[32,8192]{1,0:T(8,128)(2,1)S(1)}, u32[]{:S(2)}, u32[]{:S(2)}) collective-permute-start(bf16[32,8192]{1,0:T(8,128)(2,1)S(1)} %collective-permute-done.1.refs_3_), channel_id=1, source_target_pairs={{0,1},{1,0},{2,3},{3,2},{4,5},{5,4},{6,7},{7,6},{8,9},{9,8},{10,11... | collective-permute-start | bytes 1572872 | tf_op jit(solution)/shard_map/ppermute | solution.py:426
  18.8 7.2 %collective-permute-start.12 = (bf16[32,8192]{1,0:T(8,128)(2,1)S(1)}, bf16[32,8192]{1,0:T(8,128)(2,1)S(1)}, u32[]{:S(2)}, u32[]{:S(2)}) collective-permute-start(bf16[32,8192]{1,0:T(8,128)(2,1)S(1)} %collective-permute-done.2.refs_5_), channel_id=1, source_target_pairs={{0,1},{1,0},{2,3},{3,2},{4,5},{5,4},{6,7},{7,6},{8,9},{9,8},{10,11... | collective-permute-start | bytes 1572872 | tf_op jit(solution)/shard_map/ppermute | solution.py:426
  19.3 9.6 %collective-permute-start.9 = (bf16[32,3584]{1,0:T(8,128)(2,1)S(1)}, bf16[32,3584]{1,0:T(8,128)(2,1)S(1)}, u32[]{:S(2)}, u32[]{:S(2)}) collective-permute-start(bf16[32,3584]{1,0:T(8,128)(2,1)S(1)} %slice.12), channel_id=1, source_target_pairs={{0,4},{1,3},{2,6},{3,1},{4,0},{5,7},{6,2},{7,5},{8,12},{9,11},{10,... | collective-permute-start | bytes 688136 | tf_op jit(solution)/shard_map/ppermute | solution.py:426
  20.4 8.5 %collective-permute-start.10 = (bf16[192,256]{1,0:T(8,128)(2,1)S(1)}, bf16[192,256]{1,0:T(8,128)(2,1)S(1)}, u32[]{:S(2)}, u32[]{:S(2)}) collective-permute-start(bf16[192,256]{1,0:T(8,128)(2,1)S(1)} %get-tuple-element.64), channel_id=1, source_target_pairs={{0,4},{1,3},{2,6},{3,1},{4,0},{5,7},{6,2},{7,5},{8,12},{9,11},{10,... | collective-permute-start | bytes 294920 | tf_op jit(solution)/shard_map/ppermute | solution.py:426
  21.5 9.6 %collective-permute-start.13 = (bf16[32,4608]{1,0:T(8,128)(2,1)S(1)}, bf16[32,4608]{1,0:T(8,128)(2,1)S(1)}, u32[]{:S(2)}, u32[]{:S(2)}) collective-permute-start(bf16[32,4608]{1,0:T(8,128)(2,1)S(1)} %slice.13), channel_id=1, source_target_pairs={{0,2},{1,5},{2,0},{3,7},{4,6},{5,1},{6,4},{7,3},{8,10},{9,13},{10,... | collective-permute-start | bytes 884744 | tf_op jit(solution)/shard_map/ppermute | solution.py:426
  28.8 1.5 %collective-permute-start.14 = (bf16[32,3584]{1,0:T(8,128)(2,1)S(1)}, bf16[32,3584]{1,0:T(8,128)(2,1)S(1)}, u32[]{:S(2)}, u32[]{:S(2)}) collective-permute-start(bf16[32,3584]{1,0:T(8,128)(2,1)S(1)} %collective-permute-done.9.refs_3_), channel_id=1, source_target_pairs={{0,1},{1,0},{2,3},{3,2},{4,5},{5,4},{6,7},{7,6},{8,9},{9,8},{10,11... | collective-permute-start | bytes 688136 | tf_op jit(solution)/shard_map/ppermute | solution.py:426
  31.6 1.6 %collective-permute-start.15 = (bf16[32,2048]{1,0:T(8,128)(2,1)S(1)}, bf16[32,2048]{1,0:T(8,128)(2,1)S(1)}, u32[]{:S(2)}, u32[]{:S(2)}) collective-permute-start(bf16[32,2048]{1,0:T(8,128)(2,1)S(1)} %slice.14.refs_3_), channel_id=1, source_target_pairs={{0,1},{1,0},{2,3},{3,2},{4,5},{5,4},{6,7},{7,6},{8,9},{9,8},{10,11... | collective-permute-start | bytes 393224 | tf_op jit(solution)/shard_map/ppermute | solution.py:426
  34.6 6.1 %collective-permute-start.17 = (bf16[192,256]{1,0:T(8,128)(2,1)S(1)}, bf16[192,256]{1,0:T(8,128)(2,1)S(1)}, u32[]{:S(2)}, u32[]{:S(2)}) collective-permute-start(bf16[192,256]{1,0:T(8,128)(2,1)S(1)} %get-tuple-element.93.refs_0_), channel_id=1, source_target_pairs={{0,6},{1,7},{2,4},{3,5},{4,2},{5,3},{6,0},{7,1},{8,14},{9,15},{10,... | collective-permute-start | bytes 294920 | tf_op jit(solution)/shard_map/ppermute | solution.py:426
  37.1 5.7 %collective-permute-start.19 = (bf16[192,256]{1,0:T(8,128)(2,1)S(1)}, bf16[192,256]{1,0:T(8,128)(2,1)S(1)}, u32[]{:S(2)}, u32[]{:S(2)}) collective-permute-start(bf16[192,256]{1,0:T(8,128)(2,1)S(1)} %get-tuple-element.93.refs_0_), channel_id=1, source_target_pairs={{0,4},{1,3},{2,6},{3,1},{4,0},{5,7},{6,2},{7,5},{8,12},{9,11},{10,... | collective-permute-start | bytes 294920 | tf_op jit(solution)/shard_map/ppermute | solution.py:426
  38.5 4.6 %collective-permute-start.21 = (bf16[192,256]{1,0:T(8,128)(2,1)S(1)}, bf16[192,256]{1,0:T(8,128)(2,1)S(1)}, u32[]{:S(2)}, u32[]{:S(2)}) collective-permute-start(bf16[192,256]{1,0:T(8,128)(2,1)S(1)} %get-tuple-element.93.refs_0_), channel_id=1, source_target_pairs={{0,2},{1,5},{2,0},{3,7},{4,6},{5,1},{6,4},{7,3},{8,10},{9,13},{10,... | collective-permute-start | bytes 294920 | tf_op jit(solution)/shard_map/ppermute | solution.py:426
  38.5 4.7 %collective-permute-start.23 = (bf16[192,256]{1,0:T(8,128)(2,1)S(1)}, bf16[192,256]{1,0:T(8,128)(2,1)S(1)}, u32[]{:S(2)}, u32[]{:S(2)}) collective-permute-start(bf16[192,256]{1,0:T(8,128)(2,1)S(1)} %get-tuple-element.93.refs_0_), channel_id=1, source_target_pairs={{0,1},{1,0},{2,3},{3,2},{4,5},{5,4},{6,7},{7,6},{8,9},{9,8},{10,11... | collective-permute-start | bytes 294920 | tf_op jit(solution)/shard_map/ppermute | solution.py:426
  40.7 3.6 %collective-permute-start.18 = (bf16[192,256]{1,0:T(8,128)(2,1)S(1)}, bf16[192,256]{1,0:T(8,128)(2,1)S(1)}, u32[]{:S(2)}, u32[]{:S(2)}) collective-permute-start(bf16[192,256]{1,0:T(8,128)(2,1)S(1)} %collective-permute-done.17.refs_1_), channel_id=1, source_target_pairs={{0,1},{1,0},{2,3},{3,2},{4,5},{5,4},{6,7},{7,6},{8,9},{9,8},{10,11... | collective-permute-start | bytes 294920 | tf_op jit(solution)/shard_map/ppermute | solution.py:426
  42.7 1.6 %collective-permute-start.20 = (bf16[192,256]{1,0:T(8,128)(2,1)S(1)}, bf16[192,256]{1,0:T(8,128)(2,1)S(1)}, u32[]{:S(2)}, u32[]{:S(2)}) collective-permute-start(bf16[192,256]{1,0:T(8,128)(2,1)S(1)} %collective-permute-done.19.refs_2_), channel_id=1, source_target_pairs={{0,1},{1,0},{2,3},{3,2},{4,5},{5,4},{6,7},{7,6},{8,9},{9,8},{10,11... | collective-permute-start | bytes 294920 | tf_op jit(solution)/shard_map/ppermute | solution.py:426
  45.2 8.1 %collective-permute-start.24 = (bf16[48,1024]{1,0:T(8,128)(2,1)S(1)}, bf16[48,1024]{1,0:T(8,128)(2,1)S(1)}, u32[]{:S(2)}, u32[]{:S(2)}) collective-permute-start(bf16[48,1024]{1,0:T(8,128)(2,1)S(1)} %get-tuple-element.95), channel_id=1, source_target_pairs={{0,8},{8,16},{16,24},{24,0},{1,9},{9,17},{17,25},{25,1},{2,10},{10... | collective-permute-start | bytes 294920 | tf_op jit(solution)/shard_map/ppermute | solution.py:530
  47.7 9.5 %collective-permute-start.25 = (bf16[48,1024]{1,0:T(8,128)(2,1)S(1)}, bf16[48,1024]{1,0:T(8,128)(2,1)S(1)}, u32[]{:S(2)}, u32[]{:S(2)}) collective-permute-start(bf16[48,1024]{1,0:T(8,128)(2,1)S(1)} %get-tuple-element.96), channel_id=1, source_target_pairs={{0,16},{8,24},{16,0},{24,8},{1,17},{9,25},{17,1},{25,9},{2,18},{10... | collective-permute-start | bytes 294920 | tf_op jit(solution)/shard_map/ppermute | solution.py:530
  50.3 6.9 %collective-permute-start.26 = (bf16[48,1024]{1,0:T(8,128)(2,1)S(1)}, bf16[48,1024]{1,0:T(8,128)(2,1)S(1)}, u32[]{:S(2)}, u32[]{:S(2)}) collective-permute-start(bf16[48,1024]{1,0:T(8,128)(2,1)S(1)} %get-tuple-element.97), channel_id=1, source_target_pairs={{0,24},{8,0},{16,8},{24,16},{1,25},{9,1},{17,9},{25,17},{2,26},{10... | collective-permute-start | bytes 294920 | tf_op jit(solution)/shard_map/ppermute | solution.py:530
  (14 other events, 124.5 us)

commit v8 on v6

--- a/solution.py
+++ b/solution.py
@@ -153,11 +153,20 @@
         raw, squares, refs = refs[0][...], refs[1][:, :1], refs[2:]
     else:
         raw, squares = 0.0, 0.0
+    def rows_at(c):
+        return jnp.concatenate([columns(parts, c) for parts in groups], axis=0)
+
+    ahead = 1.0
+    if not start and last:
+        for c in range(0, width, span):
+            squares = squares + jnp.sum(rows_at(c) ** 2, axis=-1, keepdims=True)
+        ahead = lax.rsqrt(squares / depth + eps)
     for c in range(0, width, span):
-        x = jnp.concatenate([columns(parts, c) for parts in groups], axis=0)
-        squares = squares + jnp.sum(x * x, axis=-1, keepdims=True)
+        x = rows_at(c)
+        if start or not last:
+            squares = squares + jnp.sum(x * x, axis=-1, keepdims=True)
         cols = slice(start + c, start + c + span)
-        scaled = (x * gain_ref[:, cols].astype(F32)).astype(BF16)
+        scaled = (x * ahead * gain_ref[:, cols].astype(F32)).astype(BF16)
         raw = raw + dot_nn(scaled, weight_ref[0, cols, :])
     if not last:
         refs[0][...] = raw
@@ -165,7 +174,7 @@
         return
     out_ref = refs[-1]
     rows = groups[0][0].shape[0]
-    inverse = lax.rsqrt(squares / depth + eps)
+    inverse = lax.rsqrt(squares / depth + eps) if start else 1.0
     q_gain = q_gain_ref[...].astype(F32)
     for c in range(0, heads_width, HEAD_DIM):
         head = raw[:, c : c + HEAD_DIM] * inverse

time: 56 us -> 56 us (level)
  Pallas kernels: 12.3 us -> 12.9 us
  transfers between devices with their start and end apart: 27 -> 27, of which waited for: 13 -> 12; matrix products, arithmetic and copies ran while one was open for 0% -> 0% of each run, Pallas kernels for 18% -> 19%
where the time goes in v8:
time: 56 us; the launch traced here: 55.8 us
  starting transfers between devices  22 us (39%)
  waiting for transfers between devices  16 us (29%)
  Pallas kernels  12.9 us (23%)
  local copies, waits for them, and re-layouts  3.28 us (6%)
  between operations  0.9 us (2%)
  other arithmetic  0.72 us (1%)
    ppermute x24, starting transfers between devices, exchange(): lax.ppermute(x, 'tensor', [(i, i ^ pair[i % 2]) for i in range(count)])  16 us
    ppermute x24, waiting for transfers between devices, exchange(): lax.ppermute(x, 'tensor', [(i, i ^ pair[i % 2]) for i in range(count)])  11.2 us
    pallas_call x5, Pallas kernels, queries_of(): pl.pallas_call(functools.partial(query_kernel, [len(parts) for parts in g...  6.44 us
    ppermute x3, starting transfers between devices, shards(): arrived.append(lax.ppermute(leaving[k - 1], 'section', perm))  5.97 us
    ppermute x3, waiting for transfers between devices, shards(): arrived.append(lax.ppermute(leaving[k - 1], 'section', perm))  4.77 us
    unnamed x22, local copies, waits for them, and re-layouts  3.22 us
    pallas_call x2, Pallas kernels, attention(): pl.pallas_call(functools.partial(attention_kernel, places, count, rows, l...  2.11 us
    pallas_call x2, Pallas kernels, feature_gradient(): pl.pallas_call(functools.partial(grad_kernel, pairs, per_kv, sections, be...  1.89 us
  transfers between devices with their start and end apart: 27, of which 12 were waited for; matrix products, arithmetic and copies ran while one was open for 0% of the time, Pallas kernels for 19%

profile of v8, /device:TPU:0, one launch (start us, length us, event | category | flops | bytes accessed | tf_op | source)
XLA Modules:
  0.0 55.8 jit_solution(7694719882304512938)
XLA Ops:
  0.6 3.0 %collective-permute-start.1 = (bf16[32,8192]{1,0:T(8,128)(2,1)}, bf16[32,8192]{1,0:T(8,128)(2,1)S(1)}, u32[]{:S(2)}, u32[]{:S(2)}) collective-permute-start(bf16[32,8192]{1,0:T(8,128)(2,1)} %bitcast.1), channel_id=1, source_target_pairs={{0,2},{1,5},{2,0},{3,7},{4,6},{5,1},{6,4},{7,3},{8,10},{9,13},{10,... | collective-permute-start | bytes 1572872 | tf_op jit(solution)/shard_map/ppermute | solution.py:435
  3.6 1.5 %collective-permute-start.2 = (bf16[32,8192]{1,0:T(8,128)(2,1)}, bf16[32,8192]{1,0:T(8,128)(2,1)S(1)}, u32[]{:S(2)}, u32[]{:S(2)}) collective-permute-start(bf16[32,8192]{1,0:T(8,128)(2,1)} %bitcast.2), channel_id=1, source_target_pairs={{0,4},{1,3},{2,6},{3,1},{4,0},{5,7},{6,2},{7,5},{8,12},{9,11},{10,... | collective-permute-start | bytes 1572872 | tf_op jit(solution)/shard_map/ppermute | solution.py:435
  5.2 2.2 %copy-done.1 = bf16[1,1024,2048]{2,1,0:T(8,128)(2,1)S(1)} copy-done((bf16[1,1024,2048]{2,1,0:T(8,128)(2,1)S(1)}, bf16[1,1024,2048]{2,1,0:T(8,128)(2,1)}, u32[]{:S(2)}) %copy-start.1) | copy-done | bytes 4194328
  7.4 1.0 %copy-done.3 = bf16[192,1024]{1,0:T(8,128)(2,1)S(1)} copy-done((bf16[192,1024]{1,0:T(8,128)(2,1)S(1)}, bf16[192,1024]{1,0:T(8,128)(2,1)}, u32[]{:S(2)}) %copy-start.3) | copy-done | bytes 393240
  11.3 0.9 %collective-permute-done.6.refs_3_ = f32[192,256]{1,0:T(8,128)S(1)} collective-permute-done((f32[192,256]{1,0:T(8,128)S(1)}, f32[192,256]{1,0:T(8,128)S(1)}, u32[]{:S(2)}, u32[]{:S(2)}) %collective-permute-start.6) | collective-permute-done | bytes 196640 | tf_op jit(solution)/shard_map/ppermute | solution.py:435
  13.8 1.3 %collective-permute-start.8 = (bf16[192,256]{1,0:T(8,128)(2,1)S(1)}, bf16[192,256]{1,0:T(8,128)(2,1)S(1)}, u32[]{:S(2)}, u32[]{:S(2)}) collective-permute-start(bf16[192,256]{1,0:T(8,128)(2,1)S(1)} %get-tuple-element.57), channel_id=1, source_target_pairs={{0,2},{1,5},{2,0},{3,7},{4,6},{5,1},{6,4},{7,3},{8,10},{9,13},{10,... | collective-permute-start | bytes 294920 | tf_op jit(solution)/shard_map/ppermute | solution.py:435
  15.1 2.6 %collective-permute-done.7.refs_2_ = bf16[192,256]{1,0:T(8,128)(2,1)S(1)} collective-permute-done((bf16[192,256]{1,0:T(8,128)(2,1)S(1)}, bf16[192,256]{1,0:T(8,128)(2,1)S(1)}, u32[]{:S(2)}, u32[]{:S(2)}) %collective-permute-start.7) | collective-permute-done | bytes 98336 | tf_op jit(solution)/shard_map/ppermute | solution.py:435
  17.7 1.1 %collective-permute-done.8.refs_3_ = bf16[192,256]{1,0:T(8,128)(2,1)S(1)} collective-permute-done((bf16[192,256]{1,0:T(8,128)(2,1)S(1)}, bf16[192,256]{1,0:T(8,128)(2,1)S(1)}, u32[]{:S(2)}, u32[]{:S(2)}) %collective-permute-start.8) | collective-permute-done | bytes 98336 | tf_op jit(solution)/shard_map/ppermute | solution.py:435
  19.3 1.1 %collective-permute-start.9 = (bf16[32,3584]{1,0:T(8,128)(2,1)S(1)}, bf16[32,3584]{1,0:T(8,128)(2,1)S(1)}, u32[]{:S(2)}, u32[]{:S(2)}) collective-permute-start(bf16[32,3584]{1,0:T(8,128)(2,1)S(1)} %slice.12), channel_id=1, source_target_pairs={{0,4},{1,3},{2,6},{3,1},{4,0},{5,7},{6,2},{7,5},{8,12},{9,11},{10,... | collective-permute-start | bytes 688136 | tf_op jit(solution)/shard_map/ppermute | solution.py:435
  20.4 1.1 %collective-permute-start.10 = (bf16[192,256]{1,0:T(8,128)(2,1)S(1)}, bf16[192,256]{1,0:T(8,128)(2,1)S(1)}, u32[]{:S(2)}, u32[]{:S(2)}) collective-permute-start(bf16[192,256]{1,0:T(8,128)(2,1)S(1)} %get-tuple-element.64), channel_id=1, source_target_pairs={{0,4},{1,3},{2,6},{3,1},{4,0},{5,7},{6,2},{7,5},{8,12},{9,11},{10,... | collective-permute-start | bytes 294920 | tf_op jit(solution)/shard_map/ppermute | solution.py:435
  21.5 1.1 %collective-permute-start.13 = (bf16[32,4608]{1,0:T(8,128)(2,1)S(1)}, bf16[32,4608]{1,0:T(8,128)(2,1)S(1)}, u32[]{:S(2)}, u32[]{:S(2)}) collective-permute-start(bf16[32,4608]{1,0:T(8,128)(2,1)S(1)} %slice.13), channel_id=1, source_target_pairs={{0,4},{1,3},{2,6},{3,1},{4,0},{5,7},{6,2},{7,5},{8,12},{9,11},{10,... | collective-permute-start | bytes 884744 | tf_op jit(solution)/shard_map/ppermute | solution.py:435
  22.6 2.5 %queries_own_chip.1 = (bf16[64,512]{1,0:T(8,128)(2,1)S(1)}, f32[256,128]{1,0:T(8,128)S(1)}, f32[2,8,96]{2,1,0:T(8,128)S(1)}) custom-call(s32[2]{0:T(128)S(1)} %copy-done.9, s32[2]{0:T(128)S(1)} %copy-done.10, bf16[1,8192]{1,0:T(2,128)(2,1)S(1)} %copy-done.5, bf16[1,8192,512]{2,1,0:T(8,128)(2,1)S(1)} %copy-done, bf16[1,128]{1,0:T(2,128)(2,1)S(1)} %copy-done.7, ...), custom_call_target="tpu_custom_call" | custom-call | tf_op jit(solution)/shard_map/queries_own_chip/pallas_call | solution.py:208
  25.1 2.0 %queries_neighbours.1.refs_3_ = bf16[128,512]{1,0:T(8,128)(2,1)S(1)} custom-call(bf16[1,8192]{1,0:T(2,128)(2,1)S(1)} %copy-done.5, bf16[1,8192,512]{2,1,0:T(8,128)(2,1)S(1)} %copy-done, bf16[1,128]{1,0:T(2,128)(2,1)S(1)} %copy-done.7, bf16[32,8192]{1,0:T(8,128)(2,1)S(1)} %collective-permute-done.1.refs_3_, ...), custom_call_target="tpu_custom_call" | custom-call | tf_op jit(solution)/shard_map/queries_neighbours/pallas_call | solution.py:208
  27.5 1.3 %attention_first.1 = (f32[192,512]{1,0:T(8,128)S(1)}, f32[192,128]{1,0:T(8,128)S(1)}, f32[192,128]{1,0:T(8,128)S(1)}, bf16[192,128]{1,0:T(8,128)(2,1)S(1)}, bf16...) custom-call(f32[256,128]{1,0:T(8,128)S(1)} %get-tuple-element.50.refs_0_, ...), custom_call_target="tpu_custom_call" | custom-call | tf_op jit(solution)/shard_map/attention_first/pallas_call | solution.py:326
  33.1 2.5 %collective-permute-start.17 = (bf16[192,256]{1,0:T(8,128)(2,1)S(1)}, bf16[192,256]{1,0:T(8,128)(2,1)S(1)}, u32[]{:S(2)}, u32[]{:S(2)}) collective-permute-start(bf16[192,256]{1,0:T(8,128)(2,1)S(1)} %get-tuple-element.93.refs_0_), channel_id=1, source_target_pairs={{0,6},{1,7},{2,4},{3,5},{4,2},{5,3},{6,0},{7,1},{8,14},{9,15},{10,... | collective-permute-start | bytes 294920 | tf_op jit(solution)/shard_map/ppermute | solution.py:435
  35.5 1.1 %collective-permute-start.19 = (bf16[192,256]{1,0:T(8,128)(2,1)S(1)}, bf16[192,256]{1,0:T(8,128)(2,1)S(1)}, u32[]{:S(2)}, u32[]{:S(2)}) collective-permute-start(bf16[192,256]{1,0:T(8,128)(2,1)S(1)} %get-tuple-element.93.refs_0_), channel_id=1, source_target_pairs={{0,4},{1,3},{2,6},{3,1},{4,0},{5,7},{6,2},{7,5},{8,12},{9,11},{10,... | collective-permute-start | bytes 294920 | tf_op jit(solution)/shard_map/ppermute | solution.py:435
  36.6 2.9 %collective-permute-done.17.refs_1_ = bf16[192,256]{1,0:T(8,128)(2,1)S(1)} collective-permute-done((bf16[192,256]{1,0:T(8,128)(2,1)S(1)}, bf16[192,256]{1,0:T(8,128)(2,1)S(1)}, u32[]{:S(2)}, u32[]{:S(2)}) %collective-permute-start.17) | collective-permute-done | bytes 98336 | tf_op jit(solution)/shard_map/ppermute | solution.py:435
  39.5 1.6 %collective-permute-done.19.refs_2_ = bf16[192,256]{1,0:T(8,128)(2,1)S(1)} collective-permute-done((bf16[192,256]{1,0:T(8,128)(2,1)S(1)}, bf16[192,256]{1,0:T(8,128)(2,1)S(1)}, u32[]{:S(2)}, u32[]{:S(2)}) %collective-permute-start.19) | collective-permute-done | bytes 98336 | tf_op jit(solution)/shard_map/ppermute | solution.py:435
  41.6 1.1 %feature_grad_first.1.refs_4_ = f32[192,1024]{1,0:T(8,128)S(1)} custom-call(bf16[192,256]{1,0:T(8,128)(2,1)S(1)} %get-tuple-element.93.refs_0_, bf16[192,256]{1,0:T(8,128)(2,1)S(1)} %collective-permute-done.17.refs_1_, bf16[192,256]{1,0:T(8,128)(2,1)S(1)} %collective-permute-done.19.refs_2_, bf16[192,256]{1,0:T(8,128)(2,1)S(1)} %collective-permute-done.21.refs_3_, ...), custom_call_target="tpu_custom_call" | custom-call | tf_op jit(solution)/shard_map/feature_grad_first/pallas_call | solution.py:415
  43.6 2.0 %collective-permute-start.24 = (bf16[48,1024]{1,0:T(8,128)(2,1)S(1)}, bf16[48,1024]{1,0:T(8,128)(2,1)S(1)}, u32[]{:S(2)}, u32[]{:S(2)}) collective-permute-start(bf16[48,1024]{1,0:T(8,128)(2,1)S(1)} %get-tuple-element.95), channel_id=1, source_target_pairs={{0,8},{8,16},{16,24},{24,0},{1,9},{9,17},{17,25},{25,1},{2,10},{10... | collective-permute-start | bytes 294920 | tf_op jit(solution)/shard_map/ppermute | solution.py:535
  45.6 2.6 %collective-permute-start.25 = (bf16[48,1024]{1,0:T(8,128)(2,1)S(1)}, bf16[48,1024]{1,0:T(8,128)(2,1)S(1)}, u32[]{:S(2)}, u32[]{:S(2)}) collective-permute-start(bf16[48,1024]{1,0:T(8,128)(2,1)S(1)} %get-tuple-element.96), channel_id=1, source_target_pairs={{0,16},{8,24},{16,0},{24,8},{1,17},{9,25},{17,1},{25,9},{2,18},{10... | collective-permute-start | bytes 294920 | tf_op jit(solution)/shard_map/ppermute | solution.py:535
  48.2 1.4 %collective-permute-start.26 = (bf16[48,1024]{1,0:T(8,128)(2,1)S(1)}, bf16[48,1024]{1,0:T(8,128)(2,1)S(1)}, u32[]{:S(2)}, u32[]{:S(2)}) collective-permute-start(bf16[48,1024]{1,0:T(8,128)(2,1)S(1)} %get-tuple-element.97), channel_id=1, source_target_pairs={{0,24},{8,0},{16,8},{24,16},{1,25},{9,1},{17,9},{25,17},{2,26},{10... | collective-permute-start | bytes 294920 | tf_op jit(solution)/shard_map/ppermute | solution.py:535
  50.3 1.0 %collective-permute-done.24 = bf16[48,1024]{1,0:T(8,128)(2,1)S(1)} collective-permute-done((bf16[48,1024]{1,0:T(8,128)(2,1)S(1)}, bf16[48,1024]{1,0:T(8,128)(2,1)S(1)}, u32[]{:S(2)}, u32[]{:S(2)}) %collective-permute-start.24) | collective-permute-done | bytes 98336 | tf_op jit(solution)/shard_map/ppermute | solution.py:535
  51.3 3.8 %collective-permute-done.25 = bf16[48,1024]{1,0:T(8,128)(2,1)S(1)} collective-permute-done((bf16[48,1024]{1,0:T(8,128)(2,1)S(1)}, bf16[48,1024]{1,0:T(8,128)(2,1)S(1)}, u32[]{:S(2)}, u32[]{:S(2)}) %collective-permute-start.25) | collective-permute-done | bytes 98336 | tf_op jit(solution)/shard_map/ppermute | solution.py:535
  (70 shorter events, 12.6 us)
Async XLA Ops:
  0.6 18.1 %collective-permute-start.1 = (bf16[32,8192]{1,0:T(8,128)(2,1)}, bf16[32,8192]{1,0:T(8,128)(2,1)S(1)}, u32[]{:S(2)}, u32[]{:S(2)}) collective-permute-start(bf16[32,8192]{1,0:T(8,128)(2,1)} %bitcast.1), channel_id=1, source_target_pairs={{0,2},{1,5},{2,0},{3,7},{4,6},{5,1},{6,4},{7,3},{8,10},{9,13},{10,... | collective-permute-start | bytes 1572872 | tf_op jit(solution)/shard_map/ppermute | solution.py:435
  3.6 15.1 %collective-permute-start.2 = (bf16[32,8192]{1,0:T(8,128)(2,1)}, bf16[32,8192]{1,0:T(8,128)(2,1)S(1)}, u32[]{:S(2)}, u32[]{:S(2)}) collective-permute-start(bf16[32,8192]{1,0:T(8,128)(2,1)} %bitcast.2), channel_id=1, source_target_pairs={{0,4},{1,3},{2,6},{3,1},{4,0},{5,7},{6,2},{7,5},{8,12},{9,11},{10,... | collective-permute-start | bytes 1572872 | tf_op jit(solution)/shard_map/ppermute | solution.py:435
  9.2 1.5 %collective-permute-start.3 = (f32[192,256]{1,0:T(8,128)S(1)}, f32[192,256]{1,0:T(8,128)S(1)}, u32[]{:S(2)}, u32[]{:S(2)}) collective-permute-start(f32[192,256]{1,0:T(8,128)S(1)} %get-tuple-element.52), channel_id=1, source_target_pairs={{0,1},{1,0},{2,3},{3,2},{4,5},{5,4},{6,7},{7,6},{8,9},{9,8},{10,11... | collective-permute-start | bytes 589832 | tf_op jit(solution)/shard_map/ppermute | solution.py:435
  9.3 1.7 %collective-permute-start.4 = (f32[192,256]{1,0:T(8,128)S(1)}, f32[192,256]{1,0:T(8,128)S(1)}, u32[]{:S(2)}, u32[]{:S(2)}) collective-permute-start(f32[192,256]{1,0:T(8,128)S(1)} %get-tuple-element.53), channel_id=1, source_target_pairs={{0,1},{1,0},{2,3},{3,2},{4,5},{5,4},{6,7},{7,6},{8,9},{9,8},{10,11... | collective-permute-start | bytes 589832 | tf_op jit(solution)/shard_map/ppermute | solution.py:435
  9.8 1.5 %collective-permute-start.5 = (f32[192,256]{1,0:T(8,128)S(1)}, f32[192,256]{1,0:T(8,128)S(1)}, u32[]{:S(2)}, u32[]{:S(2)}) collective-permute-start(f32[192,256]{1,0:T(8,128)S(1)} %get-tuple-element.54), channel_id=1, source_target_pairs={{0,1},{1,0},{2,3},{3,2},{4,5},{5,4},{6,7},{7,6},{8,9},{9,8},{10,11... | collective-permute-start | bytes 589832 | tf_op jit(solution)/shard_map/ppermute | solution.py:435
  13.0 4.7 %collective-permute-start.7 = (bf16[192,256]{1,0:T(8,128)(2,1)S(1)}, bf16[192,256]{1,0:T(8,128)(2,1)S(1)}, u32[]{:S(2)}, u32[]{:S(2)}) collective-permute-start(bf16[192,256]{1,0:T(8,128)(2,1)S(1)} %get-tuple-element.56), channel_id=1, source_target_pairs={{0,2},{1,5},{2,0},{3,7},{4,6},{5,1},{6,4},{7,3},{8,10},{9,13},{10,... | collective-permute-start | bytes 294920 | tf_op jit(solution)/shard_map/ppermute | solution.py:435
  13.8 4.9 %collective-permute-start.8 = (bf16[192,256]{1,0:T(8,128)(2,1)S(1)}, bf16[192,256]{1,0:T(8,128)(2,1)S(1)}, u32[]{:S(2)}, u32[]{:S(2)}) collective-permute-start(bf16[192,256]{1,0:T(8,128)(2,1)S(1)} %get-tuple-element.57), channel_id=1, source_target_pairs={{0,2},{1,5},{2,0},{3,7},{4,6},{5,1},{6,4},{7,3},{8,10},{9,13},{10,... | collective-permute-start | bytes 294920 | tf_op jit(solution)/shard_map/ppermute | solution.py:435
  15.1 6.5 %collective-permute-start = (bf16[32,8192]{1,0:T(8,128)(2,1)S(1)}, bf16[32,8192]{1,0:T(8,128)(2,1)S(1)}, u32[]{:S(2)}, u32[]{:S(2)}) collective-permute-start(bf16[32,8192]{1,0:T(8,128)(2,1)S(1)} %bitcast.3), channel_id=1, source_target_pairs={{0,1},{1,0},{2,3},{3,2},{4,5},{5,4},{6,7},{7,6},{8,9},{9,8},{10,11... | collective-permute-start | bytes 1572872 | tf_op jit(solution)/shard_map/ppermute | solution.py:435
  18.7 6.4 %collective-permute-start.11 = (bf16[32,8192]{1,0:T(8,128)(2,1)S(1)}, bf16[32,8192]{1,0:T(8,128)(2,1)S(1)}, u32[]{:S(2)}, u32[]{:S(2)}) collective-permute-start(bf16[32,8192]{1,0:T(8,128)(2,1)S(1)} %collective-permute-done.1.refs_3_), channel_id=1, source_target_pairs={{0,1},{1,0},{2,3},{3,2},{4,5},{5,4},{6,7},{7,6},{8,9},{9,8},{10,11... | collective-permute-start | bytes 1572872 | tf_op jit(solution)/shard_map/ppermute | solution.py:435
  18.8 6.4 %collective-permute-start.12 = (bf16[32,8192]{1,0:T(8,128)(2,1)S(1)}, bf16[32,8192]{1,0:T(8,128)(2,1)S(1)}, u32[]{:S(2)}, u32[]{:S(2)}) collective-permute-start(bf16[32,8192]{1,0:T(8,128)(2,1)S(1)} %collective-permute-done.2.refs_5_), channel_id=1, source_target_pairs={{0,1},{1,0},{2,3},{3,2},{4,5},{5,4},{6,7},{7,6},{8,9},{9,8},{10,11... | collective-permute-start | bytes 1572872 | tf_op jit(solution)/shard_map/ppermute | solution.py:435
  19.3 7.9 %collective-permute-start.9 = (bf16[32,3584]{1,0:T(8,128)(2,1)S(1)}, bf16[32,3584]{1,0:T(8,128)(2,1)S(1)}, u32[]{:S(2)}, u32[]{:S(2)}) collective-permute-start(bf16[32,3584]{1,0:T(8,128)(2,1)S(1)} %slice.12), channel_id=1, source_target_pairs={{0,4},{1,3},{2,6},{3,1},{4,0},{5,7},{6,2},{7,5},{8,12},{9,11},{10,... | collective-permute-start | bytes 688136 | tf_op jit(solution)/shard_map/ppermute | solution.py:435
  20.4 6.8 %collective-permute-start.10 = (bf16[192,256]{1,0:T(8,128)(2,1)S(1)}, bf16[192,256]{1,0:T(8,128)(2,1)S(1)}, u32[]{:S(2)}, u32[]{:S(2)}) collective-permute-start(bf16[192,256]{1,0:T(8,128)(2,1)S(1)} %get-tuple-element.64), channel_id=1, source_target_pairs={{0,4},{1,3},{2,6},{3,1},{4,0},{5,7},{6,2},{7,5},{8,12},{9,11},{10,... | collective-permute-start | bytes 294920 | tf_op jit(solution)/shard_map/ppermute | solution.py:435
  21.5 8.1 %collective-permute-start.13 = (bf16[32,4608]{1,0:T(8,128)(2,1)S(1)}, bf16[32,4608]{1,0:T(8,128)(2,1)S(1)}, u32[]{:S(2)}, u32[]{:S(2)}) collective-permute-start(bf16[32,4608]{1,0:T(8,128)(2,1)S(1)} %slice.13), channel_id=1, source_target_pairs={{0,4},{1,3},{2,6},{3,1},{4,0},{5,7},{6,2},{7,5},{8,12},{9,11},{10,... | collective-permute-start | bytes 884744 | tf_op jit(solution)/shard_map/ppermute | solution.py:435
  27.2 1.6 %collective-permute-start.14 = (bf16[32,3584]{1,0:T(8,128)(2,1)S(1)}, bf16[32,3584]{1,0:T(8,128)(2,1)S(1)}, u32[]{:S(2)}, u32[]{:S(2)}) collective-permute-start(bf16[32,3584]{1,0:T(8,128)(2,1)S(1)} %collective-permute-done.9.refs_3_), channel_id=1, source_target_pairs={{0,1},{1,0},{2,3},{3,2},{4,5},{5,4},{6,7},{7,6},{8,9},{9,8},{10,11... | collective-permute-start | bytes 688136 | tf_op jit(solution)/shard_map/ppermute | solution.py:435
  30.0 1.7 %collective-permute-start.15 = (bf16[32,2048]{1,0:T(8,128)(2,1)S(1)}, bf16[32,2048]{1,0:T(8,128)(2,1)S(1)}, u32[]{:S(2)}, u32[]{:S(2)}) collective-permute-start(bf16[32,2048]{1,0:T(8,128)(2,1)S(1)} %slice.14.refs_3_), channel_id=1, source_target_pairs={{0,1},{1,0},{2,3},{3,2},{4,5},{5,4},{6,7},{7,6},{8,9},{9,8},{10,11... | collective-permute-start | bytes 393224 | tf_op jit(solution)/shard_map/ppermute | solution.py:435
  33.1 6.4 %collective-permute-start.17 = (bf16[192,256]{1,0:T(8,128)(2,1)S(1)}, bf16[192,256]{1,0:T(8,128)(2,1)S(1)}, u32[]{:S(2)}, u32[]{:S(2)}) collective-permute-start(bf16[192,256]{1,0:T(8,128)(2,1)S(1)} %get-tuple-element.93.refs_0_), channel_id=1, source_target_pairs={{0,6},{1,7},{2,4},{3,5},{4,2},{5,3},{6,0},{7,1},{8,14},{9,15},{10,... | collective-permute-start | bytes 294920 | tf_op jit(solution)/shard_map/ppermute | solution.py:435
  35.5 5.6 %collective-permute-start.19 = (bf16[192,256]{1,0:T(8,128)(2,1)S(1)}, bf16[192,256]{1,0:T(8,128)(2,1)S(1)}, u32[]{:S(2)}, u32[]{:S(2)}) collective-permute-start(bf16[192,256]{1,0:T(8,128)(2,1)S(1)} %get-tuple-element.93.refs_0_), channel_id=1, source_target_pairs={{0,4},{1,3},{2,6},{3,1},{4,0},{5,7},{6,2},{7,5},{8,12},{9,11},{10,... | collective-permute-start | bytes 294920 | tf_op jit(solution)/shard_map/ppermute | solution.py:435
  36.6 4.6 %collective-permute-start.21 = (bf16[192,256]{1,0:T(8,128)(2,1)S(1)}, bf16[192,256]{1,0:T(8,128)(2,1)S(1)}, u32[]{:S(2)}, u32[]{:S(2)}) collective-permute-start(bf16[192,256]{1,0:T(8,128)(2,1)S(1)} %get-tuple-element.93.refs_0_), channel_id=1, source_target_pairs={{0,2},{1,5},{2,0},{3,7},{4,6},{5,1},{6,4},{7,3},{8,10},{9,13},{10,... | collective-permute-start | bytes 294920 | tf_op jit(solution)/shard_map/ppermute | solution.py:435
  36.6 5.0 %collective-permute-start.23 = (bf16[192,256]{1,0:T(8,128)(2,1)S(1)}, bf16[192,256]{1,0:T(8,128)(2,1)S(1)}, u32[]{:S(2)}, u32[]{:S(2)}) collective-permute-start(bf16[192,256]{1,0:T(8,128)(2,1)S(1)} %get-tuple-element.93.refs_0_), channel_id=1, source_target_pairs={{0,1},{1,0},{2,3},{3,2},{4,5},{5,4},{6,7},{7,6},{8,9},{9,8},{10,11... | collective-permute-start | bytes 294920 | tf_op jit(solution)/shard_map/ppermute | solution.py:435
  39.5 3.2 %collective-permute-start.18 = (bf16[192,256]{1,0:T(8,128)(2,1)S(1)}, bf16[192,256]{1,0:T(8,128)(2,1)S(1)}, u32[]{:S(2)}, u32[]{:S(2)}) collective-permute-start(bf16[192,256]{1,0:T(8,128)(2,1)S(1)} %collective-permute-done.17.refs_1_), channel_id=1, source_target_pairs={{0,1},{1,0},{2,3},{3,2},{4,5},{5,4},{6,7},{7,6},{8,9},{9,8},{10,11... | collective-permute-start | bytes 294920 | tf_op jit(solution)/shard_map/ppermute | solution.py:435
  41.1 1.6 %collective-permute-start.20 = (bf16[192,256]{1,0:T(8,128)(2,1)S(1)}, bf16[192,256]{1,0:T(8,128)(2,1)S(1)}, u32[]{:S(2)}, u32[]{:S(2)}) collective-permute-start(bf16[192,256]{1,0:T(8,128)(2,1)S(1)} %collective-permute-done.19.refs_2_), channel_id=1, source_target_pairs={{0,1},{1,0},{2,3},{3,2},{4,5},{5,4},{6,7},{7,6},{8,9},{9,8},{10,11... | collective-permute-start | bytes 294920 | tf_op jit(solution)/shard_map/ppermute | solution.py:435
  43.6 7.7 %collective-permute-start.24 = (bf16[48,1024]{1,0:T(8,128)(2,1)S(1)}, bf16[48,1024]{1,0:T(8,128)(2,1)S(1)}, u32[]{:S(2)}, u32[]{:S(2)}) collective-permute-start(bf16[48,1024]{1,0:T(8,128)(2,1)S(1)} %get-tuple-element.95), channel_id=1, source_target_pairs={{0,8},{8,16},{16,24},{24,0},{1,9},{9,17},{17,25},{25,1},{2,10},{10... | collective-permute-start | bytes 294920 | tf_op jit(solution)/shard_map/ppermute | solution.py:535
  45.6 9.5 %collective-permute-start.25 = (bf16[48,1024]{1,0:T(8,128)(2,1)S(1)}, bf16[48,1024]{1,0:T(8,128)(2,1)S(1)}, u32[]{:S(2)}, u32[]{:S(2)}) collective-permute-start(bf16[48,1024]{1,0:T(8,128)(2,1)S(1)} %get-tuple-element.96), channel_id=1, source_target_pairs={{0,16},{8,24},{16,0},{24,8},{1,17},{9,25},{17,1},{25,9},{2,18},{10... | collective-permute-start | bytes 294920 | tf_op jit(solution)/shard_map/ppermute | solution.py:535
  48.2 6.9 %collective-permute-start.26 = (bf16[48,1024]{1,0:T(8,128)(2,1)S(1)}, bf16[48,1024]{1,0:T(8,128)(2,1)S(1)}, u32[]{:S(2)}, u32[]{:S(2)}) collective-permute-start(bf16[48,1024]{1,0:T(8,128)(2,1)S(1)} %get-tuple-element.97), channel_id=1, source_target_pairs={{0,24},{8,0},{16,8},{24,16},{1,25},{9,1},{17,9},{25,17},{2,26},{10... | collective-permute-start | bytes 294920 | tf_op jit(solution)/shard_map/ppermute | solution.py:535
  (14 other events, 116.9 us)

commit v9 on v8

--- a/solution.py
+++ b/solution.py
@@ -226,9 +226,13 @@
     return out[0] if last and not scalars else out
 
 
-def attention_kernel(places, count, rows, last, sizes, *refs):
+def attention_kernel(places, count, rows, last, sizes, project, *refs):
     token_ref, slot_ref, refs = refs[0], refs[1], refs[2:]
     queries_refs, refs = refs[:sizes], refs[sizes:]
+    if last:
+        held = 1 + (rows % 16 != 0)
+        query_kernel(*project, 0, 0, *queries_refs, *refs[-held:])
+        queries_refs, refs = refs[len(refs) - held : len(refs) - held + 1], refs[:-held]
     grad_ref, k_gain_ref, refs = refs[0], refs[1], refs[2:]
     narrow = rows % 16 != 0
     if narrow:
@@ -308,7 +312,7 @@
         block_ref[:, HEAD_DIM:] = d_values_ref[...].astype(BF16)
 
 
-def attention(live, queries, places, count, grad_out, k_gain, state, last):
+def attention(live, queries, places, count, grad_out, k_gain, state, last, project=()):
     rows, width = grad_out.shape[1] // count, grad_out.shape[2]
     image_rows = MB * SLOTS
     vector = jax.ShapeDtypeStruct((image_rows, HEAD_DIM), F32)
@@ -322,9 +326,13 @@
         out_shape = [attended, vector, vector, rounded, rounded, vector, vector]
     if rows % 16 != 0:
         scratch += [pltpu.VMEM(grad_out.shape[1:], F32)]
+    if last:
+        scratch.append(pltpu.VMEM(attended.shape, BF16))
+        if rows % 16 != 0:
+            scratch.append(pltpu.VMEM(attended.shape, F32))
     operands = [*queries, grad_out, k_gain, *state]
     return pl.pallas_call(
-        functools.partial(attention_kernel, places, count, rows, last, len(queries)),
+        functools.partial(attention_kernel, places, count, rows, last, len(queries), project),
         in_specs=[whole()] * (2 + len(operands)),
         out_specs=[whole()] * len(out_shape),
         out_shape=out_shape,
@@ -514,9 +522,14 @@
     pieces = {pair: (x[:, :split], x[:, split:]) for pair, x in second_half.items()}
     far, rest = [both_cores({pair: x[i] for pair, x in pieces.items()}) for i in range(2)]
     sums = queries(far, "queries_forwarded_second", start=cuts[1], before=sums)
-    q_far = queries(rest, "queries_forwarded_last", start=cuts[2], before=sums)
-    far = places_of(far)
-    late, block = attention(live, [q_far], [far], count, grad_out, k_gain, state, last=True)
+    far = places_of(rest)
+    groups = list(rest.values())
+    slots = [(far.index(even), far.index(odd)) for even, odd in rest]
+    project = ([len(group) for group in groups], slots, cuts[2])
+    left = [in_gain, w_query, q_gain, *[x for group in groups for x in group], *sums]
+    late, block = attention(
+        live, left, [far], count, grad_out, k_gain, state, last=True, project=project
+    )
     attended = assemble([places_of(near) + places_of(next_to), far], [early, late], grad_out)
 
     same_core = {(0, 0): block}

time: 56 us -> 56 us (level)
    pallas_call x5 -> x4, Pallas kernels: 6.44 us -> 5.85 us  [queries_of(): pl.pallas_call(functools.partial(query_kernel, [len(parts) for parts in g...]
where the time goes in v9:
time: 56 us; the launch traced here: 55.8 us
  starting transfers between devices  22 us (39%)
  waiting for transfers between devices  16 us (29%)
  Pallas kernels  12.8 us (23%)
  local copies, waits for them, and re-layouts  3.29 us (6%)
  between operations  0.89 us (2%)
  other arithmetic  0.72 us (1%)
    ppermute x24, starting transfers between devices, exchange(): lax.ppermute(x, 'tensor', [(i, i ^ pair[i % 2]) for i in range(count)])  16 us
    ppermute x24, waiting for transfers between devices, exchange(): lax.ppermute(x, 'tensor', [(i, i ^ pair[i % 2]) for i in range(count)])  11.2 us
    ppermute x3, starting transfers between devices, shards(): arrived.append(lax.ppermute(leaving[k - 1], 'section', perm))  5.97 us
    pallas_call x4, Pallas kernels, queries_of(): pl.pallas_call(functools.partial(query_kernel, [len(parts) for parts in g...  5.85 us
    ppermute x3, waiting for transfers between devices, shards(): arrived.append(lax.ppermute(leaving[k - 1], 'section', perm))  4.76 us
    unnamed x22, local copies, waits for them, and re-layouts  3.22 us
    pallas_call x2, Pallas kernels, attention(): pl.pallas_call(functools.partial(attention_kernel, places, count, rows, l...  2.67 us
    pallas_call x2, Pallas kernels, feature_gradient(): pl.pallas_call(functools.partial(grad_kernel, pairs, per_kv, sections, be...  1.89 us
  transfers between devices with their start and end apart: 27, of which 12 were waited for; matrix products, arithmetic and copies ran while one was open for 0% of the time, Pallas kernels for 19%

profile of v9, /device:TPU:0, one launch (start us, length us, event | category | flops | bytes accessed | tf_op | source)
XLA Modules:
  0.0 55.8 jit_solution(15058248774090003150)
XLA Ops:
  0.6 3.0 %collective-permute-start.1 = (bf16[32,8192]{1,0:T(8,128)(2,1)}, bf16[32,8192]{1,0:T(8,128)(2,1)S(1)}, u32[]{:S(2)}, u32[]{:S(2)}) collective-permute-start(bf16[32,8192]{1,0:T(8,128)(2,1)} %bitcast.1), channel_id=1, source_target_pairs={{0,2},{1,5},{2,0},{3,7},{4,6},{5,1},{6,4},{7,3},{8,10},{9,13},{10,... | collective-permute-start | bytes 1572872 | tf_op jit(solution)/shard_map/ppermute | solution.py:443
  3.6 1.5 %collective-permute-start.2 = (bf16[32,8192]{1,0:T(8,128)(2,1)}, bf16[32,8192]{1,0:T(8,128)(2,1)S(1)}, u32[]{:S(2)}, u32[]{:S(2)}) collective-permute-start(bf16[32,8192]{1,0:T(8,128)(2,1)} %bitcast.2), channel_id=1, source_target_pairs={{0,4},{1,3},{2,6},{3,1},{4,0},{5,7},{6,2},{7,5},{8,12},{9,11},{10,... | collective-permute-start | bytes 1572872 | tf_op jit(solution)/shard_map/ppermute | solution.py:443
  5.2 2.2 %copy-done.1 = bf16[1,1024,2048]{2,1,0:T(8,128)(2,1)S(1)} copy-done((bf16[1,1024,2048]{2,1,0:T(8,128)(2,1)S(1)}, bf16[1,1024,2048]{2,1,0:T(8,128)(2,1)}, u32[]{:S(2)}) %copy-start.1) | copy-done | bytes 4194328
  7.4 1.0 %copy-done.3 = bf16[192,1024]{1,0:T(8,128)(2,1)S(1)} copy-done((bf16[192,1024]{1,0:T(8,128)(2,1)S(1)}, bf16[192,1024]{1,0:T(8,128)(2,1)}, u32[]{:S(2)}) %copy-start.3) | copy-done | bytes 393240
  13.8 1.3 %collective-permute-start.8 = (bf16[192,256]{1,0:T(8,128)(2,1)S(1)}, bf16[192,256]{1,0:T(8,128)(2,1)S(1)}, u32[]{:S(2)}, u32[]{:S(2)}) collective-permute-start(bf16[192,256]{1,0:T(8,128)(2,1)S(1)} %get-tuple-element.57), channel_id=1, source_target_pairs={{0,2},{1,5},{2,0},{3,7},{4,6},{5,1},{6,4},{7,3},{8,10},{9,13},{10,... | collective-permute-start | bytes 294920 | tf_op jit(solution)/shard_map/ppermute | solution.py:443
  15.1 2.6 %collective-permute-done.7.refs_2_ = bf16[192,256]{1,0:T(8,128)(2,1)S(1)} collective-permute-done((bf16[192,256]{1,0:T(8,128)(2,1)S(1)}, bf16[192,256]{1,0:T(8,128)(2,1)S(1)}, u32[]{:S(2)}, u32[]{:S(2)}) %collective-permute-start.7) | collective-permute-done | bytes 98336 | tf_op jit(solution)/shard_map/ppermute | solution.py:443
  17.7 1.1 %collective-permute-done.8.refs_3_ = bf16[192,256]{1,0:T(8,128)(2,1)S(1)} collective-permute-done((bf16[192,256]{1,0:T(8,128)(2,1)S(1)}, bf16[192,256]{1,0:T(8,128)(2,1)S(1)}, u32[]{:S(2)}, u32[]{:S(2)}) %collective-permute-start.8) | collective-permute-done | bytes 98336 | tf_op jit(solution)/shard_map/ppermute | solution.py:443
  19.3 1.1 %collective-permute-start.9 = (bf16[32,3584]{1,0:T(8,128)(2,1)S(1)}, bf16[32,3584]{1,0:T(8,128)(2,1)S(1)}, u32[]{:S(2)}, u32[]{:S(2)}) collective-permute-start(bf16[32,3584]{1,0:T(8,128)(2,1)S(1)} %slice.12), channel_id=1, source_target_pairs={{0,4},{1,3},{2,6},{3,1},{4,0},{5,7},{6,2},{7,5},{8,12},{9,11},{10,... | collective-permute-start | bytes 688136 | tf_op jit(solution)/shard_map/ppermute | solution.py:443
  20.4 1.1 %collective-permute-start.10 = (bf16[192,256]{1,0:T(8,128)(2,1)S(1)}, bf16[192,256]{1,0:T(8,128)(2,1)S(1)}, u32[]{:S(2)}, u32[]{:S(2)}) collective-permute-start(bf16[192,256]{1,0:T(8,128)(2,1)S(1)} %get-tuple-element.64), channel_id=1, source_target_pairs={{0,4},{1,3},{2,6},{3,1},{4,0},{5,7},{6,2},{7,5},{8,12},{9,11},{10,... | collective-permute-start | bytes 294920 | tf_op jit(solution)/shard_map/ppermute | solution.py:443
  21.5 1.1 %collective-permute-start.13 = (bf16[32,4608]{1,0:T(8,128)(2,1)S(1)}, bf16[32,4608]{1,0:T(8,128)(2,1)S(1)}, u32[]{:S(2)}, u32[]{:S(2)}) collective-permute-start(bf16[32,4608]{1,0:T(8,128)(2,1)S(1)} %slice.13), channel_id=1, source_target_pairs={{0,4},{1,3},{2,6},{3,1},{4,0},{5,7},{6,2},{7,5},{8,12},{9,11},{10,... | collective-permute-start | bytes 884744 | tf_op jit(solution)/shard_map/ppermute | solution.py:443
  22.6 2.5 %queries_own_chip.1 = (bf16[64,512]{1,0:T(8,128)(2,1)S(1)}, f32[256,128]{1,0:T(8,128)S(1)}, f32[2,8,96]{2,1,0:T(8,128)S(1)}) custom-call(s32[2]{0:T(128)S(1)} %copy-done.9, s32[2]{0:T(128)S(1)} %copy-done.10, bf16[1,8192]{1,0:T(2,128)(2,1)S(1)} %copy-done.5, bf16[1,8192,512]{2,1,0:T(8,128)(2,1)S(1)} %copy-done, bf16[1,128]{1,0:T(2,128)(2,1)S(1)} %copy-done.7, ...), custom_call_target="tpu_custom_call" | custom-call | tf_op jit(solution)/shard_map/queries_own_chip/pallas_call | solution.py:208
  25.1 2.0 %queries_neighbours.1.refs_3_ = bf16[128,512]{1,0:T(8,128)(2,1)S(1)} custom-call(bf16[1,8192]{1,0:T(2,128)(2,1)S(1)} %copy-done.5, bf16[1,8192,512]{2,1,0:T(8,128)(2,1)S(1)} %copy-done, bf16[1,128]{1,0:T(2,128)(2,1)S(1)} %copy-done.7, bf16[32,8192]{1,0:T(8,128)(2,1)S(1)} %collective-permute-done.1.refs_3_, ...), custom_call_target="tpu_custom_call" | custom-call | tf_op jit(solution)/shard_map/queries_neighbours/pallas_call | solution.py:208
  27.5 1.3 %attention_first.1 = (f32[192,512]{1,0:T(8,128)S(1)}, f32[192,128]{1,0:T(8,128)S(1)}, f32[192,128]{1,0:T(8,128)S(1)}, bf16[192,128]{1,0:T(8,128)(2,1)S(1)}, bf16...) custom-call(f32[256,128]{1,0:T(8,128)S(1)} %get-tuple-element.50.refs_0_, ...), custom_call_target="tpu_custom_call" | custom-call | tf_op jit(solution)/shard_map/attention_first/pallas_call | solution.py:334
  31.7 1.4 %attention_last.1 = (f32[64,512]{1,0:T(8,128)S(1)}, bf16[192,256]{1,0:T(8,128)(2,1)S(1)}) custom-call(f32[256,128]{1,0:T(8,128)S(1)} %get-tuple-element.50.refs_0_, f32[2,8,96]{2,1,0:T(8,128)S(1)} %get-tuple-element.51.refs_1_, bf16[1,8192]{1,0:T(2,128)(2,1)S(1)} %copy-done.5, bf16[1,8192,512]{2,1,0:T(8,128)(2,1)S(1)} %copy-done, ...), custom_call_target="tpu_custom_call" | custom-call | tf_op jit(solution)/shard_map/attention_last/pallas_call | solution.py:334
  33.0 2.5 %collective-permute-start.17 = (bf16[192,256]{1,0:T(8,128)(2,1)S(1)}, bf16[192,256]{1,0:T(8,128)(2,1)S(1)}, u32[]{:S(2)}, u32[]{:S(2)}) collective-permute-start(bf16[192,256]{1,0:T(8,128)(2,1)S(1)} %get-tuple-element.93.refs_0_), channel_id=1, source_target_pairs={{0,6},{1,7},{2,4},{3,5},{4,2},{5,3},{6,0},{7,1},{8,14},{9,15},{10,... | collective-permute-start | bytes 294920 | tf_op jit(solution)/shard_map/ppermute | solution.py:443
  35.5 1.1 %collective-permute-start.19 = (bf16[192,256]{1,0:T(8,128)(2,1)S(1)}, bf16[192,256]{1,0:T(8,128)(2,1)S(1)}, u32[]{:S(2)}, u32[]{:S(2)}) collective-permute-start(bf16[192,256]{1,0:T(8,128)(2,1)S(1)} %get-tuple-element.93.refs_0_), channel_id=1, source_target_pairs={{0,4},{1,3},{2,6},{3,1},{4,0},{5,7},{6,2},{7,5},{8,12},{9,11},{10,... | collective-permute-start | bytes 294920 | tf_op jit(solution)/shard_map/ppermute | solution.py:443
  36.6 2.9 %collective-permute-done.17.refs_1_ = bf16[192,256]{1,0:T(8,128)(2,1)S(1)} collective-permute-done((bf16[192,256]{1,0:T(8,128)(2,1)S(1)}, bf16[192,256]{1,0:T(8,128)(2,1)S(1)}, u32[]{:S(2)}, u32[]{:S(2)}) %collective-permute-start.17) | collective-permute-done | bytes 98336 | tf_op jit(solution)/shard_map/ppermute | solution.py:443
  39.5 1.6 %collective-permute-done.19.refs_2_ = bf16[192,256]{1,0:T(8,128)(2,1)S(1)} collective-permute-done((bf16[192,256]{1,0:T(8,128)(2,1)S(1)}, bf16[192,256]{1,0:T(8,128)(2,1)S(1)}, u32[]{:S(2)}, u32[]{:S(2)}) %collective-permute-start.19) | collective-permute-done | bytes 98336 | tf_op jit(solution)/shard_map/ppermute | solution.py:443
  41.6 1.1 %feature_grad_first.1.refs_4_ = f32[192,1024]{1,0:T(8,128)S(1)} custom-call(bf16[192,256]{1,0:T(8,128)(2,1)S(1)} %get-tuple-element.93.refs_0_, bf16[192,256]{1,0:T(8,128)(2,1)S(1)} %collective-permute-done.17.refs_1_, bf16[192,256]{1,0:T(8,128)(2,1)S(1)} %collective-permute-done.19.refs_2_, bf16[192,256]{1,0:T(8,128)(2,1)S(1)} %collective-permute-done.21.refs_3_, ...), custom_call_target="tpu_custom_call" | custom-call | tf_op jit(solution)/shard_map/feature_grad_first/pallas_call | solution.py:423
  43.5 2.0 %collective-permute-start.24 = (bf16[48,1024]{1,0:T(8,128)(2,1)S(1)}, bf16[48,1024]{1,0:T(8,128)(2,1)S(1)}, u32[]{:S(2)}, u32[]{:S(2)}) collective-permute-start(bf16[48,1024]{1,0:T(8,128)(2,1)S(1)} %get-tuple-element.95), channel_id=1, source_target_pairs={{0,8},{8,16},{16,24},{24,0},{1,9},{9,17},{17,25},{25,1},{2,10},{10... | collective-permute-start | bytes 294920 | tf_op jit(solution)/shard_map/ppermute | solution.py:548
  45.6 2.6 %collective-permute-start.25 = (bf16[48,1024]{1,0:T(8,128)(2,1)S(1)}, bf16[48,1024]{1,0:T(8,128)(2,1)S(1)}, u32[]{:S(2)}, u32[]{:S(2)}) collective-permute-start(bf16[48,1024]{1,0:T(8,128)(2,1)S(1)} %get-tuple-element.96), channel_id=1, source_target_pairs={{0,16},{8,24},{16,0},{24,8},{1,17},{9,25},{17,1},{25,9},{2,18},{10... | collective-permute-start | bytes 294920 | tf_op jit(solution)/shard_map/ppermute | solution.py:548
  48.2 1.3 %collective-permute-start.26 = (bf16[48,1024]{1,0:T(8,128)(2,1)S(1)}, bf16[48,1024]{1,0:T(8,128)(2,1)S(1)}, u32[]{:S(2)}, u32[]{:S(2)}) collective-permute-start(bf16[48,1024]{1,0:T(8,128)(2,1)S(1)} %get-tuple-element.97), channel_id=1, source_target_pairs={{0,24},{8,0},{16,8},{24,16},{1,25},{9,1},{17,9},{25,17},{2,26},{10... | collective-permute-start | bytes 294920 | tf_op jit(solution)/shard_map/ppermute | solution.py:548
  50.3 1.0 %collective-permute-done.24 = bf16[48,1024]{1,0:T(8,128)(2,1)S(1)} collective-permute-done((bf16[48,1024]{1,0:T(8,128)(2,1)S(1)}, bf16[48,1024]{1,0:T(8,128)(2,1)S(1)}, u32[]{:S(2)}, u32[]{:S(2)}) %collective-permute-start.24) | collective-permute-done | bytes 98336 | tf_op jit(solution)/shard_map/ppermute | solution.py:548
  51.3 3.8 %collective-permute-done.25 = bf16[48,1024]{1,0:T(8,128)(2,1)S(1)} collective-permute-done((bf16[48,1024]{1,0:T(8,128)(2,1)S(1)}, bf16[48,1024]{1,0:T(8,128)(2,1)S(1)}, u32[]{:S(2)}, u32[]{:S(2)}) %collective-permute-start.25) | collective-permute-done | bytes 98336 | tf_op jit(solution)/shard_map/ppermute | solution.py:548
  (69 shorter events, 12.1 us)
Async XLA Ops:
  0.6 18.1 %collective-permute-start.1 = (bf16[32,8192]{1,0:T(8,128)(2,1)}, bf16[32,8192]{1,0:T(8,128)(2,1)S(1)}, u32[]{:S(2)}, u32[]{:S(2)}) collective-permute-start(bf16[32,8192]{1,0:T(8,128)(2,1)} %bitcast.1), channel_id=1, source_target_pairs={{0,2},{1,5},{2,0},{3,7},{4,6},{5,1},{6,4},{7,3},{8,10},{9,13},{10,... | collective-permute-start | bytes 1572872 | tf_op jit(solution)/shard_map/ppermute | solution.py:443
  3.6 15.1 %collective-permute-start.2 = (bf16[32,8192]{1,0:T(8,128)(2,1)}, bf16[32,8192]{1,0:T(8,128)(2,1)S(1)}, u32[]{:S(2)}, u32[]{:S(2)}) collective-permute-start(bf16[32,8192]{1,0:T(8,128)(2,1)} %bitcast.2), channel_id=1, source_target_pairs={{0,4},{1,3},{2,6},{3,1},{4,0},{5,7},{6,2},{7,5},{8,12},{9,11},{10,... | collective-permute-start | bytes 1572872 | tf_op jit(solution)/shard_map/ppermute | solution.py:443
  9.2 1.5 %collective-permute-start.3 = (f32[192,256]{1,0:T(8,128)S(1)}, f32[192,256]{1,0:T(8,128)S(1)}, u32[]{:S(2)}, u32[]{:S(2)}) collective-permute-start(f32[192,256]{1,0:T(8,128)S(1)} %get-tuple-element.52), channel_id=1, source_target_pairs={{0,1},{1,0},{2,3},{3,2},{4,5},{5,4},{6,7},{7,6},{8,9},{9,8},{10,11... | collective-permute-start | bytes 589832 | tf_op jit(solution)/shard_map/ppermute | solution.py:443
  9.3 1.7 %collective-permute-start.4 = (f32[192,256]{1,0:T(8,128)S(1)}, f32[192,256]{1,0:T(8,128)S(1)}, u32[]{:S(2)}, u32[]{:S(2)}) collective-permute-start(f32[192,256]{1,0:T(8,128)S(1)} %get-tuple-element.53), channel_id=1, source_target_pairs={{0,1},{1,0},{2,3},{3,2},{4,5},{5,4},{6,7},{7,6},{8,9},{9,8},{10,11... | collective-permute-start | bytes 589832 | tf_op jit(solution)/shard_map/ppermute | solution.py:443
  9.8 1.5 %collective-permute-start.5 = (f32[192,256]{1,0:T(8,128)S(1)}, f32[192,256]{1,0:T(8,128)S(1)}, u32[]{:S(2)}, u32[]{:S(2)}) collective-permute-start(f32[192,256]{1,0:T(8,128)S(1)} %get-tuple-element.54), channel_id=1, source_target_pairs={{0,1},{1,0},{2,3},{3,2},{4,5},{5,4},{6,7},{7,6},{8,9},{9,8},{10,11... | collective-permute-start | bytes 589832 | tf_op jit(solution)/shard_map/ppermute | solution.py:443
  13.0 4.7 %collective-permute-start.7 = (bf16[192,256]{1,0:T(8,128)(2,1)S(1)}, bf16[192,256]{1,0:T(8,128)(2,1)S(1)}, u32[]{:S(2)}, u32[]{:S(2)}) collective-permute-start(bf16[192,256]{1,0:T(8,128)(2,1)S(1)} %get-tuple-element.56), channel_id=1, source_target_pairs={{0,2},{1,5},{2,0},{3,7},{4,6},{5,1},{6,4},{7,3},{8,10},{9,13},{10,... | collective-permute-start | bytes 294920 | tf_op jit(solution)/shard_map/ppermute | solution.py:443
  13.8 4.9 %collective-permute-start.8 = (bf16[192,256]{1,0:T(8,128)(2,1)S(1)}, bf16[192,256]{1,0:T(8,128)(2,1)S(1)}, u32[]{:S(2)}, u32[]{:S(2)}) collective-permute-start(bf16[192,256]{1,0:T(8,128)(2,1)S(1)} %get-tuple-element.57), channel_id=1, source_target_pairs={{0,2},{1,5},{2,0},{3,7},{4,6},{5,1},{6,4},{7,3},{8,10},{9,13},{10,... | collective-permute-start | bytes 294920 | tf_op jit(solution)/shard_map/ppermute | solution.py:443
  15.1 6.5 %collective-permute-start = (bf16[32,8192]{1,0:T(8,128)(2,1)S(1)}, bf16[32,8192]{1,0:T(8,128)(2,1)S(1)}, u32[]{:S(2)}, u32[]{:S(2)}) collective-permute-start(bf16[32,8192]{1,0:T(8,128)(2,1)S(1)} %bitcast.3), channel_id=1, source_target_pairs={{0,1},{1,0},{2,3},{3,2},{4,5},{5,4},{6,7},{7,6},{8,9},{9,8},{10,11... | collective-permute-start | bytes 1572872 | tf_op jit(solution)/shard_map/ppermute | solution.py:443
  18.7 6.4 %collective-permute-start.11 = (bf16[32,8192]{1,0:T(8,128)(2,1)S(1)}, bf16[32,8192]{1,0:T(8,128)(2,1)S(1)}, u32[]{:S(2)}, u32[]{:S(2)}) collective-permute-start(bf16[32,8192]{1,0:T(8,128)(2,1)S(1)} %collective-permute-done.1.refs_3_), channel_id=1, source_target_pairs={{0,1},{1,0},{2,3},{3,2},{4,5},{5,4},{6,7},{7,6},{8,9},{9,8},{10,11... | collective-permute-start | bytes 1572872 | tf_op jit(solution)/shard_map/ppermute | solution.py:443
  18.8 6.4 %collective-permute-start.12 = (bf16[32,8192]{1,0:T(8,128)(2,1)S(1)}, bf16[32,8192]{1,0:T(8,128)(2,1)S(1)}, u32[]{:S(2)}, u32[]{:S(2)}) collective-permute-start(bf16[32,8192]{1,0:T(8,128)(2,1)S(1)} %collective-permute-done.2.refs_5_), channel_id=1, source_target_pairs={{0,1},{1,0},{2,3},{3,2},{4,5},{5,4},{6,7},{7,6},{8,9},{9,8},{10,11... | collective-permute-start | bytes 1572872 | tf_op jit(solution)/shard_map/ppermute | solution.py:443
  19.3 7.9 %collective-permute-start.9 = (bf16[32,3584]{1,0:T(8,128)(2,1)S(1)}, bf16[32,3584]{1,0:T(8,128)(2,1)S(1)}, u32[]{:S(2)}, u32[]{:S(2)}) collective-permute-start(bf16[32,3584]{1,0:T(8,128)(2,1)S(1)} %slice.12), channel_id=1, source_target_pairs={{0,4},{1,3},{2,6},{3,1},{4,0},{5,7},{6,2},{7,5},{8,12},{9,11},{10,... | collective-permute-start | bytes 688136 | tf_op jit(solution)/shard_map/ppermute | solution.py:443
  20.4 6.8 %collective-permute-start.10 = (bf16[192,256]{1,0:T(8,128)(2,1)S(1)}, bf16[192,256]{1,0:T(8,128)(2,1)S(1)}, u32[]{:S(2)}, u32[]{:S(2)}) collective-permute-start(bf16[192,256]{1,0:T(8,128)(2,1)S(1)} %get-tuple-element.64), channel_id=1, source_target_pairs={{0,4},{1,3},{2,6},{3,1},{4,0},{5,7},{6,2},{7,5},{8,12},{9,11},{10,... | collective-permute-start | bytes 294920 | tf_op jit(solution)/shard_map/ppermute | solution.py:443
  21.5 8.1 %collective-permute-start.13 = (bf16[32,4608]{1,0:T(8,128)(2,1)S(1)}, bf16[32,4608]{1,0:T(8,128)(2,1)S(1)}, u32[]{:S(2)}, u32[]{:S(2)}) collective-permute-start(bf16[32,4608]{1,0:T(8,128)(2,1)S(1)} %slice.13), channel_id=1, source_target_pairs={{0,4},{1,3},{2,6},{3,1},{4,0},{5,7},{6,2},{7,5},{8,12},{9,11},{10,... | collective-permute-start | bytes 884744 | tf_op jit(solution)/shard_map/ppermute | solution.py:443
  27.2 1.6 %collective-permute-start.14 = (bf16[32,3584]{1,0:T(8,128)(2,1)S(1)}, bf16[32,3584]{1,0:T(8,128)(2,1)S(1)}, u32[]{:S(2)}, u32[]{:S(2)}) collective-permute-start(bf16[32,3584]{1,0:T(8,128)(2,1)S(1)} %collective-permute-done.9.refs_3_), channel_id=1, source_target_pairs={{0,1},{1,0},{2,3},{3,2},{4,5},{5,4},{6,7},{7,6},{8,9},{9,8},{10,11... | collective-permute-start | bytes 688136 | tf_op jit(solution)/shard_map/ppermute | solution.py:443
  30.0 1.7 %collective-permute-start.15 = (bf16[32,2048]{1,0:T(8,128)(2,1)S(1)}, bf16[32,2048]{1,0:T(8,128)(2,1)S(1)}, u32[]{:S(2)}, u32[]{:S(2)}) collective-permute-start(bf16[32,2048]{1,0:T(8,128)(2,1)S(1)} %slice.14.refs_5_), channel_id=1, source_target_pairs={{0,1},{1,0},{2,3},{3,2},{4,5},{5,4},{6,7},{7,6},{8,9},{9,8},{10,11... | collective-permute-start | bytes 393224 | tf_op jit(solution)/shard_map/ppermute | solution.py:443
  33.0 6.4 %collective-permute-start.17 = (bf16[192,256]{1,0:T(8,128)(2,1)S(1)}, bf16[192,256]{1,0:T(8,128)(2,1)S(1)}, u32[]{:S(2)}, u32[]{:S(2)}) collective-permute-start(bf16[192,256]{1,0:T(8,128)(2,1)S(1)} %get-tuple-element.93.refs_0_), channel_id=1, source_target_pairs={{0,6},{1,7},{2,4},{3,5},{4,2},{5,3},{6,0},{7,1},{8,14},{9,15},{10,... | collective-permute-start | bytes 294920 | tf_op jit(solution)/shard_map/ppermute | solution.py:443
  35.5 5.6 %collective-permute-start.19 = (bf16[192,256]{1,0:T(8,128)(2,1)S(1)}, bf16[192,256]{1,0:T(8,128)(2,1)S(1)}, u32[]{:S(2)}, u32[]{:S(2)}) collective-permute-start(bf16[192,256]{1,0:T(8,128)(2,1)S(1)} %get-tuple-element.93.refs_0_), channel_id=1, source_target_pairs={{0,4},{1,3},{2,6},{3,1},{4,0},{5,7},{6,2},{7,5},{8,12},{9,11},{10,... | collective-permute-start | bytes 294920 | tf_op jit(solution)/shard_map/ppermute | solution.py:443
  36.6 4.6 %collective-permute-start.21 = (bf16[192,256]{1,0:T(8,128)(2,1)S(1)}, bf16[192,256]{1,0:T(8,128)(2,1)S(1)}, u32[]{:S(2)}, u32[]{:S(2)}) collective-permute-start(bf16[192,256]{1,0:T(8,128)(2,1)S(1)} %get-tuple-element.93.refs_0_), channel_id=1, source_target_pairs={{0,2},{1,5},{2,0},{3,7},{4,6},{5,1},{6,4},{7,3},{8,10},{9,13},{10,... | collective-permute-start | bytes 294920 | tf_op jit(solution)/shard_map/ppermute | solution.py:443
  36.6 5.0 %collective-permute-start.23 = (bf16[192,256]{1,0:T(8,128)(2,1)S(1)}, bf16[192,256]{1,0:T(8,128)(2,1)S(1)}, u32[]{:S(2)}, u32[]{:S(2)}) collective-permute-start(bf16[192,256]{1,0:T(8,128)(2,1)S(1)} %get-tuple-element.93.refs_0_), channel_id=1, source_target_pairs={{0,1},{1,0},{2,3},{3,2},{4,5},{5,4},{6,7},{7,6},{8,9},{9,8},{10,11... | collective-permute-start | bytes 294920 | tf_op jit(solution)/shard_map/ppermute | solution.py:443
  39.5 3.2 %collective-permute-start.18 = (bf16[192,256]{1,0:T(8,128)(2,1)S(1)}, bf16[192,256]{1,0:T(8,128)(2,1)S(1)}, u32[]{:S(2)}, u32[]{:S(2)}) collective-permute-start(bf16[192,256]{1,0:T(8,128)(2,1)S(1)} %collective-permute-done.17.refs_1_), channel_id=1, source_target_pairs={{0,1},{1,0},{2,3},{3,2},{4,5},{5,4},{6,7},{7,6},{8,9},{9,8},{10,11... | collective-permute-start | bytes 294920 | tf_op jit(solution)/shard_map/ppermute | solution.py:443
  41.1 1.6 %collective-permute-start.20 = (bf16[192,256]{1,0:T(8,128)(2,1)S(1)}, bf16[192,256]{1,0:T(8,128)(2,1)S(1)}, u32[]{:S(2)}, u32[]{:S(2)}) collective-permute-start(bf16[192,256]{1,0:T(8,128)(2,1)S(1)} %collective-permute-done.19.refs_2_), channel_id=1, source_target_pairs={{0,1},{1,0},{2,3},{3,2},{4,5},{5,4},{6,7},{7,6},{8,9},{9,8},{10,11... | collective-permute-start | bytes 294920 | tf_op jit(solution)/shard_map/ppermute | solution.py:443
  43.5 7.7 %collective-permute-start.24 = (bf16[48,1024]{1,0:T(8,128)(2,1)S(1)}, bf16[48,1024]{1,0:T(8,128)(2,1)S(1)}, u32[]{:S(2)}, u32[]{:S(2)}) collective-permute-start(bf16[48,1024]{1,0:T(8,128)(2,1)S(1)} %get-tuple-element.95), channel_id=1, source_target_pairs={{0,8},{8,16},{16,24},{24,0},{1,9},{9,17},{17,25},{25,1},{2,10},{10... | collective-permute-start | bytes 294920 | tf_op jit(solution)/shard_map/ppermute | solution.py:548
  45.6 9.5 %collective-permute-start.25 = (bf16[48,1024]{1,0:T(8,128)(2,1)S(1)}, bf16[48,1024]{1,0:T(8,128)(2,1)S(1)}, u32[]{:S(2)}, u32[]{:S(2)}) collective-permute-start(bf16[48,1024]{1,0:T(8,128)(2,1)S(1)} %get-tuple-element.96), channel_id=1, source_target_pairs={{0,16},{8,24},{16,0},{24,8},{1,17},{9,25},{17,1},{25,9},{2,18},{10... | collective-permute-start | bytes 294920 | tf_op jit(solution)/shard_map/ppermute | solution.py:548
  48.2 6.9 %collective-permute-start.26 = (bf16[48,1024]{1,0:T(8,128)(2,1)S(1)}, bf16[48,1024]{1,0:T(8,128)(2,1)S(1)}, u32[]{:S(2)}, u32[]{:S(2)}) collective-permute-start(bf16[48,1024]{1,0:T(8,128)(2,1)S(1)} %get-tuple-element.97), channel_id=1, source_target_pairs={{0,24},{8,0},{16,8},{24,16},{1,25},{9,1},{17,9},{25,17},{2,26},{10... | collective-permute-start | bytes 294920 | tf_op jit(solution)/shard_map/ppermute | solution.py:548
  (14 other events, 116.8 us)

commit v10 on v9

--- a/solution.py
+++ b/solution.py
@@ -475,6 +475,9 @@
         groups = list(blocks.values())
         return queries_of(groups, slots, in_gain, w_query, q_gain, name, **more)
 
+    near = both_cores({(0, 0): own_text})
+    scalars = (tile_count, image_start)
+    q_near, *live = queries(near, "queries_own_chip", scalars=scalars)
     kv_pairs = [distance(mask) for mask in range(1 << steps)]
     other_heads = kv_partial(features, w_key_value, per_kv, [other_core(pair) for pair in kv_pairs])
     other_heads = [swap(x) for x in other_heads]
@@ -482,13 +485,10 @@
     for step in range(steps):
         kept, came = sums[::2], [exchange(x, distance(1 << step)) for x in sums[1::2]]
         if step == 0:
-            direct, came = lax.optimization_barrier((direct, came))
+            direct, came, q_near = lax.optimization_barrier((direct, came, q_near))
         if step < steps - 1:
             sums = kv_sum(kept, came)
     parts = [kept[0], came[0]]
-    near = both_cores({(0, 0): own_text})
-    scalars = (tile_count, image_start)
-    q_near, *live = queries(near, "queries_own_chip", scalars=scalars)
     forwarded = []
     for first, last in ((0, cuts[1]), (cuts[1], depth)):
         held = {mask: x[:, first:last] for mask, x in direct.items()}

time: 56 us -> 57.9 us (1.034)
  waiting for transfers between devices: 16 us -> 18.7 us
  starting transfers between devices: 22 us -> 21.3 us
    ppermute x3, waiting for transfers between devices: 4.76 us -> 7.52 us  [shards(): arrived.append(lax.ppermute(leaving[k - 1], 'section', perm))]
    ppermute x3, starting transfers between devices: 5.97 us -> 4.95 us  [shards(): arrived.append(lax.ppermute(leaving[k - 1], 'section', perm))]
  transfers between devices with their start and end apart: 27 -> 27, of which waited for: 12 -> 13; matrix products, arithmetic and copies ran while one was open for 0% -> 0% of each run, Pallas kernels for 19% -> 18%
where the time goes in v10:
time: 57.9 us; the launch traced here: 57.7 us
  starting transfers between devices  21.3 us (37%)
  waiting for transfers between devices  18.7 us (32%)
  Pallas kernels  12.8 us (22%)
  local copies, waits for them, and re-layouts  3.28 us (6%)
  between operations  0.88 us (2%)
  other arithmetic  0.72 us (1%)
    ppermute x24, starting transfers between devices, exchange(): lax.ppermute(x, 'tensor', [(i, i ^ pair[i % 2]) for i in range(count)])  16.3 us
    ppermute x24, waiting for transfers between devices, exchange(): lax.ppermute(x, 'tensor', [(i, i ^ pair[i % 2]) for i in range(count)])  11.1 us
    ppermute x3, waiting for transfers between devices, shards(): arrived.append(lax.ppermute(leaving[k - 1], 'section', perm))  7.52 us
    pallas_call x4, Pallas kernels, queries_of(): pl.pallas_call(functools.partial(query_kernel, [len(parts) for parts in g...  5.85 us
    ppermute x3, starting transfers between devices, shards(): arrived.append(lax.ppermute(leaving[k - 1], 'section', perm))  4.95 us
    unnamed x22, local copies, waits for them, and re-layouts  3.22 us
    pallas_call x2, Pallas kernels, attention(): pl.pallas_call(functools.partial(attention_kernel, places, count, rows, l...  2.67 us
    pallas_call x2, Pallas kernels, feature_gradient(): pl.pallas_call(functools.partial(grad_kernel, pairs, per_kv, sections, be...  1.89 us
  transfers between devices with their start and end apart: 27, of which 13 were waited for; matrix products, arithmetic and copies ran while one was open for 0% of the time, Pallas kernels for 18%

profile of v10, /device:TPU:0, one launch (start us, length us, event | category | flops | bytes accessed | tf_op | source)
XLA Modules:
  0.0 57.7 jit_solution(5062961150059399080)
XLA Ops:
  1.2 2.6 %collective-permute-start.1 = (bf16[32,8192]{1,0:T(8,128)(2,1)}, bf16[32,8192]{1,0:T(8,128)(2,1)S(1)}, u32[]{:S(2)}, u32[]{:S(2)}) collective-permute-start(bf16[32,8192]{1,0:T(8,128)(2,1)} %bitcast.2), channel_id=1, source_target_pairs={{0,2},{1,5},{2,0},{3,7},{4,6},{5,1},{6,4},{7,3},{8,10},{9,13},{10,... | collective-permute-start | bytes 1572872 | tf_op jit(solution)/shard_map/ppermute | solution.py:443
  3.7 1.5 %collective-permute-start.2 = (bf16[32,8192]{1,0:T(8,128)(2,1)}, bf16[32,8192]{1,0:T(8,128)(2,1)S(1)}, u32[]{:S(2)}, u32[]{:S(2)}) collective-permute-start(bf16[32,8192]{1,0:T(8,128)(2,1)} %bitcast.3), channel_id=1, source_target_pairs={{0,4},{1,3},{2,6},{3,1},{4,0},{5,7},{6,2},{7,5},{8,12},{9,11},{10,... | collective-permute-start | bytes 1572872 | tf_op jit(solution)/shard_map/ppermute | solution.py:443
  5.2 2.2 %copy-done.1 = bf16[1,1024,2048]{2,1,0:T(8,128)(2,1)S(1)} copy-done((bf16[1,1024,2048]{2,1,0:T(8,128)(2,1)S(1)}, bf16[1,1024,2048]{2,1,0:T(8,128)(2,1)}, u32[]{:S(2)}) %copy-start.1) | copy-done | bytes 4194328
  7.4 1.0 %copy-done.3 = bf16[192,1024]{1,0:T(8,128)(2,1)S(1)} copy-done((bf16[192,1024]{1,0:T(8,128)(2,1)S(1)}, bf16[192,1024]{1,0:T(8,128)(2,1)}, u32[]{:S(2)}) %copy-start.3) | copy-done | bytes 393240
  9.9 0.9 %collective-permute-done.3.refs_0_ = f32[192,256]{1,0:T(8,128)S(1)} collective-permute-done((f32[192,256]{1,0:T(8,128)S(1)}, f32[192,256]{1,0:T(8,128)S(1)}, u32[]{:S(2)}, u32[]{:S(2)}) %collective-permute-start.3) | collective-permute-done | bytes 196640 | tf_op jit(solution)/shard_map/ppermute | solution.py:443
  11.3 0.9 %collective-permute-done.5.refs_2_ = f32[192,256]{1,0:T(8,128)S(1)} collective-permute-done((f32[192,256]{1,0:T(8,128)S(1)}, f32[192,256]{1,0:T(8,128)S(1)}, u32[]{:S(2)}, u32[]{:S(2)}) %collective-permute-start.5) | collective-permute-done | bytes 196640 | tf_op jit(solution)/shard_map/ppermute | solution.py:443
  14.1 1.3 %collective-permute-start.8 = (bf16[192,256]{1,0:T(8,128)(2,1)S(1)}, bf16[192,256]{1,0:T(8,128)(2,1)S(1)}, u32[]{:S(2)}, u32[]{:S(2)}) collective-permute-start(bf16[192,256]{1,0:T(8,128)(2,1)S(1)} %get-tuple-element.58), channel_id=1, source_target_pairs={{0,2},{1,5},{2,0},{3,7},{4,6},{5,1},{6,4},{7,3},{8,10},{9,13},{10,... | collective-permute-start | bytes 294920 | tf_op jit(solution)/shard_map/ppermute | solution.py:443
  15.5 2.5 %queries_own_chip.1 = (bf16[64,512]{1,0:T(8,128)(2,1)S(1)}, f32[256,128]{1,0:T(8,128)S(1)}, f32[2,8,96]{2,1,0:T(8,128)S(1)}) custom-call(s32[2]{0:T(128)S(1)} %copy-done.9, s32[2]{0:T(128)S(1)} %copy-done.10, bf16[1,8192]{1,0:T(2,128)(2,1)S(1)} %copy-done.5, bf16[1,8192,512]{2,1,0:T(8,128)(2,1)S(1)} %copy-done, bf16[1,128]{1,0:T(2,128)(2,1)S(1)} %copy-done.7, ...), custom_call_target="tpu_custom_call" | custom-call | tf_op jit(solution)/shard_map/queries_own_chip/pallas_call | solution.py:208
  18.0 1.1 %collective-permute-done.8.refs_3_ = bf16[192,256]{1,0:T(8,128)(2,1)S(1)} collective-permute-done((bf16[192,256]{1,0:T(8,128)(2,1)S(1)}, bf16[192,256]{1,0:T(8,128)(2,1)S(1)}, u32[]{:S(2)}, u32[]{:S(2)}) %collective-permute-start.8) | collective-permute-done | bytes 98336 | tf_op jit(solution)/shard_map/ppermute | solution.py:443
  19.6 1.3 %collective-permute-start.9 = (bf16[32,3584]{1,0:T(8,128)(2,1)S(1)}, bf16[32,3584]{1,0:T(8,128)(2,1)S(1)}, u32[]{:S(2)}, u32[]{:S(2)}) collective-permute-start(bf16[32,3584]{1,0:T(8,128)(2,1)S(1)} %slice.12), channel_id=1, source_target_pairs={{0,4},{1,3},{2,6},{3,1},{4,0},{5,7},{6,2},{7,5},{8,12},{9,11},{10,... | collective-permute-start | bytes 688136 | tf_op jit(solution)/shard_map/ppermute | solution.py:443
  21.8 1.3 %collective-permute-start.13 = (bf16[32,4608]{1,0:T(8,128)(2,1)S(1)}, bf16[32,4608]{1,0:T(8,128)(2,1)S(1)}, u32[]{:S(2)}, u32[]{:S(2)}) collective-permute-start(bf16[32,4608]{1,0:T(8,128)(2,1)S(1)} %slice.13), channel_id=1, source_target_pairs={{0,4},{1,3},{2,6},{3,1},{4,0},{5,7},{6,2},{7,5},{8,12},{9,11},{10,... | collective-permute-start | bytes 884744 | tf_op jit(solution)/shard_map/ppermute | solution.py:443
  23.2 2.0 %queries_neighbours.1.refs_3_ = bf16[128,512]{1,0:T(8,128)(2,1)S(1)} custom-call(bf16[1,8192]{1,0:T(2,128)(2,1)S(1)} %copy-done.5, bf16[1,8192,512]{2,1,0:T(8,128)(2,1)S(1)} %copy-done, bf16[1,128]{1,0:T(2,128)(2,1)S(1)} %copy-done.7, bf16[32,8192]{1,0:T(8,128)(2,1)S(1)} %collective-permute-done.1.refs_3_, ...), custom_call_target="tpu_custom_call" | custom-call | tf_op jit(solution)/shard_map/queries_neighbours/pallas_call | solution.py:208
  25.2 1.6 %collective-permute-done.10.refs_7_ = bf16[192,256]{1,0:T(8,128)(2,1)S(1)} collective-permute-done((bf16[192,256]{1,0:T(8,128)(2,1)S(1)}, bf16[192,256]{1,0:T(8,128)(2,1)S(1)}, u32[]{:S(2)}, u32[]{:S(2)}) %collective-permute-start.10) | collective-permute-done | bytes 98336 | tf_op jit(solution)/shard_map/ppermute | solution.py:443
  26.8 1.3 %attention_first.1 = (f32[192,512]{1,0:T(8,128)S(1)}, f32[192,128]{1,0:T(8,128)S(1)}, f32[192,128]{1,0:T(8,128)S(1)}, bf16[192,128]{1,0:T(8,128)(2,1)S(1)}, bf16...) custom-call(f32[256,128]{1,0:T(8,128)S(1)} %get-tuple-element.51.refs_0_, ...), custom_call_target="tpu_custom_call" | custom-call | tf_op jit(solution)/shard_map/attention_first/pallas_call | solution.py:334
  29.0 0.9 %collective-permute-done.13 = bf16[32,4608]{1,0:T(8,128)(2,1)S(1)} collective-permute-done((bf16[32,4608]{1,0:T(8,128)(2,1)S(1)}, bf16[32,4608]{1,0:T(8,128)(2,1)S(1)}, u32[]{:S(2)}, u32[]{:S(2)}) %collective-permute-start.13) | collective-permute-done | bytes 294944 | tf_op jit(solution)/shard_map/ppermute | solution.py:443
  32.0 1.4 %attention_last.1 = (f32[64,512]{1,0:T(8,128)S(1)}, bf16[192,256]{1,0:T(8,128)(2,1)S(1)}) custom-call(f32[256,128]{1,0:T(8,128)S(1)} %get-tuple-element.51.refs_0_, f32[2,8,96]{2,1,0:T(8,128)S(1)} %get-tuple-element.52.refs_1_, bf16[1,8192]{1,0:T(2,128)(2,1)S(1)} %copy-done.5, bf16[1,8192,512]{2,1,0:T(8,128)(2,1)S(1)} %copy-done, ...), custom_call_target="tpu_custom_call" | custom-call | tf_op jit(solution)/shard_map/attention_last/pallas_call | solution.py:334
  33.4 2.5 %collective-permute-start.17 = (bf16[192,256]{1,0:T(8,128)(2,1)S(1)}, bf16[192,256]{1,0:T(8,128)(2,1)S(1)}, u32[]{:S(2)}, u32[]{:S(2)}) collective-permute-start(bf16[192,256]{1,0:T(8,128)(2,1)S(1)} %get-tuple-element.95.refs_0_), channel_id=1, source_target_pairs={{0,6},{1,7},{2,4},{3,5},{4,2},{5,3},{6,0},{7,1},{8,14},{9,15},{10,... | collective-permute-start | bytes 294920 | tf_op jit(solution)/shard_map/ppermute | solution.py:443
  36.9 2.9 %collective-permute-done.17.refs_1_ = bf16[192,256]{1,0:T(8,128)(2,1)S(1)} collective-permute-done((bf16[192,256]{1,0:T(8,128)(2,1)S(1)}, bf16[192,256]{1,0:T(8,128)(2,1)S(1)}, u32[]{:S(2)}, u32[]{:S(2)}) %collective-permute-start.17) | collective-permute-done | bytes 98336 | tf_op jit(solution)/shard_map/ppermute | solution.py:443
  39.8 1.4 %collective-permute-done.19.refs_2_ = bf16[192,256]{1,0:T(8,128)(2,1)S(1)} collective-permute-done((bf16[192,256]{1,0:T(8,128)(2,1)S(1)}, bf16[192,256]{1,0:T(8,128)(2,1)S(1)}, u32[]{:S(2)}, u32[]{:S(2)}) %collective-permute-start.19) | collective-permute-done | bytes 98336 | tf_op jit(solution)/shard_map/ppermute | solution.py:443
  41.8 1.1 %feature_grad_first.1.refs_4_ = f32[192,1024]{1,0:T(8,128)S(1)} custom-call(bf16[192,256]{1,0:T(8,128)(2,1)S(1)} %get-tuple-element.95.refs_0_, bf16[192,256]{1,0:T(8,128)(2,1)S(1)} %collective-permute-done.17.refs_1_, bf16[192,256]{1,0:T(8,128)(2,1)S(1)} %collective-permute-done.19.refs_2_, bf16[192,256]{1,0:T(8,128)(2,1)S(1)} %collective-permute-done.21.refs_3_, ...), custom_call_target="tpu_custom_call" | custom-call | tf_op jit(solution)/shard_map/feature_grad_first/pallas_call | solution.py:423
  43.7 3.9 %collective-permute-start.26 = (bf16[48,1024]{1,0:T(8,128)(2,1)S(1)}, bf16[48,1024]{1,0:T(8,128)(2,1)S(1)}, u32[]{:S(2)}, u32[]{:S(2)}) collective-permute-start(bf16[48,1024]{1,0:T(8,128)(2,1)S(1)} %get-tuple-element.99), channel_id=1, source_target_pairs={{0,24},{8,0},{16,8},{24,16},{1,25},{9,1},{17,9},{25,17},{2,26},{10... | collective-permute-start | bytes 294920 | tf_op jit(solution)/shard_map/ppermute | solution.py:548
  47.7 1.0 %collective-permute-start.24 = (bf16[48,1024]{1,0:T(8,128)(2,1)S(1)}, bf16[48,1024]{1,0:T(8,128)(2,1)S(1)}, u32[]{:S(2)}, u32[]{:S(2)}) collective-permute-start(bf16[48,1024]{1,0:T(8,128)(2,1)S(1)} %get-tuple-element.97), channel_id=1, source_target_pairs={{0,8},{8,16},{16,24},{24,0},{1,9},{9,17},{17,25},{25,1},{2,10},{10... | collective-permute-start | bytes 294920 | tf_op jit(solution)/shard_map/ppermute | solution.py:548
  49.4 1.4 %collective-permute-done.26 = bf16[48,1024]{1,0:T(8,128)(2,1)S(1)} collective-permute-done((bf16[48,1024]{1,0:T(8,128)(2,1)S(1)}, bf16[48,1024]{1,0:T(8,128)(2,1)S(1)}, u32[]{:S(2)}, u32[]{:S(2)}) %collective-permute-start.26) | collective-permute-done | bytes 98336 | tf_op jit(solution)/shard_map/ppermute | solution.py:548
  50.9 6.1 %collective-permute-done.25 = bf16[48,1024]{1,0:T(8,128)(2,1)S(1)} collective-permute-done((bf16[48,1024]{1,0:T(8,128)(2,1)S(1)}, bf16[48,1024]{1,0:T(8,128)(2,1)S(1)}, u32[]{:S(2)}, u32[]{:S(2)}) %collective-permute-start.25) | collective-permute-done | bytes 98336 | tf_op jit(solution)/shard_map/ppermute | solution.py:548
  (69 shorter events, 12.6 us)
Async XLA Ops:
  0.6 14.8 %collective-permute-start = (bf16[32,8192]{1,0:T(8,128)(2,1)}, bf16[32,8192]{1,0:T(8,128)(2,1)S(1)}, u32[]{:S(2)}, u32[]{:S(2)}) collective-permute-start(bf16[32,8192]{1,0:T(8,128)(2,1)} %bitcast.1), channel_id=1, source_target_pairs={{0,1},{1,0},{2,3},{3,2},{4,5},{5,4},{6,7},{7,6},{8,9},{9,8},{10,11... | collective-permute-start | bytes 1572872 | tf_op jit(solution)/shard_map/ppermute | solution.py:443
  1.2 17.9 %collective-permute-start.1 = (bf16[32,8192]{1,0:T(8,128)(2,1)}, bf16[32,8192]{1,0:T(8,128)(2,1)S(1)}, u32[]{:S(2)}, u32[]{:S(2)}) collective-permute-start(bf16[32,8192]{1,0:T(8,128)(2,1)} %bitcast.2), channel_id=1, source_target_pairs={{0,2},{1,5},{2,0},{3,7},{4,6},{5,1},{6,4},{7,3},{8,10},{9,13},{10,... | collective-permute-start | bytes 1572872 | tf_op jit(solution)/shard_map/ppermute | solution.py:443
  3.7 15.4 %collective-permute-start.2 = (bf16[32,8192]{1,0:T(8,128)(2,1)}, bf16[32,8192]{1,0:T(8,128)(2,1)S(1)}, u32[]{:S(2)}, u32[]{:S(2)}) collective-permute-start(bf16[32,8192]{1,0:T(8,128)(2,1)} %bitcast.3), channel_id=1, source_target_pairs={{0,4},{1,3},{2,6},{3,1},{4,0},{5,7},{6,2},{7,5},{8,12},{9,11},{10,... | collective-permute-start | bytes 1572872 | tf_op jit(solution)/shard_map/ppermute | solution.py:443
  9.3 1.5 %collective-permute-start.3 = (f32[192,256]{1,0:T(8,128)S(1)}, f32[192,256]{1,0:T(8,128)S(1)}, u32[]{:S(2)}, u32[]{:S(2)}) collective-permute-start(f32[192,256]{1,0:T(8,128)S(1)} %get-tuple-element.53), channel_id=1, source_target_pairs={{0,1},{1,0},{2,3},{3,2},{4,5},{5,4},{6,7},{7,6},{8,9},{9,8},{10,11... | collective-permute-start | bytes 589832 | tf_op jit(solution)/shard_map/ppermute | solution.py:443
  9.4 1.7 %collective-permute-start.4 = (f32[192,256]{1,0:T(8,128)S(1)}, f32[192,256]{1,0:T(8,128)S(1)}, u32[]{:S(2)}, u32[]{:S(2)}) collective-permute-start(f32[192,256]{1,0:T(8,128)S(1)} %get-tuple-element.54), channel_id=1, source_target_pairs={{0,1},{1,0},{2,3},{3,2},{4,5},{5,4},{6,7},{7,6},{8,9},{9,8},{10,11... | collective-permute-start | bytes 589832 | tf_op jit(solution)/shard_map/ppermute | solution.py:443
  13.3 4.7 %collective-permute-start.7 = (bf16[192,256]{1,0:T(8,128)(2,1)S(1)}, bf16[192,256]{1,0:T(8,128)(2,1)S(1)}, u32[]{:S(2)}, u32[]{:S(2)}) collective-permute-start(bf16[192,256]{1,0:T(8,128)(2,1)S(1)} %get-tuple-element.57), channel_id=1, source_target_pairs={{0,2},{1,5},{2,0},{3,7},{4,6},{5,1},{6,4},{7,3},{8,10},{9,13},{10,... | collective-permute-start | bytes 294920 | tf_op jit(solution)/shard_map/ppermute | solution.py:443
  14.1 5.0 %collective-permute-start.8 = (bf16[192,256]{1,0:T(8,128)(2,1)S(1)}, bf16[192,256]{1,0:T(8,128)(2,1)S(1)}, u32[]{:S(2)}, u32[]{:S(2)}) collective-permute-start(bf16[192,256]{1,0:T(8,128)(2,1)S(1)} %get-tuple-element.58), channel_id=1, source_target_pairs={{0,2},{1,5},{2,0},{3,7},{4,6},{5,1},{6,4},{7,3},{8,10},{9,13},{10,... | collective-permute-start | bytes 294920 | tf_op jit(solution)/shard_map/ppermute | solution.py:443
  19.1 4.1 %collective-permute-start.11 = (bf16[32,8192]{1,0:T(8,128)(2,1)S(1)}, bf16[32,8192]{1,0:T(8,128)(2,1)S(1)}, u32[]{:S(2)}, u32[]{:S(2)}) collective-permute-start(bf16[32,8192]{1,0:T(8,128)(2,1)S(1)} %collective-permute-done.1.refs_3_), channel_id=1, source_target_pairs={{0,1},{1,0},{2,3},{3,2},{4,5},{5,4},{6,7},{7,6},{8,9},{9,8},{10,11... | collective-permute-start | bytes 1572872 | tf_op jit(solution)/shard_map/ppermute | solution.py:443
  19.1 4.1 %collective-permute-start.12 = (bf16[32,8192]{1,0:T(8,128)(2,1)S(1)}, bf16[32,8192]{1,0:T(8,128)(2,1)S(1)}, u32[]{:S(2)}, u32[]{:S(2)}) collective-permute-start(bf16[32,8192]{1,0:T(8,128)(2,1)S(1)} %collective-permute-done.2.refs_5_), channel_id=1, source_target_pairs={{0,1},{1,0},{2,3},{3,2},{4,5},{5,4},{6,7},{7,6},{8,9},{9,8},{10,11... | collective-permute-start | bytes 1572872 | tf_op jit(solution)/shard_map/ppermute | solution.py:443
  19.6 7.1 %collective-permute-start.9 = (bf16[32,3584]{1,0:T(8,128)(2,1)S(1)}, bf16[32,3584]{1,0:T(8,128)(2,1)S(1)}, u32[]{:S(2)}, u32[]{:S(2)}) collective-permute-start(bf16[32,3584]{1,0:T(8,128)(2,1)S(1)} %slice.12), channel_id=1, source_target_pairs={{0,4},{1,3},{2,6},{3,1},{4,0},{5,7},{6,2},{7,5},{8,12},{9,11},{10,... | collective-permute-start | bytes 688136 | tf_op jit(solution)/shard_map/ppermute | solution.py:443
  21.0 5.8 %collective-permute-start.10 = (bf16[192,256]{1,0:T(8,128)(2,1)S(1)}, bf16[192,256]{1,0:T(8,128)(2,1)S(1)}, u32[]{:S(2)}, u32[]{:S(2)}) collective-permute-start(bf16[192,256]{1,0:T(8,128)(2,1)S(1)} %get-tuple-element.66), channel_id=1, source_target_pairs={{0,4},{1,3},{2,6},{3,1},{4,0},{5,7},{6,2},{7,5},{8,12},{9,11},{10,... | collective-permute-start | bytes 294920 | tf_op jit(solution)/shard_map/ppermute | solution.py:443
  21.8 8.1 %collective-permute-start.13 = (bf16[32,4608]{1,0:T(8,128)(2,1)S(1)}, bf16[32,4608]{1,0:T(8,128)(2,1)S(1)}, u32[]{:S(2)}, u32[]{:S(2)}) collective-permute-start(bf16[32,4608]{1,0:T(8,128)(2,1)S(1)} %slice.13), channel_id=1, source_target_pairs={{0,4},{1,3},{2,6},{3,1},{4,0},{5,7},{6,2},{7,5},{8,12},{9,11},{10,... | collective-permute-start | bytes 884744 | tf_op jit(solution)/shard_map/ppermute | solution.py:443
  26.8 1.5 %collective-permute-start.14 = (bf16[32,3584]{1,0:T(8,128)(2,1)S(1)}, bf16[32,3584]{1,0:T(8,128)(2,1)S(1)}, u32[]{:S(2)}, u32[]{:S(2)}) collective-permute-start(bf16[32,3584]{1,0:T(8,128)(2,1)S(1)} %collective-permute-done.9.refs_3_), channel_id=1, source_target_pairs={{0,1},{1,0},{2,3},{3,2},{4,5},{5,4},{6,7},{7,6},{8,9},{9,8},{10,11... | collective-permute-start | bytes 688136 | tf_op jit(solution)/shard_map/ppermute | solution.py:443
  30.0 1.9 %collective-permute-start.15 = (bf16[32,2048]{1,0:T(8,128)(2,1)S(1)}, bf16[32,2048]{1,0:T(8,128)(2,1)S(1)}, u32[]{:S(2)}, u32[]{:S(2)}) collective-permute-start(bf16[32,2048]{1,0:T(8,128)(2,1)S(1)} %slice.14.refs_5_), channel_id=1, source_target_pairs={{0,1},{1,0},{2,3},{3,2},{4,5},{5,4},{6,7},{7,6},{8,9},{9,8},{10,11... | collective-permute-start | bytes 393224 | tf_op jit(solution)/shard_map/ppermute | solution.py:443
  33.4 6.5 %collective-permute-start.17 = (bf16[192,256]{1,0:T(8,128)(2,1)S(1)}, bf16[192,256]{1,0:T(8,128)(2,1)S(1)}, u32[]{:S(2)}, u32[]{:S(2)}) collective-permute-start(bf16[192,256]{1,0:T(8,128)(2,1)S(1)} %get-tuple-element.95.refs_0_), channel_id=1, source_target_pairs={{0,6},{1,7},{2,4},{3,5},{4,2},{5,3},{6,0},{7,1},{8,14},{9,15},{10,... | collective-permute-start | bytes 294920 | tf_op jit(solution)/shard_map/ppermute | solution.py:443
  35.8 5.4 %collective-permute-start.19 = (bf16[192,256]{1,0:T(8,128)(2,1)S(1)}, bf16[192,256]{1,0:T(8,128)(2,1)S(1)}, u32[]{:S(2)}, u32[]{:S(2)}) collective-permute-start(bf16[192,256]{1,0:T(8,128)(2,1)S(1)} %get-tuple-element.95.refs_0_), channel_id=1, source_target_pairs={{0,4},{1,3},{2,6},{3,1},{4,0},{5,7},{6,2},{7,5},{8,12},{9,11},{10,... | collective-permute-start | bytes 294920 | tf_op jit(solution)/shard_map/ppermute | solution.py:443
  36.6 4.6 %collective-permute-start.21 = (bf16[192,256]{1,0:T(8,128)(2,1)S(1)}, bf16[192,256]{1,0:T(8,128)(2,1)S(1)}, u32[]{:S(2)}, u32[]{:S(2)}) collective-permute-start(bf16[192,256]{1,0:T(8,128)(2,1)S(1)} %get-tuple-element.95.refs_0_), channel_id=1, source_target_pairs={{0,2},{1,5},{2,0},{3,7},{4,6},{5,1},{6,4},{7,3},{8,10},{9,13},{10,... | collective-permute-start | bytes 294920 | tf_op jit(solution)/shard_map/ppermute | solution.py:443
  36.9 4.9 %collective-permute-start.23 = (bf16[192,256]{1,0:T(8,128)(2,1)S(1)}, bf16[192,256]{1,0:T(8,128)(2,1)S(1)}, u32[]{:S(2)}, u32[]{:S(2)}) collective-permute-start(bf16[192,256]{1,0:T(8,128)(2,1)S(1)} %get-tuple-element.95.refs_0_), channel_id=1, source_target_pairs={{0,1},{1,0},{2,3},{3,2},{4,5},{5,4},{6,7},{7,6},{8,9},{9,8},{10,11... | collective-permute-start | bytes 294920 | tf_op jit(solution)/shard_map/ppermute | solution.py:443
  39.8 3.0 %collective-permute-start.18 = (bf16[192,256]{1,0:T(8,128)(2,1)S(1)}, bf16[192,256]{1,0:T(8,128)(2,1)S(1)}, u32[]{:S(2)}, u32[]{:S(2)}) collective-permute-start(bf16[192,256]{1,0:T(8,128)(2,1)S(1)} %collective-permute-done.17.refs_1_), channel_id=1, source_target_pairs={{0,1},{1,0},{2,3},{3,2},{4,5},{5,4},{6,7},{7,6},{8,9},{9,8},{10,11... | collective-permute-start | bytes 294920 | tf_op jit(solution)/shard_map/ppermute | solution.py:443
  41.3 1.6 %collective-permute-start.20 = (bf16[192,256]{1,0:T(8,128)(2,1)S(1)}, bf16[192,256]{1,0:T(8,128)(2,1)S(1)}, u32[]{:S(2)}, u32[]{:S(2)}) collective-permute-start(bf16[192,256]{1,0:T(8,128)(2,1)S(1)} %collective-permute-done.19.refs_2_), channel_id=1, source_target_pairs={{0,1},{1,0},{2,3},{3,2},{4,5},{5,4},{6,7},{7,6},{8,9},{9,8},{10,11... | collective-permute-start | bytes 294920 | tf_op jit(solution)/shard_map/ppermute | solution.py:443
  41.3 1.6 %collective-permute-start.22 = (bf16[192,256]{1,0:T(8,128)(2,1)S(1)}, bf16[192,256]{1,0:T(8,128)(2,1)S(1)}, u32[]{:S(2)}, u32[]{:S(2)}) collective-permute-start(bf16[192,256]{1,0:T(8,128)(2,1)S(1)} %collective-permute-done.21.refs_3_), channel_id=1, source_target_pairs={{0,1},{1,0},{2,3},{3,2},{4,5},{5,4},{6,7},{7,6},{8,9},{9,8},{10,11... | collective-permute-start | bytes 294920 | tf_op jit(solution)/shard_map/ppermute | solution.py:443
  43.7 7.1 %collective-permute-start.26 = (bf16[48,1024]{1,0:T(8,128)(2,1)S(1)}, bf16[48,1024]{1,0:T(8,128)(2,1)S(1)}, u32[]{:S(2)}, u32[]{:S(2)}) collective-permute-start(bf16[48,1024]{1,0:T(8,128)(2,1)S(1)} %get-tuple-element.99), channel_id=1, source_target_pairs={{0,24},{8,0},{16,8},{24,16},{1,25},{9,1},{17,9},{25,17},{2,26},{10... | collective-permute-start | bytes 294920 | tf_op jit(solution)/shard_map/ppermute | solution.py:548
  47.7 9.3 %collective-permute-start.25 = (bf16[48,1024]{1,0:T(8,128)(2,1)S(1)}, bf16[48,1024]{1,0:T(8,128)(2,1)S(1)}, u32[]{:S(2)}, u32[]{:S(2)}) collective-permute-start(bf16[48,1024]{1,0:T(8,128)(2,1)S(1)} %get-tuple-element.98), channel_id=1, source_target_pairs={{0,16},{8,24},{16,0},{24,8},{1,17},{9,25},{17,1},{25,9},{2,18},{10... | collective-permute-start | bytes 294920 | tf_op jit(solution)/shard_map/ppermute | solution.py:548
  47.7 9.3 %collective-permute-start.24 = (bf16[48,1024]{1,0:T(8,128)(2,1)S(1)}, bf16[48,1024]{1,0:T(8,128)(2,1)S(1)}, u32[]{:S(2)}, u32[]{:S(2)}) collective-permute-start(bf16[48,1024]{1,0:T(8,128)(2,1)S(1)} %get-tuple-element.97), channel_id=1, source_target_pairs={{0,8},{8,16},{16,24},{24,0},{1,9},{9,17},{17,25},{25,1},{2,10},{10... | collective-permute-start | bytes 294920 | tf_op jit(solution)/shard_map/ppermute | solution.py:548
  (14 other events, 86.7 us)

commit v11 on v9

--- a/solution.py
+++ b/solution.py
@@ -456,7 +456,7 @@
 
     own_text = text[0]
     depth = own_text.shape[1]
-    cuts = (0, depth * 7 // 16, depth * 3 // 4, depth)
+    cuts = (0, depth * 7 // 16, depth * 11 // 16, depth)
     direct = {1 << s: exchange(own_text, distance(1 << s)) for s in range(steps)}
 
     def both_cores(blocks):

time: 56 us -> 56.4 us (level)
  transfers between devices with their start and end apart: 27 -> 27, of which waited for: 12 -> 11; matrix products, arithmetic and copies ran while one was open for 0% -> 0% of each run, Pallas kernels for 19% -> 19%
where the time goes in v11:
time: 56.4 us; the launch traced here: 56.2 us
  starting transfers between devices  22.2 us (39%)
  waiting for transfers between devices  16.2 us (29%)
  Pallas kernels  12.8 us (23%)
  local copies, waits for them, and re-layouts  3.29 us (6%)
  between operations  0.9 us (2%)
  other arithmetic  0.72 us (1%)
    ppermute x24, starting transfers between devices, exchange(): lax.ppermute(x, 'tensor', [(i, i ^ pair[i % 2]) for i in range(count)])  16.1 us
    ppermute x24, waiting for transfers between devices, exchange(): lax.ppermute(x, 'tensor', [(i, i ^ pair[i % 2]) for i in range(count)])  11.4 us
    ppermute x3, starting transfers between devices, shards(): arrived.append(lax.ppermute(leaving[k - 1], 'section', perm))  6.07 us
    pallas_call x4, Pallas kernels, queries_of(): pl.pallas_call(functools.partial(query_kernel, [len(parts) for parts in g...  5.75 us
    ppermute x3, waiting for transfers between devices, shards(): arrived.append(lax.ppermute(leaving[k - 1], 'section', perm))  4.77 us
    unnamed x22, local copies, waits for them, and re-layouts  3.22 us
    pallas_call x2, Pallas kernels, attention(): pl.pallas_call(functools.partial(attention_kernel, places, count, rows, l...  2.78 us
    pallas_call x2, Pallas kernels, feature_gradient(): pl.pallas_call(functools.partial(grad_kernel, pairs, per_kv, sections, be...  1.89 us
  transfers between devices with their start and end apart: 27, of which 11 were waited for; matrix products, arithmetic and copies ran while one was open for 0% of the time, Pallas kernels for 19%

profile of v11, /device:TPU:0, one launch (start us, length us, event | category | flops | bytes accessed | tf_op | source)
XLA Modules:
  0.0 56.2 jit_solution(6185109864029280259)
XLA Ops:
  0.6 3.0 %collective-permute-start.1 = (bf16[32,8192]{1,0:T(8,128)(2,1)}, bf16[32,8192]{1,0:T(8,128)(2,1)S(1)}, u32[]{:S(2)}, u32[]{:S(2)}) collective-permute-start(bf16[32,8192]{1,0:T(8,128)(2,1)} %bitcast.1), channel_id=1, source_target_pairs={{0,2},{1,5},{2,0},{3,7},{4,6},{5,1},{6,4},{7,3},{8,10},{9,13},{10,... | collective-permute-start | bytes 1572872 | tf_op jit(solution)/shard_map/ppermute | solution.py:443
  3.6 1.5 %collective-permute-start.2 = (bf16[32,8192]{1,0:T(8,128)(2,1)}, bf16[32,8192]{1,0:T(8,128)(2,1)S(1)}, u32[]{:S(2)}, u32[]{:S(2)}) collective-permute-start(bf16[32,8192]{1,0:T(8,128)(2,1)} %bitcast.2), channel_id=1, source_target_pairs={{0,4},{1,3},{2,6},{3,1},{4,0},{5,7},{6,2},{7,5},{8,12},{9,11},{10,... | collective-permute-start | bytes 1572872 | tf_op jit(solution)/shard_map/ppermute | solution.py:443
  5.2 2.2 %copy-done.1 = bf16[1,1024,2048]{2,1,0:T(8,128)(2,1)S(1)} copy-done((bf16[1,1024,2048]{2,1,0:T(8,128)(2,1)S(1)}, bf16[1,1024,2048]{2,1,0:T(8,128)(2,1)}, u32[]{:S(2)}) %copy-start.1) | copy-done | bytes 4194328
  7.4 1.0 %copy-done.3 = bf16[192,1024]{1,0:T(8,128)(2,1)S(1)} copy-done((bf16[192,1024]{1,0:T(8,128)(2,1)S(1)}, bf16[192,1024]{1,0:T(8,128)(2,1)}, u32[]{:S(2)}) %copy-start.3) | copy-done | bytes 393240
  13.8 1.3 %collective-permute-start.8 = (bf16[192,256]{1,0:T(8,128)(2,1)S(1)}, bf16[192,256]{1,0:T(8,128)(2,1)S(1)}, u32[]{:S(2)}, u32[]{:S(2)}) collective-permute-start(bf16[192,256]{1,0:T(8,128)(2,1)S(1)} %get-tuple-element.57), channel_id=1, source_target_pairs={{0,2},{1,5},{2,0},{3,7},{4,6},{5,1},{6,4},{7,3},{8,10},{9,13},{10,... | collective-permute-start | bytes 294920 | tf_op jit(solution)/shard_map/ppermute | solution.py:443
  15.1 2.6 %collective-permute-done.7.refs_2_ = bf16[192,256]{1,0:T(8,128)(2,1)S(1)} collective-permute-done((bf16[192,256]{1,0:T(8,128)(2,1)S(1)}, bf16[192,256]{1,0:T(8,128)(2,1)S(1)}, u32[]{:S(2)}, u32[]{:S(2)}) %collective-permute-start.7) | collective-permute-done | bytes 98336 | tf_op jit(solution)/shard_map/ppermute | solution.py:443
  17.7 1.1 %collective-permute-done.8.refs_3_ = bf16[192,256]{1,0:T(8,128)(2,1)S(1)} collective-permute-done((bf16[192,256]{1,0:T(8,128)(2,1)S(1)}, bf16[192,256]{1,0:T(8,128)(2,1)S(1)}, u32[]{:S(2)}, u32[]{:S(2)}) %collective-permute-start.8) | collective-permute-done | bytes 98336 | tf_op jit(solution)/shard_map/ppermute | solution.py:443
  19.3 1.1 %collective-permute-start.9 = (bf16[32,3584]{1,0:T(8,128)(2,1)S(1)}, bf16[32,3584]{1,0:T(8,128)(2,1)S(1)}, u32[]{:S(2)}, u32[]{:S(2)}) collective-permute-start(bf16[32,3584]{1,0:T(8,128)(2,1)S(1)} %slice.12), channel_id=1, source_target_pairs={{0,4},{1,3},{2,6},{3,1},{4,0},{5,7},{6,2},{7,5},{8,12},{9,11},{10,... | collective-permute-start | bytes 688136 | tf_op jit(solution)/shard_map/ppermute | solution.py:443
  20.4 1.1 %collective-permute-start.10 = (bf16[192,256]{1,0:T(8,128)(2,1)S(1)}, bf16[192,256]{1,0:T(8,128)(2,1)S(1)}, u32[]{:S(2)}, u32[]{:S(2)}) collective-permute-start(bf16[192,256]{1,0:T(8,128)(2,1)S(1)} %get-tuple-element.64), channel_id=1, source_target_pairs={{0,4},{1,3},{2,6},{3,1},{4,0},{5,7},{6,2},{7,5},{8,12},{9,11},{10,... | collective-permute-start | bytes 294920 | tf_op jit(solution)/shard_map/ppermute | solution.py:443
  21.5 1.1 %collective-permute-start.13 = (bf16[32,4608]{1,0:T(8,128)(2,1)S(1)}, bf16[32,4608]{1,0:T(8,128)(2,1)S(1)}, u32[]{:S(2)}, u32[]{:S(2)}) collective-permute-start(bf16[32,4608]{1,0:T(8,128)(2,1)S(1)} %slice.13), channel_id=1, source_target_pairs={{0,4},{1,3},{2,6},{3,1},{4,0},{5,7},{6,2},{7,5},{8,12},{9,11},{10,... | collective-permute-start | bytes 884744 | tf_op jit(solution)/shard_map/ppermute | solution.py:443
  22.6 2.5 %queries_own_chip.1 = (bf16[64,512]{1,0:T(8,128)(2,1)S(1)}, f32[256,128]{1,0:T(8,128)S(1)}, f32[2,8,96]{2,1,0:T(8,128)S(1)}) custom-call(s32[2]{0:T(128)S(1)} %copy-done.9, s32[2]{0:T(128)S(1)} %copy-done.10, bf16[1,8192]{1,0:T(2,128)(2,1)S(1)} %copy-done.5, bf16[1,8192,512]{2,1,0:T(8,128)(2,1)S(1)} %copy-done, bf16[1,128]{1,0:T(2,128)(2,1)S(1)} %copy-done.7, ...), custom_call_target="tpu_custom_call" | custom-call | tf_op jit(solution)/shard_map/queries_own_chip/pallas_call | solution.py:208
  25.1 2.0 %queries_neighbours.1.refs_3_ = bf16[128,512]{1,0:T(8,128)(2,1)S(1)} custom-call(bf16[1,8192]{1,0:T(2,128)(2,1)S(1)} %copy-done.5, bf16[1,8192,512]{2,1,0:T(8,128)(2,1)S(1)} %copy-done, bf16[1,128]{1,0:T(2,128)(2,1)S(1)} %copy-done.7, bf16[32,8192]{1,0:T(8,128)(2,1)S(1)} %collective-permute-done.1.refs_3_, ...), custom_call_target="tpu_custom_call" | custom-call | tf_op jit(solution)/shard_map/queries_neighbours/pallas_call | solution.py:208
  27.5 1.3 %attention_first.1 = (f32[192,512]{1,0:T(8,128)S(1)}, f32[192,128]{1,0:T(8,128)S(1)}, f32[192,128]{1,0:T(8,128)S(1)}, bf16[192,128]{1,0:T(8,128)(2,1)S(1)}, bf16...) custom-call(f32[256,128]{1,0:T(8,128)S(1)} %get-tuple-element.50.refs_0_, ...), custom_call_target="tpu_custom_call" | custom-call | tf_op jit(solution)/shard_map/attention_first/pallas_call | solution.py:334
  30.3 1.1 %collective-permute-done.16.refs_4_ = bf16[32,2048]{1,0:T(8,128)(2,1)S(1)} collective-permute-done((bf16[32,2048]{1,0:T(8,128)(2,1)S(1)}, bf16[32,2048]{1,0:T(8,128)(2,1)S(1)}, u32[]{:S(2)}, u32[]{:S(2)}) %collective-permute-start.16) | collective-permute-done | bytes 131104 | tf_op jit(solution)/shard_map/ppermute | solution.py:443
  31.9 1.5 %attention_last.1 = (f32[64,512]{1,0:T(8,128)S(1)}, bf16[192,256]{1,0:T(8,128)(2,1)S(1)}) custom-call(f32[256,128]{1,0:T(8,128)S(1)} %get-tuple-element.50.refs_0_, f32[2,8,96]{2,1,0:T(8,128)S(1)} %get-tuple-element.51.refs_1_, bf16[1,8192]{1,0:T(2,128)(2,1)S(1)} %copy-done.5, bf16[1,8192,512]{2,1,0:T(8,128)(2,1)S(1)} %copy-done, ...), custom_call_target="tpu_custom_call" | custom-call | tf_op jit(solution)/shard_map/attention_last/pallas_call | solution.py:334
  33.3 2.6 %collective-permute-start.17 = (bf16[192,256]{1,0:T(8,128)(2,1)S(1)}, bf16[192,256]{1,0:T(8,128)(2,1)S(1)}, u32[]{:S(2)}, u32[]{:S(2)}) collective-permute-start(bf16[192,256]{1,0:T(8,128)(2,1)S(1)} %get-tuple-element.93.refs_0_), channel_id=1, source_target_pairs={{0,6},{1,7},{2,4},{3,5},{4,2},{5,3},{6,0},{7,1},{8,14},{9,15},{10,... | collective-permute-start | bytes 294920 | tf_op jit(solution)/shard_map/ppermute | solution.py:443
  36.9 2.8 %collective-permute-done.17.refs_1_ = bf16[192,256]{1,0:T(8,128)(2,1)S(1)} collective-permute-done((bf16[192,256]{1,0:T(8,128)(2,1)S(1)}, bf16[192,256]{1,0:T(8,128)(2,1)S(1)}, u32[]{:S(2)}, u32[]{:S(2)}) %collective-permute-start.17) | collective-permute-done | bytes 98336 | tf_op jit(solution)/shard_map/ppermute | solution.py:443
  39.7 1.7 %collective-permute-done.19.refs_2_ = bf16[192,256]{1,0:T(8,128)(2,1)S(1)} collective-permute-done((bf16[192,256]{1,0:T(8,128)(2,1)S(1)}, bf16[192,256]{1,0:T(8,128)(2,1)S(1)}, u32[]{:S(2)}, u32[]{:S(2)}) %collective-permute-start.19) | collective-permute-done | bytes 98336 | tf_op jit(solution)/shard_map/ppermute | solution.py:443
  41.9 1.1 %feature_grad_first.1.refs_4_ = f32[192,1024]{1,0:T(8,128)S(1)} custom-call(bf16[192,256]{1,0:T(8,128)(2,1)S(1)} %get-tuple-element.93.refs_0_, bf16[192,256]{1,0:T(8,128)(2,1)S(1)} %collective-permute-done.17.refs_1_, bf16[192,256]{1,0:T(8,128)(2,1)S(1)} %collective-permute-done.19.refs_2_, bf16[192,256]{1,0:T(8,128)(2,1)S(1)} %collective-permute-done.21.refs_3_, ...), custom_call_target="tpu_custom_call" | custom-call | tf_op jit(solution)/shard_map/feature_grad_first/pallas_call | solution.py:423
  43.8 2.1 %collective-permute-start.24 = (bf16[48,1024]{1,0:T(8,128)(2,1)S(1)}, bf16[48,1024]{1,0:T(8,128)(2,1)S(1)}, u32[]{:S(2)}, u32[]{:S(2)}) collective-permute-start(bf16[48,1024]{1,0:T(8,128)(2,1)S(1)} %get-tuple-element.95), channel_id=1, source_target_pairs={{0,8},{8,16},{16,24},{24,0},{1,9},{9,17},{17,25},{25,1},{2,10},{10... | collective-permute-start | bytes 294920 | tf_op jit(solution)/shard_map/ppermute | solution.py:548
  46.0 2.6 %collective-permute-start.25 = (bf16[48,1024]{1,0:T(8,128)(2,1)S(1)}, bf16[48,1024]{1,0:T(8,128)(2,1)S(1)}, u32[]{:S(2)}, u32[]{:S(2)}) collective-permute-start(bf16[48,1024]{1,0:T(8,128)(2,1)S(1)} %get-tuple-element.96), channel_id=1, source_target_pairs={{0,16},{8,24},{16,0},{24,8},{1,17},{9,25},{17,1},{25,9},{2,18},{10... | collective-permute-start | bytes 294920 | tf_op jit(solution)/shard_map/ppermute | solution.py:548
  48.6 1.3 %collective-permute-start.26 = (bf16[48,1024]{1,0:T(8,128)(2,1)S(1)}, bf16[48,1024]{1,0:T(8,128)(2,1)S(1)}, u32[]{:S(2)}, u32[]{:S(2)}) collective-permute-start(bf16[48,1024]{1,0:T(8,128)(2,1)S(1)} %get-tuple-element.97), channel_id=1, source_target_pairs={{0,24},{8,0},{16,8},{24,16},{1,25},{9,1},{17,9},{25,17},{2,26},{10... | collective-permute-start | bytes 294920 | tf_op jit(solution)/shard_map/ppermute | solution.py:548
  50.7 1.0 %collective-permute-done.24 = bf16[48,1024]{1,0:T(8,128)(2,1)S(1)} collective-permute-done((bf16[48,1024]{1,0:T(8,128)(2,1)S(1)}, bf16[48,1024]{1,0:T(8,128)(2,1)S(1)}, u32[]{:S(2)}, u32[]{:S(2)}) %collective-permute-start.24) | collective-permute-done | bytes 98336 | tf_op jit(solution)/shard_map/ppermute | solution.py:548
  51.7 3.8 %collective-permute-done.25 = bf16[48,1024]{1,0:T(8,128)(2,1)S(1)} collective-permute-done((bf16[48,1024]{1,0:T(8,128)(2,1)S(1)}, bf16[48,1024]{1,0:T(8,128)(2,1)S(1)}, u32[]{:S(2)}, u32[]{:S(2)}) %collective-permute-start.25) | collective-permute-done | bytes 98336 | tf_op jit(solution)/shard_map/ppermute | solution.py:548
  (69 shorter events, 12.1 us)
Async XLA Ops:
  0.6 18.1 %collective-permute-start.1 = (bf16[32,8192]{1,0:T(8,128)(2,1)}, bf16[32,8192]{1,0:T(8,128)(2,1)S(1)}, u32[]{:S(2)}, u32[]{:S(2)}) collective-permute-start(bf16[32,8192]{1,0:T(8,128)(2,1)} %bitcast.1), channel_id=1, source_target_pairs={{0,2},{1,5},{2,0},{3,7},{4,6},{5,1},{6,4},{7,3},{8,10},{9,13},{10,... | collective-permute-start | bytes 1572872 | tf_op jit(solution)/shard_map/ppermute | solution.py:443
  3.6 15.1 %collective-permute-start.2 = (bf16[32,8192]{1,0:T(8,128)(2,1)}, bf16[32,8192]{1,0:T(8,128)(2,1)S(1)}, u32[]{:S(2)}, u32[]{:S(2)}) collective-permute-start(bf16[32,8192]{1,0:T(8,128)(2,1)} %bitcast.2), channel_id=1, source_target_pairs={{0,4},{1,3},{2,6},{3,1},{4,0},{5,7},{6,2},{7,5},{8,12},{9,11},{10,... | collective-permute-start | bytes 1572872 | tf_op jit(solution)/shard_map/ppermute | solution.py:443
  9.2 1.5 %collective-permute-start.3 = (f32[192,256]{1,0:T(8,128)S(1)}, f32[192,256]{1,0:T(8,128)S(1)}, u32[]{:S(2)}, u32[]{:S(2)}) collective-permute-start(f32[192,256]{1,0:T(8,128)S(1)} %get-tuple-element.52), channel_id=1, source_target_pairs={{0,1},{1,0},{2,3},{3,2},{4,5},{5,4},{6,7},{7,6},{8,9},{9,8},{10,11... | collective-permute-start | bytes 589832 | tf_op jit(solution)/shard_map/ppermute | solution.py:443
  9.3 1.7 %collective-permute-start.4 = (f32[192,256]{1,0:T(8,128)S(1)}, f32[192,256]{1,0:T(8,128)S(1)}, u32[]{:S(2)}, u32[]{:S(2)}) collective-permute-start(f32[192,256]{1,0:T(8,128)S(1)} %get-tuple-element.53), channel_id=1, source_target_pairs={{0,1},{1,0},{2,3},{3,2},{4,5},{5,4},{6,7},{7,6},{8,9},{9,8},{10,11... | collective-permute-start | bytes 589832 | tf_op jit(solution)/shard_map/ppermute | solution.py:443
  13.0 4.7 %collective-permute-start.7 = (bf16[192,256]{1,0:T(8,128)(2,1)S(1)}, bf16[192,256]{1,0:T(8,128)(2,1)S(1)}, u32[]{:S(2)}, u32[]{:S(2)}) collective-permute-start(bf16[192,256]{1,0:T(8,128)(2,1)S(1)} %get-tuple-element.56), channel_id=1, source_target_pairs={{0,2},{1,5},{2,0},{3,7},{4,6},{5,1},{6,4},{7,3},{8,10},{9,13},{10,... | collective-permute-start | bytes 294920 | tf_op jit(solution)/shard_map/ppermute | solution.py:443
  13.8 4.9 %collective-permute-start.8 = (bf16[192,256]{1,0:T(8,128)(2,1)S(1)}, bf16[192,256]{1,0:T(8,128)(2,1)S(1)}, u32[]{:S(2)}, u32[]{:S(2)}) collective-permute-start(bf16[192,256]{1,0:T(8,128)(2,1)S(1)} %get-tuple-element.57), channel_id=1, source_target_pairs={{0,2},{1,5},{2,0},{3,7},{4,6},{5,1},{6,4},{7,3},{8,10},{9,13},{10,... | collective-permute-start | bytes 294920 | tf_op jit(solution)/shard_map/ppermute | solution.py:443
  15.1 6.5 %collective-permute-start = (bf16[32,8192]{1,0:T(8,128)(2,1)S(1)}, bf16[32,8192]{1,0:T(8,128)(2,1)S(1)}, u32[]{:S(2)}, u32[]{:S(2)}) collective-permute-start(bf16[32,8192]{1,0:T(8,128)(2,1)S(1)} %bitcast.3), channel_id=1, source_target_pairs={{0,1},{1,0},{2,3},{3,2},{4,5},{5,4},{6,7},{7,6},{8,9},{9,8},{10,11... | collective-permute-start | bytes 1572872 | tf_op jit(solution)/shard_map/ppermute | solution.py:443
  18.7 6.4 %collective-permute-start.11 = (bf16[32,8192]{1,0:T(8,128)(2,1)S(1)}, bf16[32,8192]{1,0:T(8,128)(2,1)S(1)}, u32[]{:S(2)}, u32[]{:S(2)}) collective-permute-start(bf16[32,8192]{1,0:T(8,128)(2,1)S(1)} %collective-permute-done.1.refs_3_), channel_id=1, source_target_pairs={{0,1},{1,0},{2,3},{3,2},{4,5},{5,4},{6,7},{7,6},{8,9},{9,8},{10,11... | collective-permute-start | bytes 1572872 | tf_op jit(solution)/shard_map/ppermute | solution.py:443
  18.8 6.4 %collective-permute-start.12 = (bf16[32,8192]{1,0:T(8,128)(2,1)S(1)}, bf16[32,8192]{1,0:T(8,128)(2,1)S(1)}, u32[]{:S(2)}, u32[]{:S(2)}) collective-permute-start(bf16[32,8192]{1,0:T(8,128)(2,1)S(1)} %collective-permute-done.2.refs_5_), channel_id=1, source_target_pairs={{0,1},{1,0},{2,3},{3,2},{4,5},{5,4},{6,7},{7,6},{8,9},{9,8},{10,11... | collective-permute-start | bytes 1572872 | tf_op jit(solution)/shard_map/ppermute | solution.py:443
  19.3 7.9 %collective-permute-start.9 = (bf16[32,3584]{1,0:T(8,128)(2,1)S(1)}, bf16[32,3584]{1,0:T(8,128)(2,1)S(1)}, u32[]{:S(2)}, u32[]{:S(2)}) collective-permute-start(bf16[32,3584]{1,0:T(8,128)(2,1)S(1)} %slice.12), channel_id=1, source_target_pairs={{0,4},{1,3},{2,6},{3,1},{4,0},{5,7},{6,2},{7,5},{8,12},{9,11},{10,... | collective-permute-start | bytes 688136 | tf_op jit(solution)/shard_map/ppermute | solution.py:443
  20.4 6.8 %collective-permute-start.10 = (bf16[192,256]{1,0:T(8,128)(2,1)S(1)}, bf16[192,256]{1,0:T(8,128)(2,1)S(1)}, u32[]{:S(2)}, u32[]{:S(2)}) collective-permute-start(bf16[192,256]{1,0:T(8,128)(2,1)S(1)} %get-tuple-element.64), channel_id=1, source_target_pairs={{0,4},{1,3},{2,6},{3,1},{4,0},{5,7},{6,2},{7,5},{8,12},{9,11},{10,... | collective-permute-start | bytes 294920 | tf_op jit(solution)/shard_map/ppermute | solution.py:443
  21.5 8.1 %collective-permute-start.13 = (bf16[32,4608]{1,0:T(8,128)(2,1)S(1)}, bf16[32,4608]{1,0:T(8,128)(2,1)S(1)}, u32[]{:S(2)}, u32[]{:S(2)}) collective-permute-start(bf16[32,4608]{1,0:T(8,128)(2,1)S(1)} %slice.13), channel_id=1, source_target_pairs={{0,4},{1,3},{2,6},{3,1},{4,0},{5,7},{6,2},{7,5},{8,12},{9,11},{10,... | collective-permute-start | bytes 884744 | tf_op jit(solution)/shard_map/ppermute | solution.py:443
  27.2 1.6 %collective-permute-start.14 = (bf16[32,3584]{1,0:T(8,128)(2,1)S(1)}, bf16[32,3584]{1,0:T(8,128)(2,1)S(1)}, u32[]{:S(2)}, u32[]{:S(2)}) collective-permute-start(bf16[32,3584]{1,0:T(8,128)(2,1)S(1)} %collective-permute-done.9.refs_3_), channel_id=1, source_target_pairs={{0,1},{1,0},{2,3},{3,2},{4,5},{5,4},{6,7},{7,6},{8,9},{9,8},{10,11... | collective-permute-start | bytes 688136 | tf_op jit(solution)/shard_map/ppermute | solution.py:443
  29.6 2.2 %collective-permute-start.15 = (bf16[32,2560]{1,0:T(8,128)(2,1)S(1)}, bf16[32,2560]{1,0:T(8,128)(2,1)S(1)}, u32[]{:S(2)}, u32[]{:S(2)}) collective-permute-start(bf16[32,2560]{1,0:T(8,128)(2,1)S(1)} %slice.14.refs_5_), channel_id=1, source_target_pairs={{0,1},{1,0},{2,3},{3,2},{4,5},{5,4},{6,7},{7,6},{8,9},{9,8},{10,11... | collective-permute-start | bytes 491528 | tf_op jit(solution)/shard_map/ppermute | solution.py:443
  33.3 6.3 %collective-permute-start.17 = (bf16[192,256]{1,0:T(8,128)(2,1)S(1)}, bf16[192,256]{1,0:T(8,128)(2,1)S(1)}, u32[]{:S(2)}, u32[]{:S(2)}) collective-permute-start(bf16[192,256]{1,0:T(8,128)(2,1)S(1)} %get-tuple-element.93.refs_0_), channel_id=1, source_target_pairs={{0,6},{1,7},{2,4},{3,5},{4,2},{5,3},{6,0},{7,1},{8,14},{9,15},{10,... | collective-permute-start | bytes 294920 | tf_op jit(solution)/shard_map/ppermute | solution.py:443
  35.9 5.5 %collective-permute-start.19 = (bf16[192,256]{1,0:T(8,128)(2,1)S(1)}, bf16[192,256]{1,0:T(8,128)(2,1)S(1)}, u32[]{:S(2)}, u32[]{:S(2)}) collective-permute-start(bf16[192,256]{1,0:T(8,128)(2,1)S(1)} %get-tuple-element.93.refs_0_), channel_id=1, source_target_pairs={{0,4},{1,3},{2,6},{3,1},{4,0},{5,7},{6,2},{7,5},{8,12},{9,11},{10,... | collective-permute-start | bytes 294920 | tf_op jit(solution)/shard_map/ppermute | solution.py:443
  36.8 4.6 %collective-permute-start.21 = (bf16[192,256]{1,0:T(8,128)(2,1)S(1)}, bf16[192,256]{1,0:T(8,128)(2,1)S(1)}, u32[]{:S(2)}, u32[]{:S(2)}) collective-permute-start(bf16[192,256]{1,0:T(8,128)(2,1)S(1)} %get-tuple-element.93.refs_0_), channel_id=1, source_target_pairs={{0,2},{1,5},{2,0},{3,7},{4,6},{5,1},{6,4},{7,3},{8,10},{9,13},{10,... | collective-permute-start | bytes 294920 | tf_op jit(solution)/shard_map/ppermute | solution.py:443
  36.9 5.0 %collective-permute-start.23 = (bf16[192,256]{1,0:T(8,128)(2,1)S(1)}, bf16[192,256]{1,0:T(8,128)(2,1)S(1)}, u32[]{:S(2)}, u32[]{:S(2)}) collective-permute-start(bf16[192,256]{1,0:T(8,128)(2,1)S(1)} %get-tuple-element.93.refs_0_), channel_id=1, source_target_pairs={{0,1},{1,0},{2,3},{3,2},{4,5},{5,4},{6,7},{7,6},{8,9},{9,8},{10,11... | collective-permute-start | bytes 294920 | tf_op jit(solution)/shard_map/ppermute | solution.py:443
  39.7 3.3 %collective-permute-start.18 = (bf16[192,256]{1,0:T(8,128)(2,1)S(1)}, bf16[192,256]{1,0:T(8,128)(2,1)S(1)}, u32[]{:S(2)}, u32[]{:S(2)}) collective-permute-start(bf16[192,256]{1,0:T(8,128)(2,1)S(1)} %collective-permute-done.17.refs_1_), channel_id=1, source_target_pairs={{0,1},{1,0},{2,3},{3,2},{4,5},{5,4},{6,7},{7,6},{8,9},{9,8},{10,11... | collective-permute-start | bytes 294920 | tf_op jit(solution)/shard_map/ppermute | solution.py:443
  41.4 1.6 %collective-permute-start.20 = (bf16[192,256]{1,0:T(8,128)(2,1)S(1)}, bf16[192,256]{1,0:T(8,128)(2,1)S(1)}, u32[]{:S(2)}, u32[]{:S(2)}) collective-permute-start(bf16[192,256]{1,0:T(8,128)(2,1)S(1)} %collective-permute-done.19.refs_2_), channel_id=1, source_target_pairs={{0,1},{1,0},{2,3},{3,2},{4,5},{5,4},{6,7},{7,6},{8,9},{9,8},{10,11... | collective-permute-start | bytes 294920 | tf_op jit(solution)/shard_map/ppermute | solution.py:443
  41.4 1.6 %collective-permute-start.22 = (bf16[192,256]{1,0:T(8,128)(2,1)S(1)}, bf16[192,256]{1,0:T(8,128)(2,1)S(1)}, u32[]{:S(2)}, u32[]{:S(2)}) collective-permute-start(bf16[192,256]{1,0:T(8,128)(2,1)S(1)} %collective-permute-done.21.refs_3_), channel_id=1, source_target_pairs={{0,1},{1,0},{2,3},{3,2},{4,5},{5,4},{6,7},{7,6},{8,9},{9,8},{10,11... | collective-permute-start | bytes 294920 | tf_op jit(solution)/shard_map/ppermute | solution.py:443
  43.8 7.8 %collective-permute-start.24 = (bf16[48,1024]{1,0:T(8,128)(2,1)S(1)}, bf16[48,1024]{1,0:T(8,128)(2,1)S(1)}, u32[]{:S(2)}, u32[]{:S(2)}) collective-permute-start(bf16[48,1024]{1,0:T(8,128)(2,1)S(1)} %get-tuple-element.95), channel_id=1, source_target_pairs={{0,8},{8,16},{16,24},{24,0},{1,9},{9,17},{17,25},{25,1},{2,10},{10... | collective-permute-start | bytes 294920 | tf_op jit(solution)/shard_map/ppermute | solution.py:548
  46.0 9.5 %collective-permute-start.25 = (bf16[48,1024]{1,0:T(8,128)(2,1)S(1)}, bf16[48,1024]{1,0:T(8,128)(2,1)S(1)}, u32[]{:S(2)}, u32[]{:S(2)}) collective-permute-start(bf16[48,1024]{1,0:T(8,128)(2,1)S(1)} %get-tuple-element.96), channel_id=1, source_target_pairs={{0,16},{8,24},{16,0},{24,8},{1,17},{9,25},{17,1},{25,9},{2,18},{10... | collective-permute-start | bytes 294920 | tf_op jit(solution)/shard_map/ppermute | solution.py:548
  48.6 6.9 %collective-permute-start.26 = (bf16[48,1024]{1,0:T(8,128)(2,1)S(1)}, bf16[48,1024]{1,0:T(8,128)(2,1)S(1)}, u32[]{:S(2)}, u32[]{:S(2)}) collective-permute-start(bf16[48,1024]{1,0:T(8,128)(2,1)S(1)} %get-tuple-element.97), channel_id=1, source_target_pairs={{0,24},{8,0},{16,8},{24,16},{1,25},{9,1},{17,9},{25,17},{2,26},{10... | collective-permute-start | bytes 294920 | tf_op jit(solution)/shard_map/ppermute | solution.py:548
  (14 other events, 117.1 us)
